TPU v7x, 32 devices: a whole 2x2x4 slice. The times are simulated.
32 devices in a mesh: patch: 8 (over z, y), level: 4 (over x, core).
Axes of the slice: x: 2, y: 2, z: 4, core: 2. Of those that a mesh axis runs over, the one named last changes fastest.
Arguments:
- forcing: bfloat16 [4, 64, 2, 128, 128], P('level', 'patch'), may hold values from -24 to 24
- velocity: bfloat16 [4, 64, 2, 128, 128], P('level', 'patch'), may hold values from -18 to 18
- viscosity: float32 [4, 64, 128, 128], P('level', 'patch'), may hold values from 0.3 to 3
- friction: bfloat16 [4, 64, 128, 128], P('level', 'patch'), may hold values from 0.049804688 to 1
- patch_rows: int32 [4, 8], replicated, may hold values from 0 to 8, as said below
Outputs:
- adjoint: float32 [4, 64, 2, 128, 128], P('level', 'patch')
- gradient: bfloat16 [4, 64, 128, 128], P('level', 'patch')
Inputs may be any that keep to these rules, and one draw needn't show every extreme that they name: patch_rows[l, p] is the number of live rows of level l on patch index p: at most 8 // 2**l, patch_rows[0, p] >= 1 and patch_rows[l + 1, p] <= 2 * patch_rows[l, p]; in every draw some patch index holds the most rows on every level.
All inputs are finite; a program needn't handle non-finite values.
Results may differ from a plain program's by a relative error of at most 0.0005.
Values may be sent and summed in bfloat16 or wider, within the bound.
No kernel may reach another device: no remote copies, remote signals or barrier semaphores. Data moves between devices by JAX's collectives and lax.ppermute only.
A program may use at most 128 MiB of HBM per device.

v0:
```python
import jax
import jax.numpy as jnp
from jax import lax
from jax.sharding import PartitionSpec as P

relaxation = 0.5


def passed_along(value, axis, steps):
    count = lax.axis_size(axis)
    first, last = (max(0, -steps), min(count, count - steps))
    return lax.ppermute(value, axis, [(source, source + steps) for source in range(first, last)])


def cell_at(grid, row_step, col_step):
    row_total = grid.shape[-2]
    col_total = grid.shape[-1]
    return grid[
        ..., 1 + row_step : row_total - 1 + row_step, 1 + col_step : col_total - 1 + col_step
    ]


def viscosity_faces(visc_loop):
    centre = cell_at(visc_loop, 0, 0)
    east_cell = cell_at(visc_loop, 0, 1)
    west_cell = cell_at(visc_loop, 0, -1)
    north_cell = cell_at(visc_loop, 1, 0)
    south_cell = cell_at(visc_loop, -1, 0)
    return (
        east_cell,
        west_cell,
        north_cell,
        south_cell,
        0.5 * (centre + east_cell),
        0.5 * (centre + west_cell),
        0.5 * (centre + north_cell),
        0.5 * (centre + south_cell),
    )


def diagonal_terms(face_values, friction_cells):
    east_cell, west_cell, north_cell, south_cell, face_east, face_west, face_north, face_south = (
        face_values
    )
    diag_u = 4.0 * (face_east + face_west) + face_north + face_south + friction_cells
    diag_v = 4.0 * (face_north + face_south) + face_east + face_west + friction_cells
    return jnp.stack([diag_u, diag_v], axis=1)


def operator_cells(loop_cells, face_values, friction_cells):
    east_cell, west_cell, north_cell, south_cell, face_east, face_west, face_north, face_south = (
        face_values
    )
    u_loop = loop_cells[:, 0]
    v_loop = loop_cells[:, 1]
    u_centre = cell_at(u_loop, 0, 0)
    u_east = cell_at(u_loop, 0, 1)
    u_west = cell_at(u_loop, 0, -1)
    u_north = cell_at(u_loop, 1, 0)
    u_south = cell_at(u_loop, -1, 0)
    u_northeast = cell_at(u_loop, 1, 1)
    u_northwest = cell_at(u_loop, 1, -1)
    u_southeast = cell_at(u_loop, -1, 1)
    u_southwest = cell_at(u_loop, -1, -1)
    v_centre = cell_at(v_loop, 0, 0)
    v_east = cell_at(v_loop, 0, 1)
    v_west = cell_at(v_loop, 0, -1)
    v_north = cell_at(v_loop, 1, 0)
    v_south = cell_at(v_loop, -1, 0)
    v_northeast = cell_at(v_loop, 1, 1)
    v_northwest = cell_at(v_loop, 1, -1)
    v_southeast = cell_at(v_loop, -1, 1)
    v_southwest = cell_at(v_loop, -1, -1)
    cross_u = (
        east_cell * (0.5 * (v_northeast - v_southeast))
        - west_cell * (0.5 * (v_northwest - v_southwest))
        + 0.5
        * (
            north_cell * (0.5 * (v_northeast - v_northwest))
            - south_cell * (0.5 * (v_southeast - v_southwest))
        )
    )
    cross_v = (
        north_cell * (0.5 * (u_northeast - u_northwest))
        - south_cell * (0.5 * (u_southeast - u_southwest))
        + 0.5
        * (
            east_cell * (0.5 * (u_northeast - u_southeast))
            - west_cell * (0.5 * (u_northwest - u_southwest))
        )
    )
    result_u = (
        -4.0 * (face_east * (u_east - u_centre) - face_west * (u_centre - u_west))
        - (face_north * (u_north - u_centre) - face_south * (u_centre - u_south))
        - cross_u
        + friction_cells * u_centre
    )
    result_v = (
        -4.0 * (face_north * (v_north - v_centre) - face_south * (v_centre - v_south))
        - (face_east * (v_east - v_centre) - face_west * (v_centre - v_west))
        - cross_v
        + friction_cells * v_centre
    )
    return jnp.stack([result_u, result_v], axis=1)


def assemble_loop(cells, edge_table, indices):
    (
        south_index,
        north_index,
        west_index,
        east_index,
        northeast_index,
        southeast_index,
        northwest_index,
        southwest_index,
    ) = indices
    side_cells = cells.shape[-1]
    south_row = edge_table[south_index]
    north_row = edge_table[north_index]
    west_col = edge_table[west_index]
    east_col = edge_table[east_index]
    corner_northeast = edge_table[northeast_index][:, :, 0]
    corner_southeast = edge_table[southeast_index][:, :, side_cells - 1]
    corner_northwest = edge_table[northwest_index][:, :, 0]
    corner_southwest = edge_table[southwest_index][:, :, side_cells - 1]
    middle = jnp.concatenate([west_col[..., None], cells, east_col[..., None]], axis=-1)
    bottom = jnp.concatenate(
        [corner_southwest[..., None], south_row, corner_southeast[..., None]], axis=-1
    )
    top_row = jnp.concatenate(
        [corner_northwest[..., None], north_row, corner_northeast[..., None]], axis=-1
    )
    return jnp.concatenate([bottom[:, :, None], middle, top_row[:, :, None]], axis=2)


def neighbour_slots(own_rows, left_rows, right_rows, columns, slot_count):
    slot_ids = jnp.arange(slot_count, dtype=jnp.int32)
    row_ids = slot_ids // columns
    col_ids = slot_ids % columns
    alive = row_ids < own_rows
    blank = 6 * slot_count
    inside_west = col_ids > 0
    inside_east = col_ids < columns - 1
    has_south = row_ids >= 1
    has_north = row_ids + 1 < own_rows

    def choose(condition, position):
        return jnp.where(condition & alive, position, blank)

    south_index = choose(has_south, slot_count + slot_ids - columns)
    north_index = choose(has_north, slot_ids + columns)
    west_index = jnp.where(
        inside_west,
        choose(alive, 3 * slot_count + slot_ids - 1),
        choose(row_ids < left_rows, 4 * slot_count + row_ids * columns + columns - 1),
    )
    east_index = jnp.where(
        inside_east,
        choose(alive, 2 * slot_count + slot_ids + 1),
        choose(row_ids < right_rows, 5 * slot_count + row_ids * columns),
    )
    northeast_index = jnp.where(
        inside_east,
        choose(has_north, 2 * slot_count + slot_ids + columns + 1),
        choose(row_ids + 1 < right_rows, 5 * slot_count + (row_ids + 1) * columns),
    )
    southeast_index = jnp.where(
        inside_east,
        choose(has_south, 2 * slot_count + slot_ids - columns + 1),
        choose(has_south & (row_ids - 1 < right_rows), 5 * slot_count + (row_ids - 1) * columns),
    )
    northwest_index = jnp.where(
        inside_west,
        choose(has_north, 3 * slot_count + slot_ids + columns - 1),
        choose(row_ids + 1 < left_rows, 4 * slot_count + (row_ids + 1) * columns + columns - 1),
    )
    southwest_index = jnp.where(
        inside_west,
        choose(has_south, 3 * slot_count + slot_ids - columns - 1),
        choose(
            has_south & (row_ids - 1 < left_rows),
            4 * slot_count + (row_ids - 1) * columns + columns - 1,
        ),
    )
    indices = (
        south_index,
        north_index,
        west_index,
        east_index,
        northeast_index,
        southeast_index,
        northwest_index,
        southwest_index,
    )
    return (indices, alive, row_ids, col_ids)


def with_ghosts(cells, indices):
    comps = cells.shape[1]
    side_cells = cells.shape[-1]
    south_edge = cells[:, :, 0, :]
    north_edge = cells[:, :, side_cells - 1, :]
    west_edge = cells[:, :, :, 0]
    east_edge = cells[:, :, :, side_cells - 1]
    edge_stack = jnp.stack([south_edge, north_edge, west_edge, east_edge])
    slot_count = edge_stack.shape[1]
    left_east = passed_along(edge_stack[3], "patch", 1)
    right_west = passed_along(edge_stack[2], "patch", -1)
    edge_table = jnp.concatenate(
        [
            edge_stack.reshape(4 * slot_count, comps, side_cells),
            left_east,
            right_west,
            jnp.zeros((1, comps, side_cells), cells.dtype),
        ],
        axis=0,
    )
    return assemble_loop(cells, edge_table, indices)


def join_quadrants(south_west, south_east, north_west, north_east):
    bottom = jnp.concatenate([south_west, south_east], axis=-1)
    top_half = jnp.concatenate([north_west, north_east], axis=-1)
    return jnp.concatenate([bottom, top_half], axis=-2)


def parent_total(slot_count, level_count):
    best = 1
    for tier_index in range(1, level_count):
        fine_columns = 2**tier_index
        fine_rows = slot_count // fine_columns
        needed = (fine_rows - 1) // 2 * (fine_columns // 2) + fine_columns // 2
        best = max(best, needed)
    return min(best, slot_count)


def per_device(forcing, velocity, viscosity, friction, patch_rows):
    level_index = lax.axis_index("level")
    patch_index = lax.axis_index("patch")
    level_count = lax.axis_size("level")
    slot_count = forcing.shape[1]
    side_cells = forcing.shape[-1]
    half_side = side_cells // 2
    columns = jnp.left_shift(jnp.int32(1), level_index)
    level_rows = lax.dynamic_index_in_dim(patch_rows, level_index, 0, keepdims=False)
    padded_rows = jnp.concatenate(
        [jnp.zeros((1,), jnp.int32), level_rows, jnp.zeros((1,), jnp.int32)]
    )
    near_rows = lax.dynamic_slice(padded_rows, (patch_index,), (3,))
    indices, alive, row_ids, col_ids = neighbour_slots(
        near_rows[1], near_rows[0], near_rows[2], columns, slot_count
    )
    live_mask = alive.astype(jnp.float32)[:, None, None, None]
    friction_cells = friction[0].astype(jnp.float32)
    finer_level = jnp.minimum(level_index + 1, level_count - 1)
    finer_all = lax.dynamic_index_in_dim(patch_rows, finer_level, 0, keepdims=False)
    finer_rows = lax.dynamic_index_in_dim(finer_all, patch_index, 0, keepdims=False)
    child_ids = []
    covers = []
    for quad_row in range(2):
        for quad_col in range(2):
            fine_row = 2 * row_ids + quad_row
            valid = alive & (fine_row < finer_rows)
            child = jnp.where(valid, fine_row * (2 * columns) + 2 * col_ids + quad_col, slot_count)
            child_ids.append(jnp.minimum(child, slot_count))
            covers.append(
                jnp.broadcast_to(
                    valid.astype(jnp.float32)[:, None, None, None],
                    (slot_count, 1, half_side, half_side),
                )
            )
    covered = join_quadrants(covers[0], covers[1], covers[2], covers[3])
    parent_count = parent_total(slot_count, level_count)
    parent_ids = jnp.minimum(row_ids // 2 * (columns // 2) + col_ids // 2, parent_count - 1)
    quad_row_of = (row_ids % 2)[:, None, None, None]
    quad_col_of = (col_ids % 2)[:, None, None, None]
    force_cells = forcing[0].astype(jnp.float32)
    visc_loop = with_ghosts(viscosity[0][:, None], indices)[:, 0]
    face_values = viscosity_faces(visc_loop)
    diagonal = diagonal_terms(face_values, friction_cells)

    def apply_here(cells):
        return operator_cells(with_ghosts(cells, indices), face_values, friction_cells)

    def smooth(right_side, start, from_zero):
        current = start
        if from_zero:
            current = live_mask * (relaxation * right_side / diagonal)
        else:
            current = live_mask * (
                current + relaxation * (right_side - apply_here(current)) / diagonal
            )
        return current

    zero_cells = jnp.zeros((slot_count, 2, side_cells, side_cells), jnp.float32)
    solution = zero_cells
    right_side = zero_cells
    restricted = jnp.zeros((slot_count, 2, half_side // 2, 2 * half_side), jnp.float32)
    for section in range(level_count - 1, -1, -1):
        active = level_index == section
        if section == level_count - 1:
            candidate = live_mask * force_cells
        else:
            received = passed_along(restricted, "level", -1)
            quads = received.reshape(slot_count, 2, half_side, half_side)
            quad_table = jnp.concatenate(
                [quads, jnp.zeros((1, 2, half_side, half_side), jnp.float32)], axis=0
            )
            placed = join_quadrants(
                quad_table[child_ids[0]],
                quad_table[child_ids[1]],
                quad_table[child_ids[2]],
                quad_table[child_ids[3]],
            )
            candidate = live_mask * ((1.0 - covered) * force_cells + placed)
        right_side = jnp.where(active, candidate, right_side)
        solution = jnp.where(active, smooth(right_side, zero_cells, True), solution)
        if section > 0:
            residual = live_mask * (right_side - apply_here(solution))
            summed = residual.reshape(slot_count, 2, half_side, 2, half_side, 2).sum(axis=(3, 5))
            restricted = summed.reshape(slot_count, 2, half_side // 2, 2 * half_side)
    for section in range(1, level_count):
        parents_here = passed_along(solution[:parent_count], "level", 1)
        parents = parents_here[parent_ids]
        half_rows = jnp.where(
            quad_row_of == 0, parents[:, :, :half_side, :], parents[:, :, half_side:, :]
        )
        quarter = jnp.where(
            quad_col_of == 0, half_rows[..., :half_side], half_rows[..., half_side:]
        )
        correction = jnp.repeat(jnp.repeat(quarter, 2, axis=2), 2, axis=3)
        active = level_index == section
        updated = smooth(right_side, solution + live_mask * correction, False)
        solution = jnp.where(active, updated, solution)
    speed = velocity[0].astype(jnp.float32)
    product = speed[:, 0] * solution[:, 0] + speed[:, 1] * solution[:, 1]
    gradient = (-(friction_cells * product) * live_mask[:, 0]).astype(jnp.bfloat16)
    return (solution[None], gradient[None])


def solution(mesh):
    in_specs = (
        P("level", "patch", None, None, None),
        P("level", "patch", None, None, None),
        P("level", "patch", None, None),
        P("level", "patch", None, None),
        P(),
    )
    out_specs = (P("level", "patch", None, None, None), P("level", "patch", None, None))
    return jax.shard_map(
        per_device, mesh=mesh, in_specs=in_specs, out_specs=out_specs, check_vma=False
    )
```

profile of v0, /device:TPU:6, one launch (start us, length us, event | category | flops | bytes accessed | tf_op | source)
XLA Modules:
  0.0 659.0 jit_solution(14127199690709377382)
XLA Ops:
  4.4 4.3 collective-permute-start
  14.8 3.1 fusion.202
  19.9 11.4 %copy.449 = f32[1,8,2,128,128]{1,4,3,2,0:T(8,128)} copy(bf16[1,8,2,128,128]{3,1,4,2,0:T(8,128)(2,1)S(1)} %copy.446) | data formatting | bytes 1572864 | tf_op jit(solution)/shard_map/convert_element_type | solution.py:278
  31.3 21.9 %copy.450 = f32[8,2,64,2,64,2]{4,2,5,3,1,0:T(8,128)} copy(f32[8,2,64,2,64,2]{0,5,4,3,2,1:T(2,128)} %bitcast.400) | data formatting | bytes 2097152 | tf_op jit(solution)/shard_map/convert_element_type | solution.py:278
  65.5 5.0 collective-permute-start.2
  89.9 8.3 %copy.472 = f32[8,128,128]{0,2,1:T(8,128)} copy(f32[8,128,128]{1,0,2:T(8,128)} %fusion.60) | data formatting | bytes 1048576 | tf_op jit(solution)/shard_map/add | solution.py:99
  98.2 11.5 %copy.474 = f32[8,1,64,2,64,2]{4,2,5,3,1,0:T(8,128)} copy(f32[8,1,64,2,64,2]{0,5,4,3,2,1:T(2,128)} %bitcast.419) | data formatting | bytes 1048576 | tf_op jit(solution)/shard_map/stack | solution.py:104
  109.7 8.3 %copy.471 = f32[8,128,128]{0,2,1:T(8,128)} copy(f32[8,128,128]{1,0,2:T(8,128)} %fusion.59) | data formatting | bytes 1048576 | tf_op jit(solution)/shard_map/add | solution.py:93
  118.0 11.5 %copy.473 = f32[8,1,64,2,64,2]{4,2,5,3,1,0:T(8,128)} copy(f32[8,1,64,2,64,2]{0,5,4,3,2,1:T(2,128)} %bitcast.420) | data formatting | bytes 1048576 | tf_op jit(solution)/shard_map/stack | solution.py:104
  129.5 3.6 fusion.1
  133.2 3.6 copy.607
  136.8 3.5 copy.476
  144.2 5.9 copy.447
  150.1 11.5 %copy.448 = f32[8,64,2,64,2]{3,1,4,2,0:T(8,128)} copy(f32[8,64,2,64,2]{0,4,3,2,1:T(2,128)} %bitcast.421) | data formatting | bytes 1048576 | tf_op jit(solution)/shard_map/sub | solution.py:316
  183.5 3.8 multiply_select_fusion.5
  190.9 5.2 collective-permute-start.5
  199.3 14.2 %copy.481 = f32[8,2,128,128]{0,3,2,1:T(8,128)} copy(f32[8,2,128,128]{2,0,3,1:T(8,128)} %get-tuple-element.22) | data formatting | bytes 2097152 | tf_op jit(solution)/shard_map/concatenate | solution.py:225
  213.6 21.9 %copy.482 = f32[8,2,64,2,64,2]{4,2,5,3,1,0:T(8,128)} copy(f32[8,2,64,2,64,2]{0,5,4,3,2,1:T(2,128)} %bitcast.401) | data formatting | bytes 2097152 | tf_op jit(solution)/shard_map/concatenate | solution.py:225
  244.7 2.8 pad_maximum_fusion.1
  251.8 8.3 %copy.498 = f32[8,128,128]{0,2,1:T(8,128)} copy(f32[8,128,128]{1,0,2:T(8,128)} %fusion.62) | data formatting | bytes 1048576 | tf_op jit(solution)/shard_map/add | solution.py:99
  260.1 11.6 %copy.500 = f32[8,1,64,2,64,2]{4,2,5,3,1,0:T(8,128)} copy(f32[8,1,64,2,64,2]{0,5,4,3,2,1:T(2,128)} %bitcast.422) | data formatting | bytes 1048576 | tf_op jit(solution)/shard_map/stack | solution.py:104
  271.7 8.3 %copy.497 = f32[8,128,128]{0,2,1:T(8,128)} copy(f32[8,128,128]{1,0,2:T(8,128)} %fusion.61) | data formatting | bytes 1048576 | tf_op jit(solution)/shard_map/add | solution.py:93
  279.9 11.6 %copy.499 = f32[8,1,64,2,64,2]{4,2,5,3,1,0:T(8,128)} copy(f32[8,1,64,2,64,2]{0,5,4,3,2,1:T(2,128)} %bitcast.423) | data formatting | bytes 1048576 | tf_op jit(solution)/shard_map/stack | solution.py:104
  291.5 4.9 fusion.3
  296.4 3.6 copy.608
  300.0 3.5 copy.502
  305.7 4.0 collective-permute-done.7
  332.0 4.4 multiply_select_fusion.3
  340.0 4.8 collective-permute-start.8
  348.0 14.2 %copy.507 = f32[8,2,128,128]{0,3,2,1:T(8,128)} copy(f32[8,2,128,128]{2,0,3,1:T(8,128)} %get-tuple-element.20) | data formatting | bytes 2097152 | tf_op jit(solution)/shard_map/concatenate | solution.py:225
  362.2 21.9 %copy.508 = f32[8,2,64,2,64,2]{4,2,5,3,1,0:T(8,128)} copy(f32[8,2,64,2,64,2]{0,5,4,3,2,1:T(2,128)} %bitcast.402) | data formatting | bytes 2097152 | tf_op jit(solution)/shard_map/concatenate | solution.py:225
  400.5 8.3 %copy.523 = f32[8,128,128]{0,2,1:T(8,128)} copy(f32[8,128,128]{1,0,2:T(8,128)} %fusion.64) | data formatting | bytes 1048576 | tf_op jit(solution)/shard_map/add | solution.py:99
  408.8 11.5 %copy.525 = f32[8,1,64,2,64,2]{4,2,5,3,1,0:T(8,128)} copy(f32[8,1,64,2,64,2]{0,5,4,3,2,1:T(2,128)} %bitcast.424) | data formatting | bytes 1048576 | tf_op jit(solution)/shard_map/stack | solution.py:104
  420.3 8.3 %copy.522 = f32[8,128,128]{0,2,1:T(8,128)} copy(f32[8,128,128]{1,0,2:T(8,128)} %fusion.63) | data formatting | bytes 1048576 | tf_op jit(solution)/shard_map/add | solution.py:93
  428.5 11.5 %copy.524 = f32[8,1,64,2,64,2]{4,2,5,3,1,0:T(8,128)} copy(f32[8,1,64,2,64,2]{0,5,4,3,2,1:T(2,128)} %bitcast.425) | data formatting | bytes 1048576 | tf_op jit(solution)/shard_map/stack | solution.py:104
  440.1 5.8 fusion.5
  445.9 3.6 copy.609
  449.5 3.5 copy.527
  452.9 3.5 collective-permute-start.10
  456.4 4.0 collective-permute-done.10
  482.7 4.9 multiply_select_fusion.2
  493.8 6.8 %collective-permute-done.11 = f32[4,2,128,128]{2,0,3,1:T(4,128)} collective-permute-done((f32[4,2,128,128]{2,0,3,1:T(4,128)}, f32[4,2,128,128]{2,0,3,1:T(4,128)}, u32[]{:S(2)}, u32[]{:S(2)}) %collective-permute-start.11) | collective-permute-done | bytes 524320 | tf_op jit(solution)/shard_map/ppermute | solution.py:12
  516.4 4.8 collective-permute-start.12
  546.9 4.9 collective-permute-done.14
  567.8 4.8 collective-permute-start.15
  598.9 4.4 collective-permute-done.17
  619.2 5.0 collective-permute-start.18
  645.1 7.9 %fusion.38 = f32[1,8,2,128,128]{3,1,4,2,0:T(8,128)} fusion(f32[1,8,1,128,128]{3,1,4,2,0:T(8,128)S(1)} %bitcast.449, f32[1,8,1,128,128]{3,1,4,2,0:T(8,128)S(1)} %bitcast.451, f32[1,8,1,128,128]{3,1,4,2,0:T(8,128)S(1)} %bitcast.446, f32[1,8,1,128,128]{3,1,4,2,0:T(8,128)S(1)} %bitcast.448, f32[1,8,2,128,128]{3,1,4,2,0:T(8,128)S(1)} %bitcast.436, ...), kind=kLoop, calls=%fused_computation.152 | loop fusion | flops 15728640 | bytes 12582948 | tf_op jit(solution)/shard_map/jit(_where)/select_n | solution.py:335
  (518 shorter events, 290.6 us)
Async XLA Ops:
  0.6 9.0 %copy-start.95 = (s32[4,8]{1,0:T(4,128)S(1)}, s32[4,8]{1,0:T(4,128)}, u32[]{:S(2)}) copy-start(s32[4,8]{1,0:T(4,128)} %param.9) | copy-start | bytes 388
  1.9 51.3 %collective-permute-start.1 = (f32[8,1,128]{2,0,1:T(8,128)S(1)}, f32[8,1,128]{2,0,1:T(8,128)S(1)}, u32[]{:S(2)}, u32[]{:S(2)}) collective-permute-start(f32[8,1,128]{2,0,1:T(8,128)S(1)} %get-tuple-element.82), channel_id=1, source_target_pairs={{4,0},{8,4},{12,8},{16,12},{20,16},{24,20},{28,24},{5,1},{9,5},{13... | collective-permute-start | bytes 12296 | tf_op jit(solution)/shard_map/ppermute | solution.py:12
  4.4 48.9 %collective-permute-start = (f32[8,1,128]{2,0,1:T(8,128)S(1)}, f32[8,1,128]{2,0,1:T(8,128)S(1)}, u32[]{:S(2)}, u32[]{:S(2)}) collective-permute-start(f32[8,1,128]{2,0,1:T(8,128)S(1)} %get-tuple-element.83), channel_id=1, source_target_pairs={{0,4},{4,8},{8,12},{12,16},{16,20},{20,24},{24,28},{1,5},{5,9},{9,... | collective-permute-start | bytes 12296 | tf_op jit(solution)/shard_map/ppermute | solution.py:12
  12.4 7.0 %copy-start.71 = (bf16[1,8,128,128]{3,2,1,0:T(8,128)(2,1)S(1)}, bf16[1,8,128,128]{3,2,1,0:T(8,128)(2,1)}, u32[]{:S(2)}) copy-start(bf16[1,8,128,128]{3,2,1,0:T(8,128)(2,1)} %param.8) | copy-start | bytes 786436
  12.7 7.0 %copy-start.70 = (bf16[1,8,2,128,128]{4,3,2,1,0:T(8,128)(2,1)S(1)}, bf16[1,8,2,128,128]{4,3,2,1,0:T(8,128)(2,1)}, u32[]{:S(2)}) copy-start(bf16[1,8,2,128,128]{4,3,2,1,0:T(8,128)(2,1)} %param.5) | copy-start | bytes 1572868
  17.9 55.9 %copy-start.72 = (s32[1024]{0:T(1024)}, s32[1024]{0:T(1024)S(1)}, u32[]{:S(2)}) copy-start(s32[1024]{0:T(1024)S(1)} %get-tuple-element.106) | copy-start | bytes 12292
  17.9 36.6 %copy-start.74 = (s32[1024]{0:T(1024)}, s32[1024]{0:T(1024)S(1)}, u32[]{:S(2)}) copy-start(s32[1024]{0:T(1024)S(1)} %get-tuple-element.108) | copy-start | bytes 12292
  17.9 37.6 %copy-start.73 = (s32[1024]{0:T(1024)}, s32[1024]{0:T(1024)S(1)}, u32[]{:S(2)}) copy-start(s32[1024]{0:T(1024)S(1)} %get-tuple-element.109) | copy-start | bytes 12292
  18.0 38.1 %copy-start.76 = (s32[1024]{0:T(1024)}, s32[1024]{0:T(1024)S(1)}, u32[]{:S(2)}) copy-start(s32[1024]{0:T(1024)S(1)} %get-tuple-element.110) | copy-start | bytes 12292
  18.0 38.7 %copy-start.75 = (s32[1024]{0:T(1024)}, s32[1024]{0:T(1024)S(1)}, u32[]{:S(2)}) copy-start(s32[1024]{0:T(1024)S(1)} %get-tuple-element.111) | copy-start | bytes 12292
  19.4 37.9 %copy-start.78 = (s32[1024]{0:T(1024)}, s32[1024]{0:T(1024)S(1)}, u32[]{:S(2)}) copy-start(s32[1024]{0:T(1024)S(1)} %get-tuple-element.112) | copy-start | bytes 12292
  19.4 38.5 %copy-start.77 = (s32[1024]{0:T(1024)}, s32[1024]{0:T(1024)S(1)}, u32[]{:S(2)}) copy-start(s32[1024]{0:T(1024)S(1)} %get-tuple-element.113) | copy-start | bytes 12292
  19.9 11.4 %copy-start.11 = (bf16[1,8,2,128,128]{3,1,4,2,0:T(8,128)(2,1)}, bf16[1,8,2,128,128]{3,1,4,2,0:T(8,128)(2,1)S(1)}, u32[]{:S(2)}) copy-start(bf16[1,8,2,128,128]{3,1,4,2,0:T(8,128)(2,1)S(1)} %copy.446) | copy-start | bytes 1572868
  63.6 10.1 %collective-permute-start.3 = (f32[8,2,128]{2,0,1:T(8,128)S(1)}, f32[8,2,128]{2,0,1:T(8,128)S(1)}, u32[]{:S(2)}, u32[]{:S(2)}) collective-permute-start(f32[8,2,128]{2,0,1:T(8,128)S(1)} %get-tuple-element.78), channel_id=1, source_target_pairs={{4,0},{8,4},{12,8},{16,12},{20,16},{24,20},{28,24},{5,1},{9,5},{13... | collective-permute-start | bytes 24584 | tf_op jit(solution)/shard_map/ppermute | solution.py:12
  65.5 8.2 %collective-permute-start.2 = (f32[8,2,128]{2,0,1:T(8,128)S(1)}, f32[8,2,128]{2,0,1:T(8,128)S(1)}, u32[]{:S(2)}, u32[]{:S(2)}) collective-permute-start(f32[8,2,128]{2,0,1:T(8,128)S(1)} %get-tuple-element.76), channel_id=1, source_target_pairs={{0,4},{4,8},{8,12},{12,16},{16,20},{20,24},{24,28},{1,5},{5,9},{9,... | collective-permute-start | bytes 24584 | tf_op jit(solution)/shard_map/ppermute | solution.py:12
  136.8 5.4 copy-start.94
  140.2 21.5 %collective-permute-start.4 = (f32[8,2,32,128]{3,2,1,0:T(8,128)}, f32[8,2,32,128]{3,2,1,0:T(8,128)}, u32[]{:S(2)}, u32[]{:S(2)}) collective-permute-start(f32[8,2,32,128]{3,2,1,0:T(8,128)} %copy.476), channel_id=1, source_target_pairs={{1,0},{2,1},{3,2},{5,4},{6,5},{7,6},{9,8},{10,9},{11,10},{13,12},{... | collective-permute-start | bytes 786440 | tf_op jit(solution)/shard_map/ppermute | solution.py:12
  142.2 23.4 %copy-start.82 = (s32[1024]{0:T(1024)}, s32[1024]{0:T(1024)S(1)}, u32[]{:S(2)}) copy-start(s32[1024]{0:T(1024)S(1)} %pad_clamp_fusion.1) | copy-start | bytes 12292
  150.1 11.5 %copy-start.92 = (s32[8]{0:T(128)S(1)}, s32[8]{0:T(128)}, u32[]{:S(2)}) copy-start(s32[8]{0:T(128)} %get-tuple-element.85) | copy-start | bytes 100
  150.1 11.6 %copy-start.90 = (s32[8]{0:T(128)S(1)}, s32[8]{0:T(128)}, u32[]{:S(2)}) copy-start(s32[8]{0:T(128)} %get-tuple-element.87) | copy-start | bytes 100
  150.1 11.6 %copy-start.91 = (s32[8]{0:T(128)S(1)}, s32[8]{0:T(128)}, u32[]{:S(2)}) copy-start(s32[8]{0:T(128)} %get-tuple-element.90) | copy-start | bytes 100
  161.7 17.4 %copy-start.83 = (s32[1024]{0:T(1024)}, s32[1024]{0:T(1024)S(1)}, u32[]{:S(2)}) copy-start(s32[1024]{0:T(1024)S(1)} %pad_clamp_fusion.4) | copy-start | bytes 12292
  161.7 10.8 %copy-start.85 = (s32[1024]{0:T(1024)}, s32[1024]{0:T(1024)S(1)}, u32[]{:S(2)}) copy-start(s32[1024]{0:T(1024)S(1)} %get-tuple-element.104) | copy-start | bytes 12292
  161.7 12.8 %copy-start.84 = (s32[1024]{0:T(1024)}, s32[1024]{0:T(1024)S(1)}, u32[]{:S(2)}) copy-start(s32[1024]{0:T(1024)S(1)} %get-tuple-element.105) | copy-start | bytes 12292
  189.0 46.4 %collective-permute-start.6 = (f32[8,2,128]{2,0,1:T(8,128)S(1)}, f32[8,2,128]{2,0,1:T(8,128)S(1)}, u32[]{:S(2)}, u32[]{:S(2)}) collective-permute-start(f32[8,2,128]{2,0,1:T(8,128)S(1)} %get-tuple-element.72), channel_id=1, source_target_pairs={{4,0},{8,4},{12,8},{16,12},{20,16},{24,20},{28,24},{5,1},{9,5},{13... | collective-permute-start | bytes 24584 | tf_op jit(solution)/shard_map/ppermute | solution.py:12
  190.9 44.5 %collective-permute-start.5 = (f32[8,2,128]{2,0,1:T(8,128)S(1)}, f32[8,2,128]{2,0,1:T(8,128)S(1)}, u32[]{:S(2)}, u32[]{:S(2)}) collective-permute-start(f32[8,2,128]{2,0,1:T(8,128)S(1)} %get-tuple-element.70), channel_id=1, source_target_pairs={{0,4},{4,8},{8,12},{12,16},{16,20},{20,24},{24,28},{1,5},{5,9},{9,... | collective-permute-start | bytes 24584 | tf_op jit(solution)/shard_map/ppermute | solution.py:12
  303.5 6.2 collective-permute-start.7
  338.1 46.0 %collective-permute-start.9 = (f32[8,2,128]{2,0,1:T(8,128)S(1)}, f32[8,2,128]{2,0,1:T(8,128)S(1)}, u32[]{:S(2)}, u32[]{:S(2)}) collective-permute-start(f32[8,2,128]{2,0,1:T(8,128)S(1)} %get-tuple-element.66), channel_id=1, source_target_pairs={{4,0},{8,4},{12,8},{16,12},{20,16},{24,20},{28,24},{5,1},{9,5},{13... | collective-permute-start | bytes 24584 | tf_op jit(solution)/shard_map/ppermute | solution.py:12
  340.0 44.1 %collective-permute-start.8 = (f32[8,2,128]{2,0,1:T(8,128)S(1)}, f32[8,2,128]{2,0,1:T(8,128)S(1)}, u32[]{:S(2)}, u32[]{:S(2)}) collective-permute-start(f32[8,2,128]{2,0,1:T(8,128)S(1)} %get-tuple-element.64), channel_id=1, source_target_pairs={{0,4},{4,8},{8,12},{12,16},{16,20},{20,24},{24,28},{1,5},{5,9},{9,... | collective-permute-start | bytes 24584 | tf_op jit(solution)/shard_map/ppermute | solution.py:12
  452.9 7.4 %collective-permute-start.10 = (f32[8,2,32,128]{3,2,1,0:T(8,128)}, f32[8,2,32,128]{3,2,1,0:T(8,128)}, u32[]{:S(2)}, u32[]{:S(2)}) collective-permute-start(f32[8,2,32,128]{3,2,1,0:T(8,128)} %copy.527), channel_id=1, source_target_pairs={{1,0},{2,1},{3,2},{5,4},{6,5},{7,6},{9,8},{10,9},{11,10},{13,12},{... | collective-permute-start | bytes 786440 | tf_op jit(solution)/shard_map/ppermute | solution.py:12
  487.6 6.1 copy-start.93
  489.4 15.8 %copy-start.79 = (pred[8]{0:T(512)(128)(4,1)S(1)}, pred[8]{0:T(512)(128)(4,1)}, u32[]{:S(2)}) copy-start(pred[8]{0:T(512)(128)(4,1)} %get-tuple-element.12) | copy-start | bytes 28
  489.4 11.1 %collective-permute-start.11 = (f32[4,2,128,128]{2,0,3,1:T(4,128)}, f32[4,2,128,128]{2,0,3,1:T(4,128)}, u32[]{:S(2)}, u32[]{:S(2)}) collective-permute-start(f32[4,2,128,128]{2,0,3,1:T(4,128)} %slice.1047), channel_id=1, source_target_pairs={{0,1},{1,2},{2,3},{4,5},{5,6},{6,7},{8,9},{9,10},{10,11},{12,13},{... | collective-permute-start | bytes 1572872 | tf_op jit(solution)/shard_map/ppermute | solution.py:12
  493.7 12.8 %copy-start.87 = (pred[8]{0:T(512)(128)(4,1)}, pred[8]{0:T(512)(128)(4,1)S(1)}, u32[]{:S(2)}) copy-start(pred[8]{0:T(512)(128)(4,1)S(1)} %fusion.190) | copy-start | bytes 28
  493.8 12.8 %copy-start.86 = (s32[1024]{0:T(1024)}, s32[1024]{0:T(1024)S(1)}, u32[]{:S(2)}) copy-start(s32[1024]{0:T(1024)S(1)} %pad_clamp_fusion) | copy-start | bytes 12292
  514.5 9.9 %collective-permute-start.13 = (f32[8,2,128]{2,0,1:T(8,128)S(1)}, f32[8,2,128]{2,0,1:T(8,128)S(1)}, u32[]{:S(2)}, u32[]{:S(2)}) collective-permute-start(f32[8,2,128]{2,0,1:T(8,128)S(1)} %get-tuple-element.60), channel_id=1, source_target_pairs={{4,0},{8,4},{12,8},{16,12},{20,16},{24,20},{28,24},{5,1},{9,5},{13... | collective-permute-start | bytes 24584 | tf_op jit(solution)/shard_map/ppermute | solution.py:12
  516.4 8.0 %collective-permute-start.12 = (f32[8,2,128]{2,0,1:T(8,128)S(1)}, f32[8,2,128]{2,0,1:T(8,128)S(1)}, u32[]{:S(2)}, u32[]{:S(2)}) collective-permute-start(f32[8,2,128]{2,0,1:T(8,128)S(1)} %get-tuple-element.58), channel_id=1, source_target_pairs={{0,4},{4,8},{8,12},{12,16},{16,20},{20,24},{24,28},{1,5},{5,9},{9,... | collective-permute-start | bytes 24584 | tf_op jit(solution)/shard_map/ppermute | solution.py:12
  540.8 4.9 copy-start.34
  540.9 4.9 copy-start.52
  541.0 10.9 %collective-permute-start.14 = (f32[4,2,128,128]{2,0,3,1:T(4,128)S(1)}, f32[4,2,128,128]{2,0,3,1:T(4,128)}, u32[]{:S(2)}, u32[]{:S(2)}) collective-permute-start(f32[4,2,128,128]{2,0,3,1:T(4,128)S(1)} %slice.1080), channel_id=1, source_target_pairs={{0,1},{1,2},{2,3},{4,5},{5,6},{6,7},{8,9},{9,10},{10,11},{12,13},{... | collective-permute-start | bytes 1572872 | tf_op jit(solution)/shard_map/ppermute | solution.py:12
  546.9 9.7 %copy-start.80 = (pred[8]{0:T(512)(128)(4,1)S(1)}, pred[8]{0:T(512)(128)(4,1)}, u32[]{:S(2)}) copy-start(pred[8]{0:T(512)(128)(4,1)} %get-tuple-element.12) | copy-start | bytes 28
  565.9 9.9 %collective-permute-start.16 = (f32[8,2,128]{2,0,1:T(8,128)S(1)}, f32[8,2,128]{2,0,1:T(8,128)S(1)}, u32[]{:S(2)}, u32[]{:S(2)}) collective-permute-start(f32[8,2,128]{2,0,1:T(8,128)S(1)} %get-tuple-element.54), channel_id=1, source_target_pairs={{4,0},{8,4},{12,8},{16,12},{20,16},{24,20},{28,24},{5,1},{9,5},{13... | collective-permute-start | bytes 24584 | tf_op jit(solution)/shard_map/ppermute | solution.py:12
  567.8 8.0 %collective-permute-start.15 = (f32[8,2,128]{2,0,1:T(8,128)S(1)}, f32[8,2,128]{2,0,1:T(8,128)S(1)}, u32[]{:S(2)}, u32[]{:S(2)}) collective-permute-start(f32[8,2,128]{2,0,1:T(8,128)S(1)} %get-tuple-element.52), channel_id=1, source_target_pairs={{0,4},{4,8},{8,12},{12,16},{16,20},{20,24},{24,28},{1,5},{5,9},{9,... | collective-permute-start | bytes 24584 | tf_op jit(solution)/shard_map/ppermute | solution.py:12
  592.4 10.9 %collective-permute-start.17 = (f32[4,2,128,128]{2,0,3,1:T(4,128)S(1)}, f32[4,2,128,128]{2,0,3,1:T(4,128)}, u32[]{:S(2)}, u32[]{:S(2)}) collective-permute-start(f32[4,2,128,128]{2,0,3,1:T(4,128)S(1)} %slice.1113), channel_id=1, source_target_pairs={{0,1},{1,2},{2,3},{4,5},{5,6},{6,7},{8,9},{9,10},{10,11},{12,13},{... | collective-permute-start | bytes 1572872 | tf_op jit(solution)/shard_map/ppermute | solution.py:12
  598.9 9.2 %copy-start.81 = (pred[8]{0:T(512)(128)(4,1)S(1)}, pred[8]{0:T(512)(128)(4,1)}, u32[]{:S(2)}) copy-start(pred[8]{0:T(512)(128)(4,1)} %get-tuple-element.12) | copy-start | bytes 28
  617.3 10.1 %collective-permute-start.19 = (f32[8,2,128]{2,0,1:T(8,128)S(1)}, f32[8,2,128]{2,0,1:T(8,128)S(1)}, u32[]{:S(2)}, u32[]{:S(2)}) collective-permute-start(f32[8,2,128]{2,0,1:T(8,128)S(1)} %get-tuple-element.48), channel_id=1, source_target_pairs={{4,0},{8,4},{12,8},{16,12},{20,16},{24,20},{28,24},{5,1},{9,5},{13... | collective-permute-start | bytes 24584 | tf_op jit(solution)/shard_map/ppermute | solution.py:12
  619.2 8.2 %collective-permute-start.18 = (f32[8,2,128]{2,0,1:T(8,128)S(1)}, f32[8,2,128]{2,0,1:T(8,128)S(1)}, u32[]{:S(2)}, u32[]{:S(2)}) collective-permute-start(f32[8,2,128]{2,0,1:T(8,128)S(1)} %get-tuple-element.46), channel_id=1, source_target_pairs={{0,4},{4,8},{8,12},{12,16},{16,20},{20,24},{24,28},{1,5},{5,9},{9,... | collective-permute-start | bytes 24584 | tf_op jit(solution)/shard_map/ppermute | solution.py:12
  645.1 10.6 %copy-start.30 = (f32[8,2,128,128]{2,0,3,1:T(8,128)S(1)}, f32[8,2,128,128]{2,0,3,1:T(8,128)}, u32[]{:S(2)}) copy-start(f32[8,2,128,128]{2,0,3,1:T(8,128)} %get-tuple-element.18) | copy-start | bytes 3145732
  (68 other events, 166.4 us)
where the time goes:
time: 671 us; the launch traced here: 659 us
  local copies, waits for them, and re-layouts  470 us (70%)
  other arithmetic  99.9 us (15%)
  starting transfers between devices  62.2 us (9%)
  waiting for transfers between devices  24.1 us (4%)
    concatenate x4, local copies, waits for them, and re-layouts, join_quadrants(): return jnp.concatenate([bottom, top_half], axis=-2)  72.2 us
    another operation x6, local copies, waits for them, and re-layouts, operator_cells(): return jnp.stack([result_u, result_v], axis=1)  69.2 us
    ppermute x20, starting transfers between devices, passed_along(): lax.ppermute(value, axis, [(source, source + steps) for source in range(f...  62.2 us
    unnamed x213, local copies, waits for them, and re-layouts  47.6 us
    convert_element_type x2, local copies, waits for them, and re-layouts, per_device(): force_cells = forcing[0].astype(jnp.float32)  33.3 us
    add x3, local copies, waits for them, and re-layouts, operator_cells(): -4.0  24.8 us
    add x3, local copies, waits for them, and re-layouts, operator_cells(): -4.0 * (face_east * (u_east - u_centre) - face_west * (u_centre - u_west))  24.8 us
    ppermute x20, waiting for transfers between devices, passed_along(): lax.ppermute(value, axis, [(source, source + steps) for source in range(f...  24.1 us
  transfers between devices with their start and end apart: 20, of which 5 were waited for; matrix products, arithmetic and copies ran while one was open for 25% of the time, Pallas kernels for 0%

commit v1 on v0

v1 whole, which is shorter than its diff:
```python
from typing import Any, NamedTuple

import jax
import jax.numpy as jnp
from jax import lax
from jax.experimental import pallas as pl
from jax.experimental.pallas import tpu as pltpu
from jax.sharding import PartitionSpec as P

relaxation = 0.5
PAD = 8
LOW, HIGH, EDGES = 0, 1, 2
VM, SM, ANY = pltpu.VMEM, pltpu.SMEM, pl.ANY
F32 = jnp.float32
BF16 = jnp.bfloat16
VMEM_BYTES = 48 * 2**20


class Layout:
    def __init__(self, slots, side, levels, patches):
        self.slots = slots
        self.side = side
        self.levels = levels
        self.patches = patches
        self.half_slots = slots // 2
        self.half_side = side // 2
        self.span = 2 * slots

    def columns(self, level):
        return 1 << level

    def patch_rows(self, level):
        return self.slots >> level

    def rows(self, level):
        return self.patch_rows(level) * self.side

    def margin(self, level):
        return 2 << level

    def own(self, level):
        return max(1, (1 << level) // 2)

    def blocks(self, level):
        return self.own(level) + (1 if level > 0 else 0)

    def chunk(self, level):
        return 8 * max(1, 4 // self.blocks(level))


def lane_ids(side):
    return lax.broadcasted_iota(jnp.int32, (1, side), 1)


def near_counts(g, rows_ref, level, patch, odd):
    own = rows_ref[level, patch]
    east = jnp.where(
        patch + 1 < g.patches, rows_ref[level, jnp.minimum(patch + 1, g.patches - 1)], 0
    )
    west = jnp.where(patch > 0, rows_ref[level, jnp.maximum(patch - 1, 0)], 0)
    return own, jnp.where(odd, own, east), jnp.where(odd, west, own)


def lane_limits(g, level, counts, cells):
    own, east, west = (value * cells for value in counts)
    lane = lane_ids(g.side)
    margin = g.margin(level)
    first = 0 if level > 0 else g.half_side
    edges = jnp.where(
        (lane >= first) & (lane < first + margin), east, jnp.where(lane >= g.side - margin, west, 0)
    )
    if level == 0:
        return [jnp.where(lane < g.half_side, own, edges)]
    return [jnp.full((1, g.side), own, jnp.int32)] * g.own(level) + [edges]


def both_sides(g, values):
    count = len(values)
    lane = lax.broadcasted_iota(jnp.int32, values[0].shape, 1)
    toward_east = [pltpu.roll(value, g.side - 1, 1) for value in values]
    toward_west = [pltpu.roll(value, 1, 1) for value in values]
    if count == 1:
        return toward_east, toward_west
    east = [
        jnp.where(lane == g.side - 1, toward_east[(k + 1) % count], toward_east[k])
        for k in range(count)
    ]
    west = [
        jnp.where(lane == 0, toward_west[(k - 1) % count], toward_west[k]) for k in range(count)
    ]
    return east, west


def operator_chunk(g, cells, visc, fric, row, chunk, count):
    fields = []
    for comp in range(2):
        near = []
        for step in (0, 1, -1):
            line = [cells[comp, k, pl.ds(PAD + row + step, chunk), :] for k in range(count)]
            near.append((line, *both_sides(g, line)))
        fields.append(near)
    centre = [visc[k, pl.ds(PAD + row, chunk), :] for k in range(count)]
    visc_east, visc_west = both_sides(g, centre)
    out_u = []
    out_v = []
    for k in range(count):
        (u, u_e, u_w), (u_n, u_ne, u_nw), (u_s, u_se, u_sw) = (
            [value[k] for value in line] for line in fields[0]
        )
        (v, v_e, v_w), (v_n, v_ne, v_nw), (v_s, v_se, v_sw) = (
            [value[k] for value in line] for line in fields[1]
        )
        visc_north = visc[k, pl.ds(PAD + row + 1, chunk), :]
        visc_south = visc[k, pl.ds(PAD + row - 1, chunk), :]
        du_e, du_w, du_n, du_s = u_e - u, u - u_w, u_n - u, u - u_s
        dv_e, dv_w, dv_n, dv_s = v_e - v, v - v_w, v_n - v, v - v_s
        inner_u = (
            centre[k] * (8.0 * (du_e - du_w) + 2.0 * (du_n - du_s))
            + visc_east[k] * (8.0 * du_e + 2.0 * (v_ne - v_se))
            - visc_west[k] * (8.0 * du_w + 2.0 * (v_nw - v_sw))
            + visc_north * (2.0 * du_n + (v_ne - v_nw))
            - visc_south * (2.0 * du_s + (v_se - v_sw))
        )
        inner_v = (
            centre[k] * (8.0 * (dv_n - dv_s) + 2.0 * (dv_e - dv_w))
            + visc_north * (8.0 * dv_n + 2.0 * (u_ne - u_nw))
            - visc_south * (8.0 * dv_s + 2.0 * (u_se - u_sw))
            + visc_east[k] * (2.0 * dv_e + (u_ne - u_se))
            - visc_west[k] * (2.0 * dv_w + (u_nw - u_sw))
        )
        friction = fric[k, pl.ds(row, chunk), :]
        out_u.append(friction * u - inner_u)
        out_v.append(friction * v - inner_v)
    return out_u, out_v


def over_rows(rows, chunk, body):
    def step(index, carry):
        body(pl.multiple_of(index * chunk, chunk))
        return carry

    lax.fori_loop(0, rows // chunk, step, 0)


def clear_pads(ref, lead):
    width = ref.shape[-1]
    last = ref.shape[-2]
    for index in lead:
        ref[index + (slice(0, PAD), slice(None))] = jnp.zeros((PAD, width), F32)
        ref[index + (slice(last - PAD, last), slice(None))] = jnp.zeros((PAD, width), F32)


def first_smooth(g, level, d, limits, rows):
    count = g.blocks(level)
    chunk = g.chunk(level)

    def body(row):
        centre = [d.visc[k, pl.ds(PAD + row, chunk), :] for k in range(count)]
        east, west = both_sides(g, centre)
        for k in range(count):
            north = d.visc[k, pl.ds(PAD + row + 1, chunk), :]
            south = d.visc[k, pl.ds(PAD + row - 1, chunk), :]
            friction = d.fric[k, pl.ds(row, chunk), :]
            twice = 2.0 * centre[k]
            along_row = twice + east[k] + west[k]
            along_col = twice + north + south
            live = jnp.broadcast_to(limits[k] > row, (chunk, g.side))
            diag_u = 8.0 * along_row + 2.0 * along_col + friction
            diag_v = 8.0 * along_col + 2.0 * along_row + friction
            for comp, diag in ((0, diag_u), (1, diag_v)):
                weight = jnp.where(live, relaxation / diag, 0.0)
                d.weight[comp, k, pl.ds(row, chunk), :] = weight
                d.cells[comp, k, pl.ds(PAD + row, chunk), :] = (
                    weight * d.right[comp, k, pl.ds(row, chunk), :]
                )

    over_rows(rows, chunk, body)


def residual_step(g, level, d, rows, add=False):
    count = g.blocks(level)
    chunk = g.chunk(level)

    def body(row):
        applied = operator_chunk(g, d.cells, d.visc, d.fric, row, chunk, count)
        for comp in range(2):
            for k in range(count):
                weight = d.weight[comp, k, pl.ds(row, chunk), :]
                left = d.right[comp, k, pl.ds(row, chunk), :] - applied[comp][k]
                left = jnp.where(weight > 0.0, left, 0.0)
                d.right[comp, k, pl.ds(row, chunk), :] = left
                value = d.cells[comp, k, pl.ds(PAD + row, chunk), :] + weight * left
                if add:
                    value = value + d.held[comp, k, pl.ds(row, chunk), :]
                d.held[comp, k, pl.ds(row, chunk), :] = value

    over_rows(rows, chunk, body)


def corrected_step(g, level, d, rows):
    count = g.blocks(level)
    chunk = g.chunk(level)

    def body(row):
        applied = operator_chunk(g, d.cells, d.visc, d.fric, row, chunk, count)
        for comp in range(2):
            for k in range(count):
                weight = d.weight[comp, k, pl.ds(row, chunk), :]
                d.held[comp, k, pl.ds(row, chunk), :] = (
                    d.held[comp, k, pl.ds(row, chunk), :]
                    + d.cells[comp, k, pl.ds(PAD + row, chunk), :]
                    - weight * applied[comp][k]
                )

    over_rows(rows, chunk, body)


def pairings(g, fine):
    if fine == 1:
        return [[(0, LOW), (1, HIGH)]]
    parts = [[(2 * k, LOW), (2 * k + 1, HIGH)] for k in range(g.own(fine) // 2)]
    return parts + [[(g.own(fine), EDGES)]]


def target_lane(g, part, fine_lane):
    halved = jnp.right_shift(fine_lane, 1)
    if part == LOW:
        return halved
    if part == HIGH:
        return g.half_side + halved
    return halved + jnp.where(fine_lane >= g.half_side, g.half_side, 0)


def sum_matrix(g, part):
    fine = lax.broadcasted_iota(jnp.int32, (g.side, g.side), 0)
    coarse = lax.broadcasted_iota(jnp.int32, (g.side, g.side), 1)
    return jnp.where(target_lane(g, part, fine) == coarse, 1.0, 0.0).astype(BF16)


def copy_matrix(g, part):
    coarse = lax.broadcasted_iota(jnp.int32, (g.side, g.side), 0)
    fine = lax.broadcasted_iota(jnp.int32, (g.side, g.side), 1)
    return jnp.where(target_lane(g, part, fine) == coarse, 1.0, 0.0).astype(BF16)


def split_dot(values, matrix):
    high = values.astype(BF16)
    rest = (values - high.astype(F32)).astype(BF16)
    return jnp.dot(high, matrix, preferred_element_type=F32) + jnp.dot(
        rest, matrix, preferred_element_type=F32
    )


def restrict_into(g, fine, d, rows, store):
    chunk = min(rows // 2, g.half_side)
    if (rows // 2) % chunk:
        chunk = rows // 2
    parts = pairings(g, fine)
    matrices = {part: sum_matrix(g, part) for members in parts for _, part in members}

    def body(row):
        for comp in range(2):
            for coarse, members in enumerate(parts):
                total = None
                for k, part in members:
                    first = d.right[comp, k, pl.ds(2 * row, chunk, stride=2), :]
                    second = d.right[comp, k, pl.ds(2 * row + 1, chunk, stride=2), :]
                    term = split_dot(first + second, matrices[part])
                    total = term if total is None else total + term
                store(comp, coarse, row, chunk, total)

    over_rows(rows // 2, chunk, body)


def prolong_from(g, fine, d, limits, rows, load):
    chunk = min(rows // 2, g.half_side)
    if (rows // 2) % chunk:
        chunk = rows // 2
    parts = pairings(g, fine)
    matrices = {part: copy_matrix(g, part) for members in parts for _, part in members}

    def body(row):
        ids = 2 * (row + lax.broadcasted_iota(jnp.int32, (chunk, g.side), 0))
        for comp in range(2):
            for coarse, members in enumerate(parts):
                value = load(comp, coarse, row, chunk)
                for k, part in members:
                    spread = jnp.where(ids < limits[k], split_dot(value, matrices[part]), 0.0)
                    d.cells[comp, k, pl.ds(PAD + 2 * row, chunk, stride=2), :] = spread
                    d.cells[comp, k, pl.ds(PAD + 2 * row + 1, chunk, stride=2), :] = spread

    over_rows(rows // 2, chunk, body)


def pack_kernel(g, force, visc, fric, swap, edge_own, edge_other):
    level_here = lax.axis_index("level")
    side = g.side

    def plane(q, slot):
        if q < 2:
            return force[slot, q].astype(F32)
        if q == 2:
            return fric[slot].astype(F32)
        return visc[slot]

    def packed_edge(level, column, start):
        lane = lane_ids(side)
        margin = g.margin(level)
        total = jnp.zeros((side, side), F32)
        for r in range(g.patch_rows(level)):
            slot = r * g.columns(level) + column
            for q in range(4):
                base = q * g.span + r * margin
                moved = plane(q, slot)
                if (base - start) % side:
                    moved = pltpu.roll(moved, (base - start) % side, 1)
                total = jnp.where((lane >= base) & (lane < base + margin), moved, total)
        return total

    def pack_level(level):
        west_type = level % 2 == 1
        margin = g.margin(level)
        last = g.columns(level) - 1
        west_edge = packed_edge(level, 0, 0)
        east_edge = packed_edge(level, last, side - margin)
        edge_own[...] = east_edge if west_type else west_edge
        edge_other[...] = west_edge if west_type else east_edge
        if level == 0:
            lane = lane_ids(side)
            for q in range(4):
                for k in range(g.half_slots):
                    swap[q * g.half_slots + k] = jnp.where(
                        lane < g.half_side,
                        plane(q, k),
                        pltpu.roll(plane(q, k + g.half_slots), g.half_side, 1),
                    )
            swap[4 * g.half_slots] = packed_edge(0, 0, g.half_side)
            return
        own = g.own(level)
        first = own if west_type else 0
        for r in range(g.patch_rows(level)):
            for k in range(own):
                for q in range(4):
                    swap[q * g.half_slots + r * own + k] = plane(
                        q, r * g.columns(level) + first + k
                    )
        if west_type:
            swap[4 * g.half_slots] = packed_edge(level, own - 1, side - margin)
        else:
            swap[4 * g.half_slots] = packed_edge(level, own, 0)

    for level in range(g.levels):
        pl.when(level_here == level)(lambda level=level: pack_level(level))


def fill_level(g, level, west_type, d, limits, raw, got):
    force, visc, fric = raw
    swap, edge_own, edge_other = got
    side = g.side
    home = (level % 2 == 1) == west_type
    margin = g.margin(level)
    own = g.own(level)
    columns = g.columns(level)
    lane = lane_ids(side)
    edges = edge_own if home else edge_other

    def plane(q, slot):
        if q < 2:
            return force[slot, q].astype(F32)
        if q == 2:
            return fric[slot].astype(F32)
        return visc[slot]

    def unpacked(packed, q, r, place):
        shift = (place - (q * g.span + r * margin)) % side
        return pltpu.roll(packed, shift, 1) if shift else packed

    def store(q, k, r, value):
        here = pl.ds(r * side, side)
        if q < 2:
            d.right[q, k, here, :] = value
        elif q == 2:
            d.fric[k, here, :] = value
        else:
            d.visc[k, pl.ds(PAD + r * side, side), :] = jnp.where(
                limits[k] > r * side, 0.25 * value, 0.0
            )

    clear_pads(d.visc, [(k,) for k in range(g.blocks(level))])
    clear_pads(d.cells, [(c, k) for c in range(2) for k in range(g.blocks(level))])
    inner = swap[4 * g.half_slots]
    outer = edges[...]
    for r in range(g.patch_rows(level)):
        for q in range(4):
            if level == 0:
                if home:
                    value = pltpu.roll(plane(q, r), g.half_side, 1)
                    east = unpacked(outer, q, r, g.half_side)
                    value = jnp.where(
                        (lane >= g.half_side) & (lane < g.half_side + margin), east, value
                    )
                else:
                    value = swap[q * g.half_slots + r % g.half_slots]
                    if r >= g.half_slots:
                        value = pltpu.roll(value, g.half_side, 1)
                    east = unpacked(inner, q, r, g.half_side)
                    west = unpacked(outer, q, r, side - margin)
                    value = jnp.where(lane < g.half_side, value, east)
                    value = jnp.where(lane >= side - margin, west, value)
                store(q, 0, r, value)
                continue
            for k in range(own):
                if home:
                    value = plane(q, r * columns + k + (0 if west_type else own))
                else:
                    value = swap[q * g.half_slots + r * own + k]
                store(q, k, r, value)
            if west_type:
                if home:
                    east = plane(q, r * columns + own)
                else:
                    east = unpacked(inner, q, r, 0)
                west = unpacked(outer, q, r, side - margin)
            else:
                east = unpacked(outer, q, r, 0)
                if home:
                    west = plane(q, r * columns + own - 1)
                else:
                    west = unpacked(inner, q, r, side - margin)
            store(q, own, r, jnp.where(lane < g.half_side, east, west))


def joined_edges(g, edge_u, edge_v):
    lane = lane_ids(g.side)
    quarter = g.side // 4
    middle = (lane >= quarter) & (lane < g.side - quarter)
    return jnp.where(middle, pltpu.roll(edge_v, g.half_side, 1), edge_u)


class Level(NamedTuple):
    visc: Any
    fric: Any
    weight: Any
    held: Any
    right: Any = None
    cells: Any = None


def level_arrays(g, count, rows, make, working):
    shapes = [
        (count, rows + 2 * PAD, g.side),
        (count, rows, g.side),
        (2, count, rows, g.side),
        (2, count, rows, g.side),
    ]
    if working:
        shapes += [(2, count, rows, g.side), (2, count, rows + 2 * PAD, g.side)]
    return Level(*[make(shape, F32) for shape in shapes])


def level_scratch(g, level):
    return level_arrays(g, g.blocks(level), g.rows(level), pltpu.VMEM, True)


def level_state(g, level):
    return level_arrays(g, g.blocks(level), g.rows(level), jax.ShapeDtypeStruct, False)


class Copies:
    def __init__(self, sems, first=0):
        self.sems = sems
        self.used = first
        self.open = []

    def start(self, source, target):
        copy = pltpu.make_async_copy(source, target, self.sems.at[self.used])
        self.used += 1
        copy.start()
        self.open.append(copy)

    def finish(self):
        for copy in self.open:
            copy.wait()
        self.open = []


def half_of_level(g, level, held, out, copies):
    own = g.own(level)
    for r in range(g.patch_rows(level)):
        for k in range(own):
            for comp in range(2):
                copies.start(
                    held.at[comp, k, pl.ds(r * g.side, g.side)], out.at[r * own + k, comp]
                )


def down_kernel(
    g, rows_ref, force, visc, fric, swap, edge_own, edge_other, sums, mine, theirs, out, sems, edges,
    packed, levels,
):
    level_here = lax.axis_index("level")
    patch = lax.axis_index("patch")
    raw = (force, visc, fric)
    got = (swap, edge_own, edge_other)
    side = g.side
    top = g.levels - 1
    odd = level_here % 2 == 1

    def limits_of(level):
        return lane_limits(g, level, near_counts(g, rows_ref, level, patch, odd), side)

    def covered_of(level):
        return lane_limits(g, level, near_counts(g, rows_ref, level + 1, patch, odd), g.half_side)

    def filled(wanted):
        for west_type in (True, False):

            @pl.when(odd if west_type else jnp.logical_not(odd))
            def _():
                for level in wanted:
                    fill_level(g, level, west_type, levels[level], limits_of(level), raw, got)

    def set_right(level):
        covered = covered_of(level)

        def store(comp, k, row, chunk, value):
            here = pl.ds(row, chunk)
            ids = row + lax.broadcasted_iota(jnp.int32, (chunk, side), 0)
            old = levels[level].right[comp, k, here, :]
            levels[level].right[comp, k, here, :] = jnp.where(ids < covered[k], value, old)

        return store

    @pl.when(level_here >= top - 1)
    def _():
        copies = Copies(sems)
        filled((top, top - 1))
        for level in (top, top - 1):
            d = levels[level]
            first_smooth(g, level, d, limits_of(level), g.rows(level))
            residual_step(g, level, d, g.rows(level))
            for source, target in zip(d[:4], out[level]):
                copies.start(source, target)
            if level == top:
                restrict_into(g, level, d, g.rows(level), set_right(level - 1))

        def keep(comp, k, row, chunk, value):
            if k == 0:
                sums[comp, pl.ds(row, chunk), :] = value
            else:
                edges[comp, pl.ds(row, chunk), :] = value

        restrict_into(g, top - 1, levels[top - 1], g.rows(top - 1), keep)
        sums[2] = joined_edges(g, edges[0], edges[1])
        copies.finish()

    @pl.when(level_here < top - 1)
    def _():
        copies = Copies(sems)
        filled((1, 0))
        d, coarse = levels[1], levels[0]
        covered = covered_of(1)

        def uncovered(row):
            for comp in range(2):
                for k in range(g.blocks(1)):
                    here = pl.ds(row, g.chunk(1))
                    old = d.right[comp, k, here, :]
                    d.right[comp, k, here, :] = jnp.where(covered[k] > row, 0.0, old)

        over_rows(g.rows(2) // 2, g.chunk(1), uncovered)
        first_smooth(g, 1, d, limits_of(1), g.rows(1))
        residual_step(g, 1, d, g.rows(1))
        restrict_into(g, 1, d, g.rows(1), set_right(0))
        first_smooth(g, 0, coarse, limits_of(0), g.rows(0))

        def load(comp, k, row, chunk):
            return coarse.cells[comp, k, pl.ds(PAD + row, chunk), :]

        prolong_from(g, 1, d, limits_of(1), g.rows(1), load)
        corrected_step(g, 1, d, g.rows(1))
        lane = lane_ids(side)
        for comp in range(2):
            for k in range(g.half_slots):
                low = coarse.cells[comp, 0, pl.ds(PAD + k * side, side), :]
                high = coarse.cells[comp, 0, pl.ds(PAD + (k + g.half_slots) * side, side), :]
                packed[k, comp] = jnp.where(
                    lane < g.half_side, low, pltpu.roll(high, g.half_side, 1)
                )
        rows = bottom_rows(g)
        copies.start(d.visc.at[:, pl.ds(0, rows + 2 * PAD)], out[1].visc)
        copies.start(d.fric.at[:, pl.ds(0, rows)], out[1].fric)
        copies.start(d.weight.at[:, :, pl.ds(0, rows)], out[1].weight)
        copies.start(d.held.at[:, :, pl.ds(0, rows)], out[1].held)
        copies.start(coarse.weight.at[:, :, pl.ds(0, rows // 2)], out[0])

        def write(first, second):
            more = Copies(sems, copies.used)
            half_of_level(g, 1, d.held, first, more)
            more.start(packed, second)
            more.finish()

        pl.when(odd)(lambda: write(mine, theirs))
        pl.when(jnp.logical_not(odd))(lambda: write(theirs, mine))
        copies.finish()


def bottom_rows(g):
    return g.rows(2) // 2 + 2 * PAD


def bottom_kernel(
    g, rows_ref, sums, mine, theirs, state, coarse_weight, adjoint, mine_out, theirs_out, sems,
    packed, d, coarse_state, coarse_cells,
):
    level_here = lax.axis_index("level")
    patch = lax.axis_index("patch")
    side = g.side
    rows = bottom_rows(g)
    reach = g.rows(2) // 2
    top = g.levels - 1
    odd = level_here % 2 == 1

    @pl.when(level_here < top - 1)
    def _():
        copies = Copies(sems)
        for source, target in zip(state, d[:4]):
            copies.start(source, target)
        copies.start(coarse_weight, coarse_state)

        def read(source, sem):
            one = Copies(sems, sem)
            one.start(source.at[0], packed)
            one.finish()

        pl.when(odd)(lambda: read(theirs, 30))
        pl.when(jnp.logical_not(odd))(lambda: read(mine, 31))
        clear_pads(d.cells, [(c, k) for c in range(2) for k in range(2)])
        both = sums[2]
        swapped = pltpu.roll(both, g.half_side, 1)
        copies.finish()
        for comp in range(2):
            for k in range(2):
                rest = jnp.zeros((rows - reach, side), F32)
                d.right[comp, k, pl.ds(reach, rows - reach), :] = rest
                d.cells[comp, k, pl.ds(PAD + reach, rows - reach), :] = rest
                value = sums[comp] if k == 0 else (both, swapped)[comp]
                weight = d.weight[comp, k, pl.ds(0, reach), :]
                value = jnp.where(weight > 0.0, value, 0.0)
                d.right[comp, k, pl.ds(0, reach), :] = value
                d.cells[comp, k, pl.ds(PAD, reach), :] = weight * value
        residual_step(g, 1, d, rows, add=True)
        near = near_counts(g, rows_ref, 1, patch, odd)
        covered = lane_limits(g, 0, near, g.half_side)
        lane = lane_ids(side)

        def store(comp, k, row, size, value):
            here = pl.ds(row, size)
            ids = row + lax.broadcasted_iota(jnp.int32, (size, side), 0)
            change = coarse_state[comp, 0, here, :] * jnp.where(ids < covered[0], value, 0.0)
            coarse_cells[comp, here, :] = change
            packed[comp, here, :] = packed[comp, here, :] + jnp.where(
                lane < g.half_side, change, 0.0
            )

        restrict_into(g, 1, d, rows, store)

        def load(comp, k, row, size):
            return coarse_cells[comp, pl.ds(row, size), :]

        prolong_from(g, 1, d, lane_limits(g, 1, near, side), rows, load)
        corrected_step(g, 1, d, rows)
        held = d.held
        adjoint[0] = held[0, 0, pl.ds(0, side), :]
        adjoint[1] = held[1, 0, pl.ds(0, side), :]
        adjoint[2] = joined_edges(
            g, held[0, 1, pl.ds(0, side), :], held[1, 1, pl.ds(0, side), :]
        )

        def write(first, second, base):
            out = Copies(sems, base)
            for comp in range(2):
                for done in range(0, rows, side):
                    size = min(side, rows - done)
                    out.start(
                        held.at[comp, 0, pl.ds(done, size)],
                        first.at[done // side, comp, pl.ds(0, size)],
                    )
            out.start(packed, second.at[0])
            out.finish()

        pl.when(odd)(lambda: write(mine_out, theirs_out, 10))
        pl.when(jnp.logical_not(odd))(lambda: write(theirs_out, mine_out, 20))


def up_kernel(
    g, rows_ref, adjoint, mine, theirs, state, mine_out, theirs_out, sems, edges, levels
):
    level_here = lax.axis_index("level")
    patch = lax.axis_index("patch")
    side = g.side
    top = g.levels - 1
    odd = level_here % 2 == 1

    @pl.when(level_here >= top - 1)
    def _():
        copies = Copies(sems)
        for level in (top - 1, top):
            for source, target in zip(state[level], levels[level][:4]):
                copies.start(source, target)
            clear_pads(
                levels[level].cells, [(c, k) for c in range(2) for k in range(g.blocks(level))]
            )
        both = adjoint[2]
        edges[0] = both
        edges[1] = pltpu.roll(both, g.half_side, 1)

        def load_given(comp, k, row, chunk):
            return (adjoint if k == 0 else edges)[comp, pl.ds(row, chunk), :]

        def load_held(comp, k, row, chunk):
            return levels[top - 1].held[comp, k, pl.ds(row, chunk), :]

        copies.finish()
        for level, load in ((top - 1, load_given), (top, load_held)):
            near = near_counts(g, rows_ref, level, patch, odd)
            limits = lane_limits(g, level, near, side)
            prolong_from(g, level, levels[level], limits, g.rows(level), load)
            corrected_step(g, level, levels[level], g.rows(level))

        def write(first, second):
            out = Copies(sems)
            half_of_level(g, top - 1, levels[top - 1].held, second, out)
            half_of_level(g, top, levels[top].held, first, out)
            out.finish()

        pl.when(odd)(lambda: write(mine_out, theirs_out))
        pl.when(jnp.logical_not(odd))(lambda: write(theirs_out, mine_out))


def join_kernel(g, mine, given, speed, fric, adjoint, gradient):
    level_here = lax.axis_index("level")
    lane = lane_ids(g.side)

    def put(slot, parts):
        for comp in range(2):
            adjoint[slot, comp] = parts[comp]
        total = speed[slot, 0].astype(F32) * parts[0] + speed[slot, 1].astype(F32) * parts[1]
        gradient[slot] = (-(fric[slot].astype(F32) * total)).astype(BF16)

    def join_level(level):
        if level == 0:
            for k in range(g.half_slots):
                low = []
                high = []
                for comp in range(2):
                    west, east = given[k, comp], mine[k, comp]
                    low.append(
                        jnp.where(lane < g.half_side, west, pltpu.roll(east, g.half_side, 1))
                    )
                    high.append(
                        jnp.where(lane < g.half_side, pltpu.roll(west, g.half_side, 1), east)
                    )
                put(k, low)
                put(k + g.half_slots, high)
            return
        own = g.own(level)
        west_half, east_half = (mine, given) if level % 2 == 1 else (given, mine)
        for r in range(g.patch_rows(level)):
            for k in range(2 * own):
                source = west_half if k < own else east_half
                put(
                    r * g.columns(level) + k,
                    [source[r * own + k % own, comp] for comp in range(2)],
                )

    for level in range(g.levels):
        pl.when(level_here == level)(lambda level=level: join_level(level))


def run_kernel(body, ins, outs, scratch, aliases=()):
    in_trees = [jax.tree.flatten(tree) for tree, _ in ins]
    out_trees = [jax.tree.flatten(tree) for tree, _ in outs]
    scratch_trees = [jax.tree.flatten(tree) for tree in scratch]
    sizes = [len(leaves) for leaves, _ in in_trees + out_trees + scratch_trees]
    shapes = [tree for _, tree in in_trees + out_trees + scratch_trees]

    def kernel(*refs):
        given = []
        first = 0
        for size, shape in zip(sizes, shapes):
            given.append(jax.tree.unflatten(shape, refs[first : first + size]))
            first += size
        body(*given)

    def specs(groups, trees):
        return [
            pl.BlockSpec(memory_space=space)
            for (_, space), (leaves, _) in zip(groups, trees)
            for _ in leaves
        ]

    def place(trees, index):
        return sum(len(leaves) for leaves, _ in trees[:index])

    results = pl.pallas_call(
        kernel,
        out_shape=[leaf for leaves, _ in out_trees for leaf in leaves],
        in_specs=specs(ins, in_trees),
        out_specs=specs(outs, out_trees),
        scratch_shapes=[leaf for leaves, _ in scratch_trees for leaf in leaves],
        input_output_aliases={place(in_trees, a): place(out_trees, b) for a, b in aliases},
        compiler_params=pltpu.CompilerParams(vmem_limit_bytes=VMEM_BYTES),
    )(*[leaf for leaves, _ in in_trees for leaf in leaves])
    answer = []
    first = 0
    for leaves, shape in out_trees:
        answer.append(jax.tree.unflatten(shape, results[first : first + len(leaves)]))
        first += len(leaves)
    return answer


def moved(value, g, step):
    pairs = []
    for patch in range(g.patches):
        for level in range(g.levels):
            to_patch, to_level = step(patch, level)
            if 0 <= to_patch < g.patches and 0 <= to_level < g.levels:
                pairs.append((patch * g.levels + level, to_patch * g.levels + to_level))
    return lax.ppermute(value, ("patch", "level"), pairs)


def per_device(forcing, velocity, viscosity, friction, patch_rows):
    g = Layout(
        forcing.shape[1], forcing.shape[-1], lax.axis_size("level"), lax.axis_size("patch")
    )
    side = g.side
    top = g.levels - 1
    force, speed, visc, fric = forcing[0], velocity[0], viscosity[0], friction[0]
    block = jax.ShapeDtypeStruct((side, side), F32)
    half = jax.ShapeDtypeStruct((g.half_slots, 2, side, side), F32)
    three = jax.ShapeDtypeStruct((3, side, side), F32)
    sems = pltpu.SemaphoreType.DMA((40,))

    swap, edge_own, edge_other = run_kernel(
        lambda *refs: pack_kernel(g, *refs),
        [(force, VM), (visc, VM), (fric, VM)],
        [
            (jax.ShapeDtypeStruct((4 * g.half_slots + 1, side, side), F32), VM),
            (block, VM),
            (block, VM),
        ],
        [],
    )
    swap = moved(swap, g, lambda p, l: (p, l ^ 1))
    edge_own = moved(edge_own, g, lambda p, l: (p + (1 if l % 2 else -1), l))
    edge_other = moved(edge_other, g, lambda p, l: (p + (-1 if l % 2 else 1), l ^ 1))

    rows = bottom_rows(g)
    down_state = [
        jax.ShapeDtypeStruct((2, 1, rows // 2, side), F32),
        level_arrays(g, 2, rows, jax.ShapeDtypeStruct, False),
        level_state(g, top - 1),
        level_state(g, top),
    ]
    sums, mine, theirs, state = run_kernel(
        lambda *refs: down_kernel(g, *refs),
        [
            (patch_rows, SM),
            (force, VM),
            (visc, VM),
            (fric, VM),
            (swap, VM),
            (edge_own, VM),
            (edge_other, VM),
        ],
        [(three, VM), (half, ANY), (half, ANY), (down_state, ANY)],
        [
            sems,
            pltpu.VMEM((2, side, side), F32),
            pltpu.VMEM(half.shape, F32),
            [level_scratch(g, level) for level in range(g.levels)],
        ],
    )
    sums = moved(sums, g, lambda p, l: (p, l - 2))
    adjoint, mine, theirs = run_kernel(
        lambda *refs: bottom_kernel(g, *refs),
        [(patch_rows, SM), (sums, VM), (mine, ANY), (theirs, ANY), (state[1], ANY), (state[0], ANY)],
        [(three, VM), (half, ANY), (half, ANY)],
        [
            sems,
            pltpu.VMEM((2, side, side), F32),
            level_arrays(g, 2, rows, pltpu.VMEM, True),
            pltpu.VMEM((2, 1, rows // 2, side), F32),
            pltpu.VMEM((2, rows // 2, side), F32),
        ],
        [(2, 1), (3, 2)],
    )
    adjoint = moved(adjoint, g, lambda p, l: (p, l + 2))
    mine, theirs = run_kernel(
        lambda rows_ref, a, m, t, *refs: up_kernel(
            g, rows_ref, a, m, t, {top - 1: refs[0], top: refs[1]}, *refs[2:6],
            {top - 1: refs[6], top: refs[7]},
        ),
        [
            (patch_rows, SM),
            (adjoint, VM),
            (mine, ANY),
            (theirs, ANY),
            (state[top - 1], ANY),
            (state[top], ANY),
        ],
        [(half, ANY), (half, ANY)],
        [
            sems,
            pltpu.VMEM((2, side, side), F32),
            level_scratch(g, top - 1),
            level_scratch(g, top),
        ],
        [(2, 0), (3, 1)],
    )
    given = moved(theirs, g, lambda p, l: (p, l ^ 1))
    adjoint, gradient = run_kernel(
        lambda *refs: join_kernel(g, *refs),
        [(mine, VM), (given, VM), (speed, VM), (fric, VM)],
        [
            (jax.ShapeDtypeStruct((g.slots, 2, side, side), F32), VM),
            (jax.ShapeDtypeStruct((g.slots, side, side), BF16), VM),
        ],
        [],
    )
    return (adjoint[None], gradient[None])


def solution(mesh):
    fields = P("level", "patch")
    return jax.shard_map(
        per_device,
        mesh=mesh,
        in_specs=(fields, fields, fields, fields, P()),
        out_specs=(fields, fields),
        check_vma=False,
    )
```

time: 671 us -> 72.8 us (0.11)
  the two profiles are of different devices: /device:TPU:6 before, /device:TPU:19 now
where the time goes in v1:
time: 72.8 us; the launch traced here: 72.4 us
  Pallas kernels  29 us (40%)
  waiting for transfers between devices  21.3 us (29%)
  starting transfers between devices  17.3 us (24%)
  local copies, waits for them, and re-layouts  4.07 us (6%)
  between operations  0.74 us (1%)
    pallas_call x5, Pallas kernels, run_kernel(): pl.pallas_call(kernel, out_shape=[leaf for leaves, _ in out_trees for lea...  29 us
    ppermute x6, waiting for transfers between devices, moved(): return lax.ppermute(value, ('patch', 'level'), pairs)  21.3 us
    ppermute x6, starting transfers between devices, moved(): return lax.ppermute(value, ('patch', 'level'), pairs)  17.3 us
    unnamed x20, local copies, waits for them, and re-layouts  4.07 us
  transfers between devices with their start and end apart: 6, of which 5 were waited for; matrix products, arithmetic and copies ran while one was open for 0% of the time, Pallas kernels for 0%

profile of v1, /device:TPU:19, one launch (start us, length us, event | category | flops | bytes accessed | tf_op | source)
XLA Modules:
  0.0 72.4 jit_solution(5532851810316727266)
XLA Ops:
  0.6 0.0 copy-start.8
  0.6 0.0 copy-start
  0.7 0.9 %copy-done = bf16[1,8,128,128]{3,2,1,0:T(8,128)(2,1)S(1)} copy-done((bf16[1,8,128,128]{3,2,1,0:T(8,128)(2,1)S(1)}, bf16[1,8,128,128]{3,2,1,0:T(8,128)(2,1)}, u32[]{:S(2)}) %copy-start) | copy-done | bytes 262168
  1.6 0.0 copy-start.2
  1.6 1.0 %copy-done.2 = bf16[1,8,2,128,128]{4,3,2,1,0:T(8,128)(2,1)S(1)} copy-done((bf16[1,8,2,128,128]{4,3,2,1,0:T(8,128)(2,1)S(1)}, bf16[1,8,2,128,128]{4,3,2,1,0:T(8,128)(2,1)}, u32[]{:S(2)}) %copy-start.2) | copy-done | bytes 524312
  2.6 0.0 copy-start.3
  2.6 1.0 %copy-done.3 = f32[1,8,128,128]{3,2,1,0:T(8,128)S(1)} copy-done((f32[1,8,128,128]{3,2,1,0:T(8,128)S(1)}, f32[1,8,128,128]{3,2,1,0:T(8,128)}, u32[]{:S(2)}) %copy-start.3) | copy-done | bytes 524312
  3.7 0.2 shard_map.68
  3.9 0.9 %collective-permute-start = (f32[17,128,128]{2,1,0:T(8,128)S(1)}, f32[17,128,128]{2,1,0:T(8,128)S(1)}, u32[]{:S(2)}, u32[]{:S(2)}) collective-permute-start(f32[17,128,128]{2,1,0:T(8,128)S(1)} %get-tuple-element.28), channel_id=1, source_target_pairs={{0,1},{1,0},{2,3},{3,2},{4,5},{5,4},{6,7},{7,6},{8,9},{9,8},{10,11... | collective-permute-start | bytes 3342344 | tf_op jit(solution)/shard_map/ppermute | solution.py:830
  4.8 3.1 %collective-permute-start.1 = (f32[128,128]{1,0:T(8,128)S(1)}, f32[128,128]{1,0:T(8,128)S(1)}, u32[]{:S(2)}, u32[]{:S(2)}) collective-permute-start(f32[128,128]{1,0:T(8,128)S(1)} %get-tuple-element.29), channel_id=1, source_target_pairs={{1,5},{3,7},{4,0},{5,9},{6,2},{7,11},{8,4},{9,13},{10,6},{11,15},{... | collective-permute-start | bytes 196616 | tf_op jit(solution)/shard_map/ppermute | solution.py:830
  7.9 2.2 %collective-permute-start.2 = (f32[128,128]{1,0:T(8,128)S(1)}, f32[128,128]{1,0:T(8,128)S(1)}, u32[]{:S(2)}, u32[]{:S(2)}) collective-permute-start(f32[128,128]{1,0:T(8,128)S(1)} %get-tuple-element.30), channel_id=1, source_target_pairs={{0,5},{2,7},{4,9},{5,0},{6,11},{7,2},{8,13},{9,4},{10,15},{11,6},{... | collective-permute-start | bytes 196616 | tf_op jit(solution)/shard_map/ppermute | solution.py:830
  10.1 0.6 collective-permute-done.1.refs_5_
  10.8 3.6 %collective-permute-done.2.refs_6_ = f32[128,128]{1,0:T(8,128)S(1)} collective-permute-done((f32[128,128]{1,0:T(8,128)S(1)}, f32[128,128]{1,0:T(8,128)S(1)}, u32[]{:S(2)}, u32[]{:S(2)}) %collective-permute-start.2) | collective-permute-done | bytes 65568 | tf_op jit(solution)/shard_map/ppermute | solution.py:830
  14.4 0.0 collective-permute-done.refs_4_
  14.4 0.0 copy-start.9
  14.4 1.0 %copy-done.9 = f32[17,128,128]{2,1,0:T(8,128)} copy-done((f32[17,128,128]{2,1,0:T(8,128)}, f32[17,128,128]{2,1,0:T(8,128)S(1)}, u32[]{:S(2)}) %copy-start.9) | copy-done | bytes 1114136
  15.4 0.0 copy-done.8
  15.4 15.6 %shard_map.69 = (f32[3,128,128]{2,1,0:T(8,128)S(1)}, f32[4,2,128,128]{3,2,1,0:T(8,128)S(1)}, f32[4,2,128,128]{3,2,1,0:T(8,128)S(1)}, f32[2,1,72,128]{3,2,1,0:T(8...) custom-call(s32[4,8]{1,0:T(4,128)S(1)} %copy-done.8, ...), custom_call_target="tpu_custom_call" | custom-call | tf_op jit(solution)/shard_map/pallas_call | solution.py:806
  31.0 8.9 %collective-permute-start.3 = (f32[3,128,128]{2,1,0:T(8,128)S(1)}, f32[3,128,128]{2,1,0:T(8,128)S(1)}, u32[]{:S(2)}, u32[]{:S(2)}) collective-permute-start(f32[3,128,128]{2,1,0:T(8,128)S(1)} %get-tuple-element.31), channel_id=1, source_target_pairs={{2,0},{3,1},{6,4},{7,5},{10,8},{11,9},{14,12},{15,13},{18,16},{19,... | collective-permute-start | bytes 589832 | tf_op jit(solution)/shard_map/ppermute | solution.py:830
  39.9 4.2 %collective-permute-done.3.refs_1_ = f32[3,128,128]{2,1,0:T(8,128)S(1)} collective-permute-done((f32[3,128,128]{2,1,0:T(8,128)S(1)}, f32[3,128,128]{2,1,0:T(8,128)S(1)}, u32[]{:S(2)}, u32[]{:S(2)}) %collective-permute-start.3) | collective-permute-done | bytes 196640 | tf_op jit(solution)/shard_map/ppermute | solution.py:830
  44.1 0.0 copy-start.4
  44.1 0.0 copy-start.5
  44.1 0.0 copy-start.6
  44.1 0.9 %shard_map.70 = (f32[3,128,128]{2,1,0:T(8,128)S(1)}, f32[4,2,128,128]{3,2,1,0:T(8,128)S(1)}, f32[4,2,128,128]{3,2,1,0:T(8,128)S(1)}) custom-call(s32[4,8]{1,0:T(4,128)S(1)} %copy-done.8, f32[3,128,128]{2,1,0:T(8,128)S(1)} %collective-permute-done.3.refs_1_, ...), custom_call_target="tpu_custom_call", output_to_operand_aliasing={{1}: (2, {}), {2}: (3, {})} | custom-call | tf_op jit(solution)/shard_map/pallas_call | solution.py:806
  45.1 1.3 %collective-permute-start.4 = (f32[3,128,128]{2,1,0:T(8,128)S(1)}, f32[3,128,128]{2,1,0:T(8,128)S(1)}, u32[]{:S(2)}, u32[]{:S(2)}) collective-permute-start(f32[3,128,128]{2,1,0:T(8,128)S(1)} %get-tuple-element.39), channel_id=1, source_target_pairs={{0,2},{1,3},{4,6},{5,7},{8,10},{9,11},{12,14},{13,15},{16,18},{17,... | collective-permute-start | bytes 589832 | tf_op jit(solution)/shard_map/ppermute | solution.py:830
  46.4 11.3 %collective-permute-done.4.refs_1_ = f32[3,128,128]{2,1,0:T(8,128)S(1)} collective-permute-done((f32[3,128,128]{2,1,0:T(8,128)S(1)}, f32[3,128,128]{2,1,0:T(8,128)S(1)}, u32[]{:S(2)}, u32[]{:S(2)}) %collective-permute-start.4) | collective-permute-done | bytes 196640 | tf_op jit(solution)/shard_map/ppermute | solution.py:830
  57.7 0.0 copy-done.4
  57.7 0.0 copy-done.5
  57.7 0.0 copy-done.6
  57.7 0.0 copy-start.1
  57.7 0.0 copy-start.7
  57.7 11.1 %shard_map.71 = (f32[4,2,128,128]{3,2,1,0:T(8,128)S(1)}, f32[4,2,128,128]{3,2,1,0:T(8,128)S(1)}) custom-call(s32[4,8]{1,0:T(4,128)S(1)} %copy-done.8, f32[3,128,128]{2,1,0:T(8,128)S(1)} %collective-permute-done.4.refs_1_, f32[4,2,128,128]{3,2,1,0:T(8,128)S(1)} %get-tuple-element.40.refs_2_, ...), custom_call_target="tpu_custom_call", output_to_operand_aliasing={{0}: (2, {}), {1}: (3, {})} | custom-call | tf_op jit(solution)/shard_map/pallas_call | solution.py:806
  68.8 0.9 %collective-permute-start.5 = (f32[4,2,128,128]{3,2,1,0:T(8,128)S(1)}, f32[4,2,128,128]{3,2,1,0:T(8,128)S(1)}, u32[]{:S(2)}, u32[]{:S(2)}) collective-permute-start(f32[4,2,128,128]{3,2,1,0:T(8,128)S(1)} %get-tuple-element.51), channel_id=1, source_target_pairs={{0,1},{1,0},{2,3},{3,2},{4,5},{5,4},{6,7},{7,6},{8,9},{9,8},{10,11... | collective-permute-start | bytes 1572872 | tf_op jit(solution)/shard_map/ppermute | solution.py:830
  69.6 1.5 %collective-permute-done.5.refs_1_ = f32[4,2,128,128]{3,2,1,0:T(8,128)S(1)} collective-permute-done((f32[4,2,128,128]{3,2,1,0:T(8,128)S(1)}, f32[4,2,128,128]{3,2,1,0:T(8,128)S(1)}, u32[]{:S(2)}, u32[]{:S(2)}) %collective-permute-start.5) | collective-permute-done | bytes 524320 | tf_op jit(solution)/shard_map/ppermute | solution.py:830
  71.2 0.0 copy-done.1
  71.2 0.0 copy-done.7
  71.2 1.2 %shard_map.72 = (f32[8,2,128,128]{3,2,1,0:T(8,128)}, bf16[8,128,128]{2,1,0:T(8,128)(2,1)}) custom-call(f32[4,2,128,128]{3,2,1,0:T(8,128)S(1)} %get-tuple-element.50.refs_0_, f32[4,2,128,128]{3,2,1,0:T(8,128)S(1)} %collective-permute-done.5.refs_1_, bf16[8,2,128,128]{3,2,1,0:T(8,128)(2,1)S(1)} %bitcast.13, bf16[8,128,128]{2,1,0:T(8,128)(2,1)S(1)} %bitcast.8), custom_call_target="tpu_custom_call" | custom-call | tf_op jit(solution)/shard_map/pallas_call | solution.py:806
Async XLA Ops:
  0.6 14.8 %copy-start.8 = (s32[4,8]{1,0:T(4,128)S(1)}, s32[4,8]{1,0:T(4,128)}, u32[]{:S(2)}) copy-start(s32[4,8]{1,0:T(4,128)} %refs_0_.5) | copy-start | bytes 388
  0.6 1.0 %copy-start = (bf16[1,8,128,128]{3,2,1,0:T(8,128)(2,1)S(1)}, bf16[1,8,128,128]{3,2,1,0:T(8,128)(2,1)}, u32[]{:S(2)}) copy-start(bf16[1,8,128,128]{3,2,1,0:T(8,128)(2,1)} %param.8) | copy-start | bytes 786436
  1.6 1.0 %copy-start.2 = (bf16[1,8,2,128,128]{4,3,2,1,0:T(8,128)(2,1)S(1)}, bf16[1,8,2,128,128]{4,3,2,1,0:T(8,128)(2,1)}, u32[]{:S(2)}) copy-start(bf16[1,8,2,128,128]{4,3,2,1,0:T(8,128)(2,1)} %param.5) | copy-start | bytes 1572868
  2.6 1.0 %copy-start.3 = (f32[1,8,128,128]{3,2,1,0:T(8,128)S(1)}, f32[1,8,128,128]{3,2,1,0:T(8,128)}, u32[]{:S(2)}) copy-start(f32[1,8,128,128]{3,2,1,0:T(8,128)} %param.7) | copy-start | bytes 1572868
  3.9 10.5 %collective-permute-start = (f32[17,128,128]{2,1,0:T(8,128)S(1)}, f32[17,128,128]{2,1,0:T(8,128)S(1)}, u32[]{:S(2)}, u32[]{:S(2)}) collective-permute-start(f32[17,128,128]{2,1,0:T(8,128)S(1)} %get-tuple-element.28), channel_id=1, source_target_pairs={{0,1},{1,0},{2,3},{3,2},{4,5},{5,4},{6,7},{7,6},{8,9},{9,8},{10,11... | collective-permute-start | bytes 3342344 | tf_op jit(solution)/shard_map/ppermute | solution.py:830
  4.8 6.0 %collective-permute-start.1 = (f32[128,128]{1,0:T(8,128)S(1)}, f32[128,128]{1,0:T(8,128)S(1)}, u32[]{:S(2)}, u32[]{:S(2)}) collective-permute-start(f32[128,128]{1,0:T(8,128)S(1)} %get-tuple-element.29), channel_id=1, source_target_pairs={{1,5},{3,7},{4,0},{5,9},{6,2},{7,11},{8,4},{9,13},{10,6},{11,15},{... | collective-permute-start | bytes 196616 | tf_op jit(solution)/shard_map/ppermute | solution.py:830
  7.9 6.5 %collective-permute-start.2 = (f32[128,128]{1,0:T(8,128)S(1)}, f32[128,128]{1,0:T(8,128)S(1)}, u32[]{:S(2)}, u32[]{:S(2)}) collective-permute-start(f32[128,128]{1,0:T(8,128)S(1)} %get-tuple-element.30), channel_id=1, source_target_pairs={{0,5},{2,7},{4,9},{5,0},{6,11},{7,2},{8,13},{9,4},{10,15},{11,6},{... | collective-permute-start | bytes 196616 | tf_op jit(solution)/shard_map/ppermute | solution.py:830
  14.4 1.0 %copy-start.9 = (f32[17,128,128]{2,1,0:T(8,128)}, f32[17,128,128]{2,1,0:T(8,128)S(1)}, u32[]{:S(2)}) copy-start(f32[17,128,128]{2,1,0:T(8,128)S(1)} %collective-permute-done.refs_4_) | copy-start | bytes 3342340
  31.0 13.1 %collective-permute-start.3 = (f32[3,128,128]{2,1,0:T(8,128)S(1)}, f32[3,128,128]{2,1,0:T(8,128)S(1)}, u32[]{:S(2)}, u32[]{:S(2)}) collective-permute-start(f32[3,128,128]{2,1,0:T(8,128)S(1)} %get-tuple-element.31), channel_id=1, source_target_pairs={{2,0},{3,1},{6,4},{7,5},{10,8},{11,9},{14,12},{15,13},{18,16},{19,... | collective-permute-start | bytes 589832 | tf_op jit(solution)/shard_map/ppermute | solution.py:830
  44.1 13.6 %copy-start.4 = (f32[2,3,256,128]{3,2,1,0:T(8,128)S(1)}, f32[2,3,256,128]{3,2,1,0:T(8,128)}, u32[]{:S(2)}) copy-start(f32[2,3,256,128]{3,2,1,0:T(8,128)} %get-tuple-element.44.refs_6_) | copy-start | bytes 2359300
  44.1 13.6 %copy-start.5 = (f32[2,3,256,128]{3,2,1,0:T(8,128)S(1)}, f32[2,3,256,128]{3,2,1,0:T(8,128)}, u32[]{:S(2)}) copy-start(f32[2,3,256,128]{3,2,1,0:T(8,128)} %get-tuple-element.45.refs_7_) | copy-start | bytes 2359300
  44.1 13.6 %copy-start.6 = (f32[2,5,128,128]{3,2,1,0:T(8,128)S(1)}, f32[2,5,128,128]{3,2,1,0:T(8,128)}, u32[]{:S(2)}) copy-start(f32[2,5,128,128]{3,2,1,0:T(8,128)} %get-tuple-element.49.refs_11_) | copy-start | bytes 1966084
  45.1 12.6 %collective-permute-start.4 = (f32[3,128,128]{2,1,0:T(8,128)S(1)}, f32[3,128,128]{2,1,0:T(8,128)S(1)}, u32[]{:S(2)}, u32[]{:S(2)}) collective-permute-start(f32[3,128,128]{2,1,0:T(8,128)S(1)} %get-tuple-element.39), channel_id=1, source_target_pairs={{0,2},{1,3},{4,6},{5,7},{8,10},{9,11},{12,14},{13,15},{16,18},{17,... | collective-permute-start | bytes 589832 | tf_op jit(solution)/shard_map/ppermute | solution.py:830
  57.7 13.5 %copy-start.1 = (bf16[1,8,128,128]{3,2,1,0:T(8,128)(2,1)S(1)}, bf16[1,8,128,128]{3,2,1,0:T(8,128)(2,1)}, u32[]{:S(2)}) copy-start(bf16[1,8,128,128]{3,2,1,0:T(8,128)(2,1)} %param.8) | copy-start | bytes 786436
  57.7 13.5 %copy-start.7 = (bf16[1,8,2,128,128]{4,3,2,1,0:T(8,128)(2,1)S(1)}, bf16[1,8,2,128,128]{4,3,2,1,0:T(8,128)(2,1)}, u32[]{:S(2)}) copy-start(bf16[1,8,2,128,128]{4,3,2,1,0:T(8,128)(2,1)} %param.6) | copy-start | bytes 1572868
  68.8 2.4 %collective-permute-start.5 = (f32[4,2,128,128]{3,2,1,0:T(8,128)S(1)}, f32[4,2,128,128]{3,2,1,0:T(8,128)S(1)}, u32[]{:S(2)}, u32[]{:S(2)}) collective-permute-start(f32[4,2,128,128]{3,2,1,0:T(8,128)S(1)} %get-tuple-element.51), channel_id=1, source_target_pairs={{0,1},{1,0},{2,3},{3,2},{4,5},{5,4},{6,7},{7,6},{8,9},{9,8},{10,11... | collective-permute-start | bytes 1572872 | tf_op jit(solution)/shard_map/ppermute | solution.py:830

commit v2 on v1

v2 whole, which is shorter than its diff:
```python
from typing import Any, NamedTuple

import jax
import jax.numpy as jnp
from jax import lax
from jax.experimental import pallas as pl
from jax.experimental.pallas import tpu as pltpu
from jax.sharding import PartitionSpec as P

relaxation = 0.5
PAD = 8
LOW, HIGH, EDGES = 0, 1, 2
VM, SM, HBM = pltpu.VMEM, pltpu.SMEM, pltpu.HBM
F32 = jnp.float32
BF16 = jnp.bfloat16
VMEM_BYTES = 30 * 2**20


class Layout:
    def __init__(self, slots, side, levels, patches):
        self.slots = slots
        self.side = side
        self.levels = levels
        self.patches = patches
        self.half_slots = slots // 2
        self.half_side = side // 2
        self.span = 2 * slots

    def columns(self, level):
        return 1 << level

    def patch_rows(self, level):
        return self.slots >> level

    def rows(self, level):
        return self.patch_rows(level) * self.side

    def margin(self, level):
        return 2 << level

    def own(self, level):
        return max(1, (1 << level) // 2)

    def blocks(self, level):
        return self.own(level) + (1 if level > 0 else 0)

    def chunk(self, level, rows):
        size = 8 * max(1, 14 // self.blocks(level))
        while rows % size or (rows % self.side == 0 and self.side % size):
            size -= 8
        return size


def lane_ids(side):
    return lax.broadcasted_iota(jnp.int32, (1, side), 1)


def near_counts(g, rows_ref, level, patch, odd):
    own = rows_ref[level, patch]
    east = jnp.where(
        patch + 1 < g.patches, rows_ref[level, jnp.minimum(patch + 1, g.patches - 1)], 0
    )
    west = jnp.where(patch > 0, rows_ref[level, jnp.maximum(patch - 1, 0)], 0)
    return own, jnp.where(odd, own, east), jnp.where(odd, west, own)


def lane_limits(g, level, counts, cells):
    own, east, west = (value * cells for value in counts)
    lane = lane_ids(g.side)
    margin = g.margin(level)
    first = 0 if level > 0 else g.half_side
    edges = jnp.where(
        (lane >= first) & (lane < first + margin), east, jnp.where(lane >= g.side - margin, west, 0)
    )
    if level == 0:
        return [jnp.where(lane < g.half_side, own, edges)]
    return [jnp.full((1, g.side), own, jnp.int32)] * g.own(level) + [edges]


def one_side(g, values, east):
    count = len(values)
    turned = [pltpu.roll(value, g.side - 1 if east else 1, 1) for value in values]
    if count == 1:
        return turned
    lane = lax.broadcasted_iota(jnp.int32, values[0].shape, 1)
    last = lane == (g.side - 1 if east else 0)
    step = 1 if east else -1
    return [jnp.where(last, turned[(k + step) % count], turned[k]) for k in range(count)]


def both_sides(g, values):
    return one_side(g, values, True), one_side(g, values, False)


def over_rows(rows, chunk, body):
    def step(index, carry):
        body(pl.multiple_of(index * chunk, chunk))
        return carry

    lax.fori_loop(0, rows // chunk, step, 0)


def clear_pads(ref, lead):
    width = ref.shape[-1]
    last = ref.shape[-2]
    for index in lead:
        ref[index + (slice(0, PAD), slice(None))] = jnp.zeros((PAD, width), F32)
        ref[index + (slice(last - PAD, last), slice(None))] = jnp.zeros((PAD, width), F32)


def off_diagonal_step(g, level, d, start, stop):
    count = g.blocks(level)
    chunk = g.chunk(level, stop - start)

    def body(row):
        row = row + start
        here = pl.ds(row, chunk)
        inner = pl.ds(PAD + row, chunk)

        def line(comp, step):
            rows = pl.ds(PAD + row + step, chunk)
            return [d.cells[comp, k, rows, :] for k in range(count)]

        centre = [line(comp, 0) for comp in range(2)]
        beside = [both_sides(g, centre[comp]) for comp in range(2)]
        products = []
        for k in range(count):
            visc = d.visc[k, inner, :]
            half = 0.5 * visc
            (u, v) = (centre[comp][k] for comp in range(2))
            (u_e, u_w), (v_e, v_w) = ((beside[c][0][k], beside[c][1][k]) for c in range(2))
            u_n, v_n = (d.cells[c, k, pl.ds(PAD + row + 1, chunk), :] for c in range(2))
            u_s, v_s = (d.cells[c, k, pl.ds(PAD + row - 1, chunk), :] for c in range(2))
            one_u, one_v = visc * u, visc * v
            four_u, four_v = 4.0 * one_u, 4.0 * one_v
            cross_u, cross_v = half * (v_e - v_w), visc * (u_e - u_w)
            d.north[0, k, inner, :] = one_u + cross_u
            d.south[0, k, inner, :] = one_u - cross_u
            d.north[1, k, inner, :] = four_v + cross_v
            d.south[1, k, inner, :] = four_v - cross_v
            cross_u, cross_v = visc * (v_n - v_s), half * (u_n - u_s)
            products.append(
                (
                    four_u + cross_u,
                    four_u - cross_u,
                    one_v + cross_v,
                    one_v - cross_v,
                    visc * (4.0 * (u_e + u_w) + (u_n + u_s)),
                    visc * (4.0 * (v_n + v_s) + (v_e + v_w)),
                )
            )
        for comp in range(2):
            east = one_side(g, [item[2 * comp] for item in products], True)
            west = one_side(g, [item[2 * comp + 1] for item in products], False)
            for k in range(count):
                d.part[comp, k, here, :] = products[k][4 + comp] + east[k] + west[k]

    over_rows(stop - start, chunk, body)


def off_diagonal(d, comp, k, row, chunk):
    return (
        d.part[comp, k, pl.ds(row, chunk), :]
        + d.north[comp, k, pl.ds(PAD + row + 1, chunk), :]
        + d.south[comp, k, pl.ds(PAD + row - 1, chunk), :]
    )


def smooth_weights(g, level, d, limits, rows, from_zero):
    count = g.blocks(level)
    chunk = g.chunk(level, rows)

    def body(row):
        here = pl.ds(row, chunk)
        inner = pl.ds(PAD + row, chunk)
        centre = [d.visc[k, inner, :] for k in range(count)]
        east, west = both_sides(g, centre)
        for k in range(count):
            north = d.visc[k, pl.ds(PAD + row + 1, chunk), :]
            south = d.visc[k, pl.ds(PAD + row - 1, chunk), :]
            friction = d.fric[k, here, :]
            twice = 2.0 * centre[k]
            along_row = twice + east[k] + west[k]
            along_col = twice + north + south
            ids = row + lax.broadcasted_iota(jnp.int32, (chunk, g.side), 0)
            live = ids < limits[k]
            diag_u = 4.0 * along_row + along_col + friction
            diag_v = 4.0 * along_col + along_row + friction
            for comp, diag in ((0, diag_u), (1, diag_v)):
                weight = jnp.where(live, relaxation / diag, 0.0)
                d.weight[comp, k, here, :] = weight
                if from_zero:
                    d.cells[comp, k, inner, :] = weight * d.right[comp, k, here, :]

    over_rows(rows, chunk, body)


def residual_step(g, level, d, start, stop):
    count = g.blocks(level)
    chunk = g.chunk(level, stop - start)
    off_diagonal_step(g, level, d, start, stop)

    def body(row):
        row = row + start
        here = pl.ds(row, chunk)
        for comp in range(2):
            for k in range(count):
                weight = d.weight[comp, k, here, :]
                left = (1.0 - relaxation) * d.right[comp, k, here, :] + off_diagonal(
                    d, comp, k, row, chunk
                )
                left = jnp.where(weight > 0.0, left, 0.0)
                d.left[comp, k, here, :] = left
                d.held[comp, k, here, :] = (
                    d.cells[comp, k, pl.ds(PAD + row, chunk), :] + weight * left
                )

    over_rows(stop - start, chunk, body)


def corrected_step(g, level, d, start, stop, store):
    count = g.blocks(level)
    chunk = g.chunk(level, stop - start)
    off_diagonal_step(g, level, d, start, stop)

    def body(row):
        row = row + start
        here = pl.ds(row, chunk)
        for comp in range(2):
            for k in range(count):
                value = (
                    d.held[comp, k, here, :]
                    + (1.0 - relaxation) * d.cells[comp, k, pl.ds(PAD + row, chunk), :]
                    + d.weight[comp, k, here, :] * off_diagonal(d, comp, k, row, chunk)
                )
                store(comp, k, row, chunk, value)

    over_rows(stop - start, chunk, body)


def pairings(g, fine):
    if fine == 1:
        return [[(0, LOW), (1, HIGH)]]
    parts = [[(2 * k, LOW), (2 * k + 1, HIGH)] for k in range(g.own(fine) // 2)]
    return parts + [[(g.own(fine), EDGES)]]


def target_lane(g, part, fine_lane):
    halved = jnp.right_shift(fine_lane, 1)
    if part == LOW:
        return halved
    if part == HIGH:
        return g.half_side + halved
    return halved + jnp.where(fine_lane >= g.half_side, g.half_side, 0)


def sum_matrix(g, part):
    fine = lax.broadcasted_iota(jnp.int32, (g.side, g.side), 0)
    coarse = lax.broadcasted_iota(jnp.int32, (g.side, g.side), 1)
    return jnp.where(target_lane(g, part, fine) == coarse, 1.0, 0.0).astype(BF16)


def copy_matrix(g, part):
    coarse = lax.broadcasted_iota(jnp.int32, (g.side, g.side), 0)
    fine = lax.broadcasted_iota(jnp.int32, (g.side, g.side), 1)
    return jnp.where(target_lane(g, part, fine) == coarse, 1.0, 0.0).astype(BF16)


def split_dot(values, matrix):
    high = values.astype(BF16)
    rest = (values - high.astype(F32)).astype(BF16)
    return jnp.dot(high, matrix, preferred_element_type=F32) + jnp.dot(
        rest, matrix, preferred_element_type=F32
    )


def restrict_into(g, fine, d, start, stop, store):
    rows = stop - start
    chunk = min(rows // 2, g.half_side)
    if (rows // 2) % chunk:
        chunk = rows // 2
    parts = pairings(g, fine)
    matrices = {part: sum_matrix(g, part) for members in parts for _, part in members}

    def body(row):
        row = row + start // 2
        for comp in range(2):
            for coarse, members in enumerate(parts):
                total = None
                for k, part in members:
                    first = d.left[comp, k, pl.ds(2 * row, chunk, stride=2), :]
                    second = d.left[comp, k, pl.ds(2 * row + 1, chunk, stride=2), :]
                    term = split_dot(first + second, matrices[part])
                    total = term if total is None else total + term
                store(comp, coarse, row, chunk, total)

    over_rows(rows // 2, chunk, body)


def prolong_from(g, fine, d, limits, start, stop, load):
    rows = stop - start
    chunk = min(rows // 2, g.half_side)
    if (rows // 2) % chunk:
        chunk = rows // 2
    parts = pairings(g, fine)
    matrices = {part: copy_matrix(g, part) for members in parts for _, part in members}

    def body(row):
        row = row + start // 2
        ids = 2 * (row + lax.broadcasted_iota(jnp.int32, (chunk, g.side), 0))
        for comp in range(2):
            for coarse, members in enumerate(parts):
                value = load(comp, coarse, row, chunk)
                for k, part in members:
                    spread = jnp.where(ids < limits[k], split_dot(value, matrices[part]), 0.0)
                    d.cells[comp, k, pl.ds(PAD + 2 * row, chunk, stride=2), :] = spread
                    d.cells[comp, k, pl.ds(PAD + 2 * row + 1, chunk, stride=2), :] = spread

    over_rows(rows // 2, chunk, body)


def pack_kernel(g, force_in, visc_in, fric_in, swap, edge_own, edge_other, force, visc, fric, sems):
    level_here = lax.axis_index("level")
    copies = Copies(sems)
    for source, target in ((force_in, force), (visc_in, visc), (fric_in, fric)):
        copies.start(source, target)
    copies.finish()
    side = g.side

    def plane(q, slot):
        if q < 2:
            return force[slot, q].astype(F32)
        if q == 2:
            return fric[slot].astype(F32)
        return visc[slot]

    def packed_edge(level, column, start):
        lane = lane_ids(side)
        margin = g.margin(level)
        total = jnp.zeros((side, side), F32)
        for r in range(g.patch_rows(level)):
            slot = r * g.columns(level) + column
            for q in range(4):
                base = q * g.span + r * margin
                moved = plane(q, slot)
                if (base - start) % side:
                    moved = pltpu.roll(moved, (base - start) % side, 1)
                total = jnp.where((lane >= base) & (lane < base + margin), moved, total)
        return total

    def pack_level(level):
        west_type = level % 2 == 1
        margin = g.margin(level)
        last = g.columns(level) - 1
        west_edge = packed_edge(level, 0, 0)
        east_edge = packed_edge(level, last, side - margin)
        edge_own[...] = east_edge if west_type else west_edge
        edge_other[...] = west_edge if west_type else east_edge
        if level == 0:
            lane = lane_ids(side)
            for q in range(4):
                for k in range(g.half_slots):
                    swap[q * g.half_slots + k] = jnp.where(
                        lane < g.half_side,
                        plane(q, k),
                        pltpu.roll(plane(q, k + g.half_slots), g.half_side, 1),
                    )
            swap[4 * g.half_slots] = packed_edge(0, 0, g.half_side)
            return
        own = g.own(level)
        first = own if west_type else 0
        for r in range(g.patch_rows(level)):
            for k in range(own):
                for q in range(4):
                    swap[q * g.half_slots + r * own + k] = plane(
                        q, r * g.columns(level) + first + k
                    )
        if west_type:
            swap[4 * g.half_slots] = packed_edge(level, own - 1, side - margin)
        else:
            swap[4 * g.half_slots] = packed_edge(level, own, 0)

    for level in range(g.levels):
        pl.when(level_here == level)(lambda level=level: pack_level(level))


def fill_level(g, level, west_type, d, limits, covered, raw, got):
    force, visc, fric = raw
    swap, edge_own, edge_other = got
    side = g.side
    home = (level % 2 == 1) == west_type
    margin = g.margin(level)
    own = g.own(level)
    columns = g.columns(level)
    lane = lane_ids(side)
    edges = edge_own if home else edge_other

    def plane(q, slot):
        if q < 2:
            return force[slot, q].astype(F32)
        if q == 2:
            return fric[slot].astype(F32)
        return visc[slot]

    def unpacked(packed, q, r, place):
        shift = (place - (q * g.span + r * margin)) % side
        return pltpu.roll(packed, shift, 1) if shift else packed

    def store(q, k, r, value):
        here = pl.ds(r * side, side)
        if q < 2:
            if covered is not None:
                ids = r * side + lax.broadcasted_iota(jnp.int32, (side, side), 0)
                value = jnp.where(ids < covered[k], 0.0, value)
            d.right[q, k, here, :] = value
        elif q == 2:
            d.fric[k, here, :] = value
        else:
            d.visc[k, pl.ds(PAD + r * side, side), :] = jnp.where(
                limits[k] > r * side, 0.5 * value, 0.0
            )

    inner = swap[4 * g.half_slots]
    outer = edges[...]
    for r in range(g.patch_rows(level)):
        for q in range(4):
            if level == 0:
                if home:
                    value = pltpu.roll(plane(q, r), g.half_side, 1)
                    east = unpacked(outer, q, r, g.half_side)
                    value = jnp.where(
                        (lane >= g.half_side) & (lane < g.half_side + margin), east, value
                    )
                else:
                    value = swap[q * g.half_slots + r % g.half_slots]
                    if r >= g.half_slots:
                        value = pltpu.roll(value, g.half_side, 1)
                    east = unpacked(inner, q, r, g.half_side)
                    west = unpacked(outer, q, r, side - margin)
                    value = jnp.where(lane < g.half_side, value, east)
                    value = jnp.where(lane >= side - margin, west, value)
                store(q, 0, r, value)
                continue
            for k in range(own):
                if home:
                    value = plane(q, r * columns + k + (0 if west_type else own))
                else:
                    value = swap[q * g.half_slots + r * own + k]
                store(q, k, r, value)
            if west_type:
                if home:
                    east = plane(q, r * columns + own)
                else:
                    east = unpacked(inner, q, r, 0)
                west = unpacked(outer, q, r, side - margin)
            else:
                east = unpacked(outer, q, r, 0)
                if home:
                    west = plane(q, r * columns + own - 1)
                else:
                    west = unpacked(inner, q, r, side - margin)
            store(q, own, r, jnp.where(lane < g.half_side, east, west))


def joined_edges(g, edge_u, edge_v):
    lane = lane_ids(g.side)
    quarter = g.side // 4
    middle = (lane >= quarter) & (lane < g.side - quarter)
    return jnp.where(middle, pltpu.roll(edge_v, g.half_side, 1), edge_u)


class Level(NamedTuple):
    visc: Any
    weight: Any
    right: Any = None
    held: Any = None
    fric: Any = None
    cells: Any = None
    part: Any = None
    north: Any = None
    south: Any = None
    left: Any = None


def level_array(g, count, rows, make, comps, pad):
    shape = (count, rows + (2 * PAD if pad else 0), g.side)
    return make((2, *shape) if comps else shape, F32)


def kept_arrays(g, level, make, held):
    count, rows = g.blocks(level), g.rows(level)
    visc = level_array(g, count, rows, make, False, True)
    two = level_array(g, count, rows, make, True, False)
    return Level(visc, two, held=two) if held else Level(visc, two, right=two)


def step_arrays(g, level, rows):
    count = g.blocks(level)
    padded = level_array(g, count, rows, pltpu.VMEM, True, True)
    return dict(
        cells=padded,
        part=level_array(g, count, rows, pltpu.VMEM, True, False),
        north=padded,
        south=padded,
    )


def clear_level(g, level, d):
    blocks = range(g.blocks(level))
    both = [(c, k) for c in range(2) for k in blocks]
    for ref in (d.cells, d.north, d.south):
        clear_pads(ref, both)


def merged(first, second):
    return Level(*[b if a is None else a for a, b in zip(first, second)])


class Copies:
    def __init__(self, sems, first=0):
        self.sems = sems
        self.used = first
        self.open = []

    def start(self, source, target):
        copy = pltpu.make_async_copy(source, target, self.sems.at[self.used])
        self.used += 1
        copy.start()
        self.open.append(copy)

    def finish(self):
        for copy in self.open:
            copy.wait()
        self.open = []


def bottom_rows(g):
    return g.rows(2) // 2 + 4 * PAD


def kept_rows(g):
    return g.rows(2) // 2 + 2 * PAD


def down_kernel(
    g, rows_ref, force, visc, fric, swap, edge_own, edge_other, sums, kept, edges, scratch
):
    level_here = lax.axis_index("level")
    patch = lax.axis_index("patch")
    raw = (force, visc, fric)
    got = (swap, edge_own, edge_other)
    side = g.side
    top = g.levels - 1
    odd = level_here % 2 == 1
    levels = [merged(a, b) for a, b in zip(kept, scratch)]

    def limits_of(level):
        return lane_limits(g, level, near_counts(g, rows_ref, level, patch, odd), side)

    def covered_of(level):
        return lane_limits(g, level, near_counts(g, rows_ref, level + 1, patch, odd), g.half_side)

    def filled(wanted, covered):
        for level in wanted:
            clear_pads(levels[level].visc, [(k,) for k in range(g.blocks(level))])
        for west_type in (True, False):

            @pl.when(odd if west_type else jnp.logical_not(odd))
            def _():
                for level in wanted:
                    fill_level(
                        g, level, west_type, levels[level], limits_of(level),
                        covered.get(level), raw, got,
                    )

    @pl.when(level_here >= top - 1)
    def _():
        filled((top, top - 1), {})
        covered = covered_of(top - 1)

        def set_right(comp, k, row, chunk, value):
            here = pl.ds(row, chunk)
            ids = row + lax.broadcasted_iota(jnp.int32, (chunk, side), 0)
            old = levels[top - 1].right[comp, k, here, :]
            levels[top - 1].right[comp, k, here, :] = jnp.where(ids < covered[k], value, old)

        def keep(comp, k, row, chunk, value):
            (sums if k == 0 else edges)[comp, pl.ds(row, chunk), :] = value

        for level in (top, top - 1):
            d = levels[level]
            clear_level(g, level, d)
            smooth_weights(g, level, d, limits_of(level), g.rows(level), True)
            residual_step(g, level, d, 0, g.rows(level))
            restrict_into(g, level, d, 0, g.rows(level), set_right if level == top else keep)
        sums[2] = joined_edges(g, edges[0], edges[1])

    @pl.when(level_here < top - 1)
    def _():
        filled((1, 0), {1: covered_of(1)})
        for level in (1, 0):
            smooth_weights(g, level, levels[level], limits_of(level), g.rows(level), False)


def bottom_levels(g, rows_ref, patch, odd, start, stop, fine, coarse, new_sums, store_fine, store_coarse):
    side = g.side
    count, chunk = g.blocks(1), g.chunk(1, stop - start)
    clear_level(g, 1, fine)
    if new_sums is not None:
        reach = g.rows(2) // 2
        for comp in range(2):
            for k in range(count):
                here = pl.ds(0, reach)
                fine.right[comp, k, here, :] = fine.right[comp, k, here, :] + new_sums(comp, k)

    def body(row):
        here = pl.ds(start + row, chunk)
        for comp in range(2):
            for k in range(count):
                fine.cells[comp, k, pl.ds(PAD + start + row, chunk), :] = (
                    fine.weight[comp, k, here, :] * fine.right[comp, k, here, :]
                )

    over_rows(stop - start, chunk, body)
    residual_step(g, 1, fine, start, stop)
    near = near_counts(g, rows_ref, 1, patch, odd)
    covered = lane_limits(g, 0, near, g.half_side)

    def smooth_coarse(comp, k, row, size, value):
        here = pl.ds(row, size)
        ids = row + lax.broadcasted_iota(jnp.int32, (size, side), 0)
        value = jnp.where(ids < covered[0], value, coarse.right[comp, 0, here, :])
        value = coarse.weight[comp, 0, here, :] * value
        coarse.cells[comp, 0, here, :] = value
        store_coarse(comp, row, size, value)

    restrict_into(g, 1, fine, start, stop, smooth_coarse)

    def load(comp, k, row, size):
        return coarse.cells[comp, 0, pl.ds(row, size), :]

    prolong_from(g, 1, fine, lane_limits(g, 1, near, side), start, stop, load)
    corrected_step(g, 1, fine, start, stop, store_fine)


def bottom_kernel(g, rows_ref, sums, kept, coarse_kept, adjoint, own_rows, coarse_rows, edges, scratch, coarse_cells):
    level_here = lax.axis_index("level")
    patch = lax.axis_index("patch")
    side = g.side
    rows = bottom_rows(g)
    top = g.levels - 1
    odd = level_here % 2 == 1

    @pl.when(level_here < top - 1)
    def _():
        reach = g.rows(2) // 2
        both = sums[2]
        swapped = pltpu.roll(both, g.half_side, 1)
        fine = merged(Level(kept.visc, kept.weight), scratch)
        for comp in range(2):
            for k in range(g.blocks(1)):
                fine.right[comp, k] = kept.right[comp, k, pl.ds(0, rows), :]

        def new_sums(comp, k):
            value = sums[comp] if k == 0 else (both, swapped)[comp]
            return jnp.where(kept.weight[comp, k, pl.ds(0, reach), :] > 0.0, value, 0.0)

        def store_fine(comp, k, row, chunk, value):
            (own_rows if k == 0 else edges)[comp, pl.ds(row, chunk), :] = value

        def store_coarse(comp, row, size, value):
            coarse_rows[comp, pl.ds(row, size), :] = value

        coarse = Level(None, coarse_kept.weight, coarse_kept.right, cells=coarse_cells)
        bottom_levels(
            g, rows_ref, patch, odd, 0, rows, fine, coarse, new_sums, store_fine, store_coarse
        )
        adjoint[0] = own_rows[0, pl.ds(0, side), :]
        adjoint[1] = own_rows[1, pl.ds(0, side), :]
        adjoint[2] = joined_edges(g, edges[0, pl.ds(0, side), :], edges[1, pl.ds(0, side), :])


def up_kernel(
    g, rows_ref, adjoint, own_rows, coarse_rows, kept, mine, theirs, edges, scratch, coarse_cells, finer,
    coarser,
):
    level_here = lax.axis_index("level")
    patch = lax.axis_index("patch")
    side = g.side
    top = g.levels - 1
    odd = level_here % 2 == 1
    levels = [merged(a, b) for a, b in zip(kept, scratch)]

    def hand_out():
        def write(first, second):
            for k in range(g.half_slots):
                for comp in range(2):
                    first[k, comp] = finer[k, comp]
                    second[k, comp] = coarser[k, comp]

        pl.when(odd)(lambda: write(mine, theirs))
        pl.when(jnp.logical_not(odd))(lambda: write(theirs, mine))

    @pl.when(level_here >= top - 1)
    def _():
        both = adjoint[2]
        edges[0] = both
        edges[1] = pltpu.roll(both, g.half_side, 1)

        def load_given(comp, k, row, chunk):
            return (adjoint if k == 0 else edges)[comp, pl.ds(row, chunk), :]

        def load_held(comp, k, row, chunk):
            return levels[top - 1].held[comp, k, pl.ds(row, chunk), :]

        def store_in(level, out, hold):
            own = g.own(level)

            def store(comp, k, row, chunk, value):
                if hold:
                    levels[level].held[comp, k, pl.ds(row, chunk), :] = value
                if k < own:
                    group, place = row // side, row % side
                    out[group * own + k, comp, pl.ds(pl.multiple_of(place, 8), chunk), :] = value

            return store

        for level, load, out in ((top - 1, load_given, coarser), (top, load_held, finer)):
            d = levels[level]
            clear_level(g, level, d)
            near = near_counts(g, rows_ref, level, patch, odd)
            rows = g.rows(level)
            prolong_from(g, level, d, lane_limits(g, level, near, side), 0, rows, load)
            corrected_step(g, level, d, 0, rows, store_in(level, out, level < top))
        hand_out()

    @pl.when(level_here < top - 1)
    def _():
        rows = g.rows(1)
        first = g.rows(2) // 2
        done = kept_rows(g)
        fine, coarse = levels[1], levels[0]._replace(cells=coarse_cells)

        def store_fine(comp, k, row, chunk, value):
            if k == 0:
                group, place = row // side, row % side
                finer[group, comp, pl.ds(pl.multiple_of(place, 8), chunk), :] = value

        def store_coarse(comp, row, size, value):
            pass

        bottom_levels(
            g, rows_ref, patch, odd, first, rows, fine, coarse, None, store_fine, store_coarse
        )
        lane = lane_ids(side)
        for comp in range(2):
            finer[0, comp] = own_rows[comp, pl.ds(0, side), :]
            finer[1, comp, pl.ds(0, done - side), :] = own_rows[comp, pl.ds(side, done - side), :]
            coarse_cells[comp, 0, pl.ds(0, done // 2), :] = coarse_rows[
                comp, pl.ds(0, done // 2), :
            ]
            for k in range(g.half_slots):
                parts = []
                for group in (k, k + g.half_slots):
                    here = pl.ds(group * side, side)
                    if group * side < rows // 2:
                        parts.append(coarse_cells[comp, 0, here, :])
                    else:
                        parts.append(
                            coarse.weight[comp, 0, here, :] * coarse.right[comp, 0, here, :]
                        )
                coarser[k, comp] = jnp.where(
                    lane < g.half_side, parts[0], pltpu.roll(parts[1], g.half_side, 1)
                )
        hand_out()


def join_kernel(g, mine, given, speed, fric, adjoint, gradient):
    level_here = lax.axis_index("level")
    lane = lane_ids(g.side)

    def put(slot, parts):
        for comp in range(2):
            adjoint[slot, comp] = parts[comp]
        total = speed[slot, 0].astype(F32) * parts[0] + speed[slot, 1].astype(F32) * parts[1]
        gradient[slot] = (-(fric[slot].astype(F32) * total)).astype(BF16)

    def join_level(level):
        if level == 0:
            for k in range(g.half_slots):
                low = []
                high = []
                for comp in range(2):
                    west, east = given[k, comp], mine[k, comp]
                    low.append(
                        jnp.where(lane < g.half_side, west, pltpu.roll(east, g.half_side, 1))
                    )
                    high.append(
                        jnp.where(lane < g.half_side, pltpu.roll(west, g.half_side, 1), east)
                    )
                put(k, low)
                put(k + g.half_slots, high)
            return
        own = g.own(level)
        west_half, east_half = (mine, given) if level % 2 == 1 else (given, mine)
        for r in range(g.patch_rows(level)):
            for k in range(2 * own):
                source = west_half if k < own else east_half
                put(
                    r * g.columns(level) + k,
                    [source[r * own + k % own, comp] for comp in range(2)],
                )

    for level in range(g.levels):
        pl.when(level_here == level)(lambda level=level: join_level(level))


def run_kernel(body, ins, outs, scratch):
    in_trees = [jax.tree.flatten(tree) for tree, _ in ins]
    out_trees = [jax.tree.flatten(tree) for tree, _ in outs]
    scratch_trees = [jax.tree.flatten(tree) for tree in scratch]
    sizes = [len(leaves) for leaves, _ in in_trees + out_trees + scratch_trees]
    shapes = [tree for _, tree in in_trees + out_trees + scratch_trees]

    def kernel(*refs):
        given = []
        first = 0
        for size, shape in zip(sizes, shapes):
            given.append(jax.tree.unflatten(shape, refs[first : first + size]))
            first += size
        body(*given)

    def specs(groups, trees):
        return [
            pl.BlockSpec(memory_space=space)
            for (_, space), (leaves, _) in zip(groups, trees)
            for _ in leaves
        ]

    results = pl.pallas_call(
        kernel,
        out_shape=[leaf for leaves, _ in out_trees for leaf in leaves],
        in_specs=specs(ins, in_trees),
        out_specs=specs(outs, out_trees),
        scratch_shapes=[leaf for leaves, _ in scratch_trees for leaf in leaves],
        compiler_params=pltpu.CompilerParams(vmem_limit_bytes=VMEM_BYTES),
    )(*[leaf for leaves, _ in in_trees for leaf in leaves])
    answer = []
    first = 0
    for leaves, shape in out_trees:
        answer.append(jax.tree.unflatten(shape, results[first : first + len(leaves)]))
        first += len(leaves)
    return answer


def moved(value, g, step):
    pairs = []
    for patch in range(g.patches):
        for level in range(g.levels):
            to_patch, to_level = step(patch, level)
            if 0 <= to_patch < g.patches and 0 <= to_level < g.levels:
                pairs.append((patch * g.levels + level, to_patch * g.levels + to_level))
    return lax.ppermute(value, ("patch", "level"), pairs)


def per_device(forcing, velocity, viscosity, friction, patch_rows):
    g = Layout(
        forcing.shape[1], forcing.shape[-1], lax.axis_size("level"), lax.axis_size("patch")
    )
    side = g.side
    top = g.levels - 1
    force, speed, visc, fric = forcing[0], velocity[0], viscosity[0], friction[0]
    make = jax.ShapeDtypeStruct
    block = make((side, side), F32)
    half = make((g.half_slots, 2, side, side), F32)
    three = make((3, side, side), F32)
    two = pltpu.VMEM((2, side, side), F32)
    sems = pltpu.SemaphoreType.DMA((4,))

    swap, edge_own, edge_other, force, visc, fric = run_kernel(
        lambda *refs: pack_kernel(g, *refs),
        [(force, HBM), (visc, HBM), (fric, HBM)],
        [
            (make((4 * g.half_slots + 1, side, side), F32), VM),
            (block, VM),
            (block, VM),
            (make(force.shape, force.dtype), VM),
            (make(visc.shape, visc.dtype), VM),
            (make(fric.shape, fric.dtype), VM),
        ],
        [sems],
    )
    swap = moved(swap, g, lambda p, l: (p, l ^ 1))
    edge_own = moved(edge_own, g, lambda p, l: (p + (1 if l % 2 else -1), l))
    edge_other = moved(edge_other, g, lambda p, l: (p + (-1 if l % 2 else 1), l ^ 1))

    def down_scratch(level):
        count, rows = g.blocks(level), g.rows(level)
        fric_here = level_array(g, count, rows, pltpu.VMEM, False, False)
        if level < top - 1:
            return Level(None, None, fric=fric_here)
        both = level_array(g, count, rows, pltpu.VMEM, True, False)
        return Level(None, None, right=both, fric=fric_here, left=both, **step_arrays(g, level, rows))

    sums, kept = run_kernel(
        lambda *refs: down_kernel(g, *refs),
        [
            (patch_rows, SM),
            (force, VM),
            (visc, VM),
            (fric, VM),
            (swap, VM),
            (edge_own, VM),
            (edge_other, VM),
        ],
        [
            (three, VM),
            ([kept_arrays(g, level, make, level >= top - 1) for level in range(g.levels)], VM),
        ],
        [two, [down_scratch(level) for level in range(g.levels)]],
    )
    sums = moved(sums, g, lambda p, l: (p, l - 2))
    rows = bottom_rows(g)
    part = level_array(g, g.blocks(1), rows, pltpu.VMEM, True, False)
    adjoint, own_rows, coarse_rows = run_kernel(
        lambda *refs: bottom_kernel(g, *refs),
        [(patch_rows, SM), (sums, VM), (kept[1], VM), (kept[0], VM)],
        [
            (three, VM),
            (make((2, rows, side), F32), VM),
            (make((2, rows // 2, side), F32), VM),
        ],
        [
            pltpu.VMEM((2, rows, side), F32),
            Level(None, None, right=part, held=part, left=part, **step_arrays(g, 1, rows)),
            pltpu.VMEM((2, 1, rows // 2, side), F32),
        ],
    )
    adjoint = moved(adjoint, g, lambda p, l: (p, l + 2))

    def up_scratch(level):
        if level == 0:
            return Level(None, None)
        rows = g.rows(level)
        both = level_array(g, g.blocks(level), rows, pltpu.VMEM, True, False)
        more = dict(held=both, left=both) if level == 1 else {}
        return Level(None, None, **more, **step_arrays(g, level, rows))

    mine, theirs = run_kernel(
        lambda *refs: up_kernel(g, *refs),
        [(patch_rows, SM), (adjoint, VM), (own_rows, VM), (coarse_rows, VM), (kept, VM)],
        [(half, VM), (half, VM)],
        [
            two,
            [up_scratch(level) for level in range(g.levels)],
            pltpu.VMEM((2, 1, g.rows(1) // 2, side), F32),
            pltpu.VMEM(half.shape, F32),
            pltpu.VMEM(half.shape, F32),
        ],
    )
    given = moved(theirs, g, lambda p, l: (p, l ^ 1))
    adjoint, gradient = run_kernel(
        lambda *refs: join_kernel(g, *refs),
        [(mine, VM), (given, VM), (speed, VM), (fric, VM)],
        [
            (make((g.slots, 2, side, side), F32), VM),
            (make((g.slots, side, side), BF16), VM),
        ],
        [],
    )
    return (adjoint[None], gradient[None])


def solution(mesh):
    fields = P("level", "patch")
    return jax.shard_map(
        per_device,
        mesh=mesh,
        in_specs=(fields, fields, fields, fields, P()),
        out_specs=(fields, fields),
        check_vma=False,
    )
```

time: 72.8 us -> 47.6 us (0.65)
  the two profiles are of different devices: /device:TPU:19 before, /device:TPU:21 now
where the time goes in v2:
time: 47.6 us; the launch traced here: 47.2 us
  Pallas kernels  16.4 us (34%)
  waiting for transfers between devices  16.3 us (34%)
  starting transfers between devices  10.7 us (22%)
  local copies, waits for them, and re-layouts  3.04 us (6%)
  between operations  0.73 us (2%)
    pallas_call x5, Pallas kernels, run_kernel(): pl.pallas_call(kernel, out_shape=[leaf for leaves, _ in out_trees for lea...  16.4 us
    ppermute x6, waiting for transfers between devices, moved(): return lax.ppermute(value, ('patch', 'level'), pairs)  16.3 us
    ppermute x6, starting transfers between devices, moved(): return lax.ppermute(value, ('patch', 'level'), pairs)  10.7 us
    unnamed x10, local copies, waits for them, and re-layouts  3.04 us
  transfers between devices with their start and end apart: 6, of which 4 were waited for; matrix products, arithmetic and copies ran while one was open for 0% of the time, Pallas kernels for 0%

profile of v2, /device:TPU:21, one launch (start us, length us, event | category | flops | bytes accessed | tf_op | source)
XLA Modules:
  0.0 47.2 jit_solution(16282452934815686879)
XLA Ops:
  0.6 0.0 copy-start.4
  0.6 0.0 copy-start.1
  0.7 1.0 %copy-done.1 = bf16[1,8,2,128,128]{4,3,2,1,0:T(8,128)(2,1)S(1)} copy-done((bf16[1,8,2,128,128]{4,3,2,1,0:T(8,128)(2,1)S(1)}, bf16[1,8,2,128,128]{4,3,2,1,0:T(8,128)(2,1)}, u32[]{:S(2)}) %copy-start.1) | copy-done | bytes 524312
  1.7 0.0 copy-start.2
  1.7 1.0 %copy-done.2 = f32[1,8,128,128]{3,2,1,0:T(8,128)S(1)} copy-done((f32[1,8,128,128]{3,2,1,0:T(8,128)S(1)}, f32[1,8,128,128]{3,2,1,0:T(8,128)}, u32[]{:S(2)}) %copy-start.2) | copy-done | bytes 524312
  2.7 0.0 copy-start.3
  2.7 0.9 %copy-done.3 = bf16[1,8,128,128]{3,2,1,0:T(8,128)(2,1)S(1)} copy-done((bf16[1,8,128,128]{3,2,1,0:T(8,128)(2,1)S(1)}, bf16[1,8,128,128]{3,2,1,0:T(8,128)(2,1)}, u32[]{:S(2)}) %copy-start.3) | copy-done | bytes 262168
  3.7 0.7 %shard_map.68 = (f32[17,128,128]{2,1,0:T(8,128)S(1)}, f32[128,128]{1,0:T(8,128)S(1)}, f32[128,128]{1,0:T(8,128)S(1)}, bf16[8,2,128,128]{3,2,1,0:T(8,128)(2,1)S(1...) custom-call(bf16[8,2,128,128]{3,2,1,0:T(8,128)(2,1)S(1)} %bitcast.7, f32[8,128,128]{2,1,0:T(8,128)S(1)} %bitcast.8, ...), custom_call_target="tpu_custom_call" | custom-call | tf_op jit(solution)/shard_map/pallas_call | solution.py:840
  4.4 1.5 %collective-permute-start = (f32[17,128,128]{2,1,0:T(8,128)S(1)}, f32[17,128,128]{2,1,0:T(8,128)S(1)}, u32[]{:S(2)}, u32[]{:S(2)}) collective-permute-start(f32[17,128,128]{2,1,0:T(8,128)S(1)} %get-tuple-element.31), channel_id=1, source_target_pairs={{0,1},{1,0},{2,3},{3,2},{4,5},{5,4},{6,7},{7,6},{8,9},{9,8},{10,11... | collective-permute-start | bytes 3342344 | tf_op jit(solution)/shard_map/ppermute | solution.py:863
  5.9 3.1 %collective-permute-start.1 = (f32[128,128]{1,0:T(8,128)S(1)}, f32[128,128]{1,0:T(8,128)S(1)}, u32[]{:S(2)}, u32[]{:S(2)}) collective-permute-start(f32[128,128]{1,0:T(8,128)S(1)} %get-tuple-element.32), channel_id=1, source_target_pairs={{1,5},{3,7},{4,0},{5,9},{6,2},{7,11},{8,4},{9,13},{10,6},{11,15},{... | collective-permute-start | bytes 196616 | tf_op jit(solution)/shard_map/ppermute | solution.py:863
  9.1 2.2 %collective-permute-start.2 = (f32[128,128]{1,0:T(8,128)S(1)}, f32[128,128]{1,0:T(8,128)S(1)}, u32[]{:S(2)}, u32[]{:S(2)}) collective-permute-start(f32[128,128]{1,0:T(8,128)S(1)} %get-tuple-element.33), channel_id=1, source_target_pairs={{0,5},{2,7},{4,9},{5,0},{6,11},{7,2},{8,13},{9,4},{10,15},{11,6},{... | collective-permute-start | bytes 196616 | tf_op jit(solution)/shard_map/ppermute | solution.py:863
  11.3 0.0 collective-permute-done.1.refs_5_
  11.3 3.6 %collective-permute-done.2.refs_6_ = f32[128,128]{1,0:T(8,128)S(1)} collective-permute-done((f32[128,128]{1,0:T(8,128)S(1)}, f32[128,128]{1,0:T(8,128)S(1)}, u32[]{:S(2)}, u32[]{:S(2)}) %collective-permute-start.2) | collective-permute-done | bytes 65568 | tf_op jit(solution)/shard_map/ppermute | solution.py:863
  14.9 0.0 collective-permute-done.refs_4_
  14.9 0.0 copy-done.4
  14.9 5.5 %shard_map.69 = (f32[3,128,128]{2,1,0:T(8,128)S(1)}, f32[1,1040,128]{2,1,0:T(8,128)S(1)}, f32[2,1,1024,128]{3,2,1,0:T(8,128)S(1)}, f32[2,1,1024,128]{3,2,1,0:T(8...) custom-call(s32[4,8]{1,0:T(4,128)S(1)} %copy-done.4, ...), custom_call_target="tpu_custom_call" | custom-call | tf_op jit(solution)/shard_map/pallas_call | solution.py:840
  20.4 1.3 %collective-permute-start.3 = (f32[3,128,128]{2,1,0:T(8,128)S(1)}, f32[3,128,128]{2,1,0:T(8,128)S(1)}, u32[]{:S(2)}, u32[]{:S(2)}) collective-permute-start(f32[3,128,128]{2,1,0:T(8,128)S(1)} %get-tuple-element.34), channel_id=1, source_target_pairs={{2,0},{3,1},{6,4},{7,5},{10,8},{11,9},{14,12},{15,13},{18,16},{19,... | collective-permute-start | bytes 589832 | tf_op jit(solution)/shard_map/ppermute | solution.py:863
  21.7 7.3 %collective-permute-done.3.refs_1_ = f32[3,128,128]{2,1,0:T(8,128)S(1)} collective-permute-done((f32[3,128,128]{2,1,0:T(8,128)S(1)}, f32[3,128,128]{2,1,0:T(8,128)S(1)}, u32[]{:S(2)}, u32[]{:S(2)}) %collective-permute-start.3) | collective-permute-done | bytes 196640 | tf_op jit(solution)/shard_map/ppermute | solution.py:863
  28.9 2.8 %shard_map.70 = (f32[3,128,128]{2,1,0:T(8,128)S(1)}, f32[2,160,128]{2,1,0:T(8,128)S(1)}, f32[2,80,128]{2,1,0:T(8,128)S(1)}) custom-call(s32[4,8]{1,0:T(4,128)S(1)} %copy-done.4, f32[3,128,128]{2,1,0:T(8,128)S(1)} %collective-permute-done.3.refs_1_, f32[2,528,128]{2,1,0:T(8,128)S(1)} %get-tuple-element.35.refs_2_.refs_7_, ...), custom_call_target="tpu_custom_call" | custom-call | tf_op jit(solution)/shard_map/pallas_call | solution.py:840
  31.7 1.3 %collective-permute-start.4 = (f32[3,128,128]{2,1,0:T(8,128)S(1)}, f32[3,128,128]{2,1,0:T(8,128)S(1)}, u32[]{:S(2)}, u32[]{:S(2)}) collective-permute-start(f32[3,128,128]{2,1,0:T(8,128)S(1)} %get-tuple-element.41), channel_id=1, source_target_pairs={{0,2},{1,3},{4,6},{5,7},{8,10},{9,11},{12,14},{13,15},{16,18},{17,... | collective-permute-start | bytes 589832 | tf_op jit(solution)/shard_map/ppermute | solution.py:863
  33.0 3.9 %collective-permute-done.4.refs_1_ = f32[3,128,128]{2,1,0:T(8,128)S(1)} collective-permute-done((f32[3,128,128]{2,1,0:T(8,128)S(1)}, f32[3,128,128]{2,1,0:T(8,128)S(1)}, u32[]{:S(2)}, u32[]{:S(2)}) %collective-permute-start.4) | collective-permute-done | bytes 196640 | tf_op jit(solution)/shard_map/ppermute | solution.py:863
  36.9 0.0 copy-start
  36.9 6.2 %shard_map.71 = (f32[4,2,128,128]{3,2,1,0:T(8,128)S(1)}, f32[4,2,128,128]{3,2,1,0:T(8,128)S(1)}) custom-call(s32[4,8]{1,0:T(4,128)S(1)} %copy-done.4, f32[3,128,128]{2,1,0:T(8,128)S(1)} %collective-permute-done.4.refs_1_, f32[2,160,128]{2,1,0:T(8,128)S(1)} %get-tuple-element.42.refs_2_, f32[2,80,128]{2,1,0:T(8,128)S(1)} %get-tuple-element.43.refs_3_, ...), custom_call_target="tpu_custom_call" | custom-call | tf_op jit(solution)/shard_map/pallas_call | solution.py:840
  43.1 1.3 %collective-permute-start.5 = (f32[4,2,128,128]{3,2,1,0:T(8,128)S(1)}, f32[4,2,128,128]{3,2,1,0:T(8,128)S(1)}, u32[]{:S(2)}, u32[]{:S(2)}) collective-permute-start(f32[4,2,128,128]{3,2,1,0:T(8,128)S(1)} %get-tuple-element.51), channel_id=1, source_target_pairs={{0,1},{1,0},{2,3},{3,2},{4,5},{5,4},{6,7},{7,6},{8,9},{9,8},{10,11... | collective-permute-start | bytes 1572872 | tf_op jit(solution)/shard_map/ppermute | solution.py:863
  44.4 1.5 %collective-permute-done.5.refs_1_ = f32[4,2,128,128]{3,2,1,0:T(8,128)S(1)} collective-permute-done((f32[4,2,128,128]{3,2,1,0:T(8,128)S(1)}, f32[4,2,128,128]{3,2,1,0:T(8,128)S(1)}, u32[]{:S(2)}, u32[]{:S(2)}) %collective-permute-start.5) | collective-permute-done | bytes 524320 | tf_op jit(solution)/shard_map/ppermute | solution.py:863
  45.9 0.0 copy-done
  45.9 1.2 %shard_map.72 = (f32[8,2,128,128]{3,2,1,0:T(8,128)}, bf16[8,128,128]{2,1,0:T(8,128)(2,1)}) custom-call(f32[4,2,128,128]{3,2,1,0:T(8,128)S(1)} %get-tuple-element.50.refs_0_, f32[4,2,128,128]{3,2,1,0:T(8,128)S(1)} %collective-permute-done.5.refs_1_, bf16[8,2,128,128]{3,2,1,0:T(8,128)(2,1)S(1)} %bitcast.6, bf16[8,128,128]{2,1,0:T(8,128)(2,1)S(1)} %get-tuple-element.30.refs_3_), custom_call_target="tpu_custom_call" | custom-call | tf_op jit(solution)/shard_map/pallas_call | solution.py:840
Async XLA Ops:
  0.6 14.2 %copy-start.4 = (s32[4,8]{1,0:T(4,128)S(1)}, s32[4,8]{1,0:T(4,128)}, u32[]{:S(2)}) copy-start(s32[4,8]{1,0:T(4,128)} %refs_0_.5) | copy-start | bytes 388
  0.6 1.0 %copy-start.1 = (bf16[1,8,2,128,128]{4,3,2,1,0:T(8,128)(2,1)S(1)}, bf16[1,8,2,128,128]{4,3,2,1,0:T(8,128)(2,1)}, u32[]{:S(2)}) copy-start(bf16[1,8,2,128,128]{4,3,2,1,0:T(8,128)(2,1)} %param.5) | copy-start | bytes 1572868
  1.7 1.0 %copy-start.2 = (f32[1,8,128,128]{3,2,1,0:T(8,128)S(1)}, f32[1,8,128,128]{3,2,1,0:T(8,128)}, u32[]{:S(2)}) copy-start(f32[1,8,128,128]{3,2,1,0:T(8,128)} %param.7) | copy-start | bytes 1572868
  2.7 0.9 %copy-start.3 = (bf16[1,8,128,128]{3,2,1,0:T(8,128)(2,1)S(1)}, bf16[1,8,128,128]{3,2,1,0:T(8,128)(2,1)}, u32[]{:S(2)}) copy-start(bf16[1,8,128,128]{3,2,1,0:T(8,128)(2,1)} %param.8) | copy-start | bytes 786436
  4.4 10.4 %collective-permute-start = (f32[17,128,128]{2,1,0:T(8,128)S(1)}, f32[17,128,128]{2,1,0:T(8,128)S(1)}, u32[]{:S(2)}, u32[]{:S(2)}) collective-permute-start(f32[17,128,128]{2,1,0:T(8,128)S(1)} %get-tuple-element.31), channel_id=1, source_target_pairs={{0,1},{1,0},{2,3},{3,2},{4,5},{5,4},{6,7},{7,6},{8,9},{9,8},{10,11... | collective-permute-start | bytes 3342344 | tf_op jit(solution)/shard_map/ppermute | solution.py:863
  5.9 5.4 %collective-permute-start.1 = (f32[128,128]{1,0:T(8,128)S(1)}, f32[128,128]{1,0:T(8,128)S(1)}, u32[]{:S(2)}, u32[]{:S(2)}) collective-permute-start(f32[128,128]{1,0:T(8,128)S(1)} %get-tuple-element.32), channel_id=1, source_target_pairs={{1,5},{3,7},{4,0},{5,9},{6,2},{7,11},{8,4},{9,13},{10,6},{11,15},{... | collective-permute-start | bytes 196616 | tf_op jit(solution)/shard_map/ppermute | solution.py:863
  9.1 5.8 %collective-permute-start.2 = (f32[128,128]{1,0:T(8,128)S(1)}, f32[128,128]{1,0:T(8,128)S(1)}, u32[]{:S(2)}, u32[]{:S(2)}) collective-permute-start(f32[128,128]{1,0:T(8,128)S(1)} %get-tuple-element.33), channel_id=1, source_target_pairs={{0,5},{2,7},{4,9},{5,0},{6,11},{7,2},{8,13},{9,4},{10,15},{11,6},{... | collective-permute-start | bytes 196616 | tf_op jit(solution)/shard_map/ppermute | solution.py:863
  20.4 8.6 %collective-permute-start.3 = (f32[3,128,128]{2,1,0:T(8,128)S(1)}, f32[3,128,128]{2,1,0:T(8,128)S(1)}, u32[]{:S(2)}, u32[]{:S(2)}) collective-permute-start(f32[3,128,128]{2,1,0:T(8,128)S(1)} %get-tuple-element.34), channel_id=1, source_target_pairs={{2,0},{3,1},{6,4},{7,5},{10,8},{11,9},{14,12},{15,13},{18,16},{19,... | collective-permute-start | bytes 589832 | tf_op jit(solution)/shard_map/ppermute | solution.py:863
  31.7 5.2 %collective-permute-start.4 = (f32[3,128,128]{2,1,0:T(8,128)S(1)}, f32[3,128,128]{2,1,0:T(8,128)S(1)}, u32[]{:S(2)}, u32[]{:S(2)}) collective-permute-start(f32[3,128,128]{2,1,0:T(8,128)S(1)} %get-tuple-element.41), channel_id=1, source_target_pairs={{0,2},{1,3},{4,6},{5,7},{8,10},{9,11},{12,14},{13,15},{16,18},{17,... | collective-permute-start | bytes 589832 | tf_op jit(solution)/shard_map/ppermute | solution.py:863
  36.9 9.0 %copy-start = (bf16[1,8,2,128,128]{4,3,2,1,0:T(8,128)(2,1)S(1)}, bf16[1,8,2,128,128]{4,3,2,1,0:T(8,128)(2,1)}, u32[]{:S(2)}) copy-start(bf16[1,8,2,128,128]{4,3,2,1,0:T(8,128)(2,1)} %param.6) | copy-start | bytes 1572868
  43.1 2.8 %collective-permute-start.5 = (f32[4,2,128,128]{3,2,1,0:T(8,128)S(1)}, f32[4,2,128,128]{3,2,1,0:T(8,128)S(1)}, u32[]{:S(2)}, u32[]{:S(2)}) collective-permute-start(f32[4,2,128,128]{3,2,1,0:T(8,128)S(1)} %get-tuple-element.51), channel_id=1, source_target_pairs={{0,1},{1,0},{2,3},{3,2},{4,5},{5,4},{6,7},{7,6},{8,9},{9,8},{10,11... | collective-permute-start | bytes 1572872 | tf_op jit(solution)/shard_map/ppermute | solution.py:863

commit v3 on v2

--- a/solution.py
+++ b/solution.py
@@ -14,6 +14,7 @@
 F32 = jnp.float32
 BF16 = jnp.bfloat16
 VMEM_BYTES = 30 * 2**20
+FIRST_BYTES = 60 * 2**20
 
 
 class Layout:
@@ -319,7 +320,7 @@
     over_rows(rows // 2, chunk, body)
 
 
-def pack_kernel(g, force_in, visc_in, fric_in, swap, edge_own, edge_other, force, visc, fric, sems):
+def pack_kernel(g, force_in, visc_in, fric_in, swap, edge_own, edge_other, sems, force, visc, fric):
     level_here = lax.axis_index("level")
     copies = Copies(sems)
     for source, target in ((force_in, force), (visc_in, visc), (fric_in, fric)):
@@ -487,13 +488,6 @@
     return make((2, *shape) if comps else shape, F32)
 
 
-def kept_arrays(g, level, make, held):
-    count, rows = g.blocks(level), g.rows(level)
-    visc = level_array(g, count, rows, make, False, True)
-    two = level_array(g, count, rows, make, True, False)
-    return Level(visc, two, held=two) if held else Level(visc, two, right=two)
-
-
 def step_arrays(g, level, rows):
     count = g.blocks(level)
     padded = level_array(g, count, rows, pltpu.VMEM, True, True)
@@ -534,31 +528,89 @@
         self.open = []
 
 
-def bottom_rows(g):
-    return g.rows(2) // 2 + 4 * PAD
+def low_rows(g):
+    return g.rows(2) // 2 + 2 * PAD
 
 
 def kept_rows(g):
-    return g.rows(2) // 2 + 2 * PAD
-
-
-def down_kernel(
-    g, rows_ref, force, visc, fric, swap, edge_own, edge_other, sums, kept, edges, scratch
+    return g.rows(2) // 2 + PAD
+
+
+def lent_rows(g):
+    return low_rows(g), -(-low_rows(g) // 2 // 16) * 16
+
+
+def lent_planes(level):
+    visc = level[3]
+    high = visc.astype(BF16)
+    return [value.astype(BF16) for value in level[:3]] + [
+        high,
+        (visc - high.astype(F32)).astype(BF16),
+    ]
+
+
+def lend(g, fine, coarse, out):
+    rows, less = lent_rows(g)
+    side, margin = g.side, g.margin(1)
+    lane = lane_ids(side)
+
+    def block(level, k, size):
+        here = pl.ds(0, size)
+        return (
+            level.right[0, k, here, :],
+            level.right[1, k, here, :],
+            level.fric[k, here, :],
+            level.visc[k, pl.ds(PAD, size), :],
+        )
+
+    planes = lent_planes(block(fine, 0, rows))
+    for index, value in enumerate(planes):
+        out[pl.ds(index * rows, rows), :] = value
+    first = len(planes) * rows
+    for index, value in enumerate(lent_planes(block(coarse, 0, less))):
+        out[pl.ds(first + index * less, less), :] = value
+    first += len(planes) * less
+    total = jnp.zeros((rows, side), F32)
+    for index, value in enumerate(lent_planes(block(fine, 1, rows))):
+        base = 2 * margin * index
+        value = pltpu.roll(value.astype(F32), margin + base, 1)
+        total = jnp.where((lane >= base) & (lane < base + 2 * margin), value, total)
+    out[pl.ds(first, rows), :] = total.astype(BF16)
+
+
+def borrow(g, lent, limits, fine, coarse):
+    rows, less = lent_rows(g)
+    side, margin = g.side, g.margin(1)
+
+    def put(level, number, k, size, values):
+        here = pl.ds(0, size)
+        ids = lax.broadcasted_iota(jnp.int32, (size, side), 0)
+        level.right[0, k, here, :] = values[0]
+        level.right[1, k, here, :] = values[1]
+        level.fric[k, here, :] = values[2]
+        level.visc[k, pl.ds(PAD, size), :] = jnp.where(
+            ids < limits[number][k], values[3] + values[4], 0.0
+        )
+
+    def planes(first, size):
+        return [lent[pl.ds(first + index * size, size), :].astype(F32) for index in range(5)]
+
+    put(fine, 1, 0, rows, planes(0, rows))
+    put(coarse, 0, 0, less, planes(5 * rows, less))
+    packed = lent[pl.ds(5 * (rows + less), rows), :].astype(F32)
+    values = [pltpu.roll(packed, side - margin - 2 * margin * index, 1) for index in range(5)]
+    put(fine, 1, 1, rows, values)
+
+
+def fill_kernel(
+    g, rows_ref, force, visc, fric, swap, edge_own, edge_other, levels, lent
 ):
     level_here = lax.axis_index("level")
     patch = lax.axis_index("patch")
     raw = (force, visc, fric)
     got = (swap, edge_own, edge_other)
-    side = g.side
+    odd = level_here % 2 == 1
     top = g.levels - 1
-    odd = level_here % 2 == 1
-    levels = [merged(a, b) for a, b in zip(kept, scratch)]
-
-    def limits_of(level):
-        return lane_limits(g, level, near_counts(g, rows_ref, level, patch, odd), side)
-
-    def covered_of(level):
-        return lane_limits(g, level, near_counts(g, rows_ref, level + 1, patch, odd), g.half_side)
 
     def filled(wanted, covered):
         for level in wanted:
@@ -568,21 +620,48 @@
             @pl.when(odd if west_type else jnp.logical_not(odd))
             def _():
                 for level in wanted:
+                    near = near_counts(g, rows_ref, level, patch, odd)
+                    limits = lane_limits(g, level, near, g.side)
                     fill_level(
-                        g, level, west_type, levels[level], limits_of(level),
-                        covered.get(level), raw, got,
+                        g, level, west_type, levels[level], limits, covered.get(level), raw, got
                     )
+
+    pl.when(level_here >= top - 1)(lambda: filled((top, top - 1), {}))
+
+    @pl.when(level_here < top - 1)
+    def _():
+        near = near_counts(g, rows_ref, 2, patch, odd)
+        filled((1, 0), {1: lane_limits(g, 1, near, g.half_side)})
+        lend(g, levels[1], levels[0], lent)
+
+
+def down_kernel(g, rows_ref, filled, sums, kept, edges, scratch):
+    level_here = lax.axis_index("level")
+    patch = lax.axis_index("patch")
+    side = g.side
+    top = g.levels - 1
+    odd = level_here % 2 == 1
+    levels = [merged(merged(a, b), c) for a, b, c in zip(scratch, kept, filled)]
+
+    def limits_of(level):
+        return lane_limits(g, level, near_counts(g, rows_ref, level, patch, odd), side)
 
     @pl.when(level_here >= top - 1)
     def _():
-        filled((top, top - 1), {})
-        covered = covered_of(top - 1)
+        near = near_counts(g, rows_ref, top, patch, odd)
+        covered = lane_limits(g, top - 1, near, g.half_side)
+        given = filled[top - 1].right
+        for comp in range(2):
+            for k in range(g.blocks(top - 1)):
+                rest = pl.ds(g.half_side, g.rows(top - 1) - g.half_side)
+                levels[top - 1].right[comp, k, rest, :] = given[comp, k, rest, :]
 
         def set_right(comp, k, row, chunk, value):
             here = pl.ds(row, chunk)
             ids = row + lax.broadcasted_iota(jnp.int32, (chunk, side), 0)
-            old = levels[top - 1].right[comp, k, here, :]
-            levels[top - 1].right[comp, k, here, :] = jnp.where(ids < covered[k], value, old)
+            levels[top - 1].right[comp, k, here, :] = jnp.where(
+                ids < covered[k], value, given[comp, k, here, :]
+            )
 
         def keep(comp, k, row, chunk, value):
             (sums if k == 0 else edges)[comp, pl.ds(row, chunk), :] = value
@@ -597,12 +676,11 @@
 
     @pl.when(level_here < top - 1)
     def _():
-        filled((1, 0), {1: covered_of(1)})
         for level in (1, 0):
             smooth_weights(g, level, levels[level], limits_of(level), g.rows(level), False)
 
 
-def bottom_levels(g, rows_ref, patch, odd, start, stop, fine, coarse, new_sums, store_fine, store_coarse):
+def bottom_levels(g, rows_ref, patch, odd, start, stop, fine, coarse, new_sums, store_fine):
     side = g.side
     count, chunk = g.blocks(1), g.chunk(1, stop - start)
     clear_level(g, 1, fine)
@@ -632,7 +710,6 @@
         value = jnp.where(ids < covered[0], value, coarse.right[comp, 0, here, :])
         value = coarse.weight[comp, 0, here, :] * value
         coarse.cells[comp, 0, here, :] = value
-        store_coarse(comp, row, size, value)
 
     restrict_into(g, 1, fine, start, stop, smooth_coarse)
 
@@ -643,53 +720,18 @@
     corrected_step(g, 1, fine, start, stop, store_fine)
 
 
-def bottom_kernel(g, rows_ref, sums, kept, coarse_kept, adjoint, own_rows, coarse_rows, edges, scratch, coarse_cells):
-    level_here = lax.axis_index("level")
-    patch = lax.axis_index("patch")
-    side = g.side
-    rows = bottom_rows(g)
-    top = g.levels - 1
-    odd = level_here % 2 == 1
-
-    @pl.when(level_here < top - 1)
-    def _():
-        reach = g.rows(2) // 2
-        both = sums[2]
-        swapped = pltpu.roll(both, g.half_side, 1)
-        fine = merged(Level(kept.visc, kept.weight), scratch)
-        for comp in range(2):
-            for k in range(g.blocks(1)):
-                fine.right[comp, k] = kept.right[comp, k, pl.ds(0, rows), :]
-
-        def new_sums(comp, k):
-            value = sums[comp] if k == 0 else (both, swapped)[comp]
-            return jnp.where(kept.weight[comp, k, pl.ds(0, reach), :] > 0.0, value, 0.0)
-
-        def store_fine(comp, k, row, chunk, value):
-            (own_rows if k == 0 else edges)[comp, pl.ds(row, chunk), :] = value
-
-        def store_coarse(comp, row, size, value):
-            coarse_rows[comp, pl.ds(row, size), :] = value
-
-        coarse = Level(None, coarse_kept.weight, coarse_kept.right, cells=coarse_cells)
-        bottom_levels(
-            g, rows_ref, patch, odd, 0, rows, fine, coarse, new_sums, store_fine, store_coarse
-        )
-        adjoint[0] = own_rows[0, pl.ds(0, side), :]
-        adjoint[1] = own_rows[1, pl.ds(0, side), :]
-        adjoint[2] = joined_edges(g, edges[0, pl.ds(0, side), :], edges[1, pl.ds(0, side), :])
-
-
 def up_kernel(
-    g, rows_ref, adjoint, own_rows, coarse_rows, kept, mine, theirs, edges, scratch, coarse_cells, finer,
-    coarser,
+    g, rows_ref, sums, lent, filled, kept, mine, theirs, edges, scratch, low, low_fine, low_coarse, finer, coarser
 ):
     level_here = lax.axis_index("level")
     patch = lax.axis_index("patch")
     side = g.side
     top = g.levels - 1
     odd = level_here % 2 == 1
-    levels = [merged(a, b) for a, b in zip(kept, scratch)]
+    levels = [merged(merged(a, b), c) for a, b, c in zip(scratch, kept, filled)]
+
+    def limits_of(level):
+        return lane_limits(g, level, near_counts(g, rows_ref, level, patch, odd), side)
 
     def hand_out():
         def write(first, second):
@@ -703,34 +745,45 @@
 
     @pl.when(level_here >= top - 1)
     def _():
-        both = adjoint[2]
-        edges[0] = both
-        edges[1] = pltpu.roll(both, g.half_side, 1)
-
-        def load_given(comp, k, row, chunk):
-            return (adjoint if k == 0 else edges)[comp, pl.ds(row, chunk), :]
+        rows, less = lent_rows(g)
+        limits = {level: limits_of(level) for level in (0, 1)}
+        clear_pads(low_fine.visc, [(k,) for k in range(g.blocks(1))])
+        clear_pads(low_coarse.visc, [(k,) for k in range(g.blocks(0))])
+        borrow(g, lent, limits, low_fine, low_coarse)
+        smooth_weights(g, 1, low_fine, limits[1], rows, False)
+        smooth_weights(g, 0, low_coarse, limits[0], less, False)
+
+        def store_fine(comp, k, row, chunk, value):
+            low[comp, k, pl.ds(row, chunk), :] = value
+
+        bottom_levels(
+            g, rows_ref, patch, odd, 0, rows, low_fine, low_coarse,
+            level_sums(g, sums, low_fine.weight), store_fine,
+        )
+
+        def load_low(comp, k, row, chunk):
+            return low[comp, k, pl.ds(row, chunk), :]
 
         def load_held(comp, k, row, chunk):
-            return levels[top - 1].held[comp, k, pl.ds(row, chunk), :]
+            return edges[comp, k, pl.ds(row, chunk), :]
 
         def store_in(level, out, hold):
             own = g.own(level)
 
             def store(comp, k, row, chunk, value):
                 if hold:
-                    levels[level].held[comp, k, pl.ds(row, chunk), :] = value
+                    edges[comp, k, pl.ds(row, chunk), :] = value
                 if k < own:
                     group, place = row // side, row % side
                     out[group * own + k, comp, pl.ds(pl.multiple_of(place, 8), chunk), :] = value
 
             return store
 
-        for level, load, out in ((top - 1, load_given, coarser), (top, load_held, finer)):
+        for level, load, out in ((top - 1, load_low, coarser), (top, load_held, finer)):
             d = levels[level]
             clear_level(g, level, d)
-            near = near_counts(g, rows_ref, level, patch, odd)
             rows = g.rows(level)
-            prolong_from(g, level, d, lane_limits(g, level, near, side), 0, rows, load)
+            prolong_from(g, level, d, limits_of(level), 0, rows, load)
             corrected_step(g, level, d, 0, rows, store_in(level, out, level < top))
         hand_out()
 
@@ -738,33 +791,22 @@
     def _():
         rows = g.rows(1)
         first = g.rows(2) // 2
-        done = kept_rows(g)
-        fine, coarse = levels[1], levels[0]._replace(cells=coarse_cells)
+        fine, coarse = levels[1], levels[0]
 
         def store_fine(comp, k, row, chunk, value):
             if k == 0:
                 group, place = row // side, row % side
                 finer[group, comp, pl.ds(pl.multiple_of(place, 8), chunk), :] = value
 
-        def store_coarse(comp, row, size, value):
-            pass
-
-        bottom_levels(
-            g, rows_ref, patch, odd, first, rows, fine, coarse, None, store_fine, store_coarse
-        )
+        bottom_levels(g, rows_ref, patch, odd, first, rows, fine, coarse, None, store_fine)
         lane = lane_ids(side)
         for comp in range(2):
-            finer[0, comp] = own_rows[comp, pl.ds(0, side), :]
-            finer[1, comp, pl.ds(0, done - side), :] = own_rows[comp, pl.ds(side, done - side), :]
-            coarse_cells[comp, 0, pl.ds(0, done // 2), :] = coarse_rows[
-                comp, pl.ds(0, done // 2), :
-            ]
             for k in range(g.half_slots):
                 parts = []
                 for group in (k, k + g.half_slots):
                     here = pl.ds(group * side, side)
                     if group * side < rows // 2:
-                        parts.append(coarse_cells[comp, 0, here, :])
+                        parts.append(coarse.cells[comp, 0, here, :])
                     else:
                         parts.append(
                             coarse.weight[comp, 0, here, :] * coarse.right[comp, 0, here, :]
@@ -773,6 +815,69 @@
                     lane < g.half_side, parts[0], pltpu.roll(parts[1], g.half_side, 1)
                 )
         hand_out()
+
+
+def level_sums(g, sums, weight):
+    reach = g.rows(2) // 2
+
+    def value(comp, k):
+        found = sums[comp] if k == 0 else sums[2]
+        if k and comp:
+            found = pltpu.roll(found, g.half_side, 1)
+        return jnp.where(weight[comp, k, pl.ds(0, reach), :] > 0.0, found, 0.0)
+
+    return value
+
+
+def low_kernel(
+    g, rows_ref, sums, filled, kept, mine_in, theirs_in, mine, theirs, scratch, low_coarse, own_rows
+):
+    level_here = lax.axis_index("level")
+    patch = lax.axis_index("patch")
+    side = g.side
+    top = g.levels - 1
+    odd = level_here % 2 == 1
+    for k in range(g.half_slots):
+        for comp in range(2):
+            mine[k, comp] = mine_in[k, comp]
+            theirs[k, comp] = theirs_in[k, comp]
+
+    @pl.when(level_here < top - 1)
+    def _():
+        rows, _ = lent_rows(g)
+        done = kept_rows(g)
+        fine = merged(Level(filled[1].visc, kept[1].weight), scratch)
+        coarse = merged(Level(None, kept[0].weight, filled[0].right), low_coarse)
+        for comp in range(2):
+            for k in range(g.blocks(1)):
+                fine.right[comp, k] = filled[1].right[comp, k, pl.ds(0, rows), :]
+
+        def store_fine(comp, k, row, chunk, value):
+            if k == 0:
+                own_rows[comp, pl.ds(row, chunk), :] = value
+
+        bottom_levels(
+            g, rows_ref, patch, odd, 0, rows, fine, coarse,
+            level_sums(g, sums, fine.weight), store_fine,
+        )
+        lane = lane_ids(side)
+        size = rows // 2
+        ids = lax.broadcasted_iota(jnp.int32, (size, side), 0)
+        ours = (ids < done // 2) & (lane < g.half_side)
+
+        def write(first, second):
+            for comp in range(2):
+                first[0, comp] = own_rows[comp, pl.ds(0, side), :]
+                first[1, comp, pl.ds(0, done - side), :] = own_rows[
+                    comp, pl.ds(side, done - side), :
+                ]
+                here = pl.ds(0, size)
+                second[0, comp, here, :] = jnp.where(
+                    ours, coarse.cells[comp, 0, here, :], second[0, comp, here, :]
+                )
+
+        pl.when(odd)(lambda: write(mine, theirs))
+        pl.when(jnp.logical_not(odd))(lambda: write(theirs, mine))
 
 
 def join_kernel(g, mine, given, speed, fric, adjoint, gradient):
@@ -815,7 +920,7 @@
         pl.when(level_here == level)(lambda level=level: join_level(level))
 
 
-def run_kernel(body, ins, outs, scratch):
+def run_kernel(body, ins, outs, scratch, grant=VMEM_BYTES):
     in_trees = [jax.tree.flatten(tree) for tree, _ in ins]
     out_trees = [jax.tree.flatten(tree) for tree, _ in outs]
     scratch_trees = [jax.tree.flatten(tree) for tree in scratch]
@@ -843,7 +948,7 @@
         in_specs=specs(ins, in_trees),
         out_specs=specs(outs, out_trees),
         scratch_shapes=[leaf for leaves, _ in scratch_trees for leaf in leaves],
-        compiler_params=pltpu.CompilerParams(vmem_limit_bytes=VMEM_BYTES),
+        compiler_params=pltpu.CompilerParams(vmem_limit_bytes=grant),
     )(*[leaf for leaves, _ in in_trees for leaf in leaves])
     answer = []
     first = 0
@@ -871,39 +976,42 @@
     top = g.levels - 1
     force, speed, visc, fric = forcing[0], velocity[0], viscosity[0], friction[0]
     make = jax.ShapeDtypeStruct
+    vmem = pltpu.VMEM
     block = make((side, side), F32)
     half = make((g.half_slots, 2, side, side), F32)
     three = make((3, side, side), F32)
-    two = pltpu.VMEM((2, side, side), F32)
-    sems = pltpu.SemaphoreType.DMA((4,))
-
-    swap, edge_own, edge_other, force, visc, fric = run_kernel(
+
+    def array(level, rows, kind, comps, pad):
+        return level_array(g, g.blocks(level), rows, kind, comps, pad)
+
+    swap, edge_own, edge_other = run_kernel(
         lambda *refs: pack_kernel(g, *refs),
         [(force, HBM), (visc, HBM), (fric, HBM)],
+        [(make((4 * g.half_slots + 1, side, side), F32), VM), (block, VM), (block, VM)],
         [
-            (make((4 * g.half_slots + 1, side, side), F32), VM),
-            (block, VM),
-            (block, VM),
-            (make(force.shape, force.dtype), VM),
-            (make(visc.shape, visc.dtype), VM),
-            (make(fric.shape, fric.dtype), VM),
+            pltpu.SemaphoreType.DMA((4,)),
+            vmem(force.shape, force.dtype),
+            vmem(visc.shape, visc.dtype),
+            vmem(fric.shape, fric.dtype),
         ],
-        [sems],
+        FIRST_BYTES,
     )
     swap = moved(swap, g, lambda p, l: (p, l ^ 1))
     edge_own = moved(edge_own, g, lambda p, l: (p + (1 if l % 2 else -1), l))
     edge_other = moved(edge_other, g, lambda p, l: (p + (-1 if l % 2 else 1), l ^ 1))
 
-    def down_scratch(level):
-        count, rows = g.blocks(level), g.rows(level)
-        fric_here = level_array(g, count, rows, pltpu.VMEM, False, False)
-        if level < top - 1:
-            return Level(None, None, fric=fric_here)
-        both = level_array(g, count, rows, pltpu.VMEM, True, False)
-        return Level(None, None, right=both, fric=fric_here, left=both, **step_arrays(g, level, rows))
-
-    sums, kept = run_kernel(
-        lambda *refs: down_kernel(g, *refs),
+    fields = [
+        Level(
+            array(level, g.rows(level), make, False, True),
+            None,
+            right=array(level, g.rows(level), make, True, False),
+            fric=array(level, g.rows(level), make, False, False),
+        )
+        for level in range(g.levels)
+    ]
+    rows, less = lent_rows(g)
+    filled, lent = run_kernel(
+        lambda *refs: fill_kernel(g, *refs),
         [
             (patch_rows, SM),
             (force, VM),
@@ -913,49 +1021,79 @@
             (edge_own, VM),
             (edge_other, VM),
         ],
-        [
-            (three, VM),
-            ([kept_arrays(g, level, make, level >= top - 1) for level in range(g.levels)], VM),
-        ],
-        [two, [down_scratch(level) for level in range(g.levels)]],
-    )
-    sums = moved(sums, g, lambda p, l: (p, l - 2))
-    rows = bottom_rows(g)
-    part = level_array(g, g.blocks(1), rows, pltpu.VMEM, True, False)
-    adjoint, own_rows, coarse_rows = run_kernel(
-        lambda *refs: bottom_kernel(g, *refs),
-        [(patch_rows, SM), (sums, VM), (kept[1], VM), (kept[0], VM)],
-        [
-            (three, VM),
-            (make((2, rows, side), F32), VM),
-            (make((2, rows // 2, side), F32), VM),
-        ],
-        [
-            pltpu.VMEM((2, rows, side), F32),
-            Level(None, None, right=part, held=part, left=part, **step_arrays(g, 1, rows)),
-            pltpu.VMEM((2, 1, rows // 2, side), F32),
-        ],
-    )
-    adjoint = moved(adjoint, g, lambda p, l: (p, l + 2))
+        [(fields, VM), (make((5 * (rows + less) + rows, side), BF16), VM)],
+        [],
+    )
+    lent = moved(lent, g, lambda p, l: (p, l + 2))
+
+    def kept_of(level):
+        two = array(level, g.rows(level), make, True, False)
+        return Level(None, two, held=two if level >= top - 1 else None)
+
+    def down_scratch(level):
+        if level < top - 1:
+            return Level(None, None)
+        both = array(level, g.rows(level), vmem, True, False)
+        more = dict(right=both) if level < top else {}
+        return Level(None, None, left=both, **more, **step_arrays(g, level, g.rows(level)))
+
+    sums, kept = run_kernel(
+        lambda *refs: down_kernel(g, *refs),
+        [(patch_rows, SM), (filled, VM)],
+        [(three, VM), ([kept_of(level) for level in range(g.levels)], VM)],
+        [vmem((2, side, side), F32), [down_scratch(level) for level in range(g.levels)]],
+    )
+    sums_there = moved(sums, g, lambda p, l: (p, l - 2))
 
     def up_scratch(level):
         if level == 0:
-            return Level(None, None)
-        rows = g.rows(level)
-        both = level_array(g, g.blocks(level), rows, pltpu.VMEM, True, False)
+            return Level(None, None, cells=vmem((2, 1, g.rows(1) // 2, side), F32))
+        both = array(level, g.rows(level), vmem, True, False)
         more = dict(held=both, left=both) if level == 1 else {}
-        return Level(None, None, **more, **step_arrays(g, level, rows))
-
+        return Level(None, None, **more, **step_arrays(g, level, g.rows(level)))
+
+    low_both = array(1, rows, vmem, True, False)
+    low_steps = dict(held=low_both, left=low_both, right=low_both, **step_arrays(g, 1, rows))
     mine, theirs = run_kernel(
         lambda *refs: up_kernel(g, *refs),
-        [(patch_rows, SM), (adjoint, VM), (own_rows, VM), (coarse_rows, VM), (kept, VM)],
+        [(patch_rows, SM), (sums, VM), (lent, VM), (filled, VM), (kept, VM)],
         [(half, VM), (half, VM)],
         [
-            two,
+            array(top - 1, g.rows(top - 1), vmem, True, False),
             [up_scratch(level) for level in range(g.levels)],
-            pltpu.VMEM((2, 1, g.rows(1) // 2, side), F32),
-            pltpu.VMEM(half.shape, F32),
-            pltpu.VMEM(half.shape, F32),
+            low_both,
+            Level(
+                array(1, rows, vmem, False, True),
+                low_both,
+                fric=array(1, rows, vmem, False, False),
+                **low_steps,
+            ),
+            Level(
+                array(0, less, vmem, False, True),
+                array(0, less, vmem, True, False),
+                right=array(0, less, vmem, True, False),
+                fric=array(0, less, vmem, False, False),
+                cells=array(0, less, vmem, True, False),
+            ),
+            vmem(half.shape, F32),
+            vmem(half.shape, F32),
+        ],
+    )
+    mine, theirs = run_kernel(
+        lambda *refs: low_kernel(g, *refs),
+        [
+            (patch_rows, SM),
+            (sums_there, VM),
+            (filled[:2], VM),
+            (kept[:2], VM),
+            (mine, VM),
+            (theirs, VM),
+        ],
+        [(half, VM), (half, VM)],
+        [
+            Level(None, None, **low_steps),
+            Level(None, None, cells=array(0, less, vmem, True, False)),
+            vmem((2, rows, side), F32),
         ],
     )
     given = moved(theirs, g, lambda p, l: (p, l ^ 1))

time: 47.6 us -> 37.7 us (0.79)
  waiting for transfers between devices: 16.3 us -> 7.65 us
  local copies, waits for them, and re-layouts: 3.04 us -> 0.02 us
  Pallas kernels: 16.4 us -> 19.2 us
  starting transfers between devices: 10.7 us -> 9.84 us
    ppermute x6, waiting for transfers between devices: 16.3 us -> 7.65 us  [moved(): return lax.ppermute(value, ('patch', 'level'), pairs)]
    unnamed x10, local copies, waits for them, and re-layouts: 3.04 us -> 0.02 us
    pallas_call x5 -> x6, Pallas kernels: 16.4 us -> 19.2 us  [run_kernel(): pl.pallas_call(kernel, out_shape=[leaf for leaves, _ in out_trees for lea...]
    ppermute x6, starting transfers between devices: 10.7 us -> 9.84 us  [moved(): return lax.ppermute(value, ('patch', 'level'), pairs)]
  transfers between devices with their start and end apart: 6 -> 6, of which waited for: 4 -> 3; matrix products, arithmetic and copies ran while one was open for 0% -> 0% of each run, Pallas kernels for 0% -> 27%
where the time goes in v3:
time: 37.7 us; the launch traced here: 37.5 us
  Pallas kernels  19.2 us (51%)
  starting transfers between devices  9.84 us (26%)
  waiting for transfers between devices  7.65 us (20%)
  between operations  0.78 us (2%)
    pallas_call x6, Pallas kernels, run_kernel(): pl.pallas_call(kernel, out_shape=[leaf for leaves, _ in out_trees for lea...  19.2 us
    ppermute x6, starting transfers between devices, moved(): return lax.ppermute(value, ('patch', 'level'), pairs)  9.84 us
    ppermute x6, waiting for transfers between devices, moved(): return lax.ppermute(value, ('patch', 'level'), pairs)  7.65 us
  transfers between devices with their start and end apart: 6, of which 3 were waited for; matrix products, arithmetic and copies ran while one was open for 0% of the time, Pallas kernels for 27%

profile of v3, /device:TPU:21, one launch (start us, length us, event | category | flops | bytes accessed | tf_op | source)
XLA Modules:
  0.0 37.5 jit_solution(4043956921779809018)
XLA Ops:
  0.6 0.0 copy-start
  0.6 0.0 copy-start.2
  0.7 0.0 copy-start.1
  0.7 0.0 copy-start.4
  0.7 3.0 %shard_map.68 = (f32[17,128,128]{2,1,0:T(8,128)}, f32[128,128]{1,0:T(8,128)}, f32[128,128]{1,0:T(8,128)}) custom-call(bf16[8,2,128,128]{3,2,1,0:T(8,128)(2,1)} %bitcast.9, f32[8,128,128]{2,1,0:T(8,128)} %bitcast.11, bf16[8,128,128]{2,1,0:T(8,128)(2,1)} %bitcast.6), custom_call_target="tpu_custom_call" | custom-call | tf_op jit(solution)/shard_map/pallas_call | solution.py:945
  3.7 1.5 %collective-permute-start = (f32[17,128,128]{2,1,0:T(8,128)}, f32[17,128,128]{2,1,0:T(8,128)S(1)}, u32[]{:S(2)}, u32[]{:S(2)}) collective-permute-start(f32[17,128,128]{2,1,0:T(8,128)} %get-tuple-element.31), channel_id=1, source_target_pairs={{0,1},{1,0},{2,3},{3,2},{4,5},{5,4},{6,7},{7,6},{8,9},{9,8},{10,11... | collective-permute-start | bytes 3342344 | tf_op jit(solution)/shard_map/ppermute | solution.py:968
  5.2 3.1 %collective-permute-start.1 = (f32[128,128]{1,0:T(8,128)}, f32[128,128]{1,0:T(8,128)S(1)}, u32[]{:S(2)}, u32[]{:S(2)}) collective-permute-start(f32[128,128]{1,0:T(8,128)} %get-tuple-element.32), channel_id=1, source_target_pairs={{1,5},{3,7},{4,0},{5,9},{6,2},{7,11},{8,4},{9,13},{10,6},{11,15},{... | collective-permute-start | bytes 196616 | tf_op jit(solution)/shard_map/ppermute | solution.py:968
  8.3 2.2 %collective-permute-start.2 = (f32[128,128]{1,0:T(8,128)}, f32[128,128]{1,0:T(8,128)S(1)}, u32[]{:S(2)}, u32[]{:S(2)}) collective-permute-start(f32[128,128]{1,0:T(8,128)} %get-tuple-element.33), channel_id=1, source_target_pairs={{0,5},{2,7},{4,9},{5,0},{6,11},{7,2},{8,13},{9,4},{10,15},{11,6},{... | collective-permute-start | bytes 196616 | tf_op jit(solution)/shard_map/ppermute | solution.py:968
  10.6 0.0 collective-permute-done.1.refs_5_
  10.6 3.8 %collective-permute-done.2.refs_6_ = f32[128,128]{1,0:T(8,128)S(1)} collective-permute-done((f32[128,128]{1,0:T(8,128)}, f32[128,128]{1,0:T(8,128)S(1)}, u32[]{:S(2)}, u32[]{:S(2)}) %collective-permute-start.2) | collective-permute-done | bytes 65568 | tf_op jit(solution)/shard_map/ppermute | solution.py:968
  14.3 0.0 collective-permute-done.refs_4_
  14.3 0.0 copy-done
  14.3 0.0 copy-done.2
  14.4 0.0 copy-done.1
  14.4 0.0 copy-done.4
  14.4 2.4 %shard_map.69 = (f32[1,1040,128]{2,1,0:T(8,128)S(1)}, f32[2,1,1024,128]{3,2,1,0:T(8,128)S(1)}, f32[1,1024,128]{2,1,0:T(8,128)S(1)}, f32[2,528,128]{2,1,0:T(8,128...) custom-call(s32[4,8]{1,0:T(4,128)S(1)} %copy-done.4, ...), custom_call_target="tpu_custom_call" | custom-call | tf_op jit(solution)/shard_map/pallas_call | solution.py:945
  16.8 1.3 %collective-permute-start.4 = (bf16[1264,128]{1,0:T(8,128)(2,1)S(1)}, bf16[1264,128]{1,0:T(8,128)(2,1)S(1)}, u32[]{:S(2)}, u32[]{:S(2)}) collective-permute-start(bf16[1264,128]{1,0:T(8,128)(2,1)S(1)} %get-tuple-element.49), channel_id=1, source_target_pairs={{0,2},{1,3},{4,6},{5,7},{8,10},{9,11},{12,14},{13,15},{16,18},{17,... | collective-permute-start | bytes 970760 | tf_op jit(solution)/shard_map/ppermute | solution.py:968
  18.1 3.8 %shard_map.70 = (f32[3,128,128]{2,1,0:T(8,128)S(1)}, f32[2,1,1024,128]{3,2,1,0:T(8,128)S(1)}, f32[2,2,512,128]{3,2,1,0:T(8,128)S(1)}, f32[2,3,256,128]{3,2,1,0:T...) custom-call(s32[4,8]{1,0:T(4,128)S(1)} %copy-done.4, ...), custom_call_target="tpu_custom_call" | custom-call | tf_op jit(solution)/shard_map/pallas_call | solution.py:945
  21.9 1.3 %collective-permute-start.3 = (f32[3,128,128]{2,1,0:T(8,128)S(1)}, f32[3,128,128]{2,1,0:T(8,128)S(1)}, u32[]{:S(2)}, u32[]{:S(2)}) collective-permute-start(f32[3,128,128]{2,1,0:T(8,128)S(1)} %get-tuple-element.46.refs_1_), channel_id=1, source_target_pairs={{2,0},{3,1},{6,4},{7,5},{10,8},{11,9},{14,12},{15,13},{18,16},{19,... | collective-permute-start | bytes 589832 | tf_op jit(solution)/shard_map/ppermute | solution.py:968
  23.2 2.3 %collective-permute-done.4.refs_2_ = bf16[1264,128]{1,0:T(8,128)(2,1)S(1)} collective-permute-done((bf16[1264,128]{1,0:T(8,128)(2,1)S(1)}, bf16[1264,128]{1,0:T(8,128)(2,1)S(1)}, u32[]{:S(2)}, u32[]{:S(2)}) %collective-permute-start.4) | collective-permute-done | bytes 323616 | tf_op jit(solution)/shard_map/ppermute | solution.py:968
  25.5 6.2 %shard_map.71 = (f32[4,2,128,128]{3,2,1,0:T(8,128)S(1)}, f32[4,2,128,128]{3,2,1,0:T(8,128)S(1)}) custom-call(s32[4,8]{1,0:T(4,128)S(1)} %copy-done.4, f32[3,128,128]{2,1,0:T(8,128)S(1)} %get-tuple-element.46.refs_1_, bf16[1264,128]{1,0:T(8,128)(2,1)S(1)} %collective-permute-done.4.refs_2_, f32[1,1040,128]{2,1,0:T(8,128)S(1)} %get-tuple-element.34.refs_1_.refs_3_.refs_2_, ...), custom_call_target="tpu_custom_call" | custom-call | tf_op jit(solution)/shard_map/pallas_call | solution.py:945
  31.7 0.0 collective-permute-done.3.refs_1_
  31.8 0.0 copy-start.3
  31.8 2.5 %shard_map.72 = (f32[4,2,128,128]{3,2,1,0:T(8,128)S(1)}, f32[4,2,128,128]{3,2,1,0:T(8,128)S(1)}) custom-call(s32[4,8]{1,0:T(4,128)S(1)} %copy-done.4, f32[3,128,128]{2,1,0:T(8,128)S(1)} %collective-permute-done.3.refs_1_, f32[1,1040,128]{2,1,0:T(8,128)S(1)} %get-tuple-element.34.refs_1_.refs_3_.refs_2_, ...), custom_call_target="tpu_custom_call" | custom-call | tf_op jit(solution)/shard_map/pallas_call | solution.py:945
  34.3 0.4 %collective-permute-start.5 = (f32[4,2,128,128]{3,2,1,0:T(8,128)S(1)}, f32[4,2,128,128]{3,2,1,0:T(8,128)S(1)}, u32[]{:S(2)}, u32[]{:S(2)}) collective-permute-start(f32[4,2,128,128]{3,2,1,0:T(8,128)S(1)} %get-tuple-element.57), channel_id=1, source_target_pairs={{0,1},{1,0},{2,3},{3,2},{4,5},{5,4},{6,7},{7,6},{8,9},{9,8},{10,11... | collective-permute-start | bytes 1572872 | tf_op jit(solution)/shard_map/ppermute | solution.py:968
  34.7 1.6 %collective-permute-done.5.refs_1_ = f32[4,2,128,128]{3,2,1,0:T(8,128)S(1)} collective-permute-done((f32[4,2,128,128]{3,2,1,0:T(8,128)S(1)}, f32[4,2,128,128]{3,2,1,0:T(8,128)S(1)}, u32[]{:S(2)}, u32[]{:S(2)}) %collective-permute-start.5) | collective-permute-done | bytes 524320 | tf_op jit(solution)/shard_map/ppermute | solution.py:968
  36.3 0.0 copy-done.3
  36.3 1.2 %shard_map.73 = (f32[8,2,128,128]{3,2,1,0:T(8,128)}, bf16[8,128,128]{2,1,0:T(8,128)(2,1)}) custom-call(f32[4,2,128,128]{3,2,1,0:T(8,128)S(1)} %get-tuple-element.56.refs_0_, f32[4,2,128,128]{3,2,1,0:T(8,128)S(1)} %collective-permute-done.5.refs_1_, bf16[8,2,128,128]{3,2,1,0:T(8,128)(2,1)S(1)} %bitcast.13, bf16[8,128,128]{2,1,0:T(8,128)(2,1)S(1)} %bitcast.8), custom_call_target="tpu_custom_call" | custom-call | tf_op jit(solution)/shard_map/pallas_call | solution.py:945
Async XLA Ops:
  0.6 13.7 %copy-start = (bf16[1,8,128,128]{3,2,1,0:T(8,128)(2,1)S(1)}, bf16[1,8,128,128]{3,2,1,0:T(8,128)(2,1)}, u32[]{:S(2)}) copy-start(bf16[1,8,128,128]{3,2,1,0:T(8,128)(2,1)} %param.8) | copy-start | bytes 786436
  0.6 13.7 %copy-start.2 = (f32[1,8,128,128]{3,2,1,0:T(8,128)S(1)}, f32[1,8,128,128]{3,2,1,0:T(8,128)}, u32[]{:S(2)}) copy-start(f32[1,8,128,128]{3,2,1,0:T(8,128)} %param.7) | copy-start | bytes 1572868
  0.7 13.7 %copy-start.1 = (bf16[1,8,2,128,128]{4,3,2,1,0:T(8,128)(2,1)S(1)}, bf16[1,8,2,128,128]{4,3,2,1,0:T(8,128)(2,1)}, u32[]{:S(2)}) copy-start(bf16[1,8,2,128,128]{4,3,2,1,0:T(8,128)(2,1)} %param.5) | copy-start | bytes 1572868
  0.7 13.7 %copy-start.4 = (s32[4,8]{1,0:T(4,128)S(1)}, s32[4,8]{1,0:T(4,128)}, u32[]{:S(2)}) copy-start(s32[4,8]{1,0:T(4,128)} %refs_0_.7) | copy-start | bytes 388
  3.7 10.6 %collective-permute-start = (f32[17,128,128]{2,1,0:T(8,128)}, f32[17,128,128]{2,1,0:T(8,128)S(1)}, u32[]{:S(2)}, u32[]{:S(2)}) collective-permute-start(f32[17,128,128]{2,1,0:T(8,128)} %get-tuple-element.31), channel_id=1, source_target_pairs={{0,1},{1,0},{2,3},{3,2},{4,5},{5,4},{6,7},{7,6},{8,9},{9,8},{10,11... | collective-permute-start | bytes 3342344 | tf_op jit(solution)/shard_map/ppermute | solution.py:968
  5.2 5.4 %collective-permute-start.1 = (f32[128,128]{1,0:T(8,128)}, f32[128,128]{1,0:T(8,128)S(1)}, u32[]{:S(2)}, u32[]{:S(2)}) collective-permute-start(f32[128,128]{1,0:T(8,128)} %get-tuple-element.32), channel_id=1, source_target_pairs={{1,5},{3,7},{4,0},{5,9},{6,2},{7,11},{8,4},{9,13},{10,6},{11,15},{... | collective-permute-start | bytes 196616 | tf_op jit(solution)/shard_map/ppermute | solution.py:968
  8.3 6.0 %collective-permute-start.2 = (f32[128,128]{1,0:T(8,128)}, f32[128,128]{1,0:T(8,128)S(1)}, u32[]{:S(2)}, u32[]{:S(2)}) collective-permute-start(f32[128,128]{1,0:T(8,128)} %get-tuple-element.33), channel_id=1, source_target_pairs={{0,5},{2,7},{4,9},{5,0},{6,11},{7,2},{8,13},{9,4},{10,15},{11,6},{... | collective-permute-start | bytes 196616 | tf_op jit(solution)/shard_map/ppermute | solution.py:968
  16.8 8.7 %collective-permute-start.4 = (bf16[1264,128]{1,0:T(8,128)(2,1)S(1)}, bf16[1264,128]{1,0:T(8,128)(2,1)S(1)}, u32[]{:S(2)}, u32[]{:S(2)}) collective-permute-start(bf16[1264,128]{1,0:T(8,128)(2,1)S(1)} %get-tuple-element.49), channel_id=1, source_target_pairs={{0,2},{1,3},{4,6},{5,7},{8,10},{9,11},{12,14},{13,15},{16,18},{17,... | collective-permute-start | bytes 970760 | tf_op jit(solution)/shard_map/ppermute | solution.py:968
  21.9 9.8 %collective-permute-start.3 = (f32[3,128,128]{2,1,0:T(8,128)S(1)}, f32[3,128,128]{2,1,0:T(8,128)S(1)}, u32[]{:S(2)}, u32[]{:S(2)}) collective-permute-start(f32[3,128,128]{2,1,0:T(8,128)S(1)} %get-tuple-element.46.refs_1_), channel_id=1, source_target_pairs={{2,0},{3,1},{6,4},{7,5},{10,8},{11,9},{14,12},{15,13},{18,16},{19,... | collective-permute-start | bytes 589832 | tf_op jit(solution)/shard_map/ppermute | solution.py:968
  31.8 4.5 %copy-start.3 = (bf16[1,8,2,128,128]{4,3,2,1,0:T(8,128)(2,1)S(1)}, bf16[1,8,2,128,128]{4,3,2,1,0:T(8,128)(2,1)}, u32[]{:S(2)}) copy-start(bf16[1,8,2,128,128]{4,3,2,1,0:T(8,128)(2,1)} %param.6) | copy-start | bytes 1572868
  34.3 2.0 %collective-permute-start.5 = (f32[4,2,128,128]{3,2,1,0:T(8,128)S(1)}, f32[4,2,128,128]{3,2,1,0:T(8,128)S(1)}, u32[]{:S(2)}, u32[]{:S(2)}) collective-permute-start(f32[4,2,128,128]{3,2,1,0:T(8,128)S(1)} %get-tuple-element.57), channel_id=1, source_target_pairs={{0,1},{1,0},{2,3},{3,2},{4,5},{5,4},{6,7},{7,6},{8,9},{9,8},{10,11... | collective-permute-start | bytes 1572872 | tf_op jit(solution)/shard_map/ppermute | solution.py:968

commit v4 on v3

--- a/solution.py
+++ b/solution.py
@@ -10,11 +10,10 @@
 relaxation = 0.5
 PAD = 8
 LOW, HIGH, EDGES = 0, 1, 2
-VM, SM, HBM = pltpu.VMEM, pltpu.SMEM, pltpu.HBM
+VM, SM = pltpu.VMEM, pltpu.SMEM
 F32 = jnp.float32
 BF16 = jnp.bfloat16
 VMEM_BYTES = 30 * 2**20
-FIRST_BYTES = 60 * 2**20
 
 
 class Layout:
@@ -46,7 +45,7 @@
         return self.own(level) + (1 if level > 0 else 0)
 
     def chunk(self, level, rows):
-        size = 8 * max(1, 14 // self.blocks(level))
+        size = 8 * max(1, 28 // self.blocks(level))
         while rows % size or (rows % self.side == 0 and self.side % size):
             size -= 8
         return size
@@ -320,92 +319,58 @@
     over_rows(rows // 2, chunk, body)
 
 
-def pack_kernel(g, force_in, visc_in, fric_in, swap, edge_own, edge_other, sems, force, visc, fric):
+def joined_edges(g, edge_u, edge_v):
+    lane = lane_ids(g.side)
+    quarter = g.side // 4
+    middle = (lane >= quarter) & (lane < g.side - quarter)
+    return jnp.where(middle, pltpu.roll(edge_v, g.half_side, 1), edge_u)
+
+
+def plane(raw, q, slot):
+    force, visc, fric = raw
+    if q < 2:
+        return force[slot, q].astype(F32)
+    return (fric if q == 2 else visc)[slot].astype(F32)
+
+
+def edge_lane(g, level, q, r):
+    return (0 if level % 2 else g.half_side) + q * g.span + r * g.margin(level)
+
+
+def edge_kernel(g, own, other, edge):
     level_here = lax.axis_index("level")
-    copies = Copies(sems)
-    for source, target in ((force_in, force), (visc_in, visc), (fric_in, fric)):
-        copies.start(source, target)
-    copies.finish()
     side = g.side
 
-    def plane(q, slot):
-        if q < 2:
-            return force[slot, q].astype(F32)
-        if q == 2:
-            return fric[slot].astype(F32)
-        return visc[slot]
-
-    def packed_edge(level, column, start):
+    def pack(here):
         lane = lane_ids(side)
-        margin = g.margin(level)
         total = jnp.zeros((side, side), F32)
-        for r in range(g.patch_rows(level)):
-            slot = r * g.columns(level) + column
-            for q in range(4):
-                base = q * g.span + r * margin
-                moved = plane(q, slot)
-                if (base - start) % side:
-                    moved = pltpu.roll(moved, (base - start) % side, 1)
-                total = jnp.where((lane >= base) & (lane < base + margin), moved, total)
-        return total
-
-    def pack_level(level):
-        west_type = level % 2 == 1
-        margin = g.margin(level)
-        last = g.columns(level) - 1
-        west_edge = packed_edge(level, 0, 0)
-        east_edge = packed_edge(level, last, side - margin)
-        edge_own[...] = east_edge if west_type else west_edge
-        edge_other[...] = west_edge if west_type else east_edge
-        if level == 0:
-            lane = lane_ids(side)
-            for q in range(4):
-                for k in range(g.half_slots):
-                    swap[q * g.half_slots + k] = jnp.where(
-                        lane < g.half_side,
-                        plane(q, k),
-                        pltpu.roll(plane(q, k + g.half_slots), g.half_side, 1),
-                    )
-            swap[4 * g.half_slots] = packed_edge(0, 0, g.half_side)
-            return
-        own = g.own(level)
-        first = own if west_type else 0
-        for r in range(g.patch_rows(level)):
-            for k in range(own):
+        for level in (here | 1, here & ~1):
+            raw = own if level == here else other
+            margin = g.margin(level)
+            column, start = (0, 0) if here % 2 else (g.columns(level) - 1, side - margin)
+            for r in range(g.patch_rows(level)):
                 for q in range(4):
-                    swap[q * g.half_slots + r * own + k] = plane(
-                        q, r * g.columns(level) + first + k
-                    )
-        if west_type:
-            swap[4 * g.half_slots] = packed_edge(level, own - 1, side - margin)
-        else:
-            swap[4 * g.half_slots] = packed_edge(level, own, 0)
-
-    for level in range(g.levels):
-        pl.when(level_here == level)(lambda level=level: pack_level(level))
-
-
-def fill_level(g, level, west_type, d, limits, covered, raw, got):
-    force, visc, fric = raw
-    swap, edge_own, edge_other = got
+                    base = edge_lane(g, level, q, r)
+                    value = plane(raw, q, r * g.columns(level) + column)
+                    if (base - start) % side:
+                        value = pltpu.roll(value, (base - start) % side, 1)
+                    total = jnp.where((lane >= base) & (lane < base + margin), value, total)
+        edge[...] = total
+
+    for here in range(g.levels):
+        pl.when(level_here == here)(lambda here=here: pack(here))
+
+
+def fill_level(g, level, west_type, d, limits, covered, raw, edge, groups):
     side = g.side
-    home = (level % 2 == 1) == west_type
     margin = g.margin(level)
     own = g.own(level)
     columns = g.columns(level)
     lane = lane_ids(side)
-    edges = edge_own if home else edge_other
-
-    def plane(q, slot):
-        if q < 2:
-            return force[slot, q].astype(F32)
-        if q == 2:
-            return fric[slot].astype(F32)
-        return visc[slot]
-
-    def unpacked(packed, q, r, place):
-        shift = (place - (q * g.span + r * margin)) % side
-        return pltpu.roll(packed, shift, 1) if shift else packed
+
+    def outer(q, r, place):
+        shift = (place - edge_lane(g, level, q, r)) % side
+        return pltpu.roll(edge[...], shift, 1) if shift else edge[...]
 
     def store(q, k, r, value):
         here = pl.ds(r * side, side)
@@ -421,53 +386,26 @@
                 limits[k] > r * side, 0.5 * value, 0.0
             )
 
-    inner = swap[4 * g.half_slots]
-    outer = edges[...]
-    for r in range(g.patch_rows(level)):
+    clear_pads(d.visc, [(k,) for k in range(g.blocks(level))])
+    for r in range(groups):
         for q in range(4):
-            if level == 0:
-                if home:
-                    value = pltpu.roll(plane(q, r), g.half_side, 1)
-                    east = unpacked(outer, q, r, g.half_side)
-                    value = jnp.where(
-                        (lane >= g.half_side) & (lane < g.half_side + margin), east, value
-                    )
+            if level == 0 and west_type:
+                west = outer(q, r, side - margin)
+                store(q, 0, r, jnp.where(lane >= side - margin, west, plane(raw, q, r)))
+            elif level == 0:
+                value = pltpu.roll(plane(raw, q, r), g.half_side, 1)
+                here = (lane >= g.half_side) & (lane < g.half_side + margin)
+                store(q, 0, r, jnp.where(here, outer(q, r, g.half_side), value))
+            else:
+                for k in range(own):
+                    store(q, k, r, plane(raw, q, r * columns + k + (0 if west_type else own)))
+                if west_type:
+                    east = plane(raw, q, r * columns + own)
+                    west = outer(q, r, side - margin)
                 else:
-                    value = swap[q * g.half_slots + r % g.half_slots]
-                    if r >= g.half_slots:
-                        value = pltpu.roll(value, g.half_side, 1)
-                    east = unpacked(inner, q, r, g.half_side)
-                    west = unpacked(outer, q, r, side - margin)
-                    value = jnp.where(lane < g.half_side, value, east)
-                    value = jnp.where(lane >= side - margin, west, value)
-                store(q, 0, r, value)
-                continue
-            for k in range(own):
-                if home:
-                    value = plane(q, r * columns + k + (0 if west_type else own))
-                else:
-                    value = swap[q * g.half_slots + r * own + k]
-                store(q, k, r, value)
-            if west_type:
-                if home:
-                    east = plane(q, r * columns + own)
-                else:
-                    east = unpacked(inner, q, r, 0)
-                west = unpacked(outer, q, r, side - margin)
-            else:
-                east = unpacked(outer, q, r, 0)
-                if home:
-                    west = plane(q, r * columns + own - 1)
-                else:
-                    west = unpacked(inner, q, r, side - margin)
-            store(q, own, r, jnp.where(lane < g.half_side, east, west))
-
-
-def joined_edges(g, edge_u, edge_v):
-    lane = lane_ids(g.side)
-    quarter = g.side // 4
-    middle = (lane >= quarter) & (lane < g.side - quarter)
-    return jnp.where(middle, pltpu.roll(edge_v, g.half_side, 1), edge_u)
+                    east = outer(q, r, 0)
+                    west = plane(raw, q, r * columns + own - 1)
+                store(q, own, r, jnp.where(lane < g.half_side, east, west))
 
 
 class Level(NamedTuple):
@@ -602,45 +540,54 @@
     put(fine, 1, 1, rows, values)
 
 
-def fill_kernel(
-    g, rows_ref, force, visc, fric, swap, edge_own, edge_other, levels, lent
-):
+def fill_pair(g, rows_ref, own, other, edge, levels, wanted, groups):
     level_here = lax.axis_index("level")
     patch = lax.axis_index("patch")
-    raw = (force, visc, fric)
-    got = (swap, edge_own, edge_other)
     odd = level_here % 2 == 1
+    for west_type in (True, False):
+
+        @pl.when(odd if west_type else jnp.logical_not(odd))
+        def _():
+            for level in wanted:
+                near = near_counts(g, rows_ref, level, patch, odd)
+                limits = lane_limits(g, level, near, g.side)
+                covered = None
+                if level == 1:
+                    finer = near_counts(g, rows_ref, 2, patch, odd)
+                    covered = lane_limits(g, 1, finer, g.half_side)
+                home = (level % 2 == 1) == west_type
+                raw = own if home else other
+                fill_level(
+                    g, level, west_type, levels[level], limits, covered, raw, edge, groups(level)
+                )
+
+
+def fill_kernel(g, rows_ref, own, other, edge, filled, lent, low):
+    level_here = lax.axis_index("level")
     top = g.levels - 1
 
-    def filled(wanted, covered):
-        for level in wanted:
-            clear_pads(levels[level].visc, [(k,) for k in range(g.blocks(level))])
-        for west_type in (True, False):
-
-            @pl.when(odd if west_type else jnp.logical_not(odd))
-            def _():
-                for level in wanted:
-                    near = near_counts(g, rows_ref, level, patch, odd)
-                    limits = lane_limits(g, level, near, g.side)
-                    fill_level(
-                        g, level, west_type, levels[level], limits, covered.get(level), raw, got
-                    )
-
-    pl.when(level_here >= top - 1)(lambda: filled((top, top - 1), {}))
+    @pl.when(level_here >= top - 1)
+    def _():
+        levels = dict(zip((top - 1, top), filled))
+        fill_pair(g, rows_ref, own, other, edge, levels, (top, top - 1), g.patch_rows)
 
     @pl.when(level_here < top - 1)
     def _():
-        near = near_counts(g, rows_ref, 2, patch, odd)
-        filled((1, 0), {1: lane_limits(g, 1, near, g.half_side)})
-        lend(g, levels[1], levels[0], lent)
-
-
-def down_kernel(g, rows_ref, filled, sums, kept, edges, scratch):
+        fill_pair(g, rows_ref, own, other, edge, low, (1, 0), lambda level: low_groups(g, level))
+        lend(g, low[1], low[0], lent)
+
+
+def low_groups(g, level):
+    return -(-lent_rows(g)[1 - level] // g.side)
+
+
+def down_kernel(g, rows_ref, own, other, edge, upper, sums, kept, lower, edges, scratch):
     level_here = lax.axis_index("level")
     patch = lax.axis_index("patch")
     side = g.side
     top = g.levels - 1
     odd = level_here % 2 == 1
+    filled = [*lower, *upper]
     levels = [merged(merged(a, b), c) for a, b, c in zip(scratch, kept, filled)]
 
     def limits_of(level):
@@ -676,6 +623,7 @@
 
     @pl.when(level_here < top - 1)
     def _():
+        fill_pair(g, rows_ref, own, other, edge, levels, (1, 0), g.patch_rows)
         for level in (1, 0):
             smooth_weights(g, level, levels[level], limits_of(level), g.rows(level), False)
 
@@ -984,21 +932,12 @@
     def array(level, rows, kind, comps, pad):
         return level_array(g, g.blocks(level), rows, kind, comps, pad)
 
-    swap, edge_own, edge_other = run_kernel(
-        lambda *refs: pack_kernel(g, *refs),
-        [(force, HBM), (visc, HBM), (fric, HBM)],
-        [(make((4 * g.half_slots + 1, side, side), F32), VM), (block, VM), (block, VM)],
-        [
-            pltpu.SemaphoreType.DMA((4,)),
-            vmem(force.shape, force.dtype),
-            vmem(visc.shape, visc.dtype),
-            vmem(fric.shape, fric.dtype),
-        ],
-        FIRST_BYTES,
-    )
-    swap = moved(swap, g, lambda p, l: (p, l ^ 1))
-    edge_own = moved(edge_own, g, lambda p, l: (p + (1 if l % 2 else -1), l))
-    edge_other = moved(edge_other, g, lambda p, l: (p + (-1 if l % 2 else 1), l ^ 1))
+    own = (force, visc, fric)
+    other = tuple(moved(value, g, lambda p, l: (p, l ^ 1)) for value in own)
+    (edge,) = run_kernel(
+        lambda *refs: edge_kernel(g, *refs), [(own, VM), (other, VM)], [(block, VM)], []
+    )
+    edge = moved(edge, g, lambda p, l: (p + (-1 if l % 2 else 1), l ^ 1))
 
     fields = [
         Level(
@@ -1010,19 +949,22 @@
         for level in range(g.levels)
     ]
     rows, less = lent_rows(g)
-    filled, lent = run_kernel(
+    given = [(patch_rows, SM), (own, VM), (other, VM), (edge, VM)]
+
+    def low_scratch(level):
+        size = low_groups(g, level) * side
+        return Level(
+            array(level, size, vmem, False, True),
+            None,
+            right=array(level, size, vmem, True, False),
+            fric=array(level, size, vmem, False, False),
+        )
+
+    upper, lent = run_kernel(
         lambda *refs: fill_kernel(g, *refs),
-        [
-            (patch_rows, SM),
-            (force, VM),
-            (visc, VM),
-            (fric, VM),
-            (swap, VM),
-            (edge_own, VM),
-            (edge_other, VM),
-        ],
-        [(fields, VM), (make((5 * (rows + less) + rows, side), BF16), VM)],
-        [],
+        given,
+        [(fields[top - 1 :], VM), (make((5 * (rows + less) + rows, side), BF16), VM)],
+        [[low_scratch(level) for level in (0, 1)]],
     )
     lent = moved(lent, g, lambda p, l: (p, l + 2))
 
@@ -1037,12 +979,17 @@
         more = dict(right=both) if level < top else {}
         return Level(None, None, left=both, **more, **step_arrays(g, level, g.rows(level)))
 
-    sums, kept = run_kernel(
+    sums, kept, lower = run_kernel(
         lambda *refs: down_kernel(g, *refs),
-        [(patch_rows, SM), (filled, VM)],
-        [(three, VM), ([kept_of(level) for level in range(g.levels)], VM)],
+        [*given, (upper, VM)],
+        [
+            (three, VM),
+            ([kept_of(level) for level in range(g.levels)], VM),
+            (fields[: top - 1], VM),
+        ],
         [vmem((2, side, side), F32), [down_scratch(level) for level in range(g.levels)]],
     )
+    filled = [*lower, *upper]
     sums_there = moved(sums, g, lambda p, l: (p, l - 2))
 
     def up_scratch(level):
@@ -1096,10 +1043,10 @@
             vmem((2, rows, side), F32),
         ],
     )
-    given = moved(theirs, g, lambda p, l: (p, l ^ 1))
+    received = moved(theirs, g, lambda p, l: (p, l ^ 1))
     adjoint, gradient = run_kernel(
         lambda *refs: join_kernel(g, *refs),
-        [(mine, VM), (given, VM), (speed, VM), (fric, VM)],
+        [(mine, VM), (received, VM), (speed, VM), (fric, VM)],
         [
             (make((g.slots, 2, side, side), F32), VM),
             (make((g.slots, side, side), BF16), VM),

time: 37.7 us -> 37.1 us (0.984); the launches traced: 37.5 us -> 36.5 us
  Pallas kernels: 19.2 us -> 14.1 us
  local copies, waits for them, and re-layouts: 0.02 us -> 3.05 us
  waiting for transfers between devices: 7.65 us -> 9.59 us
  starting transfers between devices: 9.84 us -> 9.04 us
    pallas_call x6, Pallas kernels: 19.2 us -> 14.1 us  [run_kernel(): pl.pallas_call(kernel, out_shape=[leaf for leaves, _ in out_trees for lea...]
    unnamed x10 -> x12, local copies, waits for them, and re-layouts: 0.02 us -> 3.05 us
    ppermute x6 -> x7, waiting for transfers between devices: 7.65 us -> 9.59 us  [moved(): return lax.ppermute(value, ('patch', 'level'), pairs)]
    ppermute x6 -> x7, starting transfers between devices: 9.84 us -> 9.04 us  [moved(): return lax.ppermute(value, ('patch', 'level'), pairs)]
  transfers between devices with their start and end apart: 6 -> 7, of which waited for: 3 -> 4; matrix products, arithmetic and copies ran while one was open for 0% -> 0% of each run, Pallas kernels for 27% -> 24%
where the time goes in v4:
time: 37.1 us; the launch traced here: 36.5 us
  Pallas kernels  14.1 us (38%)
  waiting for transfers between devices  9.59 us (26%)
  starting transfers between devices  9.04 us (24%)
  local copies, waits for them, and re-layouts  3.05 us (8%)
  between operations  0.73 us (2%)
    pallas_call x6, Pallas kernels, run_kernel(): pl.pallas_call(kernel, out_shape=[leaf for leaves, _ in out_trees for lea...  14.1 us
    ppermute x7, waiting for transfers between devices, moved(): return lax.ppermute(value, ('patch', 'level'), pairs)  9.59 us
    ppermute x7, starting transfers between devices, moved(): return lax.ppermute(value, ('patch', 'level'), pairs)  9.04 us
    unnamed x12, local copies, waits for them, and re-layouts  3.05 us
  transfers between devices with their start and end apart: 7, of which 4 were waited for; matrix products, arithmetic and copies ran while one was open for 0% of the time, Pallas kernels for 24%

profile of v4, /device:TPU:21, one launch (start us, length us, event | category | flops | bytes accessed | tf_op | source)
XLA Modules:
  0.0 36.5 jit_solution(10577212601966654505)
XLA Ops:
  0.6 0.7 %collective-permute-start = (bf16[8,2,128,128]{3,2,1,0:T(8,128)(2,1)}, bf16[8,2,128,128]{3,2,1,0:T(8,128)(2,1)S(1)}, u32[]{:S(2)}, u32[]{:S(2)}) collective-permute-start(bf16[8,2,128,128]{3,2,1,0:T(8,128)(2,1)} %bitcast.6), channel_id=1, source_target_pairs={{0,1},{1,0},{2,3},{3,2},{4,5},{5,4},{6,7},{7,6},{8,9},{9,8},{10,11... | collective-permute-start | bytes 1572872 | tf_op jit(solution)/shard_map/ppermute | solution.py:916
  1.4 0.0 copy-start.5
  1.4 0.1 collective-permute-start.1
  1.5 0.4 %collective-permute-start.2 = (bf16[8,128,128]{2,1,0:T(8,128)(2,1)}, bf16[8,128,128]{2,1,0:T(8,128)(2,1)S(1)}, u32[]{:S(2)}, u32[]{:S(2)}) collective-permute-start(bf16[8,128,128]{2,1,0:T(8,128)(2,1)} %bitcast.14), channel_id=1, source_target_pairs={{0,1},{1,0},{2,3},{3,2},{4,5},{5,4},{6,7},{7,6},{8,9},{9,8},{10,11... | collective-permute-start | bytes 786440 | tf_op jit(solution)/shard_map/ppermute | solution.py:916
  1.9 2.4 %collective-permute-done.2.refs_5_.refs_6_ = bf16[8,128,128]{2,1,0:T(8,128)(2,1)S(1)} collective-permute-done((bf16[8,128,128]{2,1,0:T(8,128)(2,1)}, bf16[8,128,128]{2,1,0:T(8,128)(2,1)S(1)}, u32[]{:S(2)}, u32[]{:S(2)}) %collective-permute-start.2) | collective-permute-done | bytes 262176 | tf_op jit(solution)/shard_map/ppermute | solution.py:916
  4.2 0.0 collective-permute-done.refs_3_.refs_4_
  4.2 0.0 collective-permute-done.1.refs_4_.refs_5_
  4.2 0.0 copy-start
  4.3 1.0 %copy-done = bf16[1,8,2,128,128]{4,3,2,1,0:T(8,128)(2,1)S(1)} copy-done((bf16[1,8,2,128,128]{4,3,2,1,0:T(8,128)(2,1)S(1)}, bf16[1,8,2,128,128]{4,3,2,1,0:T(8,128)(2,1)}, u32[]{:S(2)}) %copy-start) | copy-done | bytes 524312
  5.3 0.0 copy-start.1
  5.3 1.0 %copy-done.1 = f32[1,8,128,128]{3,2,1,0:T(8,128)S(1)} copy-done((f32[1,8,128,128]{3,2,1,0:T(8,128)S(1)}, f32[1,8,128,128]{3,2,1,0:T(8,128)}, u32[]{:S(2)}) %copy-start.1) | copy-done | bytes 524312
  6.3 0.0 copy-start.2
  6.3 0.9 %copy-done.2 = bf16[1,8,128,128]{3,2,1,0:T(8,128)(2,1)S(1)} copy-done((bf16[1,8,128,128]{3,2,1,0:T(8,128)(2,1)S(1)}, bf16[1,8,128,128]{3,2,1,0:T(8,128)(2,1)}, u32[]{:S(2)}) %copy-start.2) | copy-done | bytes 262168
  7.3 0.6 %shard_map.68 = f32[128,128]{1,0:T(8,128)S(1)} custom-call(bf16[8,2,128,128]{3,2,1,0:T(8,128)(2,1)S(1)} %bitcast.7, f32[8,128,128]{2,1,0:T(8,128)S(1)} %bitcast.11, bf16[8,128,128]{2,1,0:T(8,128)(2,1)S(1)} %bitcast.15, bf16[8,2,128,128]{3,2,1,0:T(8,128)(2,1)S(1)} %collective-permute-done.refs_3_.refs_4_, ...), custom_call_target="tpu_custom_call" | custom-call | tf_op jit(solution)/shard_map/pallas_call | solution.py:893
  7.9 2.4 %collective-permute-start.3 = (f32[128,128]{1,0:T(8,128)S(1)}, f32[128,128]{1,0:T(8,128)S(1)}, u32[]{:S(2)}, u32[]{:S(2)}) collective-permute-start(f32[128,128]{1,0:T(8,128)S(1)} %shard_map.68), channel_id=1, source_target_pairs={{0,5},{2,7},{4,9},{5,0},{6,11},{7,2},{8,13},{9,4},{10,15},{11,6},{... | collective-permute-start | bytes 196616 | tf_op jit(solution)/shard_map/ppermute | solution.py:916
  10.3 4.1 %collective-permute-done.3.refs_7_ = f32[128,128]{1,0:T(8,128)S(1)} collective-permute-done((f32[128,128]{1,0:T(8,128)S(1)}, f32[128,128]{1,0:T(8,128)S(1)}, u32[]{:S(2)}, u32[]{:S(2)}) %collective-permute-start.3) | collective-permute-done | bytes 65568 | tf_op jit(solution)/shard_map/ppermute | solution.py:916
  14.3 0.0 copy-done.5
  14.3 1.0 %shard_map.69 = (f32[3,272,128]{2,1,0:T(8,128)S(1)}, f32[2,3,256,128]{3,2,1,0:T(8,128)S(1)}, f32[3,256,128]{2,1,0:T(8,128)S(1)}, f32[5,144,128]{2,1,0:T(8,128)S(...) custom-call(s32[4,8]{1,0:T(4,128)S(1)} %copy-done.5, ...), custom_call_target="tpu_custom_call" | custom-call | tf_op jit(solution)/shard_map/pallas_call | solution.py:893
  15.3 2.7 %collective-permute-start.5 = (bf16[1264,128]{1,0:T(8,128)(2,1)S(1)}, bf16[1264,128]{1,0:T(8,128)(2,1)S(1)}, u32[]{:S(2)}, u32[]{:S(2)}) collective-permute-start(bf16[1264,128]{1,0:T(8,128)(2,1)S(1)} %get-tuple-element.43), channel_id=1, source_target_pairs={{0,2},{1,3},{4,6},{5,7},{8,10},{9,11},{12,14},{13,15},{16,18},{17,... | collective-permute-start | bytes 970760 | tf_op jit(solution)/shard_map/ppermute | solution.py:916
  18.0 3.5 %shard_map.70 = (f32[3,128,128]{2,1,0:T(8,128)S(1)}, f32[2,1,1024,128]{3,2,1,0:T(8,128)S(1)}, f32[2,2,512,128]{3,2,1,0:T(8,128)S(1)}, f32[2,3,256,128]{3,2,1,0:T...) custom-call(s32[4,8]{1,0:T(4,128)S(1)} %copy-done.5, ...), custom_call_target="tpu_custom_call" | custom-call | tf_op jit(solution)/shard_map/pallas_call | solution.py:893
  21.5 1.3 %collective-permute-start.4 = (f32[3,128,128]{2,1,0:T(8,128)S(1)}, f32[3,128,128]{2,1,0:T(8,128)S(1)}, u32[]{:S(2)}, u32[]{:S(2)}) collective-permute-start(f32[3,128,128]{2,1,0:T(8,128)S(1)} %get-tuple-element.34.refs_1_), channel_id=1, source_target_pairs={{2,0},{3,1},{6,4},{7,5},{10,8},{11,9},{14,12},{15,13},{18,16},{19,... | collective-permute-start | bytes 589832 | tf_op jit(solution)/shard_map/ppermute | solution.py:916
  22.8 1.6 %collective-permute-done.5.refs_2_ = bf16[1264,128]{1,0:T(8,128)(2,1)S(1)} collective-permute-done((bf16[1264,128]{1,0:T(8,128)(2,1)S(1)}, bf16[1264,128]{1,0:T(8,128)(2,1)S(1)}, u32[]{:S(2)}, u32[]{:S(2)}) %collective-permute-start.5) | collective-permute-done | bytes 323616 | tf_op jit(solution)/shard_map/ppermute | solution.py:916
  24.5 5.4 %shard_map.71 = (f32[4,2,128,128]{3,2,1,0:T(8,128)S(1)}, f32[4,2,128,128]{3,2,1,0:T(8,128)S(1)}) custom-call(s32[4,8]{1,0:T(4,128)S(1)} %copy-done.5, f32[3,128,128]{2,1,0:T(8,128)S(1)} %get-tuple-element.34.refs_1_, bf16[1264,128]{1,0:T(8,128)(2,1)S(1)} %collective-permute-done.5.refs_2_, f32[1,1040,128]{2,1,0:T(8,128)S(1)} %get-tuple-element.35.refs_3_.refs_2_, ...), custom_call_target="tpu_custom_call" | custom-call | tf_op jit(solution)/shard_map/pallas_call | solution.py:893
  29.8 0.0 collective-permute-done.4.refs_1_
  29.8 0.0 copy-start.3
  29.9 0.0 copy-start.4
  29.9 2.4 %shard_map.72 = (f32[4,2,128,128]{3,2,1,0:T(8,128)S(1)}, f32[4,2,128,128]{3,2,1,0:T(8,128)S(1)}) custom-call(s32[4,8]{1,0:T(4,128)S(1)} %copy-done.5, f32[3,128,128]{2,1,0:T(8,128)S(1)} %collective-permute-done.4.refs_1_, f32[1,1040,128]{2,1,0:T(8,128)S(1)} %get-tuple-element.35.refs_3_.refs_2_, f32[2,1,1024,128]{3,2,1,0:T(8,128)S(1)} %get-tuple-element.36.refs_4_.refs_3_, ...), custom_call_target="tpu_custom_call" | custom-call | tf_op jit(solution)/shard_map/pallas_call | solution.py:893
  32.2 1.4 %collective-permute-start.6 = (f32[4,2,128,128]{3,2,1,0:T(8,128)S(1)}, f32[4,2,128,128]{3,2,1,0:T(8,128)S(1)}, u32[]{:S(2)}, u32[]{:S(2)}) collective-permute-start(f32[4,2,128,128]{3,2,1,0:T(8,128)S(1)} %get-tuple-element.51), channel_id=1, source_target_pairs={{0,1},{1,0},{2,3},{3,2},{4,5},{5,4},{6,7},{7,6},{8,9},{9,8},{10,11... | collective-permute-start | bytes 1572872 | tf_op jit(solution)/shard_map/ppermute | solution.py:916
  33.7 1.5 %collective-permute-done.6.refs_1_ = f32[4,2,128,128]{3,2,1,0:T(8,128)S(1)} collective-permute-done((f32[4,2,128,128]{3,2,1,0:T(8,128)S(1)}, f32[4,2,128,128]{3,2,1,0:T(8,128)S(1)}, u32[]{:S(2)}, u32[]{:S(2)}) %collective-permute-start.6) | collective-permute-done | bytes 524320 | tf_op jit(solution)/shard_map/ppermute | solution.py:916
  35.2 0.0 copy-done.3
  35.2 0.0 copy-done.4
  35.2 1.2 %shard_map.73 = (f32[8,2,128,128]{3,2,1,0:T(8,128)}, bf16[8,128,128]{2,1,0:T(8,128)(2,1)}) custom-call(f32[4,2,128,128]{3,2,1,0:T(8,128)S(1)} %get-tuple-element.50.refs_0_, f32[4,2,128,128]{3,2,1,0:T(8,128)S(1)} %collective-permute-done.6.refs_1_, bf16[8,2,128,128]{3,2,1,0:T(8,128)(2,1)S(1)} %bitcast.19, bf16[8,128,128]{2,1,0:T(8,128)(2,1)S(1)} %bitcast.18), custom_call_target="tpu_custom_call" | custom-call | tf_op jit(solution)/shard_map/pallas_call | solution.py:893
Async XLA Ops:
  0.6 3.6 %collective-permute-start = (bf16[8,2,128,128]{3,2,1,0:T(8,128)(2,1)}, bf16[8,2,128,128]{3,2,1,0:T(8,128)(2,1)S(1)}, u32[]{:S(2)}, u32[]{:S(2)}) collective-permute-start(bf16[8,2,128,128]{3,2,1,0:T(8,128)(2,1)} %bitcast.6), channel_id=1, source_target_pairs={{0,1},{1,0},{2,3},{3,2},{4,5},{5,4},{6,7},{7,6},{8,9},{9,8},{10,11... | collective-permute-start | bytes 1572872 | tf_op jit(solution)/shard_map/ppermute | solution.py:916
  1.4 13.0 %copy-start.5 = (s32[4,8]{1,0:T(4,128)S(1)}, s32[4,8]{1,0:T(4,128)}, u32[]{:S(2)}) copy-start(s32[4,8]{1,0:T(4,128)} %refs_0_.7) | copy-start | bytes 388
  1.4 2.9 %collective-permute-start.1 = (f32[8,128,128]{2,1,0:T(8,128)}, f32[8,128,128]{2,1,0:T(8,128)S(1)}, u32[]{:S(2)}, u32[]{:S(2)}) collective-permute-start(f32[8,128,128]{2,1,0:T(8,128)} %bitcast.10), channel_id=1, source_target_pairs={{0,1},{1,0},{2,3},{3,2},{4,5},{5,4},{6,7},{7,6},{8,9},{9,8},{10,11... | collective-permute-start | bytes 1572872 | tf_op jit(solution)/shard_map/ppermute | solution.py:916
  1.5 2.8 %collective-permute-start.2 = (bf16[8,128,128]{2,1,0:T(8,128)(2,1)}, bf16[8,128,128]{2,1,0:T(8,128)(2,1)S(1)}, u32[]{:S(2)}, u32[]{:S(2)}) collective-permute-start(bf16[8,128,128]{2,1,0:T(8,128)(2,1)} %bitcast.14), channel_id=1, source_target_pairs={{0,1},{1,0},{2,3},{3,2},{4,5},{5,4},{6,7},{7,6},{8,9},{9,8},{10,11... | collective-permute-start | bytes 786440 | tf_op jit(solution)/shard_map/ppermute | solution.py:916
  4.2 1.0 %copy-start = (bf16[1,8,2,128,128]{4,3,2,1,0:T(8,128)(2,1)S(1)}, bf16[1,8,2,128,128]{4,3,2,1,0:T(8,128)(2,1)}, u32[]{:S(2)}) copy-start(bf16[1,8,2,128,128]{4,3,2,1,0:T(8,128)(2,1)} %param.5) | copy-start | bytes 1572868
  5.3 1.0 %copy-start.1 = (f32[1,8,128,128]{3,2,1,0:T(8,128)S(1)}, f32[1,8,128,128]{3,2,1,0:T(8,128)}, u32[]{:S(2)}) copy-start(f32[1,8,128,128]{3,2,1,0:T(8,128)} %param.7) | copy-start | bytes 1572868
  6.3 0.9 %copy-start.2 = (bf16[1,8,128,128]{3,2,1,0:T(8,128)(2,1)S(1)}, bf16[1,8,128,128]{3,2,1,0:T(8,128)(2,1)}, u32[]{:S(2)}) copy-start(bf16[1,8,128,128]{3,2,1,0:T(8,128)(2,1)} %param.8) | copy-start | bytes 786436
  7.9 6.5 %collective-permute-start.3 = (f32[128,128]{1,0:T(8,128)S(1)}, f32[128,128]{1,0:T(8,128)S(1)}, u32[]{:S(2)}, u32[]{:S(2)}) collective-permute-start(f32[128,128]{1,0:T(8,128)S(1)} %shard_map.68), channel_id=1, source_target_pairs={{0,5},{2,7},{4,9},{5,0},{6,11},{7,2},{8,13},{9,4},{10,15},{11,6},{... | collective-permute-start | bytes 196616 | tf_op jit(solution)/shard_map/ppermute | solution.py:916
  15.3 9.1 %collective-permute-start.5 = (bf16[1264,128]{1,0:T(8,128)(2,1)S(1)}, bf16[1264,128]{1,0:T(8,128)(2,1)S(1)}, u32[]{:S(2)}, u32[]{:S(2)}) collective-permute-start(bf16[1264,128]{1,0:T(8,128)(2,1)S(1)} %get-tuple-element.43), channel_id=1, source_target_pairs={{0,2},{1,3},{4,6},{5,7},{8,10},{9,11},{12,14},{13,15},{16,18},{17,... | collective-permute-start | bytes 970760 | tf_op jit(solution)/shard_map/ppermute | solution.py:916
  21.5 8.3 %collective-permute-start.4 = (f32[3,128,128]{2,1,0:T(8,128)S(1)}, f32[3,128,128]{2,1,0:T(8,128)S(1)}, u32[]{:S(2)}, u32[]{:S(2)}) collective-permute-start(f32[3,128,128]{2,1,0:T(8,128)S(1)} %get-tuple-element.34.refs_1_), channel_id=1, source_target_pairs={{2,0},{3,1},{6,4},{7,5},{10,8},{11,9},{14,12},{15,13},{18,16},{19,... | collective-permute-start | bytes 589832 | tf_op jit(solution)/shard_map/ppermute | solution.py:916
  29.8 5.4 %copy-start.3 = (bf16[1,8,128,128]{3,2,1,0:T(8,128)(2,1)S(1)}, bf16[1,8,128,128]{3,2,1,0:T(8,128)(2,1)}, u32[]{:S(2)}) copy-start(bf16[1,8,128,128]{3,2,1,0:T(8,128)(2,1)} %param.8) | copy-start | bytes 786436
  29.9 5.4 %copy-start.4 = (bf16[1,8,2,128,128]{4,3,2,1,0:T(8,128)(2,1)S(1)}, bf16[1,8,2,128,128]{4,3,2,1,0:T(8,128)(2,1)}, u32[]{:S(2)}) copy-start(bf16[1,8,2,128,128]{4,3,2,1,0:T(8,128)(2,1)} %param.6) | copy-start | bytes 1572868
  32.2 3.0 %collective-permute-start.6 = (f32[4,2,128,128]{3,2,1,0:T(8,128)S(1)}, f32[4,2,128,128]{3,2,1,0:T(8,128)S(1)}, u32[]{:S(2)}, u32[]{:S(2)}) collective-permute-start(f32[4,2,128,128]{3,2,1,0:T(8,128)S(1)} %get-tuple-element.51), channel_id=1, source_target_pairs={{0,1},{1,0},{2,3},{3,2},{4,5},{5,4},{6,7},{7,6},{8,9},{9,8},{10,11... | collective-permute-start | bytes 1572872 | tf_op jit(solution)/shard_map/ppermute | solution.py:916

commit v5 on v4

--- a/solution.py
+++ b/solution.py
@@ -14,6 +14,7 @@
 F32 = jnp.float32
 BF16 = jnp.bfloat16
 VMEM_BYTES = 30 * 2**20
+FIRST_BYTES = 60 * 2**20
 
 
 class Layout:
@@ -108,52 +109,51 @@
         ref[index + (slice(last - PAD, last), slice(None))] = jnp.zeros((PAD, width), F32)
 
 
+def off_diagonal_rows(g, d, row, size, count):
+    here = pl.ds(row, size)
+    inner = pl.ds(PAD + row, size)
+    centre = [[d.cells[comp, k, inner, :] for k in range(count)] for comp in range(2)]
+    beside = [both_sides(g, centre[comp]) for comp in range(2)]
+    products = []
+    for k in range(count):
+        visc = d.visc[k, inner, :]
+        half = 0.5 * visc
+        (u, v) = (centre[comp][k] for comp in range(2))
+        (u_e, u_w), (v_e, v_w) = ((beside[c][0][k], beside[c][1][k]) for c in range(2))
+        u_n, v_n = (d.cells[c, k, pl.ds(PAD + row + 1, size), :] for c in range(2))
+        u_s, v_s = (d.cells[c, k, pl.ds(PAD + row - 1, size), :] for c in range(2))
+        one_u, one_v = visc * u, visc * v
+        four_u, four_v = 4.0 * one_u, 4.0 * one_v
+        cross_u, cross_v = half * (v_e - v_w), visc * (u_e - u_w)
+        d.north[0, k, inner, :] = one_u + cross_u
+        d.south[0, k, inner, :] = one_u - cross_u
+        d.north[1, k, inner, :] = four_v + cross_v
+        d.south[1, k, inner, :] = four_v - cross_v
+        cross_u, cross_v = visc * (v_n - v_s), half * (u_n - u_s)
+        products.append(
+            (
+                four_u + cross_u,
+                four_u - cross_u,
+                one_v + cross_v,
+                one_v - cross_v,
+                visc * (4.0 * (u_e + u_w) + (u_n + u_s)),
+                visc * (4.0 * (v_n + v_s) + (v_e + v_w)),
+            )
+        )
+    for comp in range(2):
+        east = one_side(g, [item[2 * comp] for item in products], True)
+        west = one_side(g, [item[2 * comp + 1] for item in products], False)
+        for k in range(count):
+            d.part[comp, k, here, :] = products[k][4 + comp] + east[k] + west[k]
+
+
 def off_diagonal_step(g, level, d, start, stop):
     count = g.blocks(level)
     chunk = g.chunk(level, stop - start)
 
     def body(row):
-        row = row + start
-        here = pl.ds(row, chunk)
-        inner = pl.ds(PAD + row, chunk)
-
-        def line(comp, step):
-            rows = pl.ds(PAD + row + step, chunk)
-            return [d.cells[comp, k, rows, :] for k in range(count)]
-
-        centre = [line(comp, 0) for comp in range(2)]
-        beside = [both_sides(g, centre[comp]) for comp in range(2)]
-        products = []
-        for k in range(count):
-            visc = d.visc[k, inner, :]
-            half = 0.5 * visc
-            (u, v) = (centre[comp][k] for comp in range(2))
-            (u_e, u_w), (v_e, v_w) = ((beside[c][0][k], beside[c][1][k]) for c in range(2))
-            u_n, v_n = (d.cells[c, k, pl.ds(PAD + row + 1, chunk), :] for c in range(2))
-            u_s, v_s = (d.cells[c, k, pl.ds(PAD + row - 1, chunk), :] for c in range(2))
-            one_u, one_v = visc * u, visc * v
-            four_u, four_v = 4.0 * one_u, 4.0 * one_v
-            cross_u, cross_v = half * (v_e - v_w), visc * (u_e - u_w)
-            d.north[0, k, inner, :] = one_u + cross_u
-            d.south[0, k, inner, :] = one_u - cross_u
-            d.north[1, k, inner, :] = four_v + cross_v
-            d.south[1, k, inner, :] = four_v - cross_v
-            cross_u, cross_v = visc * (v_n - v_s), half * (u_n - u_s)
-            products.append(
-                (
-                    four_u + cross_u,
-                    four_u - cross_u,
-                    one_v + cross_v,
-                    one_v - cross_v,
-                    visc * (4.0 * (u_e + u_w) + (u_n + u_s)),
-                    visc * (4.0 * (v_n + v_s) + (v_e + v_w)),
-                )
-            )
-        for comp in range(2):
-            east = one_side(g, [item[2 * comp] for item in products], True)
-            west = one_side(g, [item[2 * comp + 1] for item in products], False)
-            for k in range(count):
-                d.part[comp, k, here, :] = products[k][4 + comp] + east[k] + west[k]
+        for step in range(0, chunk, 8):
+            off_diagonal_rows(g, d, start + row + step, 8, count)
 
     over_rows(stop - start, chunk, body)
 
@@ -170,27 +170,32 @@
     count = g.blocks(level)
     chunk = g.chunk(level, rows)
 
-    def body(row):
-        here = pl.ds(row, chunk)
-        inner = pl.ds(PAD + row, chunk)
+    def some_rows(row):
+        here = pl.ds(row, 8)
+        inner = pl.ds(PAD + row, 8)
         centre = [d.visc[k, inner, :] for k in range(count)]
         east, west = both_sides(g, centre)
         for k in range(count):
-            north = d.visc[k, pl.ds(PAD + row + 1, chunk), :]
-            south = d.visc[k, pl.ds(PAD + row - 1, chunk), :]
+            north = d.visc[k, pl.ds(PAD + row + 1, 8), :]
+            south = d.visc[k, pl.ds(PAD + row - 1, 8), :]
             friction = d.fric[k, here, :]
             twice = 2.0 * centre[k]
             along_row = twice + east[k] + west[k]
             along_col = twice + north + south
-            ids = row + lax.broadcasted_iota(jnp.int32, (chunk, g.side), 0)
-            live = ids < limits[k]
+            live = jnp.broadcast_to(limits[k], (8, g.side)) > row
             diag_u = 4.0 * along_row + along_col + friction
             diag_v = 4.0 * along_col + along_row + friction
             for comp, diag in ((0, diag_u), (1, diag_v)):
-                weight = jnp.where(live, relaxation / diag, 0.0)
+                guess = pl.reciprocal(diag, approx=True)
+                weight = guess * (2.0 * relaxation - relaxation * diag * guess)
+                weight = jnp.where(live, weight, 0.0)
                 d.weight[comp, k, here, :] = weight
                 if from_zero:
                     d.cells[comp, k, inner, :] = weight * d.right[comp, k, here, :]
+
+    def body(row):
+        for step in range(0, chunk, 8):
+            some_rows(row + step)
 
     over_rows(rows, chunk, body)
 
@@ -337,25 +342,58 @@
     return (0 if level % 2 else g.half_side) + q * g.span + r * g.margin(level)
 
 
-def edge_kernel(g, own, other, edge):
+def packed_edge(g, here, level, patch_of):
+    side = g.side
+    lane = lane_ids(side)
+    margin = g.margin(level)
+    start = 0 if here % 2 else side - margin
+    total = jnp.zeros((side, side), F32)
+    for r in range(g.patch_rows(level)):
+        for q in range(4):
+            base = edge_lane(g, level, q, r)
+            value = patch_of(q, r)
+            if (base - start) % side:
+                value = pltpu.roll(value, (base - start) % side, 1)
+            total = jnp.where((lane >= base) & (lane < base + margin), value, total)
+    return total
+
+
+def edge_column(g, here, level):
+    return 0 if here % 2 else g.columns(level) - 1
+
+
+def first_edge_kernel(g, own, edge, sems, held):
     level_here = lax.axis_index("level")
-    side = g.side
+
+    def pack(level):
+        copies = Copies(sems)
+        rows = g.patch_rows(level)
+        if g.columns(level) == 1:
+            for source, target in zip(own, held):
+                copies.start(source, target)
+        else:
+            for r in range(rows):
+                slot = r * g.columns(level) + edge_column(g, level, level)
+                for source, target in zip(own, held):
+                    copies.start(source.at[slot], target.at[r])
+        copies.finish()
+        edge[...] = packed_edge(g, level, level, lambda q, r: plane(held, q, r))
+
+    for level in range(g.levels):
+        pl.when(level_here == level)(lambda level=level: pack(level))
+
+
+def edge_kernel(g, first, other, edge):
+    level_here = lax.axis_index("level")
 
     def pack(here):
-        lane = lane_ids(side)
-        total = jnp.zeros((side, side), F32)
-        for level in (here | 1, here & ~1):
-            raw = own if level == here else other
-            margin = g.margin(level)
-            column, start = (0, 0) if here % 2 else (g.columns(level) - 1, side - margin)
-            for r in range(g.patch_rows(level)):
-                for q in range(4):
-                    base = edge_lane(g, level, q, r)
-                    value = plane(raw, q, r * g.columns(level) + column)
-                    if (base - start) % side:
-                        value = pltpu.roll(value, (base - start) % side, 1)
-                    total = jnp.where((lane >= base) & (lane < base + margin), value, total)
-        edge[...] = total
+        level = here ^ 1
+        column = edge_column(g, here, level)
+
+        def patch_of(q, r):
+            return plane(other, q, r * g.columns(level) + column)
+
+        edge[...] = first[...] + packed_edge(g, here, level, patch_of)
 
     for here in range(g.levels):
         pl.when(level_here == here)(lambda here=here: pack(here))
@@ -478,66 +516,104 @@
     return low_rows(g), -(-low_rows(g) // 2 // 16) * 16
 
 
-def lent_planes(level):
-    visc = level[3]
+def lent_forcing(g):
+    return [count * g.half_side for count in range(1, g.patch_rows(2) + 1)]
+
+
+def lent_size(g):
+    rows, less = lent_rows(g)
+    return 3 * rows + 2 * 16 * len(lent_forcing(g)) + 5 * less
+
+
+def pair_of(visc):
     high = visc.astype(BF16)
-    return [value.astype(BF16) for value in level[:3]] + [
-        high,
-        (visc - high.astype(F32)).astype(BF16),
-    ]
+    return [high, (visc - high.astype(F32)).astype(BF16)]
+
+
+def margin_shift(g, index):
+    margin = g.margin(1)
+    base = g.half_side + PAD + 2 * margin * index
+    return base, (margin + base) % g.side
 
 
 def lend(g, fine, coarse, out):
     rows, less = lent_rows(g)
-    side, margin = g.side, g.margin(1)
+    side = g.side
     lane = lane_ids(side)
+    place = [0]
+
+    def put(value):
+        size = value.shape[0]
+        out[pl.ds(place[0], size), :] = value.astype(BF16)
+        place[0] += size
 
     def block(level, k, size):
         here = pl.ds(0, size)
-        return (
+        return [
             level.right[0, k, here, :],
             level.right[1, k, here, :],
             level.fric[k, here, :],
-            level.visc[k, pl.ds(PAD, size), :],
-        )
-
-    planes = lent_planes(block(fine, 0, rows))
-    for index, value in enumerate(planes):
-        out[pl.ds(index * rows, rows), :] = value
-    first = len(planes) * rows
-    for index, value in enumerate(lent_planes(block(coarse, 0, less))):
-        out[pl.ds(first + index * less, less), :] = value
-    first += len(planes) * less
+            *pair_of(level.visc[k, pl.ds(PAD, size), :]),
+        ]
+
+    put(fine.fric[0, pl.ds(0, rows), :])
+    for value in pair_of(fine.visc[0, pl.ds(PAD, rows), :]):
+        put(value)
+    for comp in range(2):
+        for first in lent_forcing(g):
+            put(fine.right[comp, 0, pl.ds(first, 16), :])
     total = jnp.zeros((rows, side), F32)
-    for index, value in enumerate(lent_planes(block(fine, 1, rows))):
-        base = 2 * margin * index
-        value = pltpu.roll(value.astype(F32), margin + base, 1)
-        total = jnp.where((lane >= base) & (lane < base + 2 * margin), value, total)
-    out[pl.ds(first, rows), :] = total.astype(BF16)
+    for index, value in enumerate(block(fine, 1, rows)):
+        base, shift = margin_shift(g, index)
+        value = pltpu.roll(value.astype(F32), shift, 1)
+        total = jnp.where((lane >= base) & (lane < base + 2 * g.margin(1)), value, total)
+    spare = (lane >= g.half_side + PAD) & (lane < side - PAD)
+    for index, value in enumerate(block(coarse, 0, less)):
+        value = value.astype(F32)
+        if index == 2:
+            value = jnp.where(spare, total[:less], value)
+        if index == 3:
+            more = rows - less
+            put(jnp.where(spare, total[less:], value[:more]))
+            value = value[more:]
+        put(value)
 
 
 def borrow(g, lent, limits, fine, coarse):
     rows, less = lent_rows(g)
-    side, margin = g.side, g.margin(1)
-
-    def put(level, number, k, size, values):
-        here = pl.ds(0, size)
-        ids = lax.broadcasted_iota(jnp.int32, (size, side), 0)
-        level.right[0, k, here, :] = values[0]
-        level.right[1, k, here, :] = values[1]
-        level.fric[k, here, :] = values[2]
-        level.visc[k, pl.ds(PAD, size), :] = jnp.where(
-            ids < limits[number][k], values[3] + values[4], 0.0
-        )
-
-    def planes(first, size):
-        return [lent[pl.ds(first + index * size, size), :].astype(F32) for index in range(5)]
-
-    put(fine, 1, 0, rows, planes(0, rows))
-    put(coarse, 0, 0, less, planes(5 * rows, less))
-    packed = lent[pl.ds(5 * (rows + less), rows), :].astype(F32)
-    values = [pltpu.roll(packed, side - margin - 2 * margin * index, 1) for index in range(5)]
-    put(fine, 1, 1, rows, values)
+    side = g.side
+    place = [0]
+
+    def take(size):
+        value = lent[pl.ds(place[0], size), :].astype(F32)
+        place[0] += size
+        return value
+
+    def put_visc(level, number, k, first, value):
+        size = value.shape[0]
+        ids = first + lax.broadcasted_iota(jnp.int32, (size, side), 0)
+        level.visc[k, pl.ds(PAD + first, size), :] = jnp.where(ids < limits[number][k], value, 0.0)
+
+    fine.fric[0, pl.ds(0, rows), :] = take(rows)
+    high = take(rows)
+    put_visc(fine, 1, 0, 0, high + take(rows))
+    for comp in range(2):
+        fine.right[comp, 0] = jnp.zeros((rows, side), F32)
+        for first in lent_forcing(g):
+            fine.right[comp, 0, pl.ds(first, 16), :] = take(16)
+    planes = [take(less) for _ in range(5)]
+    for comp in range(2):
+        coarse.right[comp, 0] = planes[comp]
+    coarse.fric[0] = planes[2]
+    put_visc(coarse, 0, 0, 0, planes[3] + planes[4])
+    for first, packed in ((0, planes[2]), (less, planes[3][: rows - less])):
+        size = packed.shape[0]
+        here = pl.ds(first, size)
+        values = [pltpu.roll(packed, side - margin_shift(g, i)[1], 1) for i in range(5)]
+        for comp in range(2):
+            fine.right[comp, 1, here, :] = values[comp]
+        fine.fric[1, here, :] = values[2]
+        put_visc(fine, 1, 1, first, values[3] + values[4])
 
 
 def fill_pair(g, rows_ref, own, other, edge, levels, wanted, groups):
@@ -935,7 +1011,17 @@
     own = (force, visc, fric)
     other = tuple(moved(value, g, lambda p, l: (p, l ^ 1)) for value in own)
     (edge,) = run_kernel(
-        lambda *refs: edge_kernel(g, *refs), [(own, VM), (other, VM)], [(block, VM)], []
+        lambda *refs: first_edge_kernel(g, *refs),
+        [(own, pltpu.HBM)],
+        [(block, VM)],
+        [
+            pltpu.SemaphoreType.DMA((3 * g.slots,)),
+            tuple(vmem(value.shape, value.dtype) for value in own),
+        ],
+        FIRST_BYTES,
+    )
+    (edge,) = run_kernel(
+        lambda *refs: edge_kernel(g, *refs), [(edge, VM), (other, VM)], [(block, VM)], []
     )
     edge = moved(edge, g, lambda p, l: (p + (-1 if l % 2 else 1), l ^ 1))
 
@@ -963,7 +1049,7 @@
     upper, lent = run_kernel(
         lambda *refs: fill_kernel(g, *refs),
         given,
-        [(fields[top - 1 :], VM), (make((5 * (rows + less) + rows, side), BF16), VM)],
+        [(fields[top - 1 :], VM), (make((lent_size(g), side), BF16), VM)],
         [[low_scratch(level) for level in (0, 1)]],
     )
     lent = moved(lent, g, lambda p, l: (p, l + 2))

time: 37.1 us -> 34.1 us (0.919)
  waiting for transfers between devices: 9.59 us -> 6.37 us
  local copies, waits for them, and re-layouts: 3.05 us -> 0.94 us
  Pallas kernels: 14.1 us -> 16 us
  starting transfers between devices: 9.04 us -> 9.72 us
    ppermute x7, waiting for transfers between devices: 9.59 us -> 6.37 us  [moved(): return lax.ppermute(value, ('patch', 'level'), pairs)]
    unnamed x12, local copies, waits for them, and re-layouts: 3.05 us -> 0.94 us
    pallas_call x6 -> x7, Pallas kernels: 14.1 us -> 16 us  [run_kernel(): pl.pallas_call(kernel, out_shape=[leaf for leaves, _ in out_trees for lea...]
    ppermute x7, starting transfers between devices: 9.04 us -> 9.72 us  [moved(): return lax.ppermute(value, ('patch', 'level'), pairs)]
  transfers between devices with their start and end apart: 7 -> 7, of which waited for: 4 -> 4; matrix products, arithmetic and copies ran while one was open for 0% -> 0% of each run, Pallas kernels for 24% -> 33%
where the time goes in v5:
time: 34.1 us; the launch traced here: 33.8 us
  Pallas kernels  16 us (47%)
  starting transfers between devices  9.72 us (29%)
  waiting for transfers between devices  6.37 us (19%)
  local copies, waits for them, and re-layouts  0.94 us (3%)
  between operations  0.75 us (2%)
    pallas_call x7, Pallas kernels, run_kernel(): pl.pallas_call(kernel, out_shape=[leaf for leaves, _ in out_trees for lea...  16 us
    ppermute x7, starting transfers between devices, moved(): return lax.ppermute(value, ('patch', 'level'), pairs)  9.72 us
    ppermute x7, waiting for transfers between devices, moved(): return lax.ppermute(value, ('patch', 'level'), pairs)  6.37 us
    unnamed x12, local copies, waits for them, and re-layouts  0.94 us
  transfers between devices with their start and end apart: 7, of which 4 were waited for; matrix products, arithmetic and copies ran while one was open for 0% of the time, Pallas kernels for 33%

profile of v5, /device:TPU:21, one launch (start us, length us, event | category | flops | bytes accessed | tf_op | source)
XLA Modules:
  0.0 33.8 jit_solution(9752499774101387288)
XLA Ops:
  0.6 0.7 %collective-permute-start = (bf16[8,2,128,128]{3,2,1,0:T(8,128)(2,1)}, bf16[8,2,128,128]{3,2,1,0:T(8,128)(2,1)S(1)}, u32[]{:S(2)}, u32[]{:S(2)}) collective-permute-start(bf16[8,2,128,128]{3,2,1,0:T(8,128)(2,1)} %bitcast.6), channel_id=1, source_target_pairs={{0,1},{1,0},{2,3},{3,2},{4,5},{5,4},{6,7},{7,6},{8,9},{9,8},{10,11... | collective-permute-start | bytes 1572872 | tf_op jit(solution)/shard_map/ppermute | solution.py:992
  1.4 0.1 collective-permute-start.1
  1.5 0.4 %collective-permute-start.2 = (bf16[8,128,128]{2,1,0:T(8,128)(2,1)}, bf16[8,128,128]{2,1,0:T(8,128)(2,1)S(1)}, u32[]{:S(2)}, u32[]{:S(2)}) collective-permute-start(bf16[8,128,128]{2,1,0:T(8,128)(2,1)} %bitcast.14), channel_id=1, source_target_pairs={{0,1},{1,0},{2,3},{3,2},{4,5},{5,4},{6,7},{7,6},{8,9},{9,8},{10,11... | collective-permute-start | bytes 786440 | tf_op jit(solution)/shard_map/ppermute | solution.py:992
  1.9 0.0 copy-start.5
  1.9 2.2 %shard_map.68.refs_0_ = f32[128,128]{1,0:T(8,128)} custom-call(bf16[8,2,128,128]{3,2,1,0:T(8,128)(2,1)} %bitcast.7, f32[8,128,128]{2,1,0:T(8,128)} %bitcast.11, bf16[8,128,128]{2,1,0:T(8,128)(2,1)} %bitcast.15), custom_call_target="tpu_custom_call" | custom-call | tf_op jit(solution)/shard_map/pallas_call | solution.py:969
  4.1 0.0 copy-start
  4.1 0.0 copy-start.1
  4.1 0.0 copy-start.2
  4.1 0.1 collective-permute-done.2.refs_3_.refs_6_
  4.2 0.0 collective-permute-done.refs_1_.refs_4_
  4.2 0.0 collective-permute-done.1.refs_2_.refs_5_
  4.2 0.0 copy-start.4
  4.3 0.9 %copy-done.4 = f32[128,128]{1,0:T(8,128)S(1)} copy-done((f32[128,128]{1,0:T(8,128)S(1)}, f32[128,128]{1,0:T(8,128)}, u32[]{:S(2)}) %copy-start.4) | copy-done | bytes 65560
  5.2 0.4 %shard_map.69 = f32[128,128]{1,0:T(8,128)S(1)} custom-call(f32[128,128]{1,0:T(8,128)S(1)} %copy-done.4, bf16[8,2,128,128]{3,2,1,0:T(8,128)(2,1)S(1)} %collective-permute-done.refs_1_.refs_4_, f32[8,128,128]{2,1,0:T(8,128)S(1)} %collective-permute-done.1.refs_2_.refs_5_, bf16[8,128,128]{2,1,0:T(8,128)(2,1)S(1)} %collective-permute-done.2.refs_3_.refs_6_), custom_call_target="tpu_custom_call" | custom-call | tf_op jit(solution)/shard_map/pallas_call | solution.py:969
  5.6 2.2 %collective-permute-start.3 = (f32[128,128]{1,0:T(8,128)S(1)}, f32[128,128]{1,0:T(8,128)S(1)}, u32[]{:S(2)}, u32[]{:S(2)}) collective-permute-start(f32[128,128]{1,0:T(8,128)S(1)} %shard_map.69), channel_id=1, source_target_pairs={{0,5},{2,7},{4,9},{5,0},{6,11},{7,2},{8,13},{9,4},{10,15},{11,6},{... | collective-permute-start | bytes 196616 | tf_op jit(solution)/shard_map/ppermute | solution.py:992
  7.8 4.1 %collective-permute-done.3.refs_7_ = f32[128,128]{1,0:T(8,128)S(1)} collective-permute-done((f32[128,128]{1,0:T(8,128)S(1)}, f32[128,128]{1,0:T(8,128)S(1)}, u32[]{:S(2)}, u32[]{:S(2)}) %collective-permute-start.3) | collective-permute-done | bytes 65568 | tf_op jit(solution)/shard_map/ppermute | solution.py:992
  11.9 0.0 copy-done.5
  11.9 0.0 copy-done
  11.9 0.0 copy-done.1
  11.9 0.0 copy-done.2
  11.9 1.0 %shard_map.70 = (f32[3,272,128]{2,1,0:T(8,128)S(1)}, f32[2,3,256,128]{3,2,1,0:T(8,128)S(1)}, f32[3,256,128]{2,1,0:T(8,128)S(1)}, f32[5,144,128]{2,1,0:T(8,128)S(...) custom-call(s32[4,8]{1,0:T(4,128)S(1)} %copy-done.5, ...), custom_call_target="tpu_custom_call" | custom-call | tf_op jit(solution)/shard_map/pallas_call | solution.py:969
  12.9 2.9 %collective-permute-start.5 = (bf16[896,128]{1,0:T(8,128)(2,1)S(1)}, bf16[896,128]{1,0:T(8,128)(2,1)S(1)}, u32[]{:S(2)}, u32[]{:S(2)}) collective-permute-start(bf16[896,128]{1,0:T(8,128)(2,1)S(1)} %get-tuple-element.43), channel_id=1, source_target_pairs={{0,2},{1,3},{4,6},{5,7},{8,10},{9,11},{12,14},{13,15},{16,18},{17,... | collective-permute-start | bytes 688136 | tf_op jit(solution)/shard_map/ppermute | solution.py:992
  15.8 3.7 %shard_map.71 = (f32[3,128,128]{2,1,0:T(8,128)S(1)}, f32[2,1,1024,128]{3,2,1,0:T(8,128)S(1)}, f32[2,2,512,128]{3,2,1,0:T(8,128)S(1)}, f32[2,3,256,128]{3,2,1,0:T...) custom-call(s32[4,8]{1,0:T(4,128)S(1)} %copy-done.5, ...), custom_call_target="tpu_custom_call" | custom-call | tf_op jit(solution)/shard_map/pallas_call | solution.py:969
  19.4 1.3 %collective-permute-start.4 = (f32[3,128,128]{2,1,0:T(8,128)S(1)}, f32[3,128,128]{2,1,0:T(8,128)S(1)}, u32[]{:S(2)}, u32[]{:S(2)}) collective-permute-start(f32[3,128,128]{2,1,0:T(8,128)S(1)} %get-tuple-element.34.refs_1_), channel_id=1, source_target_pairs={{2,0},{3,1},{6,4},{7,5},{10,8},{11,9},{14,12},{15,13},{18,16},{19,... | collective-permute-start | bytes 589832 | tf_op jit(solution)/shard_map/ppermute | solution.py:992
  20.7 0.0 collective-permute-done.5.refs_2_
  20.8 5.2 %shard_map.72 = (f32[4,2,128,128]{3,2,1,0:T(8,128)S(1)}, f32[4,2,128,128]{3,2,1,0:T(8,128)S(1)}) custom-call(s32[4,8]{1,0:T(4,128)S(1)} %copy-done.5, f32[3,128,128]{2,1,0:T(8,128)S(1)} %get-tuple-element.34.refs_1_, bf16[896,128]{1,0:T(8,128)(2,1)S(1)} %collective-permute-done.5.refs_2_, f32[1,1040,128]{2,1,0:T(8,128)S(1)} %get-tuple-element.35.refs_3_.refs_2_, ...), custom_call_target="tpu_custom_call" | custom-call | tf_op jit(solution)/shard_map/pallas_call | solution.py:969
  26.0 0.6 %collective-permute-done.4.refs_1_ = f32[3,128,128]{2,1,0:T(8,128)S(1)} collective-permute-done((f32[3,128,128]{2,1,0:T(8,128)S(1)}, f32[3,128,128]{2,1,0:T(8,128)S(1)}, u32[]{:S(2)}, u32[]{:S(2)}) %collective-permute-start.4) | collective-permute-done | bytes 196640 | tf_op jit(solution)/shard_map/ppermute | solution.py:992
  26.6 0.0 copy-start.3
  26.6 2.3 %shard_map.73 = (f32[4,2,128,128]{3,2,1,0:T(8,128)S(1)}, f32[4,2,128,128]{3,2,1,0:T(8,128)S(1)}) custom-call(s32[4,8]{1,0:T(4,128)S(1)} %copy-done.5, f32[3,128,128]{2,1,0:T(8,128)S(1)} %collective-permute-done.4.refs_1_, f32[1,1040,128]{2,1,0:T(8,128)S(1)} %get-tuple-element.35.refs_3_.refs_2_, f32[2,1,1024,128]{3,2,1,0:T(8,128)S(1)} %get-tuple-element.36.refs_4_.refs_3_, ...), custom_call_target="tpu_custom_call" | custom-call | tf_op jit(solution)/shard_map/pallas_call | solution.py:969
  28.9 2.1 %collective-permute-start.6 = (f32[4,2,128,128]{3,2,1,0:T(8,128)S(1)}, f32[4,2,128,128]{3,2,1,0:T(8,128)S(1)}, u32[]{:S(2)}, u32[]{:S(2)}) collective-permute-start(f32[4,2,128,128]{3,2,1,0:T(8,128)S(1)} %get-tuple-element.51), channel_id=1, source_target_pairs={{0,1},{1,0},{2,3},{3,2},{4,5},{5,4},{6,7},{7,6},{8,9},{9,8},{10,11... | collective-permute-start | bytes 1572872 | tf_op jit(solution)/shard_map/ppermute | solution.py:992
  31.0 1.5 %collective-permute-done.6.refs_1_ = f32[4,2,128,128]{3,2,1,0:T(8,128)S(1)} collective-permute-done((f32[4,2,128,128]{3,2,1,0:T(8,128)S(1)}, f32[4,2,128,128]{3,2,1,0:T(8,128)S(1)}, u32[]{:S(2)}, u32[]{:S(2)}) %collective-permute-start.6) | collective-permute-done | bytes 524320 | tf_op jit(solution)/shard_map/ppermute | solution.py:992
  32.6 0.0 copy-done.3
  32.6 1.2 %shard_map.74 = (f32[8,2,128,128]{3,2,1,0:T(8,128)}, bf16[8,128,128]{2,1,0:T(8,128)(2,1)}) custom-call(f32[4,2,128,128]{3,2,1,0:T(8,128)S(1)} %get-tuple-element.50.refs_0_, f32[4,2,128,128]{3,2,1,0:T(8,128)S(1)} %collective-permute-done.6.refs_1_, bf16[8,2,128,128]{3,2,1,0:T(8,128)(2,1)S(1)} %bitcast.19, bf16[8,128,128]{2,1,0:T(8,128)(2,1)S(1)} %bitcast.18), custom_call_target="tpu_custom_call" | custom-call | tf_op jit(solution)/shard_map/pallas_call | solution.py:969
Async XLA Ops:
  0.6 3.6 %collective-permute-start = (bf16[8,2,128,128]{3,2,1,0:T(8,128)(2,1)}, bf16[8,2,128,128]{3,2,1,0:T(8,128)(2,1)S(1)}, u32[]{:S(2)}, u32[]{:S(2)}) collective-permute-start(bf16[8,2,128,128]{3,2,1,0:T(8,128)(2,1)} %bitcast.6), channel_id=1, source_target_pairs={{0,1},{1,0},{2,3},{3,2},{4,5},{5,4},{6,7},{7,6},{8,9},{9,8},{10,11... | collective-permute-start | bytes 1572872 | tf_op jit(solution)/shard_map/ppermute | solution.py:992
  1.4 2.9 %collective-permute-start.1 = (f32[8,128,128]{2,1,0:T(8,128)}, f32[8,128,128]{2,1,0:T(8,128)S(1)}, u32[]{:S(2)}, u32[]{:S(2)}) collective-permute-start(f32[8,128,128]{2,1,0:T(8,128)} %bitcast.10), channel_id=1, source_target_pairs={{0,1},{1,0},{2,3},{3,2},{4,5},{5,4},{6,7},{7,6},{8,9},{9,8},{10,11... | collective-permute-start | bytes 1572872 | tf_op jit(solution)/shard_map/ppermute | solution.py:992
  1.5 2.8 %collective-permute-start.2 = (bf16[8,128,128]{2,1,0:T(8,128)(2,1)}, bf16[8,128,128]{2,1,0:T(8,128)(2,1)S(1)}, u32[]{:S(2)}, u32[]{:S(2)}) collective-permute-start(bf16[8,128,128]{2,1,0:T(8,128)(2,1)} %bitcast.14), channel_id=1, source_target_pairs={{0,1},{1,0},{2,3},{3,2},{4,5},{5,4},{6,7},{7,6},{8,9},{9,8},{10,11... | collective-permute-start | bytes 786440 | tf_op jit(solution)/shard_map/ppermute | solution.py:992
  1.9 10.0 %copy-start.5 = (s32[4,8]{1,0:T(4,128)S(1)}, s32[4,8]{1,0:T(4,128)}, u32[]{:S(2)}) copy-start(s32[4,8]{1,0:T(4,128)} %refs_0_.7) | copy-start | bytes 388
  4.1 7.8 %copy-start = (bf16[1,8,2,128,128]{4,3,2,1,0:T(8,128)(2,1)S(1)}, bf16[1,8,2,128,128]{4,3,2,1,0:T(8,128)(2,1)}, u32[]{:S(2)}) copy-start(bf16[1,8,2,128,128]{4,3,2,1,0:T(8,128)(2,1)} %param.5) | copy-start | bytes 1572868
  4.1 7.8 %copy-start.1 = (f32[1,8,128,128]{3,2,1,0:T(8,128)S(1)}, f32[1,8,128,128]{3,2,1,0:T(8,128)}, u32[]{:S(2)}) copy-start(f32[1,8,128,128]{3,2,1,0:T(8,128)} %param.7) | copy-start | bytes 1572868
  4.1 7.8 %copy-start.2 = (bf16[1,8,128,128]{3,2,1,0:T(8,128)(2,1)S(1)}, bf16[1,8,128,128]{3,2,1,0:T(8,128)(2,1)}, u32[]{:S(2)}) copy-start(bf16[1,8,128,128]{3,2,1,0:T(8,128)(2,1)} %param.8) | copy-start | bytes 786436
  4.2 0.9 %copy-start.4 = (f32[128,128]{1,0:T(8,128)S(1)}, f32[128,128]{1,0:T(8,128)}, u32[]{:S(2)}) copy-start(f32[128,128]{1,0:T(8,128)} %shard_map.68.refs_0_) | copy-start | bytes 196612
  5.6 6.3 %collective-permute-start.3 = (f32[128,128]{1,0:T(8,128)S(1)}, f32[128,128]{1,0:T(8,128)S(1)}, u32[]{:S(2)}, u32[]{:S(2)}) collective-permute-start(f32[128,128]{1,0:T(8,128)S(1)} %shard_map.69), channel_id=1, source_target_pairs={{0,5},{2,7},{4,9},{5,0},{6,11},{7,2},{8,13},{9,4},{10,15},{11,6},{... | collective-permute-start | bytes 196616 | tf_op jit(solution)/shard_map/ppermute | solution.py:992
  12.9 7.8 %collective-permute-start.5 = (bf16[896,128]{1,0:T(8,128)(2,1)S(1)}, bf16[896,128]{1,0:T(8,128)(2,1)S(1)}, u32[]{:S(2)}, u32[]{:S(2)}) collective-permute-start(bf16[896,128]{1,0:T(8,128)(2,1)S(1)} %get-tuple-element.43), channel_id=1, source_target_pairs={{0,2},{1,3},{4,6},{5,7},{8,10},{9,11},{12,14},{13,15},{16,18},{17,... | collective-permute-start | bytes 688136 | tf_op jit(solution)/shard_map/ppermute | solution.py:992
  19.4 7.2 %collective-permute-start.4 = (f32[3,128,128]{2,1,0:T(8,128)S(1)}, f32[3,128,128]{2,1,0:T(8,128)S(1)}, u32[]{:S(2)}, u32[]{:S(2)}) collective-permute-start(f32[3,128,128]{2,1,0:T(8,128)S(1)} %get-tuple-element.34.refs_1_), channel_id=1, source_target_pairs={{2,0},{3,1},{6,4},{7,5},{10,8},{11,9},{14,12},{15,13},{18,16},{19,... | collective-permute-start | bytes 589832 | tf_op jit(solution)/shard_map/ppermute | solution.py:992
  26.6 5.9 %copy-start.3 = (bf16[1,8,2,128,128]{4,3,2,1,0:T(8,128)(2,1)S(1)}, bf16[1,8,2,128,128]{4,3,2,1,0:T(8,128)(2,1)}, u32[]{:S(2)}) copy-start(bf16[1,8,2,128,128]{4,3,2,1,0:T(8,128)(2,1)} %param.6) | copy-start | bytes 1572868
  28.9 3.6 %collective-permute-start.6 = (f32[4,2,128,128]{3,2,1,0:T(8,128)S(1)}, f32[4,2,128,128]{3,2,1,0:T(8,128)S(1)}, u32[]{:S(2)}, u32[]{:S(2)}) collective-permute-start(f32[4,2,128,128]{3,2,1,0:T(8,128)S(1)} %get-tuple-element.51), channel_id=1, source_target_pairs={{0,1},{1,0},{2,3},{3,2},{4,5},{5,4},{6,7},{7,6},{8,9},{9,8},{10,11... | collective-permute-start | bytes 1572872 | tf_op jit(solution)/shard_map/ppermute | solution.py:992

commit v6 on v5

--- a/solution.py
+++ b/solution.py
@@ -46,7 +46,7 @@
         return self.own(level) + (1 if level > 0 else 0)
 
     def chunk(self, level, rows):
-        size = 8 * max(1, 28 // self.blocks(level))
+        size = 8 * max(1, 56 // self.blocks(level))
         while rows % size or (rows % self.side == 0 and self.side % size):
             size -= 8
         return size
@@ -861,13 +861,13 @@
     side = g.side
     top = g.levels - 1
     odd = level_here % 2 == 1
-    for k in range(g.half_slots):
-        for comp in range(2):
-            mine[k, comp] = mine_in[k, comp]
-            theirs[k, comp] = theirs_in[k, comp]
 
     @pl.when(level_here < top - 1)
     def _():
+        for k in range(g.half_slots):
+            for comp in range(2):
+                mine[k, comp] = mine_in[k, comp]
+                theirs[k, comp] = theirs_in[k, comp]
         rows, _ = lent_rows(g)
         done = kept_rows(g)
         fine = merged(Level(filled[1].visc, kept[1].weight), scratch)
@@ -904,7 +904,7 @@
         pl.when(jnp.logical_not(odd))(lambda: write(theirs, mine))
 
 
-def join_kernel(g, mine, given, speed, fric, adjoint, gradient):
+def join_kernel(g, mine_up, given_up, mine_low, given_low, speed, fric, adjoint, gradient):
     level_here = lax.axis_index("level")
     lane = lane_ids(g.side)
 
@@ -915,6 +915,8 @@
         gradient[slot] = (-(fric[slot].astype(F32) * total)).astype(BF16)
 
     def join_level(level):
+        upper = level >= g.levels - 2
+        mine, given = (mine_up, given_up) if upper else (mine_low, given_low)
         if level == 0:
             for k in range(g.half_slots):
                 low = []
@@ -1087,7 +1089,7 @@
 
     low_both = array(1, rows, vmem, True, False)
     low_steps = dict(held=low_both, left=low_both, right=low_both, **step_arrays(g, 1, rows))
-    mine, theirs = run_kernel(
+    mine_up, theirs_up = run_kernel(
         lambda *refs: up_kernel(g, *refs),
         [(patch_rows, SM), (sums, VM), (lent, VM), (filled, VM), (kept, VM)],
         [(half, VM), (half, VM)],
@@ -1112,6 +1114,7 @@
             vmem(half.shape, F32),
         ],
     )
+    received_up = moved(theirs_up, g, lambda p, l: (p, l ^ 1 if l >= top - 1 else -1))
     mine, theirs = run_kernel(
         lambda *refs: low_kernel(g, *refs),
         [
@@ -1119,8 +1122,8 @@
             (sums_there, VM),
             (filled[:2], VM),
             (kept[:2], VM),
-            (mine, VM),
-            (theirs, VM),
+            (mine_up, VM),
+            (theirs_up, VM),
         ],
         [(half, VM), (half, VM)],
         [
@@ -1129,10 +1132,17 @@
             vmem((2, rows, side), F32),
         ],
     )
-    received = moved(theirs, g, lambda p, l: (p, l ^ 1))
+    received = moved(theirs, g, lambda p, l: (p, l ^ 1 if l < top - 1 else -1))
     adjoint, gradient = run_kernel(
         lambda *refs: join_kernel(g, *refs),
-        [(mine, VM), (received, VM), (speed, VM), (fric, VM)],
+        [
+            (mine_up, VM),
+            (received_up, VM),
+            (mine, VM),
+            (received, VM),
+            (speed, VM),
+            (fric, VM),
+        ],
         [
             (make((g.slots, 2, side, side), F32), VM),
             (make((g.slots, side, side), BF16), VM),

time: 34.1 us -> 35.1 us (1.029)
  starting transfers between devices: 9.72 us -> 12.3 us
  Pallas kernels: 16 us -> 14.7 us
    ppermute x7 -> x8, starting transfers between devices: 9.72 us -> 12.3 us  [moved(): return lax.ppermute(value, ('patch', 'level'), pairs)]
    pallas_call x7, Pallas kernels: 16 us -> 14.7 us  [run_kernel(): pl.pallas_call(kernel, out_shape=[leaf for leaves, _ in out_trees for lea...]
    ppermute x7 -> x8, waiting for transfers between devices: 6.37 us -> 6.11 us  [moved(): return lax.ppermute(value, ('patch', 'level'), pairs)]
  transfers between devices with their start and end apart: 7 -> 8, of which waited for: 4 -> 4; matrix products, arithmetic and copies ran while one was open for 0% -> 0% of each run, Pallas kernels for 33% -> 30%
where the time goes in v6:
time: 35.1 us; the launch traced here: 34.8 us
  Pallas kernels  14.7 us (42%)
  starting transfers between devices  12.3 us (35%)
  waiting for transfers between devices  6.11 us (17%)
  local copies, waits for them, and re-layouts  0.94 us (3%)
  between operations  0.77 us (2%)
    pallas_call x7, Pallas kernels, run_kernel(): pl.pallas_call(kernel, out_shape=[leaf for leaves, _ in out_trees for lea...  14.7 us
    ppermute x8, starting transfers between devices, moved(): return lax.ppermute(value, ('patch', 'level'), pairs)  12.3 us
    ppermute x8, waiting for transfers between devices, moved(): return lax.ppermute(value, ('patch', 'level'), pairs)  6.11 us
    unnamed x12, local copies, waits for them, and re-layouts  0.94 us
  transfers between devices with their start and end apart: 8, of which 4 were waited for; matrix products, arithmetic and copies ran while one was open for 0% of the time, Pallas kernels for 30%

profile of v6, /device:TPU:21, one launch (start us, length us, event | category | flops | bytes accessed | tf_op | source)
XLA Modules:
  0.0 34.8 jit_solution(4445601514481378192)
XLA Ops:
  0.6 0.7 %collective-permute-start = (bf16[8,2,128,128]{3,2,1,0:T(8,128)(2,1)}, bf16[8,2,128,128]{3,2,1,0:T(8,128)(2,1)S(1)}, u32[]{:S(2)}, u32[]{:S(2)}) collective-permute-start(bf16[8,2,128,128]{3,2,1,0:T(8,128)(2,1)} %bitcast.6), channel_id=1, source_target_pairs={{0,1},{1,0},{2,3},{3,2},{4,5},{5,4},{6,7},{7,6},{8,9},{9,8},{10,11... | collective-permute-start | bytes 1572872 | tf_op jit(solution)/shard_map/ppermute | solution.py:994
  1.4 0.1 collective-permute-start.1
  1.5 0.4 %collective-permute-start.2 = (bf16[8,128,128]{2,1,0:T(8,128)(2,1)}, bf16[8,128,128]{2,1,0:T(8,128)(2,1)S(1)}, u32[]{:S(2)}, u32[]{:S(2)}) collective-permute-start(bf16[8,128,128]{2,1,0:T(8,128)(2,1)} %bitcast.14), channel_id=1, source_target_pairs={{0,1},{1,0},{2,3},{3,2},{4,5},{5,4},{6,7},{7,6},{8,9},{9,8},{10,11... | collective-permute-start | bytes 786440 | tf_op jit(solution)/shard_map/ppermute | solution.py:994
  1.9 0.0 copy-start.5
  1.9 2.2 %shard_map.68.refs_0_ = f32[128,128]{1,0:T(8,128)} custom-call(bf16[8,2,128,128]{3,2,1,0:T(8,128)(2,1)} %bitcast.7, f32[8,128,128]{2,1,0:T(8,128)} %bitcast.11, bf16[8,128,128]{2,1,0:T(8,128)(2,1)} %bitcast.15), custom_call_target="tpu_custom_call" | custom-call | tf_op jit(solution)/shard_map/pallas_call | solution.py:971
  4.1 0.0 copy-start
  4.1 0.0 copy-start.1
  4.1 0.0 copy-start.2
  4.1 0.1 collective-permute-done.2.refs_3_.refs_6_
  4.2 0.0 collective-permute-done.refs_1_.refs_4_
  4.2 0.0 collective-permute-done.1.refs_2_.refs_5_
  4.2 0.0 copy-start.4
  4.3 0.9 %copy-done.4 = f32[128,128]{1,0:T(8,128)S(1)} copy-done((f32[128,128]{1,0:T(8,128)S(1)}, f32[128,128]{1,0:T(8,128)}, u32[]{:S(2)}) %copy-start.4) | copy-done | bytes 65560
  5.2 0.4 %shard_map.69 = f32[128,128]{1,0:T(8,128)S(1)} custom-call(f32[128,128]{1,0:T(8,128)S(1)} %copy-done.4, bf16[8,2,128,128]{3,2,1,0:T(8,128)(2,1)S(1)} %collective-permute-done.refs_1_.refs_4_, f32[8,128,128]{2,1,0:T(8,128)S(1)} %collective-permute-done.1.refs_2_.refs_5_, bf16[8,128,128]{2,1,0:T(8,128)(2,1)S(1)} %collective-permute-done.2.refs_3_.refs_6_), custom_call_target="tpu_custom_call" | custom-call | tf_op jit(solution)/shard_map/pallas_call | solution.py:971
  5.6 2.2 %collective-permute-start.3 = (f32[128,128]{1,0:T(8,128)S(1)}, f32[128,128]{1,0:T(8,128)S(1)}, u32[]{:S(2)}, u32[]{:S(2)}) collective-permute-start(f32[128,128]{1,0:T(8,128)S(1)} %shard_map.69), channel_id=1, source_target_pairs={{0,5},{2,7},{4,9},{5,0},{6,11},{7,2},{8,13},{9,4},{10,15},{11,6},{... | collective-permute-start | bytes 196616 | tf_op jit(solution)/shard_map/ppermute | solution.py:994
  7.8 4.1 %collective-permute-done.3.refs_7_ = f32[128,128]{1,0:T(8,128)S(1)} collective-permute-done((f32[128,128]{1,0:T(8,128)S(1)}, f32[128,128]{1,0:T(8,128)S(1)}, u32[]{:S(2)}, u32[]{:S(2)}) %collective-permute-start.3) | collective-permute-done | bytes 65568 | tf_op jit(solution)/shard_map/ppermute | solution.py:994
  11.9 0.0 copy-done.5
  11.9 0.0 copy-done
  11.9 0.0 copy-done.1
  11.9 0.0 copy-done.2
  11.9 1.0 %shard_map.70 = (f32[3,272,128]{2,1,0:T(8,128)S(1)}, f32[2,3,256,128]{3,2,1,0:T(8,128)S(1)}, f32[3,256,128]{2,1,0:T(8,128)S(1)}, f32[5,144,128]{2,1,0:T(8,128)S(...) custom-call(s32[4,8]{1,0:T(4,128)S(1)} %copy-done.5, ...), custom_call_target="tpu_custom_call" | custom-call | tf_op jit(solution)/shard_map/pallas_call | solution.py:971
  12.9 2.9 %collective-permute-start.4 = (bf16[896,128]{1,0:T(8,128)(2,1)S(1)}, bf16[896,128]{1,0:T(8,128)(2,1)S(1)}, u32[]{:S(2)}, u32[]{:S(2)}) collective-permute-start(bf16[896,128]{1,0:T(8,128)(2,1)S(1)} %get-tuple-element.35), channel_id=1, source_target_pairs={{0,2},{1,3},{4,6},{5,7},{8,10},{9,11},{12,14},{13,15},{16,18},{17,... | collective-permute-start | bytes 688136 | tf_op jit(solution)/shard_map/ppermute | solution.py:994
  15.8 3.3 %shard_map.71 = (f32[3,128,128]{2,1,0:T(8,128)S(1)}, f32[2,1,1024,128]{3,2,1,0:T(8,128)S(1)}, f32[2,2,512,128]{3,2,1,0:T(8,128)S(1)}, f32[2,3,256,128]{3,2,1,0:T...) custom-call(s32[4,8]{1,0:T(4,128)S(1)} %copy-done.5, ...), custom_call_target="tpu_custom_call" | custom-call | tf_op jit(solution)/shard_map/pallas_call | solution.py:971
  19.1 1.3 %collective-permute-start.6 = (f32[3,128,128]{2,1,0:T(8,128)S(1)}, f32[3,128,128]{2,1,0:T(8,128)S(1)}, u32[]{:S(2)}, u32[]{:S(2)}) collective-permute-start(f32[3,128,128]{2,1,0:T(8,128)S(1)} %get-tuple-element.34.refs_1_), channel_id=1, source_target_pairs={{2,0},{3,1},{6,4},{7,5},{10,8},{11,9},{14,12},{15,13},{18,16},{19,... | collective-permute-start | bytes 589832 | tf_op jit(solution)/shard_map/ppermute | solution.py:994
  20.4 0.0 collective-permute-done.4.refs_2_
  20.4 4.8 %shard_map.72 = (f32[4,2,128,128]{3,2,1,0:T(8,128)S(1)}, f32[4,2,128,128]{3,2,1,0:T(8,128)S(1)}) custom-call(s32[4,8]{1,0:T(4,128)S(1)} %copy-done.5, f32[3,128,128]{2,1,0:T(8,128)S(1)} %get-tuple-element.34.refs_1_, bf16[896,128]{1,0:T(8,128)(2,1)S(1)} %collective-permute-done.4.refs_2_, f32[1,1040,128]{2,1,0:T(8,128)S(1)} %get-tuple-element.36.refs_3_.refs_2_, ...), custom_call_target="tpu_custom_call" | custom-call | tf_op jit(solution)/shard_map/pallas_call | solution.py:971
  25.2 1.1 %collective-permute-done.6.refs_1_ = f32[3,128,128]{2,1,0:T(8,128)S(1)} collective-permute-done((f32[3,128,128]{2,1,0:T(8,128)S(1)}, f32[3,128,128]{2,1,0:T(8,128)S(1)}, u32[]{:S(2)}, u32[]{:S(2)}) %collective-permute-start.6) | collective-permute-done | bytes 196640 | tf_op jit(solution)/shard_map/ppermute | solution.py:994
  26.3 0.0 copy-start.3
  26.3 1.8 %shard_map.73 = (f32[4,2,128,128]{3,2,1,0:T(8,128)S(1)}, f32[4,2,128,128]{3,2,1,0:T(8,128)S(1)}) custom-call(s32[4,8]{1,0:T(4,128)S(1)} %copy-done.5, f32[3,128,128]{2,1,0:T(8,128)S(1)} %collective-permute-done.6.refs_1_, f32[1,1040,128]{2,1,0:T(8,128)S(1)} %get-tuple-element.36.refs_3_.refs_2_, f32[2,1,1024,128]{3,2,1,0:T(8,128)S(1)} %get-tuple-element.37.refs_4_.refs_3_, ...), custom_call_target="tpu_custom_call" | custom-call | tf_op jit(solution)/shard_map/pallas_call | solution.py:971
  28.1 3.9 %collective-permute-start.7 = (f32[4,2,128,128]{3,2,1,0:T(8,128)S(1)}, f32[4,2,128,128]{3,2,1,0:T(8,128)S(1)}, u32[]{:S(2)}, u32[]{:S(2)}) collective-permute-start(f32[4,2,128,128]{3,2,1,0:T(8,128)S(1)} %get-tuple-element.51), channel_id=1, source_target_pairs={{0,1},{1,0},{4,5},{5,4},{8,9},{9,8},{12,13},{13,12},{16,17},{17,16... | collective-permute-start | bytes 1572872 | tf_op jit(solution)/shard_map/ppermute | solution.py:994
  32.1 0.7 %collective-permute-start.5 = (f32[4,2,128,128]{3,2,1,0:T(8,128)S(1)}, f32[4,2,128,128]{3,2,1,0:T(8,128)S(1)}, u32[]{:S(2)}, u32[]{:S(2)}) collective-permute-start(f32[4,2,128,128]{3,2,1,0:T(8,128)S(1)} %get-tuple-element.49.refs_11_), channel_id=1, source_target_pairs={{2,3},{3,2},{6,7},{7,6},{10,11},{11,10},{14,15},{15,14},{18,19},{1... | collective-permute-start | bytes 1572872 | tf_op jit(solution)/shard_map/ppermute | solution.py:994
  32.8 0.8 %collective-permute-done.7.refs_3_ = f32[4,2,128,128]{3,2,1,0:T(8,128)S(1)} collective-permute-done((f32[4,2,128,128]{3,2,1,0:T(8,128)S(1)}, f32[4,2,128,128]{3,2,1,0:T(8,128)S(1)}, u32[]{:S(2)}, u32[]{:S(2)}) %collective-permute-start.7) | collective-permute-done | bytes 524320 | tf_op jit(solution)/shard_map/ppermute | solution.py:994
  33.6 0.0 collective-permute-done.5.refs_1_
  33.6 0.0 copy-done.3
  33.6 1.2 %shard_map.74 = (f32[8,2,128,128]{3,2,1,0:T(8,128)}, bf16[8,128,128]{2,1,0:T(8,128)(2,1)}) custom-call(f32[4,2,128,128]{3,2,1,0:T(8,128)S(1)} %get-tuple-element.48.refs_10_.refs_0_, f32[4,2,128,128]{3,2,1,0:T(8,128)S(1)} %collective-permute-done.5.refs_1_, f32[4,2,128,128]{3,2,1,0:T(8,128)S(1)} %get-tuple-element.50.refs_2_, ...), custom_call_target="tpu_custom_call" | custom-call | tf_op jit(solution)/shard_map/pallas_call | solution.py:971
Async XLA Ops:
  0.6 3.6 %collective-permute-start = (bf16[8,2,128,128]{3,2,1,0:T(8,128)(2,1)}, bf16[8,2,128,128]{3,2,1,0:T(8,128)(2,1)S(1)}, u32[]{:S(2)}, u32[]{:S(2)}) collective-permute-start(bf16[8,2,128,128]{3,2,1,0:T(8,128)(2,1)} %bitcast.6), channel_id=1, source_target_pairs={{0,1},{1,0},{2,3},{3,2},{4,5},{5,4},{6,7},{7,6},{8,9},{9,8},{10,11... | collective-permute-start | bytes 1572872 | tf_op jit(solution)/shard_map/ppermute | solution.py:994
  1.4 2.9 %collective-permute-start.1 = (f32[8,128,128]{2,1,0:T(8,128)}, f32[8,128,128]{2,1,0:T(8,128)S(1)}, u32[]{:S(2)}, u32[]{:S(2)}) collective-permute-start(f32[8,128,128]{2,1,0:T(8,128)} %bitcast.10), channel_id=1, source_target_pairs={{0,1},{1,0},{2,3},{3,2},{4,5},{5,4},{6,7},{7,6},{8,9},{9,8},{10,11... | collective-permute-start | bytes 1572872 | tf_op jit(solution)/shard_map/ppermute | solution.py:994
  1.5 2.8 %collective-permute-start.2 = (bf16[8,128,128]{2,1,0:T(8,128)(2,1)}, bf16[8,128,128]{2,1,0:T(8,128)(2,1)S(1)}, u32[]{:S(2)}, u32[]{:S(2)}) collective-permute-start(bf16[8,128,128]{2,1,0:T(8,128)(2,1)} %bitcast.14), channel_id=1, source_target_pairs={{0,1},{1,0},{2,3},{3,2},{4,5},{5,4},{6,7},{7,6},{8,9},{9,8},{10,11... | collective-permute-start | bytes 786440 | tf_op jit(solution)/shard_map/ppermute | solution.py:994
  1.9 10.0 %copy-start.5 = (s32[4,8]{1,0:T(4,128)S(1)}, s32[4,8]{1,0:T(4,128)}, u32[]{:S(2)}) copy-start(s32[4,8]{1,0:T(4,128)} %refs_0_.7) | copy-start | bytes 388
  4.1 7.8 %copy-start = (bf16[1,8,2,128,128]{4,3,2,1,0:T(8,128)(2,1)S(1)}, bf16[1,8,2,128,128]{4,3,2,1,0:T(8,128)(2,1)}, u32[]{:S(2)}) copy-start(bf16[1,8,2,128,128]{4,3,2,1,0:T(8,128)(2,1)} %param.5) | copy-start | bytes 1572868
  4.1 7.8 %copy-start.1 = (f32[1,8,128,128]{3,2,1,0:T(8,128)S(1)}, f32[1,8,128,128]{3,2,1,0:T(8,128)}, u32[]{:S(2)}) copy-start(f32[1,8,128,128]{3,2,1,0:T(8,128)} %param.7) | copy-start | bytes 1572868
  4.1 7.8 %copy-start.2 = (bf16[1,8,128,128]{3,2,1,0:T(8,128)(2,1)S(1)}, bf16[1,8,128,128]{3,2,1,0:T(8,128)(2,1)}, u32[]{:S(2)}) copy-start(bf16[1,8,128,128]{3,2,1,0:T(8,128)(2,1)} %param.8) | copy-start | bytes 786436
  4.2 0.9 %copy-start.4 = (f32[128,128]{1,0:T(8,128)S(1)}, f32[128,128]{1,0:T(8,128)}, u32[]{:S(2)}) copy-start(f32[128,128]{1,0:T(8,128)} %shard_map.68.refs_0_) | copy-start | bytes 196612
  5.6 6.3 %collective-permute-start.3 = (f32[128,128]{1,0:T(8,128)S(1)}, f32[128,128]{1,0:T(8,128)S(1)}, u32[]{:S(2)}, u32[]{:S(2)}) collective-permute-start(f32[128,128]{1,0:T(8,128)S(1)} %shard_map.69), channel_id=1, source_target_pairs={{0,5},{2,7},{4,9},{5,0},{6,11},{7,2},{8,13},{9,4},{10,15},{11,6},{... | collective-permute-start | bytes 196616 | tf_op jit(solution)/shard_map/ppermute | solution.py:994
  12.9 7.5 %collective-permute-start.4 = (bf16[896,128]{1,0:T(8,128)(2,1)S(1)}, bf16[896,128]{1,0:T(8,128)(2,1)S(1)}, u32[]{:S(2)}, u32[]{:S(2)}) collective-permute-start(bf16[896,128]{1,0:T(8,128)(2,1)S(1)} %get-tuple-element.35), channel_id=1, source_target_pairs={{0,2},{1,3},{4,6},{5,7},{8,10},{9,11},{12,14},{13,15},{16,18},{17,... | collective-permute-start | bytes 688136 | tf_op jit(solution)/shard_map/ppermute | solution.py:994
  19.1 7.2 %collective-permute-start.6 = (f32[3,128,128]{2,1,0:T(8,128)S(1)}, f32[3,128,128]{2,1,0:T(8,128)S(1)}, u32[]{:S(2)}, u32[]{:S(2)}) collective-permute-start(f32[3,128,128]{2,1,0:T(8,128)S(1)} %get-tuple-element.34.refs_1_), channel_id=1, source_target_pairs={{2,0},{3,1},{6,4},{7,5},{10,8},{11,9},{14,12},{15,13},{18,16},{19,... | collective-permute-start | bytes 589832 | tf_op jit(solution)/shard_map/ppermute | solution.py:994
  26.3 7.3 %copy-start.3 = (bf16[1,8,2,128,128]{4,3,2,1,0:T(8,128)(2,1)S(1)}, bf16[1,8,2,128,128]{4,3,2,1,0:T(8,128)(2,1)}, u32[]{:S(2)}) copy-start(bf16[1,8,2,128,128]{4,3,2,1,0:T(8,128)(2,1)} %param.6) | copy-start | bytes 1572868
  28.1 5.5 %collective-permute-start.7 = (f32[4,2,128,128]{3,2,1,0:T(8,128)S(1)}, f32[4,2,128,128]{3,2,1,0:T(8,128)S(1)}, u32[]{:S(2)}, u32[]{:S(2)}) collective-permute-start(f32[4,2,128,128]{3,2,1,0:T(8,128)S(1)} %get-tuple-element.51), channel_id=1, source_target_pairs={{0,1},{1,0},{4,5},{5,4},{8,9},{9,8},{12,13},{13,12},{16,17},{17,16... | collective-permute-start | bytes 1572872 | tf_op jit(solution)/shard_map/ppermute | solution.py:994
  32.1 1.5 %collective-permute-start.5 = (f32[4,2,128,128]{3,2,1,0:T(8,128)S(1)}, f32[4,2,128,128]{3,2,1,0:T(8,128)S(1)}, u32[]{:S(2)}, u32[]{:S(2)}) collective-permute-start(f32[4,2,128,128]{3,2,1,0:T(8,128)S(1)} %get-tuple-element.49.refs_11_), channel_id=1, source_target_pairs={{2,3},{3,2},{6,7},{7,6},{10,11},{11,10},{14,15},{15,14},{18,19},{1... | collective-permute-start | bytes 1572872 | tf_op jit(solution)/shard_map/ppermute | solution.py:994

commit v7 on v5

--- a/solution.py
+++ b/solution.py
@@ -46,7 +46,7 @@
         return self.own(level) + (1 if level > 0 else 0)
 
     def chunk(self, level, rows):
-        size = 8 * max(1, 28 // self.blocks(level))
+        size = 8 * max(1, 112 // self.blocks(level))
         while rows % size or (rows % self.side == 0 and self.side % size):
             size -= 8
         return size
@@ -166,9 +166,9 @@
     )
 
 
-def smooth_weights(g, level, d, limits, rows, from_zero):
+def smooth_weights(g, level, d, limits, start, stop, from_zero):
     count = g.blocks(level)
-    chunk = g.chunk(level, rows)
+    chunk = g.chunk(level, stop - start)
 
     def some_rows(row):
         here = pl.ds(row, 8)
@@ -195,9 +195,9 @@
 
     def body(row):
         for step in range(0, chunk, 8):
-            some_rows(row + step)
-
-    over_rows(rows, chunk, body)
+            some_rows(start + row + step)
+
+    over_rows(stop - start, chunk, body)
 
 
 def residual_step(g, level, d, start, stop):
@@ -657,13 +657,16 @@
     return -(-lent_rows(g)[1 - level] // g.side)
 
 
-def down_kernel(g, rows_ref, own, other, edge, upper, sums, kept, lower, edges, scratch):
+def down_kernel(
+    g, rows_ref, own, other, edge, upper, sums, kept, low_kept, lower, edges, scratch
+):
     level_here = lax.axis_index("level")
     patch = lax.axis_index("patch")
     side = g.side
     top = g.levels - 1
     odd = level_here % 2 == 1
     filled = [*lower, *upper]
+    kept = [*(Level(None, weight) for weight in low_kept), *kept]
     levels = [merged(merged(a, b), c) for a, b, c in zip(scratch, kept, filled)]
 
     def limits_of(level):
@@ -692,7 +695,7 @@
         for level in (top, top - 1):
             d = levels[level]
             clear_level(g, level, d)
-            smooth_weights(g, level, d, limits_of(level), g.rows(level), True)
+            smooth_weights(g, level, d, limits_of(level), 0, g.rows(level), True)
             residual_step(g, level, d, 0, g.rows(level))
             restrict_into(g, level, d, 0, g.rows(level), set_right if level == top else keep)
         sums[2] = joined_edges(g, edges[0], edges[1])
@@ -700,8 +703,8 @@
     @pl.when(level_here < top - 1)
     def _():
         fill_pair(g, rows_ref, own, other, edge, levels, (1, 0), g.patch_rows)
-        for level in (1, 0):
-            smooth_weights(g, level, levels[level], limits_of(level), g.rows(level), False)
+        for level, size in zip((1, 0), lent_rows(g)):
+            smooth_weights(g, level, levels[level], limits_of(level), 0, size, False)
 
 
 def bottom_levels(g, rows_ref, patch, odd, start, stop, fine, coarse, new_sums, store_fine):
@@ -745,14 +748,17 @@
 
 
 def up_kernel(
-    g, rows_ref, sums, lent, filled, kept, mine, theirs, edges, scratch, low, low_fine, low_coarse, finer, coarser
+    g, rows_ref, sums, lent, filled, kept, mine, theirs, own_rows, coarse_rows, edges, scratch, low, low_fine,
+    low_coarse, finer, coarser,
 ):
     level_here = lax.axis_index("level")
     patch = lax.axis_index("patch")
     side = g.side
     top = g.levels - 1
     odd = level_here % 2 == 1
-    levels = [merged(merged(a, b), c) for a, b, c in zip(scratch, kept, filled)]
+    levels = [merged(a, b) for a, b in zip(scratch, filled)]
+    for level in (top - 1, top):
+        levels[level] = merged(levels[level], kept[level - top + 1])
 
     def limits_of(level):
         return lane_limits(g, level, near_counts(g, rows_ref, level, patch, odd), side)
@@ -774,8 +780,8 @@
         clear_pads(low_fine.visc, [(k,) for k in range(g.blocks(1))])
         clear_pads(low_coarse.visc, [(k,) for k in range(g.blocks(0))])
         borrow(g, lent, limits, low_fine, low_coarse)
-        smooth_weights(g, 1, low_fine, limits[1], rows, False)
-        smooth_weights(g, 0, low_coarse, limits[0], less, False)
+        smooth_weights(g, 1, low_fine, limits[1], 0, rows, False)
+        smooth_weights(g, 0, low_coarse, limits[0], 0, less, False)
 
         def store_fine(comp, k, row, chunk, value):
             low[comp, k, pl.ds(row, chunk), :] = value
@@ -815,30 +821,21 @@
     def _():
         rows = g.rows(1)
         first = g.rows(2) // 2
-        fine, coarse = levels[1], levels[0]
+        fine, coarse = levels[1], levels[0]._replace(cells=coarse_rows)
+        smooth_weights(g, 1, fine, limits_of(1), first, rows, False)
+        smooth_weights(g, 0, coarse, limits_of(0), first // 2, g.rows(0), False)
 
         def store_fine(comp, k, row, chunk, value):
             if k == 0:
-                group, place = row // side, row % side
-                finer[group, comp, pl.ds(pl.multiple_of(place, 8), chunk), :] = value
+                own_rows[comp, pl.ds(row, chunk), :] = value
 
         bottom_levels(g, rows_ref, patch, odd, first, rows, fine, coarse, None, store_fine)
-        lane = lane_ids(side)
-        for comp in range(2):
-            for k in range(g.half_slots):
-                parts = []
-                for group in (k, k + g.half_slots):
-                    here = pl.ds(group * side, side)
-                    if group * side < rows // 2:
-                        parts.append(coarse.cells[comp, 0, here, :])
-                    else:
-                        parts.append(
-                            coarse.weight[comp, 0, here, :] * coarse.right[comp, 0, here, :]
-                        )
-                coarser[k, comp] = jnp.where(
-                    lane < g.half_side, parts[0], pltpu.roll(parts[1], g.half_side, 1)
+        for r in range(rows // 2 // side, g.patch_rows(0)):
+            here = pl.ds(r * side, side)
+            for comp in range(2):
+                coarse_rows[comp, 0, here, :] = (
+                    coarse.weight[comp, 0, here, :] * coarse.right[comp, 0, here, :]
                 )
-        hand_out()
 
 
 def level_sums(g, sums, weight):
@@ -854,31 +851,34 @@
 
 
 def low_kernel(
-    g, rows_ref, sums, filled, kept, mine_in, theirs_in, mine, theirs, scratch, low_coarse, own_rows
+    g, rows_ref, sums, filled, kept, mine_in, theirs_in, own_rows, coarse_rows, mine, theirs, scratch, low_coarse, near_rows
 ):
     level_here = lax.axis_index("level")
     patch = lax.axis_index("patch")
     side = g.side
     top = g.levels - 1
     odd = level_here % 2 == 1
-    for k in range(g.half_slots):
-        for comp in range(2):
-            mine[k, comp] = mine_in[k, comp]
-            theirs[k, comp] = theirs_in[k, comp]
+
+    @pl.when(level_here >= top - 1)
+    def _():
+        for k in range(g.half_slots):
+            for comp in range(2):
+                mine[k, comp] = mine_in[k, comp]
+                theirs[k, comp] = theirs_in[k, comp]
 
     @pl.when(level_here < top - 1)
     def _():
         rows, _ = lent_rows(g)
         done = kept_rows(g)
-        fine = merged(Level(filled[1].visc, kept[1].weight), scratch)
-        coarse = merged(Level(None, kept[0].weight, filled[0].right), low_coarse)
+        fine = merged(Level(filled[1].visc, kept[1]), scratch)
+        coarse = merged(Level(None, kept[0], filled[0].right), low_coarse)
         for comp in range(2):
             for k in range(g.blocks(1)):
                 fine.right[comp, k] = filled[1].right[comp, k, pl.ds(0, rows), :]
 
         def store_fine(comp, k, row, chunk, value):
             if k == 0:
-                own_rows[comp, pl.ds(row, chunk), :] = value
+                near_rows[comp, pl.ds(row, chunk), :] = value
 
         bottom_levels(
             g, rows_ref, patch, odd, 0, rows, fine, coarse,
@@ -887,18 +887,26 @@
         lane = lane_ids(side)
         size = rows // 2
         ids = lax.broadcasted_iota(jnp.int32, (size, side), 0)
-        ours = (ids < done // 2) & (lane < g.half_side)
+
+        def coarse_group(comp, r):
+            value = coarse_rows[comp, 0, pl.ds(r * side, side), :]
+            if r:
+                return value
+            near = coarse.cells[comp, 0, pl.ds(0, size), :]
+            near = jnp.where(ids < done // 2, near, value[:size])
+            return jnp.concatenate([near, value[size:]], axis=0)
 
         def write(first, second):
             for comp in range(2):
-                first[0, comp] = own_rows[comp, pl.ds(0, side), :]
-                first[1, comp, pl.ds(0, done - side), :] = own_rows[
+                first[0, comp] = near_rows[comp, pl.ds(0, side), :]
+                for r in range(1, g.patch_rows(1)):
+                    first[r, comp] = own_rows[comp, pl.ds(r * side, side), :]
+                first[1, comp, pl.ds(0, done - side), :] = near_rows[
                     comp, pl.ds(side, done - side), :
                 ]
-                here = pl.ds(0, size)
-                second[0, comp, here, :] = jnp.where(
-                    ours, coarse.cells[comp, 0, here, :], second[0, comp, here, :]
-                )
+                for k in range(g.half_slots):
+                    high = pltpu.roll(coarse_group(comp, k + g.half_slots), g.half_side, 1)
+                    second[k, comp] = jnp.where(lane < g.half_side, coarse_group(comp, k), high)
 
         pl.when(odd)(lambda: write(mine, theirs))
         pl.when(jnp.logical_not(odd))(lambda: write(theirs, mine))
@@ -1056,7 +1064,9 @@
 
     def kept_of(level):
         two = array(level, g.rows(level), make, True, False)
-        return Level(None, two, held=two if level >= top - 1 else None)
+        return Level(None, two, held=two)
+
+    low_weights = [array(0, less, make, True, False), array(1, rows, make, True, False)]
 
     def down_scratch(level):
         if level < top - 1:
@@ -1065,12 +1075,13 @@
         more = dict(right=both) if level < top else {}
         return Level(None, None, left=both, **more, **step_arrays(g, level, g.rows(level)))
 
-    sums, kept, lower = run_kernel(
+    sums, kept, low_kept, lower = run_kernel(
         lambda *refs: down_kernel(g, *refs),
         [*given, (upper, VM)],
         [
             (three, VM),
-            ([kept_of(level) for level in range(g.levels)], VM),
+            ([kept_of(level) for level in (top - 1, top)], VM),
+            (low_weights, VM),
             (fields[: top - 1], VM),
         ],
         [vmem((2, side, side), F32), [down_scratch(level) for level in range(g.levels)]],
@@ -1079,18 +1090,25 @@
     sums_there = moved(sums, g, lambda p, l: (p, l - 2))
 
     def up_scratch(level):
+        both = array(level, g.rows(level), vmem, True, False)
         if level == 0:
-            return Level(None, None, cells=vmem((2, 1, g.rows(1) // 2, side), F32))
-        both = array(level, g.rows(level), vmem, True, False)
-        more = dict(held=both, left=both) if level == 1 else {}
-        return Level(None, None, **more, **step_arrays(g, level, g.rows(level)))
+            return Level(None, both)
+        steps = step_arrays(g, level, g.rows(level))
+        if level == 1:
+            return Level(None, both, held=both, left=both, **steps)
+        return Level(None, None, **steps)
 
     low_both = array(1, rows, vmem, True, False)
     low_steps = dict(held=low_both, left=low_both, right=low_both, **step_arrays(g, 1, rows))
-    mine, theirs = run_kernel(
+    mine, theirs, own_rows, coarse_rows = run_kernel(
         lambda *refs: up_kernel(g, *refs),
         [(patch_rows, SM), (sums, VM), (lent, VM), (filled, VM), (kept, VM)],
-        [(half, VM), (half, VM)],
+        [
+            (half, VM),
+            (half, VM),
+            (make((2, g.rows(1), side), F32), VM),
+            (make((2, 1, g.rows(0), side), F32), VM),
+        ],
         [
             array(top - 1, g.rows(top - 1), vmem, True, False),
             [up_scratch(level) for level in range(g.levels)],
@@ -1118,9 +1136,11 @@
             (patch_rows, SM),
             (sums_there, VM),
             (filled[:2], VM),
-            (kept[:2], VM),
+            (low_kept, VM),
             (mine, VM),
             (theirs, VM),
+            (own_rows, VM),
+            (coarse_rows, VM),
         ],
         [(half, VM), (half, VM)],
         [

time: 34.1 us -> 32.5 us (0.953)
  Pallas kernels: 16 us -> 14.3 us
  waiting for transfers between devices: 6.37 us -> 7.14 us
  starting transfers between devices: 9.72 us -> 9.05 us
    pallas_call x7, Pallas kernels: 16 us -> 14.3 us  [run_kernel(): pl.pallas_call(kernel, out_shape=[leaf for leaves, _ in out_trees for lea...]
    ppermute x7, waiting for transfers between devices: 6.37 us -> 7.14 us  [moved(): return lax.ppermute(value, ('patch', 'level'), pairs)]
    ppermute x7, starting transfers between devices: 9.72 us -> 9.05 us  [moved(): return lax.ppermute(value, ('patch', 'level'), pairs)]
  transfers between devices with their start and end apart: 7 -> 7, of which waited for: 4 -> 4; matrix products, arithmetic and copies ran while one was open for 0% -> 0% of each run, Pallas kernels for 33% -> 30%
where the time goes in v7:
time: 32.5 us; the launch traced here: 32.2 us
  Pallas kernels  14.3 us (44%)
  starting transfers between devices  9.05 us (28%)
  waiting for transfers between devices  7.14 us (22%)
  local copies, waits for them, and re-layouts  0.95 us (3%)
  between operations  0.76 us (2%)
    pallas_call x7, Pallas kernels, run_kernel(): pl.pallas_call(kernel, out_shape=[leaf for leaves, _ in out_trees for lea...  14.3 us
    ppermute x7, starting transfers between devices, moved(): return lax.ppermute(value, ('patch', 'level'), pairs)  9.05 us
    ppermute x7, waiting for transfers between devices, moved(): return lax.ppermute(value, ('patch', 'level'), pairs)  7.14 us
    unnamed x12, local copies, waits for them, and re-layouts  0.95 us
  transfers between devices with their start and end apart: 7, of which 4 were waited for; matrix products, arithmetic and copies ran while one was open for 0% of the time, Pallas kernels for 30%

profile of v7, /device:TPU:21, one launch (start us, length us, event | category | flops | bytes accessed | tf_op | source)
XLA Modules:
  0.0 32.2 jit_solution(1100408475902164504)
XLA Ops:
  0.6 0.7 %collective-permute-start = (bf16[8,2,128,128]{3,2,1,0:T(8,128)(2,1)}, bf16[8,2,128,128]{3,2,1,0:T(8,128)(2,1)S(1)}, u32[]{:S(2)}, u32[]{:S(2)}) collective-permute-start(bf16[8,2,128,128]{3,2,1,0:T(8,128)(2,1)} %bitcast.6), channel_id=1, source_target_pairs={{0,1},{1,0},{2,3},{3,2},{4,5},{5,4},{6,7},{7,6},{8,9},{9,8},{10,11... | collective-permute-start | bytes 1572872 | tf_op jit(solution)/shard_map/ppermute | solution.py:1000
  1.4 0.1 collective-permute-start.1
  1.5 0.4 %collective-permute-start.2 = (bf16[8,128,128]{2,1,0:T(8,128)(2,1)}, bf16[8,128,128]{2,1,0:T(8,128)(2,1)S(1)}, u32[]{:S(2)}, u32[]{:S(2)}) collective-permute-start(bf16[8,128,128]{2,1,0:T(8,128)(2,1)} %bitcast.14), channel_id=1, source_target_pairs={{0,1},{1,0},{2,3},{3,2},{4,5},{5,4},{6,7},{7,6},{8,9},{9,8},{10,11... | collective-permute-start | bytes 786440 | tf_op jit(solution)/shard_map/ppermute | solution.py:1000
  1.9 0.0 copy-start.5
  1.9 2.2 %shard_map.68.refs_0_ = f32[128,128]{1,0:T(8,128)} custom-call(bf16[8,2,128,128]{3,2,1,0:T(8,128)(2,1)} %bitcast.7, f32[8,128,128]{2,1,0:T(8,128)} %bitcast.11, bf16[8,128,128]{2,1,0:T(8,128)(2,1)} %bitcast.15), custom_call_target="tpu_custom_call" | custom-call | tf_op jit(solution)/shard_map/pallas_call | solution.py:977
  4.1 0.0 copy-start
  4.1 0.0 copy-start.1
  4.1 0.0 copy-start.2
  4.1 0.1 collective-permute-done.2.refs_3_.refs_6_
  4.2 0.0 collective-permute-done.refs_1_.refs_4_
  4.2 0.0 collective-permute-done.1.refs_2_.refs_5_
  4.2 0.0 copy-start.4
  4.3 0.9 %copy-done.4 = f32[128,128]{1,0:T(8,128)S(1)} copy-done((f32[128,128]{1,0:T(8,128)S(1)}, f32[128,128]{1,0:T(8,128)}, u32[]{:S(2)}) %copy-start.4) | copy-done | bytes 65560
  5.2 0.4 %shard_map.69 = f32[128,128]{1,0:T(8,128)S(1)} custom-call(f32[128,128]{1,0:T(8,128)S(1)} %copy-done.4, bf16[8,2,128,128]{3,2,1,0:T(8,128)(2,1)S(1)} %collective-permute-done.refs_1_.refs_4_, f32[8,128,128]{2,1,0:T(8,128)S(1)} %collective-permute-done.1.refs_2_.refs_5_, bf16[8,128,128]{2,1,0:T(8,128)(2,1)S(1)} %collective-permute-done.2.refs_3_.refs_6_), custom_call_target="tpu_custom_call" | custom-call | tf_op jit(solution)/shard_map/pallas_call | solution.py:977
  5.6 2.2 %collective-permute-start.3 = (f32[128,128]{1,0:T(8,128)S(1)}, f32[128,128]{1,0:T(8,128)S(1)}, u32[]{:S(2)}, u32[]{:S(2)}) collective-permute-start(f32[128,128]{1,0:T(8,128)S(1)} %shard_map.69), channel_id=1, source_target_pairs={{0,5},{2,7},{4,9},{5,0},{6,11},{7,2},{8,13},{9,4},{10,15},{11,6},{... | collective-permute-start | bytes 196616 | tf_op jit(solution)/shard_map/ppermute | solution.py:1000
  7.8 4.1 %collective-permute-done.3.refs_7_ = f32[128,128]{1,0:T(8,128)S(1)} collective-permute-done((f32[128,128]{1,0:T(8,128)S(1)}, f32[128,128]{1,0:T(8,128)S(1)}, u32[]{:S(2)}, u32[]{:S(2)}) %collective-permute-start.3) | collective-permute-done | bytes 65568 | tf_op jit(solution)/shard_map/ppermute | solution.py:1000
  11.9 0.0 copy-done.5
  11.9 0.0 copy-done
  11.9 0.0 copy-done.1
  11.9 0.0 copy-done.2
  11.9 1.0 %shard_map.70 = (f32[3,272,128]{2,1,0:T(8,128)S(1)}, f32[2,3,256,128]{3,2,1,0:T(8,128)S(1)}, f32[3,256,128]{2,1,0:T(8,128)S(1)}, f32[5,144,128]{2,1,0:T(8,128)S(...) custom-call(s32[4,8]{1,0:T(4,128)S(1)} %copy-done.5, ...), custom_call_target="tpu_custom_call" | custom-call | tf_op jit(solution)/shard_map/pallas_call | solution.py:977
  12.9 2.9 %collective-permute-start.5 = (bf16[896,128]{1,0:T(8,128)(2,1)S(1)}, bf16[896,128]{1,0:T(8,128)(2,1)S(1)}, u32[]{:S(2)}, u32[]{:S(2)}) collective-permute-start(bf16[896,128]{1,0:T(8,128)(2,1)S(1)} %get-tuple-element.45), channel_id=1, source_target_pairs={{0,2},{1,3},{4,6},{5,7},{8,10},{9,11},{12,14},{13,15},{16,18},{17,... | collective-permute-start | bytes 688136 | tf_op jit(solution)/shard_map/ppermute | solution.py:1000
  15.8 1.7 %shard_map.71 = (f32[3,128,128]{2,1,0:T(8,128)S(1)}, f32[2,3,256,128]{3,2,1,0:T(8,128)S(1)}, f32[2,3,256,128]{3,2,1,0:T(8,128)S(1)}, f32[2,5,128,128]{3,2,1,0:T(...) custom-call(s32[4,8]{1,0:T(4,128)S(1)} %copy-done.5, ...), custom_call_target="tpu_custom_call" | custom-call | tf_op jit(solution)/shard_map/pallas_call | solution.py:977
  17.5 1.3 %collective-permute-start.4 = (f32[3,128,128]{2,1,0:T(8,128)S(1)}, f32[3,128,128]{2,1,0:T(8,128)S(1)}, u32[]{:S(2)}, u32[]{:S(2)}) collective-permute-start(f32[3,128,128]{2,1,0:T(8,128)S(1)} %get-tuple-element.36.refs_1_), channel_id=1, source_target_pairs={{2,0},{3,1},{6,4},{7,5},{10,8},{11,9},{14,12},{15,13},{18,16},{19,... | collective-permute-start | bytes 589832 | tf_op jit(solution)/shard_map/ppermute | solution.py:1000
  18.8 1.4 %collective-permute-done.5.refs_2_ = bf16[896,128]{1,0:T(8,128)(2,1)S(1)} collective-permute-done((bf16[896,128]{1,0:T(8,128)(2,1)S(1)}, bf16[896,128]{1,0:T(8,128)(2,1)S(1)}, u32[]{:S(2)}, u32[]{:S(2)}) %collective-permute-start.5) | collective-permute-done | bytes 229408 | tf_op jit(solution)/shard_map/ppermute | solution.py:1000
  20.2 5.8 %shard_map.72 = (f32[4,2,128,128]{3,2,1,0:T(8,128)S(1)}, f32[4,2,128,128]{3,2,1,0:T(8,128)S(1)}, f32[2,512,128]{2,1,0:T(8,128)S(1)}, f32[2,1,1024,128]{3,2,1,0:T(8,128)S(1)}) custom-call(s32[4,8]{1,0:T(4,128)S(1)} %copy-done.5, f32[3,128,128]{2,1,0:T(8,128)S(1)} %get-tuple-element.36.refs_1_, bf16[896,128]{1,0:T(8,128)(2,1)S(1)} %collective-permute-done.5.refs_2_, ...), custom_call_target="tpu_custom_call" | custom-call | tf_op jit(solution)/shard_map/pallas_call | solution.py:977
  26.0 0.0 collective-permute-done.4.refs_1_
  26.0 0.0 copy-start.3
  26.0 2.0 %shard_map.73 = (f32[4,2,128,128]{3,2,1,0:T(8,128)S(1)}, f32[4,2,128,128]{3,2,1,0:T(8,128)S(1)}) custom-call(s32[4,8]{1,0:T(4,128)S(1)} %copy-done.5, f32[3,128,128]{2,1,0:T(8,128)S(1)} %collective-permute-done.4.refs_1_, f32[1,1040,128]{2,1,0:T(8,128)S(1)} %get-tuple-element.37.refs_3_.refs_2_, f32[2,1,1024,128]{3,2,1,0:T(8,128)S(1)} %get-tuple-element.38.refs_4_.refs_3_, ...), custom_call_target="tpu_custom_call" | custom-call | tf_op jit(solution)/shard_map/pallas_call | solution.py:977
  28.0 1.4 %collective-permute-start.6 = (f32[4,2,128,128]{3,2,1,0:T(8,128)S(1)}, f32[4,2,128,128]{3,2,1,0:T(8,128)S(1)}, u32[]{:S(2)}, u32[]{:S(2)}) collective-permute-start(f32[4,2,128,128]{3,2,1,0:T(8,128)S(1)} %get-tuple-element.55), channel_id=1, source_target_pairs={{0,1},{1,0},{2,3},{3,2},{4,5},{5,4},{6,7},{7,6},{8,9},{9,8},{10,11... | collective-permute-start | bytes 1572872 | tf_op jit(solution)/shard_map/ppermute | solution.py:1000
  29.4 1.5 %collective-permute-done.6.refs_1_ = f32[4,2,128,128]{3,2,1,0:T(8,128)S(1)} collective-permute-done((f32[4,2,128,128]{3,2,1,0:T(8,128)S(1)}, f32[4,2,128,128]{3,2,1,0:T(8,128)S(1)}, u32[]{:S(2)}, u32[]{:S(2)}) %collective-permute-start.6) | collective-permute-done | bytes 524320 | tf_op jit(solution)/shard_map/ppermute | solution.py:1000
  31.0 0.0 copy-done.3
  31.0 1.2 %shard_map.74 = (f32[8,2,128,128]{3,2,1,0:T(8,128)}, bf16[8,128,128]{2,1,0:T(8,128)(2,1)}) custom-call(f32[4,2,128,128]{3,2,1,0:T(8,128)S(1)} %get-tuple-element.54.refs_0_, f32[4,2,128,128]{3,2,1,0:T(8,128)S(1)} %collective-permute-done.6.refs_1_, bf16[8,2,128,128]{3,2,1,0:T(8,128)(2,1)S(1)} %bitcast.19, bf16[8,128,128]{2,1,0:T(8,128)(2,1)S(1)} %bitcast.18), custom_call_target="tpu_custom_call" | custom-call | tf_op jit(solution)/shard_map/pallas_call | solution.py:977
Async XLA Ops:
  0.6 3.6 %collective-permute-start = (bf16[8,2,128,128]{3,2,1,0:T(8,128)(2,1)}, bf16[8,2,128,128]{3,2,1,0:T(8,128)(2,1)S(1)}, u32[]{:S(2)}, u32[]{:S(2)}) collective-permute-start(bf16[8,2,128,128]{3,2,1,0:T(8,128)(2,1)} %bitcast.6), channel_id=1, source_target_pairs={{0,1},{1,0},{2,3},{3,2},{4,5},{5,4},{6,7},{7,6},{8,9},{9,8},{10,11... | collective-permute-start | bytes 1572872 | tf_op jit(solution)/shard_map/ppermute | solution.py:1000
  1.4 2.9 %collective-permute-start.1 = (f32[8,128,128]{2,1,0:T(8,128)}, f32[8,128,128]{2,1,0:T(8,128)S(1)}, u32[]{:S(2)}, u32[]{:S(2)}) collective-permute-start(f32[8,128,128]{2,1,0:T(8,128)} %bitcast.10), channel_id=1, source_target_pairs={{0,1},{1,0},{2,3},{3,2},{4,5},{5,4},{6,7},{7,6},{8,9},{9,8},{10,11... | collective-permute-start | bytes 1572872 | tf_op jit(solution)/shard_map/ppermute | solution.py:1000
  1.5 2.8 %collective-permute-start.2 = (bf16[8,128,128]{2,1,0:T(8,128)(2,1)}, bf16[8,128,128]{2,1,0:T(8,128)(2,1)S(1)}, u32[]{:S(2)}, u32[]{:S(2)}) collective-permute-start(bf16[8,128,128]{2,1,0:T(8,128)(2,1)} %bitcast.14), channel_id=1, source_target_pairs={{0,1},{1,0},{2,3},{3,2},{4,5},{5,4},{6,7},{7,6},{8,9},{9,8},{10,11... | collective-permute-start | bytes 786440 | tf_op jit(solution)/shard_map/ppermute | solution.py:1000
  1.9 10.0 %copy-start.5 = (s32[4,8]{1,0:T(4,128)S(1)}, s32[4,8]{1,0:T(4,128)}, u32[]{:S(2)}) copy-start(s32[4,8]{1,0:T(4,128)} %refs_0_.7) | copy-start | bytes 388
  4.1 7.8 %copy-start = (bf16[1,8,2,128,128]{4,3,2,1,0:T(8,128)(2,1)S(1)}, bf16[1,8,2,128,128]{4,3,2,1,0:T(8,128)(2,1)}, u32[]{:S(2)}) copy-start(bf16[1,8,2,128,128]{4,3,2,1,0:T(8,128)(2,1)} %param.5) | copy-start | bytes 1572868
  4.1 7.8 %copy-start.1 = (f32[1,8,128,128]{3,2,1,0:T(8,128)S(1)}, f32[1,8,128,128]{3,2,1,0:T(8,128)}, u32[]{:S(2)}) copy-start(f32[1,8,128,128]{3,2,1,0:T(8,128)} %param.7) | copy-start | bytes 1572868
  4.1 7.8 %copy-start.2 = (bf16[1,8,128,128]{3,2,1,0:T(8,128)(2,1)S(1)}, bf16[1,8,128,128]{3,2,1,0:T(8,128)(2,1)}, u32[]{:S(2)}) copy-start(bf16[1,8,128,128]{3,2,1,0:T(8,128)(2,1)} %param.8) | copy-start | bytes 786436
  4.2 0.9 %copy-start.4 = (f32[128,128]{1,0:T(8,128)S(1)}, f32[128,128]{1,0:T(8,128)}, u32[]{:S(2)}) copy-start(f32[128,128]{1,0:T(8,128)} %shard_map.68.refs_0_) | copy-start | bytes 196612
  5.6 6.3 %collective-permute-start.3 = (f32[128,128]{1,0:T(8,128)S(1)}, f32[128,128]{1,0:T(8,128)S(1)}, u32[]{:S(2)}, u32[]{:S(2)}) collective-permute-start(f32[128,128]{1,0:T(8,128)S(1)} %shard_map.69), channel_id=1, source_target_pairs={{0,5},{2,7},{4,9},{5,0},{6,11},{7,2},{8,13},{9,4},{10,15},{11,6},{... | collective-permute-start | bytes 196616 | tf_op jit(solution)/shard_map/ppermute | solution.py:1000
  12.9 7.3 %collective-permute-start.5 = (bf16[896,128]{1,0:T(8,128)(2,1)S(1)}, bf16[896,128]{1,0:T(8,128)(2,1)S(1)}, u32[]{:S(2)}, u32[]{:S(2)}) collective-permute-start(bf16[896,128]{1,0:T(8,128)(2,1)S(1)} %get-tuple-element.45), channel_id=1, source_target_pairs={{0,2},{1,3},{4,6},{5,7},{8,10},{9,11},{12,14},{13,15},{16,18},{17,... | collective-permute-start | bytes 688136 | tf_op jit(solution)/shard_map/ppermute | solution.py:1000
  17.5 8.5 %collective-permute-start.4 = (f32[3,128,128]{2,1,0:T(8,128)S(1)}, f32[3,128,128]{2,1,0:T(8,128)S(1)}, u32[]{:S(2)}, u32[]{:S(2)}) collective-permute-start(f32[3,128,128]{2,1,0:T(8,128)S(1)} %get-tuple-element.36.refs_1_), channel_id=1, source_target_pairs={{2,0},{3,1},{6,4},{7,5},{10,8},{11,9},{14,12},{15,13},{18,16},{19,... | collective-permute-start | bytes 589832 | tf_op jit(solution)/shard_map/ppermute | solution.py:1000
  26.0 5.0 %copy-start.3 = (bf16[1,8,2,128,128]{4,3,2,1,0:T(8,128)(2,1)S(1)}, bf16[1,8,2,128,128]{4,3,2,1,0:T(8,128)(2,1)}, u32[]{:S(2)}) copy-start(bf16[1,8,2,128,128]{4,3,2,1,0:T(8,128)(2,1)} %param.6) | copy-start | bytes 1572868
  28.0 3.0 %collective-permute-start.6 = (f32[4,2,128,128]{3,2,1,0:T(8,128)S(1)}, f32[4,2,128,128]{3,2,1,0:T(8,128)S(1)}, u32[]{:S(2)}, u32[]{:S(2)}) collective-permute-start(f32[4,2,128,128]{3,2,1,0:T(8,128)S(1)} %get-tuple-element.55), channel_id=1, source_target_pairs={{0,1},{1,0},{2,3},{3,2},{4,5},{5,4},{6,7},{7,6},{8,9},{9,8},{10,11... | collective-permute-start | bytes 1572872 | tf_op jit(solution)/shard_map/ppermute | solution.py:1000

commit v8 on v7

--- a/solution.py
+++ b/solution.py
@@ -522,7 +522,7 @@
 
 def lent_size(g):
     rows, less = lent_rows(g)
-    return 3 * rows + 2 * 16 * len(lent_forcing(g)) + 5 * less
+    return 4 * rows + 2 * 16 * len(lent_forcing(g)) + 2 * less + 16
 
 
 def pair_of(visc):
@@ -530,90 +530,176 @@
     return [high, (visc - high.astype(F32)).astype(BF16)]
 
 
-def margin_shift(g, index):
-    margin = g.margin(1)
-    base = g.half_side + PAD + 2 * margin * index
-    return base, (margin + base) % g.side
-
-
-def lend(g, fine, coarse, out):
+class Rows:
+    def __init__(self, ref):
+        self.ref = ref
+        self.place = 0
+
+    def put(self, value):
+        size = value.shape[0]
+        self.ref[pl.ds(self.place, size), :] = value.astype(BF16)
+        self.place += size
+
+    def take(self, size):
+        value = self.ref[pl.ds(self.place, size), :].astype(F32)
+        self.place += size
+        return value
+
+
+def side_by_side(g, low, high):
+    lane = lane_ids(g.side)
+    return jnp.where(
+        lane < g.half_side, low.astype(F32), pltpu.roll(high.astype(F32), g.half_side, 1)
+    )
+
+
+def lend(g, west_type, own, other, out):
+    rows, less = lent_rows(g)
+    side = g.side
+    fine, coarse = (own, other) if west_type else (other, own)
+    target = Rows(out)
+
+    def some_rows(raw, q, slot, first, size):
+        here = pl.ds(first, size)
+        force, visc, fric = raw
+        value = force[slot, q, here, :] if q < 2 else (fric if q == 2 else visc)[slot, here, :]
+        return 0.5 * value if q == 3 else value
+
+    def fine_rows(q, first, size, column=0 if west_type else g.own(1)):
+        parts = []
+        while size:
+            group, place = first // side, first % side
+            part = min(size, side - place)
+            slot = group * g.columns(1) + column
+            parts.append(some_rows(fine, q, slot, place, part))
+            first, size = first + part, size - part
+        return parts
+
+    for part in fine_rows(2, 0, rows):
+        target.put(part)
+    pairs = [pair_of(part) for part in fine_rows(3, 0, rows)]
+    for index in range(2):
+        for pair in pairs:
+            target.put(pair[index])
+    for comp in range(2):
+        for first in lent_forcing(g):
+            for part in fine_rows(comp, first, 16):
+                target.put(part)
+
+    def coarse_rows(q, first, size):
+        value = some_rows(coarse, q, 0, first, size).astype(F32)
+        return value if west_type else pltpu.roll(value, g.half_side, 1)
+
+    high, rest = pair_of(coarse_rows(3, 0, less))
+    target.put(side_by_side(g, coarse_rows(2, 0, less), high))
+    target.put(rest)
+    target.put(
+        side_by_side(g, coarse_rows(0, g.half_side, 16), coarse_rows(1, g.half_side, 16))
+    )
+    lane = lane_ids(side)
+
+    def inner(level, size):
+        column = g.own(1) if west_type else g.own(1) - 1
+        total = jnp.zeros((size, side), F32)
+        for q in range(4):
+            if level:
+                parts = fine_rows(q, 0, size, column)
+                value = jnp.concatenate([part.astype(F32) for part in parts], axis=0)
+            else:
+                value = coarse_rows(q, 0, size)
+            for offset, plane_value in enumerate(pair_of(value) if q == 3 else [value]):
+                place, target_lane = margin_moves(g, level, q + offset)[1 if west_type else 0]
+                shifted = pltpu.roll(plane_value.astype(F32), (target_lane - place) % side, 1)
+                here = (lane >= target_lane) & (lane < target_lane + g.margin(level))
+                total = jnp.where(here, shifted, total)
+        return total
+
+    fine_part = inner(1, rows)
+    target.put(fine_part[:less] + inner(0, less))
+    target.put(fine_part[less:])
+
+
+def margin_moves(g, level, index):
+    margin = g.margin(level)
+    base = 2 * margin * index + (0 if level else 2 * g.margin(1) * 5)
+    return (g.side - margin, base), ((0 if level else g.half_side), base + margin)
+
+
+def edges_of(g, level, west, east):
+    lane = lane_ids(g.side)
+    middle = g.side - g.half_side // 2 if level == 0 else g.half_side
+    return jnp.where(lane < middle, east, west)
+
+
+def borrow(g, rows_ref, patch, odd, lent, edge, limits, covered, fine, coarse):
     rows, less = lent_rows(g)
     side = g.side
     lane = lane_ids(side)
-    place = [0]
-
-    def put(value):
-        size = value.shape[0]
-        out[pl.ds(place[0], size), :] = value.astype(BF16)
-        place[0] += size
-
-    def block(level, k, size):
-        here = pl.ds(0, size)
-        return [
-            level.right[0, k, here, :],
-            level.right[1, k, here, :],
-            level.fric[k, here, :],
-            *pair_of(level.visc[k, pl.ds(PAD, size), :]),
-        ]
-
-    put(fine.fric[0, pl.ds(0, rows), :])
-    for value in pair_of(fine.visc[0, pl.ds(PAD, rows), :]):
-        put(value)
-    for comp in range(2):
-        for first in lent_forcing(g):
-            put(fine.right[comp, 0, pl.ds(first, 16), :])
-    total = jnp.zeros((rows, side), F32)
-    for index, value in enumerate(block(fine, 1, rows)):
-        base, shift = margin_shift(g, index)
-        value = pltpu.roll(value.astype(F32), shift, 1)
-        total = jnp.where((lane >= base) & (lane < base + 2 * g.margin(1)), value, total)
-    spare = (lane >= g.half_side + PAD) & (lane < side - PAD)
-    for index, value in enumerate(block(coarse, 0, less)):
-        value = value.astype(F32)
-        if index == 2:
-            value = jnp.where(spare, total[:less], value)
-        if index == 3:
-            more = rows - less
-            put(jnp.where(spare, total[less:], value[:more]))
-            value = value[more:]
-        put(value)
-
-
-def borrow(g, lent, limits, fine, coarse):
-    rows, less = lent_rows(g)
-    side = g.side
-    place = [0]
-
-    def take(size):
-        value = lent[pl.ds(place[0], size), :].astype(F32)
-        place[0] += size
-        return value
-
-    def put_visc(level, number, k, first, value):
-        size = value.shape[0]
-        ids = first + lax.broadcasted_iota(jnp.int32, (size, side), 0)
-        level.visc[k, pl.ds(PAD + first, size), :] = jnp.where(ids < limits[number][k], value, 0.0)
-
-    fine.fric[0, pl.ds(0, rows), :] = take(rows)
-    high = take(rows)
-    put_visc(fine, 1, 0, 0, high + take(rows))
+    source = Rows(lent)
+
+    def masked(value, bounds, inside):
+        ids = lax.broadcasted_iota(jnp.int32, value.shape, 0)
+        return jnp.where((ids < bounds) == inside, value, 0.0)
+
+    fine.fric[0] = source.take(rows)
+    high = source.take(rows)
+    fine.visc[0, pl.ds(PAD, rows), :] = masked(high + source.take(rows), limits[1][0], True)
     for comp in range(2):
         fine.right[comp, 0] = jnp.zeros((rows, side), F32)
         for first in lent_forcing(g):
-            fine.right[comp, 0, pl.ds(first, 16), :] = take(16)
-    planes = [take(less) for _ in range(5)]
+            value = masked(source.take(16), covered[0] - first, False)
+            fine.right[comp, 0, pl.ds(first, 16), :] = value
+    first, rest, window = source.take(less), source.take(less), source.take(16)
+    inner = source.take(rows)
+
+    def margins(level, q, size):
+        indices = (q,) if q < 3 else (3, 4)
+        moves = [margin_moves(g, level, index) for index in indices]
+
+        def one(west):
+            near = sum(
+                pltpu.roll(inner[:size], (places[0] - places[1]) % side, 1)
+                for places in (move[0 if west else 1] for move in moves)
+            )
+            far = []
+            for r in range(-(-size // side)):
+                part = edge[pl.ds(0, min(side, size - r * side)), :]
+                place = moves[0][0 if west else 1][0]
+                shift = (place - edge_lane(g, level, q, r)) % side
+                far.append(pltpu.roll(part, shift, 1) if shift else part)
+            far = jnp.concatenate(far, axis=0) if len(far) > 1 else far[0]
+            far = 0.5 * far if q == 3 else far
+            return near, far
+
+        (near_west, far_west), (near_east, far_east) = one(True), one(False)
+        return edges_of(
+            g, level, jnp.where(odd, far_west, near_west), jnp.where(odd, near_east, far_east)
+        )
+
     for comp in range(2):
-        coarse.right[comp, 0] = planes[comp]
-    coarse.fric[0] = planes[2]
-    put_visc(coarse, 0, 0, 0, planes[3] + planes[4])
-    for first, packed in ((0, planes[2]), (less, planes[3][: rows - less])):
-        size = packed.shape[0]
-        here = pl.ds(first, size)
-        values = [pltpu.roll(packed, side - margin_shift(g, i)[1], 1) for i in range(5)]
-        for comp in range(2):
-            fine.right[comp, 1, here, :] = values[comp]
-        fine.fric[1, here, :] = values[2]
-        put_visc(fine, 1, 1, first, values[3] + values[4])
+        fine.right[comp, 1] = masked(margins(1, comp, rows), covered[1], False)
+    fine.fric[1] = margins(1, 2, rows)
+    fine.visc[1, pl.ds(PAD, rows), :] = masked(margins(1, 3, rows), limits[1][1], True)
+
+    def with_margins(value, q):
+        return jnp.where(lane < g.half_side, value, margins(0, q, less))
+
+    coarse.fric[0] = with_margins(first, 2)
+    value = with_margins(pltpu.roll(first, g.half_side, 1) + rest, 3)
+    coarse.visc[0, pl.ds(PAD, less), :] = masked(value, limits[0][0], True)
+    for comp in range(2):
+        value = pltpu.roll(window, g.half_side, 1) if comp else window
+        value = jnp.concatenate([jnp.zeros((g.half_side, side), F32), value], axis=0)
+        coarse.right[comp, 0] = with_margins(value, comp)
+
+
+def lend_kernel(g, own, other, edge, lent):
+    level_here = lax.axis_index("level")
+    top = g.levels - 1
+    for level in range(top - 1):
+        pl.when(level_here == level)(
+            lambda level=level: lend(g, level % 2 == 1, own, other, lent)
+        )
 
 
 def fill_pair(g, rows_ref, own, other, edge, levels, wanted, groups):
@@ -638,7 +724,7 @@
                 )
 
 
-def fill_kernel(g, rows_ref, own, other, edge, filled, lent, low):
+def fill_kernel(g, rows_ref, own, other, edge, _, __, filled):
     level_here = lax.axis_index("level")
     top = g.levels - 1
 
@@ -646,15 +732,6 @@
     def _():
         levels = dict(zip((top - 1, top), filled))
         fill_pair(g, rows_ref, own, other, edge, levels, (top, top - 1), g.patch_rows)
-
-    @pl.when(level_here < top - 1)
-    def _():
-        fill_pair(g, rows_ref, own, other, edge, low, (1, 0), lambda level: low_groups(g, level))
-        lend(g, low[1], low[0], lent)
-
-
-def low_groups(g, level):
-    return -(-lent_rows(g)[1 - level] // g.side)
 
 
 def down_kernel(
@@ -748,7 +825,7 @@
 
 
 def up_kernel(
-    g, rows_ref, sums, lent, filled, kept, mine, theirs, own_rows, coarse_rows, edges, scratch, low, low_fine,
+    g, rows_ref, sums, lent, edge, filled, kept, mine, theirs, own_rows, coarse_rows, edges, scratch, low, low_fine,
     low_coarse, finer, coarser,
 ):
     level_here = lax.axis_index("level")
@@ -779,7 +856,9 @@
         limits = {level: limits_of(level) for level in (0, 1)}
         clear_pads(low_fine.visc, [(k,) for k in range(g.blocks(1))])
         clear_pads(low_coarse.visc, [(k,) for k in range(g.blocks(0))])
-        borrow(g, lent, limits, low_fine, low_coarse)
+        finer_near = near_counts(g, rows_ref, 2, patch, odd)
+        covered = lane_limits(g, 1, finer_near, g.half_side)
+        borrow(g, rows_ref, patch, odd, lent, edge, limits, covered, low_fine, low_coarse)
         smooth_weights(g, 1, low_fine, limits[1], 0, rows, False)
         smooth_weights(g, 0, low_coarse, limits[0], 0, less, False)
 
@@ -1031,7 +1110,17 @@
     (edge,) = run_kernel(
         lambda *refs: edge_kernel(g, *refs), [(edge, VM), (other, VM)], [(block, VM)], []
     )
-    edge = moved(edge, g, lambda p, l: (p + (-1 if l % 2 else 1), l ^ 1))
+    (lent_here,) = run_kernel(
+        lambda *refs: lend_kernel(g, *refs),
+        [(own, VM), (other, VM), (edge, VM)],
+        [(make((lent_size(g), side), BF16), VM)],
+        [],
+    )
+    edge_here = edge
+    step = lambda l: -1 if l % 2 else 1
+    edge = moved(edge_here, g, lambda p, l: (p + step(l), l ^ 1))
+    edge_low = moved(edge_here, g, lambda p, l: (p + step(l), (l ^ 1) + 2))
+    lent = moved(lent_here, g, lambda p, l: (p, l + 2))
 
     fields = [
         Level(
@@ -1045,22 +1134,12 @@
     rows, less = lent_rows(g)
     given = [(patch_rows, SM), (own, VM), (other, VM), (edge, VM)]
 
-    def low_scratch(level):
-        size = low_groups(g, level) * side
-        return Level(
-            array(level, size, vmem, False, True),
-            None,
-            right=array(level, size, vmem, True, False),
-            fric=array(level, size, vmem, False, False),
-        )
-
-    upper, lent = run_kernel(
+    (upper,) = run_kernel(
         lambda *refs: fill_kernel(g, *refs),
-        given,
-        [(fields[top - 1 :], VM), (make((lent_size(g), side), BF16), VM)],
-        [[low_scratch(level) for level in (0, 1)]],
-    )
-    lent = moved(lent, g, lambda p, l: (p, l + 2))
+        [*given, (edge_low, VM), (lent_here, VM)],
+        [(fields[top - 1 :], VM)],
+        [],
+    )
 
     def kept_of(level):
         two = array(level, g.rows(level), make, True, False)
@@ -1102,7 +1181,14 @@
     low_steps = dict(held=low_both, left=low_both, right=low_both, **step_arrays(g, 1, rows))
     mine, theirs, own_rows, coarse_rows = run_kernel(
         lambda *refs: up_kernel(g, *refs),
-        [(patch_rows, SM), (sums, VM), (lent, VM), (filled, VM), (kept, VM)],
+        [
+            (patch_rows, SM),
+            (sums, VM),
+            (lent, VM),
+            (edge_low, VM),
+            (filled, VM),
+            (kept, VM),
+        ],
         [
             (half, VM),
             (half, VM),

time: 32.5 us -> 33 us (1.015)
  starting transfers between devices: 9.05 us -> 11.3 us
  waiting for transfers between devices: 7.14 us -> 5.39 us
    ppermute x7 -> x8, starting transfers between devices: 9.05 us -> 11.3 us  [moved(): return lax.ppermute(value, ('patch', 'level'), pairs)]
    ppermute x7 -> x8, waiting for transfers between devices: 7.14 us -> 5.39 us  [moved(): return lax.ppermute(value, ('patch', 'level'), pairs)]
    pallas_call x7 -> x8, Pallas kernels: 14.3 us -> 14.1 us  [run_kernel(): pl.pallas_call(kernel, out_shape=[leaf for leaves, _ in out_trees for lea...]
  transfers between devices with their start and end apart: 7 -> 8, of which waited for: 4 -> 4; matrix products, arithmetic and copies ran while one was open for 0% -> 0% of each run, Pallas kernels for 30% -> 32%
where the time goes in v8:
time: 33 us; the launch traced here: 32.5 us
  Pallas kernels  14.1 us (43%)
  starting transfers between devices  11.3 us (34%)
  waiting for transfers between devices  5.39 us (16%)
  local copies, waits for them, and re-layouts  0.95 us (3%)
  between operations  0.79 us (2%)
    pallas_call x8, Pallas kernels, run_kernel(): pl.pallas_call(kernel, out_shape=[leaf for leaves, _ in out_trees for lea...  14.1 us
    ppermute x8, starting transfers between devices, moved(): return lax.ppermute(value, ('patch', 'level'), pairs)  11.3 us
    ppermute x8, waiting for transfers between devices, moved(): return lax.ppermute(value, ('patch', 'level'), pairs)  5.39 us
    unnamed x12, local copies, waits for them, and re-layouts  0.95 us
  transfers between devices with their start and end apart: 8, of which 4 were waited for; matrix products, arithmetic and copies ran while one was open for 0% of the time, Pallas kernels for 32%

profile of v8, /device:TPU:21, one launch (start us, length us, event | category | flops | bytes accessed | tf_op | source)
XLA Modules:
  0.0 32.5 jit_solution(12817432094386639019)
XLA Ops:
  0.6 0.7 %collective-permute-start = (bf16[8,2,128,128]{3,2,1,0:T(8,128)(2,1)}, bf16[8,2,128,128]{3,2,1,0:T(8,128)(2,1)S(1)}, u32[]{:S(2)}, u32[]{:S(2)}) collective-permute-start(bf16[8,2,128,128]{3,2,1,0:T(8,128)(2,1)} %bitcast.6), channel_id=1, source_target_pairs={{0,1},{1,0},{2,3},{3,2},{4,5},{5,4},{6,7},{7,6},{8,9},{9,8},{10,11... | collective-permute-start | bytes 1572872 | tf_op jit(solution)/shard_map/ppermute | solution.py:1079
  1.4 0.1 collective-permute-start.1
  1.5 0.4 %collective-permute-start.2 = (bf16[8,128,128]{2,1,0:T(8,128)(2,1)}, bf16[8,128,128]{2,1,0:T(8,128)(2,1)S(1)}, u32[]{:S(2)}, u32[]{:S(2)}) collective-permute-start(bf16[8,128,128]{2,1,0:T(8,128)(2,1)} %bitcast.16), channel_id=1, source_target_pairs={{0,1},{1,0},{2,3},{3,2},{4,5},{5,4},{6,7},{7,6},{8,9},{9,8},{10,11... | collective-permute-start | bytes 786440 | tf_op jit(solution)/shard_map/ppermute | solution.py:1079
  1.9 2.2 %shard_map.68.refs_0_ = f32[128,128]{1,0:T(8,128)} custom-call(bf16[8,2,128,128]{3,2,1,0:T(8,128)(2,1)} %bitcast.7, f32[8,128,128]{2,1,0:T(8,128)} %bitcast.12, bf16[8,128,128]{2,1,0:T(8,128)(2,1)} %bitcast.17), custom_call_target="tpu_custom_call" | custom-call | tf_op jit(solution)/shard_map/pallas_call | solution.py:1056
  4.1 0.0 copy-start
  4.1 0.0 copy-start.1
  4.1 0.0 copy-start.2
  4.1 0.1 collective-permute-done.2.refs_3_.refs_5_.refs_6_
  4.2 0.0 collective-permute-done.refs_1_.refs_3_.refs_4_
  4.2 0.0 collective-permute-done.1.refs_2_.refs_4_.refs_5_
  4.2 0.0 copy-start.4
  4.3 0.9 %copy-done.4 = f32[128,128]{1,0:T(8,128)S(1)} copy-done((f32[128,128]{1,0:T(8,128)S(1)}, f32[128,128]{1,0:T(8,128)}, u32[]{:S(2)}) %copy-start.4) | copy-done | bytes 65560
  5.2 0.4 %shard_map.69.refs_6_ = f32[128,128]{1,0:T(8,128)S(1)} custom-call(f32[128,128]{1,0:T(8,128)S(1)} %copy-done.4, bf16[8,2,128,128]{3,2,1,0:T(8,128)(2,1)S(1)} %collective-permute-done.refs_1_.refs_3_.refs_4_, f32[8,128,128]{2,1,0:T(8,128)S(1)} %collective-permute-done.1.refs_2_.refs_4_.refs_5_, ...), custom_call_target="tpu_custom_call" | custom-call | tf_op jit(solution)/shard_map/pallas_call | solution.py:1056
  5.6 0.0 copy-start.5
  5.6 2.9 %collective-permute-start.4 = (f32[128,128]{1,0:T(8,128)S(1)}, f32[128,128]{1,0:T(8,128)S(1)}, u32[]{:S(2)}, u32[]{:S(2)}) collective-permute-start(f32[128,128]{1,0:T(8,128)S(1)} %shard_map.69.refs_6_), channel_id=1, source_target_pairs={{0,7},{4,11},{5,2},{8,15},{9,6},{12,19},{13,10},{16,23},{17,14},{2... | collective-permute-start | bytes 196616 | tf_op jit(solution)/shard_map/ppermute | solution.py:1079
  8.6 3.2 %collective-permute-start.3 = (f32[128,128]{1,0:T(8,128)S(1)}, f32[128,128]{1,0:T(8,128)S(1)}, u32[]{:S(2)}, u32[]{:S(2)}) collective-permute-start(f32[128,128]{1,0:T(8,128)S(1)} %shard_map.69.refs_6_), channel_id=1, source_target_pairs={{0,5},{2,7},{4,9},{5,0},{6,11},{7,2},{8,13},{9,4},{10,15},{11,6},{... | collective-permute-start | bytes 196616 | tf_op jit(solution)/shard_map/ppermute | solution.py:1079
  11.8 0.0 copy-done
  11.8 0.0 copy-done.1
  11.8 0.0 copy-done.2
  11.8 0.2 shard_map.70.refs_9_
  12.0 1.3 %collective-permute-start.6 = (bf16[816,128]{1,0:T(8,128)(2,1)S(1)}, bf16[816,128]{1,0:T(8,128)(2,1)S(1)}, u32[]{:S(2)}, u32[]{:S(2)}) collective-permute-start(bf16[816,128]{1,0:T(8,128)(2,1)S(1)} %shard_map.70.refs_9_), channel_id=1, source_target_pairs={{0,2},{1,3},{4,6},{5,7},{8,10},{9,11},{12,14},{13,15},{16,18},{17,... | collective-permute-start | bytes 626696 | tf_op jit(solution)/shard_map/ppermute | solution.py:1079
  13.3 0.0 collective-permute-done.4.refs_8_.refs_3_
  13.3 0.8 %collective-permute-done.3.refs_7_ = f32[128,128]{1,0:T(8,128)S(1)} collective-permute-done((f32[128,128]{1,0:T(8,128)S(1)}, f32[128,128]{1,0:T(8,128)S(1)}, u32[]{:S(2)}, u32[]{:S(2)}) %collective-permute-start.3) | collective-permute-done | bytes 65568 | tf_op jit(solution)/shard_map/ppermute | solution.py:1079
  14.1 0.0 copy-done.5
  14.1 0.6 %shard_map.71 = (f32[3,272,128]{2,1,0:T(8,128)S(1)}, f32[2,3,256,128]{3,2,1,0:T(8,128)S(1)}, f32[3,256,128]{2,1,0:T(8,128)S(1)}, f32[5,144,128]{2,1,0:T(8,128)S(...) custom-call(s32[4,8]{1,0:T(4,128)S(1)} %copy-done.5, bf16[8,2,128,128]{3,2,1,0:T(8,128)(2,1)S(1)} %bitcast.9, ...), custom_call_target="tpu_custom_call" | custom-call | tf_op jit(solution)/shard_map/pallas_call | solution.py:1056
  14.7 1.7 %shard_map.72 = (f32[3,128,128]{2,1,0:T(8,128)S(1)}, f32[2,3,256,128]{3,2,1,0:T(8,128)S(1)}, f32[2,3,256,128]{3,2,1,0:T(8,128)S(1)}, f32[2,5,128,128]{3,2,1,0:T(...) custom-call(s32[4,8]{1,0:T(4,128)S(1)} %copy-done.5, ...), custom_call_target="tpu_custom_call" | custom-call | tf_op jit(solution)/shard_map/pallas_call | solution.py:1056
  16.4 1.3 %collective-permute-start.5 = (f32[3,128,128]{2,1,0:T(8,128)S(1)}, f32[3,128,128]{2,1,0:T(8,128)S(1)}, u32[]{:S(2)}, u32[]{:S(2)}) collective-permute-start(f32[3,128,128]{2,1,0:T(8,128)S(1)} %get-tuple-element.35.refs_1_), channel_id=1, source_target_pairs={{2,0},{3,1},{6,4},{7,5},{10,8},{11,9},{14,12},{15,13},{18,16},{19,... | collective-permute-start | bytes 589832 | tf_op jit(solution)/shard_map/ppermute | solution.py:1079
  17.7 0.0 collective-permute-done.6.refs_2_
  17.7 5.8 %shard_map.73 = (f32[4,2,128,128]{3,2,1,0:T(8,128)S(1)}, f32[4,2,128,128]{3,2,1,0:T(8,128)S(1)}, f32[2,512,128]{2,1,0:T(8,128)S(1)}, f32[2,1,1024,128]{3,2,1,0:T(8,128)S(1)}) custom-call(s32[4,8]{1,0:T(4,128)S(1)} %copy-done.5, f32[3,128,128]{2,1,0:T(8,128)S(1)} %get-tuple-element.35.refs_1_, bf16[816,128]{1,0:T(8,128)(2,1)S(1)} %collective-permute-done.6.refs_2_, ...), custom_call_target="tpu_custom_call" | custom-call | tf_op jit(solution)/shard_map/pallas_call | solution.py:1056
  23.6 2.9 %collective-permute-done.5.refs_1_ = f32[3,128,128]{2,1,0:T(8,128)S(1)} collective-permute-done((f32[3,128,128]{2,1,0:T(8,128)S(1)}, f32[3,128,128]{2,1,0:T(8,128)S(1)}, u32[]{:S(2)}, u32[]{:S(2)}) %collective-permute-start.5) | collective-permute-done | bytes 196640 | tf_op jit(solution)/shard_map/ppermute | solution.py:1079
  26.4 0.0 copy-start.3
  26.4 2.0 %shard_map.74 = (f32[4,2,128,128]{3,2,1,0:T(8,128)S(1)}, f32[4,2,128,128]{3,2,1,0:T(8,128)S(1)}) custom-call(s32[4,8]{1,0:T(4,128)S(1)} %copy-done.5, f32[3,128,128]{2,1,0:T(8,128)S(1)} %collective-permute-done.5.refs_1_, f32[1,1040,128]{2,1,0:T(8,128)S(1)} %get-tuple-element.36.refs_4_.refs_2_, f32[2,1,1024,128]{3,2,1,0:T(8,128)S(1)} %get-tuple-element.37.refs_5_.refs_3_, ...), custom_call_target="tpu_custom_call" | custom-call | tf_op jit(solution)/shard_map/pallas_call | solution.py:1056
  28.4 1.3 %collective-permute-start.7 = (f32[4,2,128,128]{3,2,1,0:T(8,128)S(1)}, f32[4,2,128,128]{3,2,1,0:T(8,128)S(1)}, u32[]{:S(2)}, u32[]{:S(2)}) collective-permute-start(f32[4,2,128,128]{3,2,1,0:T(8,128)S(1)} %get-tuple-element.53), channel_id=1, source_target_pairs={{0,1},{1,0},{2,3},{3,2},{4,5},{5,4},{6,7},{7,6},{8,9},{9,8},{10,11... | collective-permute-start | bytes 1572872 | tf_op jit(solution)/shard_map/ppermute | solution.py:1079
  29.7 1.5 %collective-permute-done.7.refs_1_ = f32[4,2,128,128]{3,2,1,0:T(8,128)S(1)} collective-permute-done((f32[4,2,128,128]{3,2,1,0:T(8,128)S(1)}, f32[4,2,128,128]{3,2,1,0:T(8,128)S(1)}, u32[]{:S(2)}, u32[]{:S(2)}) %collective-permute-start.7) | collective-permute-done | bytes 524320 | tf_op jit(solution)/shard_map/ppermute | solution.py:1079
  31.3 0.0 copy-done.3
  31.3 1.2 %shard_map.75 = (f32[8,2,128,128]{3,2,1,0:T(8,128)}, bf16[8,128,128]{2,1,0:T(8,128)(2,1)}) custom-call(f32[4,2,128,128]{3,2,1,0:T(8,128)S(1)} %get-tuple-element.52.refs_0_, f32[4,2,128,128]{3,2,1,0:T(8,128)S(1)} %collective-permute-done.7.refs_1_, bf16[8,2,128,128]{3,2,1,0:T(8,128)(2,1)S(1)} %bitcast.22, bf16[8,128,128]{2,1,0:T(8,128)(2,1)S(1)} %bitcast.21), custom_call_target="tpu_custom_call" | custom-call | tf_op jit(solution)/shard_map/pallas_call | solution.py:1056
Async XLA Ops:
  0.6 3.6 %collective-permute-start = (bf16[8,2,128,128]{3,2,1,0:T(8,128)(2,1)}, bf16[8,2,128,128]{3,2,1,0:T(8,128)(2,1)S(1)}, u32[]{:S(2)}, u32[]{:S(2)}) collective-permute-start(bf16[8,2,128,128]{3,2,1,0:T(8,128)(2,1)} %bitcast.6), channel_id=1, source_target_pairs={{0,1},{1,0},{2,3},{3,2},{4,5},{5,4},{6,7},{7,6},{8,9},{9,8},{10,11... | collective-permute-start | bytes 1572872 | tf_op jit(solution)/shard_map/ppermute | solution.py:1079
  1.4 2.9 %collective-permute-start.1 = (f32[8,128,128]{2,1,0:T(8,128)}, f32[8,128,128]{2,1,0:T(8,128)S(1)}, u32[]{:S(2)}, u32[]{:S(2)}) collective-permute-start(f32[8,128,128]{2,1,0:T(8,128)} %bitcast.11), channel_id=1, source_target_pairs={{0,1},{1,0},{2,3},{3,2},{4,5},{5,4},{6,7},{7,6},{8,9},{9,8},{10,11... | collective-permute-start | bytes 1572872 | tf_op jit(solution)/shard_map/ppermute | solution.py:1079
  1.5 2.8 %collective-permute-start.2 = (bf16[8,128,128]{2,1,0:T(8,128)(2,1)}, bf16[8,128,128]{2,1,0:T(8,128)(2,1)S(1)}, u32[]{:S(2)}, u32[]{:S(2)}) collective-permute-start(bf16[8,128,128]{2,1,0:T(8,128)(2,1)} %bitcast.16), channel_id=1, source_target_pairs={{0,1},{1,0},{2,3},{3,2},{4,5},{5,4},{6,7},{7,6},{8,9},{9,8},{10,11... | collective-permute-start | bytes 786440 | tf_op jit(solution)/shard_map/ppermute | solution.py:1079
  4.1 7.7 %copy-start = (bf16[1,8,2,128,128]{4,3,2,1,0:T(8,128)(2,1)S(1)}, bf16[1,8,2,128,128]{4,3,2,1,0:T(8,128)(2,1)}, u32[]{:S(2)}) copy-start(bf16[1,8,2,128,128]{4,3,2,1,0:T(8,128)(2,1)} %param.5) | copy-start | bytes 1572868
  4.1 7.7 %copy-start.1 = (f32[1,8,128,128]{3,2,1,0:T(8,128)S(1)}, f32[1,8,128,128]{3,2,1,0:T(8,128)}, u32[]{:S(2)}) copy-start(f32[1,8,128,128]{3,2,1,0:T(8,128)} %param.7) | copy-start | bytes 1572868
  4.1 7.7 %copy-start.2 = (bf16[1,8,128,128]{3,2,1,0:T(8,128)(2,1)S(1)}, bf16[1,8,128,128]{3,2,1,0:T(8,128)(2,1)}, u32[]{:S(2)}) copy-start(bf16[1,8,128,128]{3,2,1,0:T(8,128)(2,1)} %param.8) | copy-start | bytes 786436
  4.2 0.9 %copy-start.4 = (f32[128,128]{1,0:T(8,128)S(1)}, f32[128,128]{1,0:T(8,128)}, u32[]{:S(2)}) copy-start(f32[128,128]{1,0:T(8,128)} %shard_map.68.refs_0_) | copy-start | bytes 196612
  5.6 8.5 %copy-start.5 = (s32[4,8]{1,0:T(4,128)S(1)}, s32[4,8]{1,0:T(4,128)}, u32[]{:S(2)}) copy-start(s32[4,8]{1,0:T(4,128)} %refs_0_.7) | copy-start | bytes 388
  5.6 7.7 %collective-permute-start.4 = (f32[128,128]{1,0:T(8,128)S(1)}, f32[128,128]{1,0:T(8,128)S(1)}, u32[]{:S(2)}, u32[]{:S(2)}) collective-permute-start(f32[128,128]{1,0:T(8,128)S(1)} %shard_map.69.refs_6_), channel_id=1, source_target_pairs={{0,7},{4,11},{5,2},{8,15},{9,6},{12,19},{13,10},{16,23},{17,14},{2... | collective-permute-start | bytes 196616 | tf_op jit(solution)/shard_map/ppermute | solution.py:1079
  8.6 5.6 %collective-permute-start.3 = (f32[128,128]{1,0:T(8,128)S(1)}, f32[128,128]{1,0:T(8,128)S(1)}, u32[]{:S(2)}, u32[]{:S(2)}) collective-permute-start(f32[128,128]{1,0:T(8,128)S(1)} %shard_map.69.refs_6_), channel_id=1, source_target_pairs={{0,5},{2,7},{4,9},{5,0},{6,11},{7,2},{8,13},{9,4},{10,15},{11,6},{... | collective-permute-start | bytes 196616 | tf_op jit(solution)/shard_map/ppermute | solution.py:1079
  12.0 5.8 %collective-permute-start.6 = (bf16[816,128]{1,0:T(8,128)(2,1)S(1)}, bf16[816,128]{1,0:T(8,128)(2,1)S(1)}, u32[]{:S(2)}, u32[]{:S(2)}) collective-permute-start(bf16[816,128]{1,0:T(8,128)(2,1)S(1)} %shard_map.70.refs_9_), channel_id=1, source_target_pairs={{0,2},{1,3},{4,6},{5,7},{8,10},{9,11},{12,14},{13,15},{16,18},{17,... | collective-permute-start | bytes 626696 | tf_op jit(solution)/shard_map/ppermute | solution.py:1079
  16.4 10.0 %collective-permute-start.5 = (f32[3,128,128]{2,1,0:T(8,128)S(1)}, f32[3,128,128]{2,1,0:T(8,128)S(1)}, u32[]{:S(2)}, u32[]{:S(2)}) collective-permute-start(f32[3,128,128]{2,1,0:T(8,128)S(1)} %get-tuple-element.35.refs_1_), channel_id=1, source_target_pairs={{2,0},{3,1},{6,4},{7,5},{10,8},{11,9},{14,12},{15,13},{18,16},{19,... | collective-permute-start | bytes 589832 | tf_op jit(solution)/shard_map/ppermute | solution.py:1079
  26.4 4.8 %copy-start.3 = (bf16[1,8,2,128,128]{4,3,2,1,0:T(8,128)(2,1)S(1)}, bf16[1,8,2,128,128]{4,3,2,1,0:T(8,128)(2,1)}, u32[]{:S(2)}) copy-start(bf16[1,8,2,128,128]{4,3,2,1,0:T(8,128)(2,1)} %param.6) | copy-start | bytes 1572868
  28.4 2.8 %collective-permute-start.7 = (f32[4,2,128,128]{3,2,1,0:T(8,128)S(1)}, f32[4,2,128,128]{3,2,1,0:T(8,128)S(1)}, u32[]{:S(2)}, u32[]{:S(2)}) collective-permute-start(f32[4,2,128,128]{3,2,1,0:T(8,128)S(1)} %get-tuple-element.53), channel_id=1, source_target_pairs={{0,1},{1,0},{2,3},{3,2},{4,5},{5,4},{6,7},{7,6},{8,9},{9,8},{10,11... | collective-permute-start | bytes 1572872 | tf_op jit(solution)/shard_map/ppermute | solution.py:1079

commit v9 on v8

--- a/solution.py
+++ b/solution.py
@@ -324,11 +324,27 @@
     over_rows(rows // 2, chunk, body)
 
 
-def joined_edges(g, edge_u, edge_v):
+def sums_groups(g):
+    count = g.side // (4 * g.margin(1))
+    return count, g.rows(2) // 2 // count
+
+
+def sums_moves(g, group):
+    margin = g.margin(1)
+    base = 4 * margin * group
+    return (base + margin, base), (base + 3 * margin, base + 2 * margin)
+
+
+def packed_sums(g, edges):
     lane = lane_ids(g.side)
-    quarter = g.side // 4
-    middle = (lane >= quarter) & (lane < g.side - quarter)
-    return jnp.where(middle, pltpu.roll(edge_v, g.half_side, 1), edge_u)
+    count, size = sums_groups(g)
+    total = jnp.zeros((size, g.side), F32)
+    for group in range(count):
+        for comp, (shift, first) in enumerate(sums_moves(g, group)):
+            value = pltpu.roll(edges[comp, pl.ds(group * size, size), :], shift % g.side, 1)
+            inside = (lane >= first) & (lane < first + 2 * g.margin(1))
+            total = jnp.where(inside, value, total)
+    return total
 
 
 def plane(raw, q, slot):
@@ -754,6 +770,7 @@
         near = near_counts(g, rows_ref, top, patch, odd)
         covered = lane_limits(g, top - 1, near, g.half_side)
         given = filled[top - 1].right
+        reach = g.rows(2) // 2
         for comp in range(2):
             for k in range(g.blocks(top - 1)):
                 rest = pl.ds(g.half_side, g.rows(top - 1) - g.half_side)
@@ -767,7 +784,10 @@
             )
 
         def keep(comp, k, row, chunk, value):
-            (sums if k == 0 else edges)[comp, pl.ds(row, chunk), :] = value
+            if k == 0:
+                sums[pl.ds(comp * reach + row, chunk), :] = value
+            else:
+                edges[comp, pl.ds(row, chunk), :] = value
 
         for level in (top, top - 1):
             d = levels[level]
@@ -775,7 +795,8 @@
             smooth_weights(g, level, d, limits_of(level), 0, g.rows(level), True)
             residual_step(g, level, d, 0, g.rows(level))
             restrict_into(g, level, d, 0, g.rows(level), set_right if level == top else keep)
-        sums[2] = joined_edges(g, edges[0], edges[1])
+        packed = packed_sums(g, edges)
+        sums[pl.ds(2 * reach, packed.shape[0]), :] = packed
 
     @pl.when(level_here < top - 1)
     def _():
@@ -921,9 +942,14 @@
     reach = g.rows(2) // 2
 
     def value(comp, k):
-        found = sums[comp] if k == 0 else sums[2]
-        if k and comp:
-            found = pltpu.roll(found, g.half_side, 1)
+        if k == 0:
+            found = sums[pl.ds(comp * reach, reach), :]
+        else:
+            count, size = sums_groups(g)
+            packed = sums[pl.ds(2 * reach, size), :]
+            shifts = [sums_moves(g, group)[comp][0] for group in range(count)]
+            parts = [pltpu.roll(packed, -shift % g.side, 1) for shift in shifts]
+            found = jnp.concatenate(parts, axis=0)
         return jnp.where(weight[comp, k, pl.ds(0, reach), :] > 0.0, found, 0.0)
 
     return value
@@ -1090,7 +1116,7 @@
     vmem = pltpu.VMEM
     block = make((side, side), F32)
     half = make((g.half_slots, 2, side, side), F32)
-    three = make((3, side, side), F32)
+    sums_rows = g.rows(2) + sums_groups(g)[1]
 
     def array(level, rows, kind, comps, pad):
         return level_array(g, g.blocks(level), rows, kind, comps, pad)
@@ -1158,7 +1184,7 @@
         lambda *refs: down_kernel(g, *refs),
         [*given, (upper, VM)],
         [
-            (three, VM),
+            (make((sums_rows, side), F32), VM),
             ([kept_of(level) for level in (top - 1, top)], VM),
             (low_weights, VM),
             (fields[: top - 1], VM),

time: 33 us -> 34.1 us (1.033)
  the two profiles are of different devices: /device:TPU:21 before, /device:TPU:0 now
where the time goes in v9:
time: 34.1 us; the launch traced here: 33.9 us
  Pallas kernels  15 us (44%)
  starting transfers between devices  10.8 us (32%)
  waiting for transfers between devices  6.3 us (18%)
  local copies, waits for them, and re-layouts  0.97 us (3%)
  between operations  0.8 us (2%)
    pallas_call x8, Pallas kernels, run_kernel(): pl.pallas_call(kernel, out_shape=[leaf for leaves, _ in out_trees for lea...  15 us
    ppermute x8, starting transfers between devices, moved(): return lax.ppermute(value, ('patch', 'level'), pairs)  10.8 us
    ppermute x8, waiting for transfers between devices, moved(): return lax.ppermute(value, ('patch', 'level'), pairs)  6.3 us
    unnamed x12, local copies, waits for them, and re-layouts  0.97 us
  transfers between devices with their start and end apart: 8, of which 4 were waited for; matrix products, arithmetic and copies ran while one was open for 0% of the time, Pallas kernels for 32%

profile of v9, /device:TPU:0, one launch (start us, length us, event | category | flops | bytes accessed | tf_op | source)
XLA Modules:
  0.0 33.9 jit_solution(18278908442057380983)
XLA Ops:
  0.6 0.5 %collective-permute-start = (bf16[8,2,128,128]{3,2,1,0:T(8,128)(2,1)}, bf16[8,2,128,128]{3,2,1,0:T(8,128)(2,1)S(1)}, u32[]{:S(2)}, u32[]{:S(2)}) collective-permute-start(bf16[8,2,128,128]{3,2,1,0:T(8,128)(2,1)} %bitcast.6), channel_id=1, source_target_pairs={{0,1},{1,0},{2,3},{3,2},{4,5},{5,4},{6,7},{7,6},{8,9},{9,8},{10,11... | collective-permute-start | bytes 1572872 | tf_op jit(solution)/shard_map/ppermute | solution.py:1105
  1.1 0.1 collective-permute-start.1
  1.2 0.4 %collective-permute-start.2 = (bf16[8,128,128]{2,1,0:T(8,128)(2,1)}, bf16[8,128,128]{2,1,0:T(8,128)(2,1)S(1)}, u32[]{:S(2)}, u32[]{:S(2)}) collective-permute-start(bf16[8,128,128]{2,1,0:T(8,128)(2,1)} %bitcast.16), channel_id=1, source_target_pairs={{0,1},{1,0},{2,3},{3,2},{4,5},{5,4},{6,7},{7,6},{8,9},{9,8},{10,11... | collective-permute-start | bytes 786440 | tf_op jit(solution)/shard_map/ppermute | solution.py:1105
  1.7 2.5 %shard_map.68.refs_0_ = f32[128,128]{1,0:T(8,128)} custom-call(bf16[8,2,128,128]{3,2,1,0:T(8,128)(2,1)} %bitcast.7, f32[8,128,128]{2,1,0:T(8,128)} %bitcast.12, bf16[8,128,128]{2,1,0:T(8,128)(2,1)} %bitcast.17), custom_call_target="tpu_custom_call" | custom-call | tf_op jit(solution)/shard_map/pallas_call | solution.py:1082
  4.2 0.0 copy-start
  4.2 0.0 copy-start.1
  4.2 0.0 copy-start.2
  4.2 0.0 collective-permute-done.2.refs_3_.refs_5_.refs_6_
  4.2 0.0 collective-permute-done.refs_1_.refs_3_.refs_4_
  4.2 0.0 collective-permute-done.1.refs_2_.refs_4_.refs_5_
  4.2 0.0 copy-start.4
  4.3 0.9 %copy-done.4 = f32[128,128]{1,0:T(8,128)S(1)} copy-done((f32[128,128]{1,0:T(8,128)S(1)}, f32[128,128]{1,0:T(8,128)}, u32[]{:S(2)}) %copy-start.4) | copy-done | bytes 65560
  5.2 0.2 shard_map.69.refs_6_
  5.4 0.0 copy-done
  5.4 0.0 copy-done.1
  5.5 0.0 copy-done.2
  5.5 0.0 copy-start.5
  5.5 0.3 shard_map.70.refs_9_
  5.8 4.0 %collective-permute-start.6 = (bf16[816,128]{1,0:T(8,128)(2,1)S(1)}, bf16[816,128]{1,0:T(8,128)(2,1)S(1)}, u32[]{:S(2)}, u32[]{:S(2)}) collective-permute-start(bf16[816,128]{1,0:T(8,128)(2,1)S(1)} %shard_map.70.refs_9_), channel_id=1, source_target_pairs={{0,2},{1,3},{4,6},{5,7},{8,10},{9,11},{12,14},{13,15},{16,18},{17,... | collective-permute-start | bytes 626696 | tf_op jit(solution)/shard_map/ppermute | solution.py:1105
  9.8 2.0 %collective-permute-start.4 = (f32[128,128]{1,0:T(8,128)S(1)}, f32[128,128]{1,0:T(8,128)S(1)}, u32[]{:S(2)}, u32[]{:S(2)}) collective-permute-start(f32[128,128]{1,0:T(8,128)S(1)} %shard_map.69.refs_6_), channel_id=1, source_target_pairs={{0,7},{4,11},{5,2},{8,15},{9,6},{12,19},{13,10},{16,23},{17,14},{2... | collective-permute-start | bytes 196616 | tf_op jit(solution)/shard_map/ppermute | solution.py:1105
  11.9 2.4 %collective-permute-start.3 = (f32[128,128]{1,0:T(8,128)S(1)}, f32[128,128]{1,0:T(8,128)S(1)}, u32[]{:S(2)}, u32[]{:S(2)}) collective-permute-start(f32[128,128]{1,0:T(8,128)S(1)} %shard_map.69.refs_6_), channel_id=1, source_target_pairs={{0,5},{2,7},{4,9},{5,0},{6,11},{7,2},{8,13},{9,4},{10,15},{11,6},{... | collective-permute-start | bytes 196616 | tf_op jit(solution)/shard_map/ppermute | solution.py:1105
  14.2 1.7 %collective-permute-done.4.refs_8_.refs_3_ = f32[128,128]{1,0:T(8,128)S(1)} collective-permute-done((f32[128,128]{1,0:T(8,128)S(1)}, f32[128,128]{1,0:T(8,128)S(1)}, u32[]{:S(2)}, u32[]{:S(2)}) %collective-permute-start.4) | collective-permute-done | bytes 65568 | tf_op jit(solution)/shard_map/ppermute | solution.py:1105
  16.0 1.5 %collective-permute-done.3.refs_7_ = f32[128,128]{1,0:T(8,128)S(1)} collective-permute-done((f32[128,128]{1,0:T(8,128)S(1)}, f32[128,128]{1,0:T(8,128)S(1)}, u32[]{:S(2)}, u32[]{:S(2)}) %collective-permute-start.3) | collective-permute-done | bytes 65568 | tf_op jit(solution)/shard_map/ppermute | solution.py:1105
  17.5 0.0 copy-done.5
  17.5 0.6 %shard_map.71 = (f32[3,272,128]{2,1,0:T(8,128)S(1)}, f32[2,3,256,128]{3,2,1,0:T(8,128)S(1)}, f32[3,256,128]{2,1,0:T(8,128)S(1)}, f32[5,144,128]{2,1,0:T(8,128)S(...) custom-call(s32[4,8]{1,0:T(4,128)S(1)} %copy-done.5, bf16[8,2,128,128]{3,2,1,0:T(8,128)(2,1)S(1)} %bitcast.9, ...), custom_call_target="tpu_custom_call" | custom-call | tf_op jit(solution)/shard_map/pallas_call | solution.py:1082
  18.0 2.0 %shard_map.72 = (f32[272,128]{1,0:T(8,128)S(1)}, f32[2,3,256,128]{3,2,1,0:T(8,128)S(1)}, f32[2,3,256,128]{3,2,1,0:T(8,128)S(1)}, f32[2,5,128,128]{3,2,1,0:T(8,12...) custom-call(s32[4,8]{1,0:T(4,128)S(1)} %copy-done.5, ...), custom_call_target="tpu_custom_call" | custom-call | tf_op jit(solution)/shard_map/pallas_call | solution.py:1082
  20.1 1.3 %collective-permute-start.5 = (f32[272,128]{1,0:T(8,128)S(1)}, f32[272,128]{1,0:T(8,128)S(1)}, u32[]{:S(2)}, u32[]{:S(2)}) collective-permute-start(f32[272,128]{1,0:T(8,128)S(1)} %get-tuple-element.35.refs_1_), channel_id=1, source_target_pairs={{2,0},{3,1},{6,4},{7,5},{10,8},{11,9},{14,12},{15,13},{18,16},{19,... | collective-permute-start | bytes 417800 | tf_op jit(solution)/shard_map/ppermute | solution.py:1105
  21.4 0.0 collective-permute-done.6.refs_2_
  21.4 5.9 %shard_map.73 = (f32[4,2,128,128]{3,2,1,0:T(8,128)S(1)}, f32[4,2,128,128]{3,2,1,0:T(8,128)S(1)}, f32[2,512,128]{2,1,0:T(8,128)S(1)}, f32[2,1,1024,128]{3,2,1,0:T(8,128)S(1)}) custom-call(s32[4,8]{1,0:T(4,128)S(1)} %copy-done.5, f32[272,128]{1,0:T(8,128)S(1)} %get-tuple-element.35.refs_1_, bf16[816,128]{1,0:T(8,128)(2,1)S(1)} %collective-permute-done.6.refs_2_, ...), custom_call_target="tpu_custom_call" | custom-call | tf_op jit(solution)/shard_map/pallas_call | solution.py:1082
  27.2 1.2 %collective-permute-done.5.refs_1_ = f32[272,128]{1,0:T(8,128)S(1)} collective-permute-done((f32[272,128]{1,0:T(8,128)S(1)}, f32[272,128]{1,0:T(8,128)S(1)}, u32[]{:S(2)}, u32[]{:S(2)}) %collective-permute-start.5) | collective-permute-done | bytes 139296 | tf_op jit(solution)/shard_map/ppermute | solution.py:1105
  28.4 0.0 copy-start.3
  28.4 2.0 %shard_map.74 = (f32[4,2,128,128]{3,2,1,0:T(8,128)S(1)}, f32[4,2,128,128]{3,2,1,0:T(8,128)S(1)}) custom-call(s32[4,8]{1,0:T(4,128)S(1)} %copy-done.5, f32[272,128]{1,0:T(8,128)S(1)} %collective-permute-done.5.refs_1_, f32[1,1040,128]{2,1,0:T(8,128)S(1)} %get-tuple-element.36.refs_4_.refs_2_, f32[2,1,1024,128]{3,2,1,0:T(8,128)S(1)} %get-tuple-element.37.refs_5_.refs_3_, ...), custom_call_target="tpu_custom_call" | custom-call | tf_op jit(solution)/shard_map/pallas_call | solution.py:1082
  30.5 0.1 collective-permute-start.7
  30.5 1.9 %collective-permute-done.7.refs_1_ = f32[4,2,128,128]{3,2,1,0:T(8,128)S(1)} collective-permute-done((f32[4,2,128,128]{3,2,1,0:T(8,128)S(1)}, f32[4,2,128,128]{3,2,1,0:T(8,128)S(1)}, u32[]{:S(2)}, u32[]{:S(2)}) %collective-permute-start.7) | collective-permute-done | bytes 524320 | tf_op jit(solution)/shard_map/ppermute | solution.py:1105
  32.4 0.0 copy-done.3
  32.4 1.4 %shard_map.75 = (f32[8,2,128,128]{3,2,1,0:T(8,128)}, bf16[8,128,128]{2,1,0:T(8,128)(2,1)}) custom-call(f32[4,2,128,128]{3,2,1,0:T(8,128)S(1)} %get-tuple-element.52.refs_0_, f32[4,2,128,128]{3,2,1,0:T(8,128)S(1)} %collective-permute-done.7.refs_1_, bf16[8,2,128,128]{3,2,1,0:T(8,128)(2,1)S(1)} %bitcast.22, bf16[8,128,128]{2,1,0:T(8,128)(2,1)S(1)} %bitcast.21), custom_call_target="tpu_custom_call" | custom-call | tf_op jit(solution)/shard_map/pallas_call | solution.py:1082
Async XLA Ops:
  0.6 3.6 %collective-permute-start = (bf16[8,2,128,128]{3,2,1,0:T(8,128)(2,1)}, bf16[8,2,128,128]{3,2,1,0:T(8,128)(2,1)S(1)}, u32[]{:S(2)}, u32[]{:S(2)}) collective-permute-start(bf16[8,2,128,128]{3,2,1,0:T(8,128)(2,1)} %bitcast.6), channel_id=1, source_target_pairs={{0,1},{1,0},{2,3},{3,2},{4,5},{5,4},{6,7},{7,6},{8,9},{9,8},{10,11... | collective-permute-start | bytes 1572872 | tf_op jit(solution)/shard_map/ppermute | solution.py:1105
  1.1 3.1 %collective-permute-start.1 = (f32[8,128,128]{2,1,0:T(8,128)}, f32[8,128,128]{2,1,0:T(8,128)S(1)}, u32[]{:S(2)}, u32[]{:S(2)}) collective-permute-start(f32[8,128,128]{2,1,0:T(8,128)} %bitcast.11), channel_id=1, source_target_pairs={{0,1},{1,0},{2,3},{3,2},{4,5},{5,4},{6,7},{7,6},{8,9},{9,8},{10,11... | collective-permute-start | bytes 1572872 | tf_op jit(solution)/shard_map/ppermute | solution.py:1105
  1.2 3.0 %collective-permute-start.2 = (bf16[8,128,128]{2,1,0:T(8,128)(2,1)}, bf16[8,128,128]{2,1,0:T(8,128)(2,1)S(1)}, u32[]{:S(2)}, u32[]{:S(2)}) collective-permute-start(bf16[8,128,128]{2,1,0:T(8,128)(2,1)} %bitcast.16), channel_id=1, source_target_pairs={{0,1},{1,0},{2,3},{3,2},{4,5},{5,4},{6,7},{7,6},{8,9},{9,8},{10,11... | collective-permute-start | bytes 786440 | tf_op jit(solution)/shard_map/ppermute | solution.py:1105
  4.2 1.3 %copy-start = (bf16[1,8,2,128,128]{4,3,2,1,0:T(8,128)(2,1)S(1)}, bf16[1,8,2,128,128]{4,3,2,1,0:T(8,128)(2,1)}, u32[]{:S(2)}) copy-start(bf16[1,8,2,128,128]{4,3,2,1,0:T(8,128)(2,1)} %param.5) | copy-start | bytes 1572868
  4.2 1.3 %copy-start.1 = (f32[1,8,128,128]{3,2,1,0:T(8,128)S(1)}, f32[1,8,128,128]{3,2,1,0:T(8,128)}, u32[]{:S(2)}) copy-start(f32[1,8,128,128]{3,2,1,0:T(8,128)} %param.7) | copy-start | bytes 1572868
  4.2 1.3 %copy-start.2 = (bf16[1,8,128,128]{3,2,1,0:T(8,128)(2,1)S(1)}, bf16[1,8,128,128]{3,2,1,0:T(8,128)(2,1)}, u32[]{:S(2)}) copy-start(bf16[1,8,128,128]{3,2,1,0:T(8,128)(2,1)} %param.8) | copy-start | bytes 786436
  4.2 0.9 %copy-start.4 = (f32[128,128]{1,0:T(8,128)S(1)}, f32[128,128]{1,0:T(8,128)}, u32[]{:S(2)}) copy-start(f32[128,128]{1,0:T(8,128)} %shard_map.68.refs_0_) | copy-start | bytes 196612
  5.5 12.0 %copy-start.5 = (s32[4,8]{1,0:T(4,128)S(1)}, s32[4,8]{1,0:T(4,128)}, u32[]{:S(2)}) copy-start(s32[4,8]{1,0:T(4,128)} %refs_0_.7) | copy-start | bytes 388
  5.8 15.5 %collective-permute-start.6 = (bf16[816,128]{1,0:T(8,128)(2,1)S(1)}, bf16[816,128]{1,0:T(8,128)(2,1)S(1)}, u32[]{:S(2)}, u32[]{:S(2)}) collective-permute-start(bf16[816,128]{1,0:T(8,128)(2,1)S(1)} %shard_map.70.refs_9_), channel_id=1, source_target_pairs={{0,2},{1,3},{4,6},{5,7},{8,10},{9,11},{12,14},{13,15},{16,18},{17,... | collective-permute-start | bytes 626696 | tf_op jit(solution)/shard_map/ppermute | solution.py:1105
  9.8 6.1 %collective-permute-start.4 = (f32[128,128]{1,0:T(8,128)S(1)}, f32[128,128]{1,0:T(8,128)S(1)}, u32[]{:S(2)}, u32[]{:S(2)}) collective-permute-start(f32[128,128]{1,0:T(8,128)S(1)} %shard_map.69.refs_6_), channel_id=1, source_target_pairs={{0,7},{4,11},{5,2},{8,15},{9,6},{12,19},{13,10},{16,23},{17,14},{2... | collective-permute-start | bytes 196616 | tf_op jit(solution)/shard_map/ppermute | solution.py:1105
  11.9 5.6 %collective-permute-start.3 = (f32[128,128]{1,0:T(8,128)S(1)}, f32[128,128]{1,0:T(8,128)S(1)}, u32[]{:S(2)}, u32[]{:S(2)}) collective-permute-start(f32[128,128]{1,0:T(8,128)S(1)} %shard_map.69.refs_6_), channel_id=1, source_target_pairs={{0,5},{2,7},{4,9},{5,0},{6,11},{7,2},{8,13},{9,4},{10,15},{11,6},{... | collective-permute-start | bytes 196616 | tf_op jit(solution)/shard_map/ppermute | solution.py:1105
  20.1 8.4 %collective-permute-start.5 = (f32[272,128]{1,0:T(8,128)S(1)}, f32[272,128]{1,0:T(8,128)S(1)}, u32[]{:S(2)}, u32[]{:S(2)}) collective-permute-start(f32[272,128]{1,0:T(8,128)S(1)} %get-tuple-element.35.refs_1_), channel_id=1, source_target_pairs={{2,0},{3,1},{6,4},{7,5},{10,8},{11,9},{14,12},{15,13},{18,16},{19,... | collective-permute-start | bytes 417800 | tf_op jit(solution)/shard_map/ppermute | solution.py:1105
  28.4 4.0 %copy-start.3 = (bf16[1,8,2,128,128]{4,3,2,1,0:T(8,128)(2,1)S(1)}, bf16[1,8,2,128,128]{4,3,2,1,0:T(8,128)(2,1)}, u32[]{:S(2)}) copy-start(bf16[1,8,2,128,128]{4,3,2,1,0:T(8,128)(2,1)} %param.6) | copy-start | bytes 1572868
  30.5 2.0 %collective-permute-start.7 = (f32[4,2,128,128]{3,2,1,0:T(8,128)S(1)}, f32[4,2,128,128]{3,2,1,0:T(8,128)S(1)}, u32[]{:S(2)}, u32[]{:S(2)}) collective-permute-start(f32[4,2,128,128]{3,2,1,0:T(8,128)S(1)} %get-tuple-element.53), channel_id=1, source_target_pairs={{0,1},{1,0},{2,3},{3,2},{4,5},{5,4},{6,7},{7,6},{8,9},{9,8},{10,11... | collective-permute-start | bytes 1572872 | tf_op jit(solution)/shard_map/ppermute | solution.py:1105

commit v10 on v9

--- a/solution.py
+++ b/solution.py
@@ -569,7 +569,7 @@
     )
 
 
-def lend(g, west_type, own, other, out):
+def lend(g, west_type, own, other, edge, out):
     rows, less = lent_rows(g)
     side = g.side
     fine, coarse = (own, other) if west_type else (other, own)
@@ -614,24 +614,39 @@
     )
     lane = lane_ids(side)
 
-    def inner(level, size):
+    def outer_plane(level, q, size, place):
+        parts = []
+        for r in range(-(-size // side)):
+            part = edge[pl.ds(0, min(side, size - r * side)), :]
+            shift = (place - edge_lane(g, level, q, r)) % side
+            parts.append(pltpu.roll(part, shift, 1) if shift else part)
+        value = jnp.concatenate(parts, axis=0) if len(parts) > 1 else parts[0]
+        return 0.5 * value if q == 3 else value
+
+    def margins(level, size):
         column = g.own(1) if west_type else g.own(1) - 1
         total = jnp.zeros((size, side), F32)
         for q in range(4):
             if level:
                 parts = fine_rows(q, 0, size, column)
-                value = jnp.concatenate([part.astype(F32) for part in parts], axis=0)
+                inner = jnp.concatenate([part.astype(F32) for part in parts], axis=0)
             else:
-                value = coarse_rows(q, 0, size)
-            for offset, plane_value in enumerate(pair_of(value) if q == 3 else [value]):
-                place, target_lane = margin_moves(g, level, q + offset)[1 if west_type else 0]
-                shifted = pltpu.roll(plane_value.astype(F32), (target_lane - place) % side, 1)
-                here = (lane >= target_lane) & (lane < target_lane + g.margin(level))
-                total = jnp.where(here, shifted, total)
+                inner = coarse_rows(q, 0, size)
+            for west in (True, False):
+                if west == west_type:
+                    place = margin_moves(g, level, q)[0 if west else 1][0]
+                    value = outer_plane(level, q, size, place)
+                else:
+                    value = inner
+                for offset, part in enumerate(pair_of(value) if q == 3 else [value]):
+                    place, target_lane = margin_moves(g, level, q + offset)[0 if west else 1]
+                    shifted = pltpu.roll(part.astype(F32), (target_lane - place) % side, 1)
+                    here = (lane >= target_lane) & (lane < target_lane + g.margin(level))
+                    total = jnp.where(here, shifted, total)
         return total
 
-    fine_part = inner(1, rows)
-    target.put(fine_part[:less] + inner(0, less))
+    fine_part = margins(1, rows)
+    target.put(fine_part[:less] + margins(0, less))
     target.put(fine_part[less:])
 
 
@@ -647,7 +662,7 @@
     return jnp.where(lane < middle, east, west)
 
 
-def borrow(g, rows_ref, patch, odd, lent, edge, limits, covered, fine, coarse):
+def borrow(g, lent, limits, covered, fine, coarse):
     rows, less = lent_rows(g)
     side = g.side
     lane = lane_ids(side)
@@ -666,31 +681,18 @@
             value = masked(source.take(16), covered[0] - first, False)
             fine.right[comp, 0, pl.ds(first, 16), :] = value
     first, rest, window = source.take(less), source.take(less), source.take(16)
-    inner = source.take(rows)
+    packed = source.take(rows)
 
     def margins(level, q, size):
-        indices = (q,) if q < 3 else (3, 4)
-        moves = [margin_moves(g, level, index) for index in indices]
-
-        def one(west):
-            near = sum(
-                pltpu.roll(inner[:size], (places[0] - places[1]) % side, 1)
-                for places in (move[0 if west else 1] for move in moves)
+        moves = [margin_moves(g, level, index) for index in ((q,) if q < 3 else (3, 4))]
+        west, east = (
+            sum(
+                pltpu.roll(packed[:size], (move[at][0] - move[at][1]) % side, 1)
+                for move in moves
             )
-            far = []
-            for r in range(-(-size // side)):
-                part = edge[pl.ds(0, min(side, size - r * side)), :]
-                place = moves[0][0 if west else 1][0]
-                shift = (place - edge_lane(g, level, q, r)) % side
-                far.append(pltpu.roll(part, shift, 1) if shift else part)
-            far = jnp.concatenate(far, axis=0) if len(far) > 1 else far[0]
-            far = 0.5 * far if q == 3 else far
-            return near, far
-
-        (near_west, far_west), (near_east, far_east) = one(True), one(False)
-        return edges_of(
-            g, level, jnp.where(odd, far_west, near_west), jnp.where(odd, near_east, far_east)
+            for at in range(2)
         )
+        return edges_of(g, level, west, east)
 
     for comp in range(2):
         fine.right[comp, 1] = masked(margins(1, comp, rows), covered[1], False)
@@ -707,15 +709,6 @@
         value = pltpu.roll(window, g.half_side, 1) if comp else window
         value = jnp.concatenate([jnp.zeros((g.half_side, side), F32), value], axis=0)
         coarse.right[comp, 0] = with_margins(value, comp)
-
-
-def lend_kernel(g, own, other, edge, lent):
-    level_here = lax.axis_index("level")
-    top = g.levels - 1
-    for level in range(top - 1):
-        pl.when(level_here == level)(
-            lambda level=level: lend(g, level % 2 == 1, own, other, lent)
-        )
 
 
 def fill_pair(g, rows_ref, own, other, edge, levels, wanted, groups):
@@ -740,7 +733,7 @@
                 )
 
 
-def fill_kernel(g, rows_ref, own, other, edge, _, __, filled):
+def fill_kernel(g, rows_ref, own, other, edge, filled, lent):
     level_here = lax.axis_index("level")
     top = g.levels - 1
 
@@ -748,6 +741,11 @@
     def _():
         levels = dict(zip((top - 1, top), filled))
         fill_pair(g, rows_ref, own, other, edge, levels, (top, top - 1), g.patch_rows)
+
+    for level in range(top - 1):
+        pl.when(level_here == level)(
+            lambda level=level: lend(g, level % 2 == 1, own, other, edge, lent)
+        )
 
 
 def down_kernel(
@@ -846,7 +844,7 @@
 
 
 def up_kernel(
-    g, rows_ref, sums, lent, edge, filled, kept, mine, theirs, own_rows, coarse_rows, edges, scratch, low, low_fine,
+    g, rows_ref, sums, lent, filled, kept, mine, theirs, own_rows, coarse_rows, edges, scratch, low, low_fine,
     low_coarse, finer, coarser,
 ):
     level_here = lax.axis_index("level")
@@ -879,7 +877,7 @@
         clear_pads(low_coarse.visc, [(k,) for k in range(g.blocks(0))])
         finer_near = near_counts(g, rows_ref, 2, patch, odd)
         covered = lane_limits(g, 1, finer_near, g.half_side)
-        borrow(g, rows_ref, patch, odd, lent, edge, limits, covered, low_fine, low_coarse)
+        borrow(g, lent, limits, covered, low_fine, low_coarse)
         smooth_weights(g, 1, low_fine, limits[1], 0, rows, False)
         smooth_weights(g, 0, low_coarse, limits[0], 0, less, False)
 
@@ -1136,17 +1134,7 @@
     (edge,) = run_kernel(
         lambda *refs: edge_kernel(g, *refs), [(edge, VM), (other, VM)], [(block, VM)], []
     )
-    (lent_here,) = run_kernel(
-        lambda *refs: lend_kernel(g, *refs),
-        [(own, VM), (other, VM), (edge, VM)],
-        [(make((lent_size(g), side), BF16), VM)],
-        [],
-    )
-    edge_here = edge
-    step = lambda l: -1 if l % 2 else 1
-    edge = moved(edge_here, g, lambda p, l: (p + step(l), l ^ 1))
-    edge_low = moved(edge_here, g, lambda p, l: (p + step(l), (l ^ 1) + 2))
-    lent = moved(lent_here, g, lambda p, l: (p, l + 2))
+    edge = moved(edge, g, lambda p, l: (p + (-1 if l % 2 else 1), l ^ 1))
 
     fields = [
         Level(
@@ -1160,12 +1148,13 @@
     rows, less = lent_rows(g)
     given = [(patch_rows, SM), (own, VM), (other, VM), (edge, VM)]
 
-    (upper,) = run_kernel(
+    upper, lent = run_kernel(
         lambda *refs: fill_kernel(g, *refs),
-        [*given, (edge_low, VM), (lent_here, VM)],
-        [(fields[top - 1 :], VM)],
+        given,
+        [(fields[top - 1 :], VM), (make((lent_size(g), side), BF16), VM)],
         [],
     )
+    lent = moved(lent, g, lambda p, l: (p, l + 2))
 
     def kept_of(level):
         two = array(level, g.rows(level), make, True, False)
@@ -1211,7 +1200,6 @@
             (patch_rows, SM),
             (sums, VM),
             (lent, VM),
-            (edge_low, VM),
             (filled, VM),
             (kept, VM),
         ],

time: 34.1 us -> 32.1 us (0.941)
  the two profiles are of different devices: /device:TPU:0 before, /device:TPU:21 now
where the time goes in v10:
time: 32.1 us; the launch traced here: 31.9 us
  Pallas kernels  14.7 us (46%)
  starting transfers between devices  8.76 us (27%)
  waiting for transfers between devices  6.7 us (21%)
  local copies, waits for them, and re-layouts  0.95 us (3%)
  between operations  0.75 us (2%)
    pallas_call x7, Pallas kernels, run_kernel(): pl.pallas_call(kernel, out_shape=[leaf for leaves, _ in out_trees for lea...  14.7 us
    ppermute x7, starting transfers between devices, moved(): return lax.ppermute(value, ('patch', 'level'), pairs)  8.76 us
    ppermute x7, waiting for transfers between devices, moved(): return lax.ppermute(value, ('patch', 'level'), pairs)  6.7 us
    unnamed x12, local copies, waits for them, and re-layouts  0.95 us
  transfers between devices with their start and end apart: 7, of which 4 were waited for; matrix products, arithmetic and copies ran while one was open for 0% of the time, Pallas kernels for 31%

profile of v10, /device:TPU:21, one launch (start us, length us, event | category | flops | bytes accessed | tf_op | source)
XLA Modules:
  0.0 31.9 jit_solution(937107812980869071)
XLA Ops:
  0.6 0.7 %collective-permute-start = (bf16[8,2,128,128]{3,2,1,0:T(8,128)(2,1)}, bf16[8,2,128,128]{3,2,1,0:T(8,128)(2,1)S(1)}, u32[]{:S(2)}, u32[]{:S(2)}) collective-permute-start(bf16[8,2,128,128]{3,2,1,0:T(8,128)(2,1)} %bitcast.6), channel_id=1, source_target_pairs={{0,1},{1,0},{2,3},{3,2},{4,5},{5,4},{6,7},{7,6},{8,9},{9,8},{10,11... | collective-permute-start | bytes 1572872 | tf_op jit(solution)/shard_map/ppermute | solution.py:1103
  1.4 0.1 collective-permute-start.1
  1.5 0.4 %collective-permute-start.2 = (bf16[8,128,128]{2,1,0:T(8,128)(2,1)}, bf16[8,128,128]{2,1,0:T(8,128)(2,1)S(1)}, u32[]{:S(2)}, u32[]{:S(2)}) collective-permute-start(bf16[8,128,128]{2,1,0:T(8,128)(2,1)} %bitcast.14), channel_id=1, source_target_pairs={{0,1},{1,0},{2,3},{3,2},{4,5},{5,4},{6,7},{7,6},{8,9},{9,8},{10,11... | collective-permute-start | bytes 786440 | tf_op jit(solution)/shard_map/ppermute | solution.py:1103
  1.9 0.0 copy-start.5
  1.9 2.2 %shard_map.68.refs_0_ = f32[128,128]{1,0:T(8,128)} custom-call(bf16[8,2,128,128]{3,2,1,0:T(8,128)(2,1)} %bitcast.7, f32[8,128,128]{2,1,0:T(8,128)} %bitcast.11, bf16[8,128,128]{2,1,0:T(8,128)(2,1)} %bitcast.15), custom_call_target="tpu_custom_call" | custom-call | tf_op jit(solution)/shard_map/pallas_call | solution.py:1080
  4.1 0.0 copy-start
  4.1 0.0 copy-start.1
  4.1 0.0 copy-start.2
  4.1 0.1 collective-permute-done.2.refs_3_.refs_6_
  4.2 0.0 collective-permute-done.refs_1_.refs_4_
  4.2 0.0 collective-permute-done.1.refs_2_.refs_5_
  4.2 0.0 copy-start.4
  4.3 0.9 %copy-done.4 = f32[128,128]{1,0:T(8,128)S(1)} copy-done((f32[128,128]{1,0:T(8,128)S(1)}, f32[128,128]{1,0:T(8,128)}, u32[]{:S(2)}) %copy-start.4) | copy-done | bytes 65560
  5.2 0.4 %shard_map.69 = f32[128,128]{1,0:T(8,128)S(1)} custom-call(f32[128,128]{1,0:T(8,128)S(1)} %copy-done.4, bf16[8,2,128,128]{3,2,1,0:T(8,128)(2,1)S(1)} %collective-permute-done.refs_1_.refs_4_, f32[8,128,128]{2,1,0:T(8,128)S(1)} %collective-permute-done.1.refs_2_.refs_5_, bf16[8,128,128]{2,1,0:T(8,128)(2,1)S(1)} %collective-permute-done.2.refs_3_.refs_6_), custom_call_target="tpu_custom_call" | custom-call | tf_op jit(solution)/shard_map/pallas_call | solution.py:1080
  5.6 2.2 %collective-permute-start.3 = (f32[128,128]{1,0:T(8,128)S(1)}, f32[128,128]{1,0:T(8,128)S(1)}, u32[]{:S(2)}, u32[]{:S(2)}) collective-permute-start(f32[128,128]{1,0:T(8,128)S(1)} %shard_map.69), channel_id=1, source_target_pairs={{0,5},{2,7},{4,9},{5,0},{6,11},{7,2},{8,13},{9,4},{10,15},{11,6},{... | collective-permute-start | bytes 196616 | tf_op jit(solution)/shard_map/ppermute | solution.py:1103
  7.8 4.1 %collective-permute-done.3.refs_7_ = f32[128,128]{1,0:T(8,128)S(1)} collective-permute-done((f32[128,128]{1,0:T(8,128)S(1)}, f32[128,128]{1,0:T(8,128)S(1)}, u32[]{:S(2)}, u32[]{:S(2)}) %collective-permute-start.3) | collective-permute-done | bytes 65568 | tf_op jit(solution)/shard_map/ppermute | solution.py:1103
  11.9 0.0 copy-done.5
  11.9 0.0 copy-done
  11.9 0.0 copy-done.1
  11.9 0.0 copy-done.2
  11.9 1.3 %shard_map.70 = (f32[3,272,128]{2,1,0:T(8,128)S(1)}, f32[2,3,256,128]{3,2,1,0:T(8,128)S(1)}, f32[3,256,128]{2,1,0:T(8,128)S(1)}, f32[5,144,128]{2,1,0:T(8,128)S(...) custom-call(s32[4,8]{1,0:T(4,128)S(1)} %copy-done.5, ...), custom_call_target="tpu_custom_call" | custom-call | tf_op jit(solution)/shard_map/pallas_call | solution.py:1080
  13.2 2.6 %collective-permute-start.5 = (bf16[816,128]{1,0:T(8,128)(2,1)S(1)}, bf16[816,128]{1,0:T(8,128)(2,1)S(1)}, u32[]{:S(2)}, u32[]{:S(2)}) collective-permute-start(bf16[816,128]{1,0:T(8,128)(2,1)S(1)} %get-tuple-element.45), channel_id=1, source_target_pairs={{0,2},{1,3},{4,6},{5,7},{8,10},{9,11},{12,14},{13,15},{16,18},{17,... | collective-permute-start | bytes 626696 | tf_op jit(solution)/shard_map/ppermute | solution.py:1103
  15.8 1.7 %shard_map.71 = (f32[272,128]{1,0:T(8,128)S(1)}, f32[2,3,256,128]{3,2,1,0:T(8,128)S(1)}, f32[2,3,256,128]{3,2,1,0:T(8,128)S(1)}, f32[2,5,128,128]{3,2,1,0:T(8,12...) custom-call(s32[4,8]{1,0:T(4,128)S(1)} %copy-done.5, ...), custom_call_target="tpu_custom_call" | custom-call | tf_op jit(solution)/shard_map/pallas_call | solution.py:1080
  17.5 1.3 %collective-permute-start.4 = (f32[272,128]{1,0:T(8,128)S(1)}, f32[272,128]{1,0:T(8,128)S(1)}, u32[]{:S(2)}, u32[]{:S(2)}) collective-permute-start(f32[272,128]{1,0:T(8,128)S(1)} %get-tuple-element.36.refs_1_), channel_id=1, source_target_pairs={{2,0},{3,1},{6,4},{7,5},{10,8},{11,9},{14,12},{15,13},{18,16},{19,... | collective-permute-start | bytes 417800 | tf_op jit(solution)/shard_map/ppermute | solution.py:1103
  18.8 1.0 %collective-permute-done.5.refs_2_ = bf16[816,128]{1,0:T(8,128)(2,1)S(1)} collective-permute-done((bf16[816,128]{1,0:T(8,128)(2,1)S(1)}, bf16[816,128]{1,0:T(8,128)(2,1)S(1)}, u32[]{:S(2)}, u32[]{:S(2)}) %collective-permute-start.5) | collective-permute-done | bytes 208928 | tf_op jit(solution)/shard_map/ppermute | solution.py:1103
  19.8 5.8 %shard_map.72 = (f32[4,2,128,128]{3,2,1,0:T(8,128)S(1)}, f32[4,2,128,128]{3,2,1,0:T(8,128)S(1)}, f32[2,512,128]{2,1,0:T(8,128)S(1)}, f32[2,1,1024,128]{3,2,1,0:T(8,128)S(1)}) custom-call(s32[4,8]{1,0:T(4,128)S(1)} %copy-done.5, f32[272,128]{1,0:T(8,128)S(1)} %get-tuple-element.36.refs_1_, bf16[816,128]{1,0:T(8,128)(2,1)S(1)} %collective-permute-done.5.refs_2_, ...), custom_call_target="tpu_custom_call" | custom-call | tf_op jit(solution)/shard_map/pallas_call | solution.py:1080
  25.6 0.0 collective-permute-done.4.refs_1_
  25.6 0.0 copy-start.3
  25.6 2.0 %shard_map.73 = (f32[4,2,128,128]{3,2,1,0:T(8,128)S(1)}, f32[4,2,128,128]{3,2,1,0:T(8,128)S(1)}) custom-call(s32[4,8]{1,0:T(4,128)S(1)} %copy-done.5, f32[272,128]{1,0:T(8,128)S(1)} %collective-permute-done.4.refs_1_, f32[1,1040,128]{2,1,0:T(8,128)S(1)} %get-tuple-element.37.refs_3_.refs_2_, f32[2,1,1024,128]{3,2,1,0:T(8,128)S(1)} %get-tuple-element.38.refs_4_.refs_3_, ...), custom_call_target="tpu_custom_call" | custom-call | tf_op jit(solution)/shard_map/pallas_call | solution.py:1080
  27.7 1.4 %collective-permute-start.6 = (f32[4,2,128,128]{3,2,1,0:T(8,128)S(1)}, f32[4,2,128,128]{3,2,1,0:T(8,128)S(1)}, u32[]{:S(2)}, u32[]{:S(2)}) collective-permute-start(f32[4,2,128,128]{3,2,1,0:T(8,128)S(1)} %get-tuple-element.55), channel_id=1, source_target_pairs={{0,1},{1,0},{2,3},{3,2},{4,5},{5,4},{6,7},{7,6},{8,9},{9,8},{10,11... | collective-permute-start | bytes 1572872 | tf_op jit(solution)/shard_map/ppermute | solution.py:1103
  29.1 1.5 %collective-permute-done.6.refs_1_ = f32[4,2,128,128]{3,2,1,0:T(8,128)S(1)} collective-permute-done((f32[4,2,128,128]{3,2,1,0:T(8,128)S(1)}, f32[4,2,128,128]{3,2,1,0:T(8,128)S(1)}, u32[]{:S(2)}, u32[]{:S(2)}) %collective-permute-start.6) | collective-permute-done | bytes 524320 | tf_op jit(solution)/shard_map/ppermute | solution.py:1103
  30.6 0.0 copy-done.3
  30.6 1.2 %shard_map.74 = (f32[8,2,128,128]{3,2,1,0:T(8,128)}, bf16[8,128,128]{2,1,0:T(8,128)(2,1)}) custom-call(f32[4,2,128,128]{3,2,1,0:T(8,128)S(1)} %get-tuple-element.54.refs_0_, f32[4,2,128,128]{3,2,1,0:T(8,128)S(1)} %collective-permute-done.6.refs_1_, bf16[8,2,128,128]{3,2,1,0:T(8,128)(2,1)S(1)} %bitcast.19, bf16[8,128,128]{2,1,0:T(8,128)(2,1)S(1)} %bitcast.18), custom_call_target="tpu_custom_call" | custom-call | tf_op jit(solution)/shard_map/pallas_call | solution.py:1080
Async XLA Ops:
  0.6 3.6 %collective-permute-start = (bf16[8,2,128,128]{3,2,1,0:T(8,128)(2,1)}, bf16[8,2,128,128]{3,2,1,0:T(8,128)(2,1)S(1)}, u32[]{:S(2)}, u32[]{:S(2)}) collective-permute-start(bf16[8,2,128,128]{3,2,1,0:T(8,128)(2,1)} %bitcast.6), channel_id=1, source_target_pairs={{0,1},{1,0},{2,3},{3,2},{4,5},{5,4},{6,7},{7,6},{8,9},{9,8},{10,11... | collective-permute-start | bytes 1572872 | tf_op jit(solution)/shard_map/ppermute | solution.py:1103
  1.4 2.9 %collective-permute-start.1 = (f32[8,128,128]{2,1,0:T(8,128)}, f32[8,128,128]{2,1,0:T(8,128)S(1)}, u32[]{:S(2)}, u32[]{:S(2)}) collective-permute-start(f32[8,128,128]{2,1,0:T(8,128)} %bitcast.10), channel_id=1, source_target_pairs={{0,1},{1,0},{2,3},{3,2},{4,5},{5,4},{6,7},{7,6},{8,9},{9,8},{10,11... | collective-permute-start | bytes 1572872 | tf_op jit(solution)/shard_map/ppermute | solution.py:1103
  1.5 2.8 %collective-permute-start.2 = (bf16[8,128,128]{2,1,0:T(8,128)(2,1)}, bf16[8,128,128]{2,1,0:T(8,128)(2,1)S(1)}, u32[]{:S(2)}, u32[]{:S(2)}) collective-permute-start(bf16[8,128,128]{2,1,0:T(8,128)(2,1)} %bitcast.14), channel_id=1, source_target_pairs={{0,1},{1,0},{2,3},{3,2},{4,5},{5,4},{6,7},{7,6},{8,9},{9,8},{10,11... | collective-permute-start | bytes 786440 | tf_op jit(solution)/shard_map/ppermute | solution.py:1103
  1.9 10.0 %copy-start.5 = (s32[4,8]{1,0:T(4,128)S(1)}, s32[4,8]{1,0:T(4,128)}, u32[]{:S(2)}) copy-start(s32[4,8]{1,0:T(4,128)} %refs_0_.7) | copy-start | bytes 388
  4.1 7.8 %copy-start = (bf16[1,8,2,128,128]{4,3,2,1,0:T(8,128)(2,1)S(1)}, bf16[1,8,2,128,128]{4,3,2,1,0:T(8,128)(2,1)}, u32[]{:S(2)}) copy-start(bf16[1,8,2,128,128]{4,3,2,1,0:T(8,128)(2,1)} %param.5) | copy-start | bytes 1572868
  4.1 7.8 %copy-start.1 = (f32[1,8,128,128]{3,2,1,0:T(8,128)S(1)}, f32[1,8,128,128]{3,2,1,0:T(8,128)}, u32[]{:S(2)}) copy-start(f32[1,8,128,128]{3,2,1,0:T(8,128)} %param.7) | copy-start | bytes 1572868
  4.1 7.8 %copy-start.2 = (bf16[1,8,128,128]{3,2,1,0:T(8,128)(2,1)S(1)}, bf16[1,8,128,128]{3,2,1,0:T(8,128)(2,1)}, u32[]{:S(2)}) copy-start(bf16[1,8,128,128]{3,2,1,0:T(8,128)(2,1)} %param.8) | copy-start | bytes 786436
  4.2 0.9 %copy-start.4 = (f32[128,128]{1,0:T(8,128)S(1)}, f32[128,128]{1,0:T(8,128)}, u32[]{:S(2)}) copy-start(f32[128,128]{1,0:T(8,128)} %shard_map.68.refs_0_) | copy-start | bytes 196612
  5.6 6.3 %collective-permute-start.3 = (f32[128,128]{1,0:T(8,128)S(1)}, f32[128,128]{1,0:T(8,128)S(1)}, u32[]{:S(2)}, u32[]{:S(2)}) collective-permute-start(f32[128,128]{1,0:T(8,128)S(1)} %shard_map.69), channel_id=1, source_target_pairs={{0,5},{2,7},{4,9},{5,0},{6,11},{7,2},{8,13},{9,4},{10,15},{11,6},{... | collective-permute-start | bytes 196616 | tf_op jit(solution)/shard_map/ppermute | solution.py:1103
  13.2 6.6 %collective-permute-start.5 = (bf16[816,128]{1,0:T(8,128)(2,1)S(1)}, bf16[816,128]{1,0:T(8,128)(2,1)S(1)}, u32[]{:S(2)}, u32[]{:S(2)}) collective-permute-start(bf16[816,128]{1,0:T(8,128)(2,1)S(1)} %get-tuple-element.45), channel_id=1, source_target_pairs={{0,2},{1,3},{4,6},{5,7},{8,10},{9,11},{12,14},{13,15},{16,18},{17,... | collective-permute-start | bytes 626696 | tf_op jit(solution)/shard_map/ppermute | solution.py:1103
  17.5 8.1 %collective-permute-start.4 = (f32[272,128]{1,0:T(8,128)S(1)}, f32[272,128]{1,0:T(8,128)S(1)}, u32[]{:S(2)}, u32[]{:S(2)}) collective-permute-start(f32[272,128]{1,0:T(8,128)S(1)} %get-tuple-element.36.refs_1_), channel_id=1, source_target_pairs={{2,0},{3,1},{6,4},{7,5},{10,8},{11,9},{14,12},{15,13},{18,16},{19,... | collective-permute-start | bytes 417800 | tf_op jit(solution)/shard_map/ppermute | solution.py:1103
  25.6 5.0 %copy-start.3 = (bf16[1,8,2,128,128]{4,3,2,1,0:T(8,128)(2,1)S(1)}, bf16[1,8,2,128,128]{4,3,2,1,0:T(8,128)(2,1)}, u32[]{:S(2)}) copy-start(bf16[1,8,2,128,128]{4,3,2,1,0:T(8,128)(2,1)} %param.6) | copy-start | bytes 1572868
  27.7 3.0 %collective-permute-start.6 = (f32[4,2,128,128]{3,2,1,0:T(8,128)S(1)}, f32[4,2,128,128]{3,2,1,0:T(8,128)S(1)}, u32[]{:S(2)}, u32[]{:S(2)}) collective-permute-start(f32[4,2,128,128]{3,2,1,0:T(8,128)S(1)} %get-tuple-element.55), channel_id=1, source_target_pairs={{0,1},{1,0},{2,3},{3,2},{4,5},{5,4},{6,7},{7,6},{8,9},{9,8},{10,11... | collective-permute-start | bytes 1572872 | tf_op jit(solution)/shard_map/ppermute | solution.py:1103

commit v11 on v10

--- a/solution.py
+++ b/solution.py
@@ -733,7 +733,15 @@
                 )
 
 
-def fill_kernel(g, rows_ref, own, other, edge, filled, lent):
+def lend_kernel(g, own, other, edge, lent):
+    level_here = lax.axis_index("level")
+    for level in range(g.levels - 2):
+        pl.when(level_here == level)(
+            lambda level=level: lend(g, level % 2 == 1, own, other, edge, lent)
+        )
+
+
+def fill_kernel(g, rows_ref, own, other, edge, _, filled):
     level_here = lax.axis_index("level")
     top = g.levels - 1
 
@@ -741,11 +749,6 @@
     def _():
         levels = dict(zip((top - 1, top), filled))
         fill_pair(g, rows_ref, own, other, edge, levels, (top, top - 1), g.patch_rows)
-
-    for level in range(top - 1):
-        pl.when(level_here == level)(
-            lambda level=level: lend(g, level % 2 == 1, own, other, edge, lent)
-        )
 
 
 def down_kernel(
@@ -1148,13 +1151,19 @@
     rows, less = lent_rows(g)
     given = [(patch_rows, SM), (own, VM), (other, VM), (edge, VM)]
 
-    upper, lent = run_kernel(
+    (lent_here,) = run_kernel(
+        lambda *refs: lend_kernel(g, *refs),
+        given[1:],
+        [(make((lent_size(g), side), BF16), VM)],
+        [],
+    )
+    lent = moved(lent_here, g, lambda p, l: (p, l + 2))
+    (upper,) = run_kernel(
         lambda *refs: fill_kernel(g, *refs),
-        given,
-        [(fields[top - 1 :], VM), (make((lent_size(g), side), BF16), VM)],
+        [*given, (lent_here, VM)],
+        [(fields[top - 1 :], VM)],
         [],
     )
-    lent = moved(lent, g, lambda p, l: (p, l + 2))
 
     def kept_of(level):
         two = array(level, g.rows(level), make, True, False)

time: 32.1 us -> 31.2 us (0.972)
  waiting for transfers between devices: 6.7 us -> 6.11 us
  starting transfers between devices: 8.76 us -> 8.42 us
    ppermute x7, waiting for transfers between devices: 6.7 us -> 6.11 us  [moved(): return lax.ppermute(value, ('patch', 'level'), pairs)]
    ppermute x7, starting transfers between devices: 8.76 us -> 8.42 us  [moved(): return lax.ppermute(value, ('patch', 'level'), pairs)]
    pallas_call x7 -> x8, Pallas kernels: 14.7 us -> 14.7 us  [run_kernel(): pl.pallas_call(kernel, out_shape=[leaf for leaves, _ in out_trees for lea...]
  transfers between devices with their start and end apart: 7 -> 7, of which waited for: 4 -> 4; matrix products, arithmetic and copies ran while one was open for 0% -> 0% of each run, Pallas kernels for 31% -> 33%
where the time goes in v11:
time: 31.2 us; the launch traced here: 31 us
  Pallas kernels  14.7 us (47%)
  starting transfers between devices  8.42 us (27%)
  waiting for transfers between devices  6.11 us (20%)
  local copies, waits for them, and re-layouts  0.95 us (3%)
  between operations  0.77 us (2%)
    pallas_call x8, Pallas kernels, run_kernel(): pl.pallas_call(kernel, out_shape=[leaf for leaves, _ in out_trees for lea...  14.7 us
    ppermute x7, starting transfers between devices, moved(): return lax.ppermute(value, ('patch', 'level'), pairs)  8.42 us
    ppermute x7, waiting for transfers between devices, moved(): return lax.ppermute(value, ('patch', 'level'), pairs)  6.11 us
    unnamed x12, local copies, waits for them, and re-layouts  0.95 us
  transfers between devices with their start and end apart: 7, of which 4 were waited for; matrix products, arithmetic and copies ran while one was open for 0% of the time, Pallas kernels for 33%

profile of v11, /device:TPU:21, one launch (start us, length us, event | category | flops | bytes accessed | tf_op | source)
XLA Modules:
  0.0 31.0 jit_solution(8848514180339039213)
XLA Ops:
  0.6 0.7 %collective-permute-start = (bf16[8,2,128,128]{3,2,1,0:T(8,128)(2,1)}, bf16[8,2,128,128]{3,2,1,0:T(8,128)(2,1)S(1)}, u32[]{:S(2)}, u32[]{:S(2)}) collective-permute-start(bf16[8,2,128,128]{3,2,1,0:T(8,128)(2,1)} %bitcast.6), channel_id=1, source_target_pairs={{0,1},{1,0},{2,3},{3,2},{4,5},{5,4},{6,7},{7,6},{8,9},{9,8},{10,11... | collective-permute-start | bytes 1572872 | tf_op jit(solution)/shard_map/ppermute | solution.py:1106
  1.4 0.1 collective-permute-start.1
  1.5 0.4 %collective-permute-start.2 = (bf16[8,128,128]{2,1,0:T(8,128)(2,1)}, bf16[8,128,128]{2,1,0:T(8,128)(2,1)S(1)}, u32[]{:S(2)}, u32[]{:S(2)}) collective-permute-start(bf16[8,128,128]{2,1,0:T(8,128)(2,1)} %bitcast.16), channel_id=1, source_target_pairs={{0,1},{1,0},{2,3},{3,2},{4,5},{5,4},{6,7},{7,6},{8,9},{9,8},{10,11... | collective-permute-start | bytes 786440 | tf_op jit(solution)/shard_map/ppermute | solution.py:1106
  1.9 2.2 %shard_map.68.refs_0_ = f32[128,128]{1,0:T(8,128)} custom-call(bf16[8,2,128,128]{3,2,1,0:T(8,128)(2,1)} %bitcast.7, f32[8,128,128]{2,1,0:T(8,128)} %bitcast.12, bf16[8,128,128]{2,1,0:T(8,128)(2,1)} %bitcast.17), custom_call_target="tpu_custom_call" | custom-call | tf_op jit(solution)/shard_map/pallas_call | solution.py:1083
  4.1 0.0 copy-start
  4.1 0.0 copy-start.1
  4.1 0.0 copy-start.2
  4.1 0.1 collective-permute-done.2.refs_3_.refs_5_.refs_6_
  4.2 0.0 collective-permute-done.refs_1_.refs_3_.refs_4_
  4.2 0.0 collective-permute-done.1.refs_2_.refs_4_.refs_5_
  4.2 0.0 copy-start.4
  4.3 0.9 %copy-done.4 = f32[128,128]{1,0:T(8,128)S(1)} copy-done((f32[128,128]{1,0:T(8,128)S(1)}, f32[128,128]{1,0:T(8,128)}, u32[]{:S(2)}) %copy-start.4) | copy-done | bytes 65560
  5.2 0.4 %shard_map.69 = f32[128,128]{1,0:T(8,128)S(1)} custom-call(f32[128,128]{1,0:T(8,128)S(1)} %copy-done.4, bf16[8,2,128,128]{3,2,1,0:T(8,128)(2,1)S(1)} %collective-permute-done.refs_1_.refs_3_.refs_4_, f32[8,128,128]{2,1,0:T(8,128)S(1)} %collective-permute-done.1.refs_2_.refs_4_.refs_5_, bf16[8,128,128]{2,1,0:T(8,128)(2,1)S(1)} %collective-permute-done.2.refs_3_.refs_5_.refs_6_), custom_call_target="tpu_custom_call" | custom-call | tf_op jit(solution)/shard_map/pallas_call | solution.py:1083
  5.6 0.0 copy-start.5
  5.6 2.2 %collective-permute-start.3 = (f32[128,128]{1,0:T(8,128)S(1)}, f32[128,128]{1,0:T(8,128)S(1)}, u32[]{:S(2)}, u32[]{:S(2)}) collective-permute-start(f32[128,128]{1,0:T(8,128)S(1)} %shard_map.69), channel_id=1, source_target_pairs={{0,5},{2,7},{4,9},{5,0},{6,11},{7,2},{8,13},{9,4},{10,15},{11,6},{... | collective-permute-start | bytes 196616 | tf_op jit(solution)/shard_map/ppermute | solution.py:1106
  7.8 4.1 %collective-permute-done.3.refs_6_.refs_7_ = f32[128,128]{1,0:T(8,128)S(1)} collective-permute-done((f32[128,128]{1,0:T(8,128)S(1)}, f32[128,128]{1,0:T(8,128)S(1)}, u32[]{:S(2)}, u32[]{:S(2)}) %collective-permute-start.3) | collective-permute-done | bytes 65568 | tf_op jit(solution)/shard_map/ppermute | solution.py:1106
  11.9 0.0 copy-done
  11.9 0.0 copy-done.1
  11.9 0.0 copy-done.2
  11.9 0.7 %shard_map.70.refs_8_ = bf16[816,128]{1,0:T(8,128)(2,1)S(1)} custom-call(bf16[8,2,128,128]{3,2,1,0:T(8,128)(2,1)S(1)} %bitcast.8, f32[8,128,128]{2,1,0:T(8,128)S(1)} %bitcast.13, bf16[8,128,128]{2,1,0:T(8,128)(2,1)S(1)} %bitcast.18, bf16[8,2,128,128]{3,2,1,0:T(8,128)(2,1)S(1)} %collective-permute-done.refs_1_.refs_3_.refs_4_, ...), custom_call_target="tpu_custom_call" | custom-call | tf_op jit(solution)/shard_map/pallas_call | solution.py:1083
  12.6 2.2 %collective-permute-start.5 = (bf16[816,128]{1,0:T(8,128)(2,1)S(1)}, bf16[816,128]{1,0:T(8,128)(2,1)S(1)}, u32[]{:S(2)}, u32[]{:S(2)}) collective-permute-start(bf16[816,128]{1,0:T(8,128)(2,1)S(1)} %shard_map.70.refs_8_), channel_id=1, source_target_pairs={{0,2},{1,3},{4,6},{5,7},{8,10},{9,11},{12,14},{13,15},{16,18},{17,... | collective-permute-start | bytes 626696 | tf_op jit(solution)/shard_map/ppermute | solution.py:1106
  14.9 0.0 copy-done.5
  14.9 0.6 %shard_map.71 = (f32[3,272,128]{2,1,0:T(8,128)S(1)}, f32[2,3,256,128]{3,2,1,0:T(8,128)S(1)}, f32[3,256,128]{2,1,0:T(8,128)S(1)}, f32[5,144,128]{2,1,0:T(8,128)S(...) custom-call(s32[4,8]{1,0:T(4,128)S(1)} %copy-done.5, bf16[8,2,128,128]{3,2,1,0:T(8,128)(2,1)S(1)} %bitcast.9, ...), custom_call_target="tpu_custom_call" | custom-call | tf_op jit(solution)/shard_map/pallas_call | solution.py:1083
  15.5 1.7 %shard_map.72 = (f32[272,128]{1,0:T(8,128)S(1)}, f32[2,3,256,128]{3,2,1,0:T(8,128)S(1)}, f32[2,3,256,128]{3,2,1,0:T(8,128)S(1)}, f32[2,5,128,128]{3,2,1,0:T(8,12...) custom-call(s32[4,8]{1,0:T(4,128)S(1)} %copy-done.5, ...), custom_call_target="tpu_custom_call" | custom-call | tf_op jit(solution)/shard_map/pallas_call | solution.py:1083
  17.2 1.3 %collective-permute-start.4 = (f32[272,128]{1,0:T(8,128)S(1)}, f32[272,128]{1,0:T(8,128)S(1)}, u32[]{:S(2)}, u32[]{:S(2)}) collective-permute-start(f32[272,128]{1,0:T(8,128)S(1)} %get-tuple-element.35.refs_1_), channel_id=1, source_target_pairs={{2,0},{3,1},{6,4},{7,5},{10,8},{11,9},{14,12},{15,13},{18,16},{19,... | collective-permute-start | bytes 417800 | tf_op jit(solution)/shard_map/ppermute | solution.py:1106
  18.5 0.4 %collective-permute-done.5.refs_2_ = bf16[816,128]{1,0:T(8,128)(2,1)S(1)} collective-permute-done((bf16[816,128]{1,0:T(8,128)(2,1)S(1)}, bf16[816,128]{1,0:T(8,128)(2,1)S(1)}, u32[]{:S(2)}, u32[]{:S(2)}) %collective-permute-start.5) | collective-permute-done | bytes 208928 | tf_op jit(solution)/shard_map/ppermute | solution.py:1106
  18.9 5.8 %shard_map.73 = (f32[4,2,128,128]{3,2,1,0:T(8,128)S(1)}, f32[4,2,128,128]{3,2,1,0:T(8,128)S(1)}, f32[2,512,128]{2,1,0:T(8,128)S(1)}, f32[2,1,1024,128]{3,2,1,0:T(8,128)S(1)}) custom-call(s32[4,8]{1,0:T(4,128)S(1)} %copy-done.5, f32[272,128]{1,0:T(8,128)S(1)} %get-tuple-element.35.refs_1_, bf16[816,128]{1,0:T(8,128)(2,1)S(1)} %collective-permute-done.5.refs_2_, ...), custom_call_target="tpu_custom_call" | custom-call | tf_op jit(solution)/shard_map/pallas_call | solution.py:1083
  24.7 0.0 collective-permute-done.4.refs_1_
  24.7 0.0 copy-start.3
  24.7 2.0 %shard_map.74 = (f32[4,2,128,128]{3,2,1,0:T(8,128)S(1)}, f32[4,2,128,128]{3,2,1,0:T(8,128)S(1)}) custom-call(s32[4,8]{1,0:T(4,128)S(1)} %copy-done.5, f32[272,128]{1,0:T(8,128)S(1)} %collective-permute-done.4.refs_1_, f32[1,1040,128]{2,1,0:T(8,128)S(1)} %get-tuple-element.36.refs_3_.refs_2_, f32[2,1,1024,128]{3,2,1,0:T(8,128)S(1)} %get-tuple-element.37.refs_4_.refs_3_, ...), custom_call_target="tpu_custom_call" | custom-call | tf_op jit(solution)/shard_map/pallas_call | solution.py:1083
  26.8 1.4 %collective-permute-start.6 = (f32[4,2,128,128]{3,2,1,0:T(8,128)S(1)}, f32[4,2,128,128]{3,2,1,0:T(8,128)S(1)}, u32[]{:S(2)}, u32[]{:S(2)}) collective-permute-start(f32[4,2,128,128]{3,2,1,0:T(8,128)S(1)} %get-tuple-element.53), channel_id=1, source_target_pairs={{0,1},{1,0},{2,3},{3,2},{4,5},{5,4},{6,7},{7,6},{8,9},{9,8},{10,11... | collective-permute-start | bytes 1572872 | tf_op jit(solution)/shard_map/ppermute | solution.py:1106
  28.2 1.5 %collective-permute-done.6.refs_1_ = f32[4,2,128,128]{3,2,1,0:T(8,128)S(1)} collective-permute-done((f32[4,2,128,128]{3,2,1,0:T(8,128)S(1)}, f32[4,2,128,128]{3,2,1,0:T(8,128)S(1)}, u32[]{:S(2)}, u32[]{:S(2)}) %collective-permute-start.6) | collective-permute-done | bytes 524320 | tf_op jit(solution)/shard_map/ppermute | solution.py:1106
  29.7 0.0 copy-done.3
  29.7 1.2 %shard_map.75 = (f32[8,2,128,128]{3,2,1,0:T(8,128)}, bf16[8,128,128]{2,1,0:T(8,128)(2,1)}) custom-call(f32[4,2,128,128]{3,2,1,0:T(8,128)S(1)} %get-tuple-element.52.refs_0_, f32[4,2,128,128]{3,2,1,0:T(8,128)S(1)} %collective-permute-done.6.refs_1_, bf16[8,2,128,128]{3,2,1,0:T(8,128)(2,1)S(1)} %bitcast.22, bf16[8,128,128]{2,1,0:T(8,128)(2,1)S(1)} %bitcast.21), custom_call_target="tpu_custom_call" | custom-call | tf_op jit(solution)/shard_map/pallas_call | solution.py:1083
Async XLA Ops:
  0.6 3.6 %collective-permute-start = (bf16[8,2,128,128]{3,2,1,0:T(8,128)(2,1)}, bf16[8,2,128,128]{3,2,1,0:T(8,128)(2,1)S(1)}, u32[]{:S(2)}, u32[]{:S(2)}) collective-permute-start(bf16[8,2,128,128]{3,2,1,0:T(8,128)(2,1)} %bitcast.6), channel_id=1, source_target_pairs={{0,1},{1,0},{2,3},{3,2},{4,5},{5,4},{6,7},{7,6},{8,9},{9,8},{10,11... | collective-permute-start | bytes 1572872 | tf_op jit(solution)/shard_map/ppermute | solution.py:1106
  1.4 2.9 %collective-permute-start.1 = (f32[8,128,128]{2,1,0:T(8,128)}, f32[8,128,128]{2,1,0:T(8,128)S(1)}, u32[]{:S(2)}, u32[]{:S(2)}) collective-permute-start(f32[8,128,128]{2,1,0:T(8,128)} %bitcast.11), channel_id=1, source_target_pairs={{0,1},{1,0},{2,3},{3,2},{4,5},{5,4},{6,7},{7,6},{8,9},{9,8},{10,11... | collective-permute-start | bytes 1572872 | tf_op jit(solution)/shard_map/ppermute | solution.py:1106
  1.5 2.8 %collective-permute-start.2 = (bf16[8,128,128]{2,1,0:T(8,128)(2,1)}, bf16[8,128,128]{2,1,0:T(8,128)(2,1)S(1)}, u32[]{:S(2)}, u32[]{:S(2)}) collective-permute-start(bf16[8,128,128]{2,1,0:T(8,128)(2,1)} %bitcast.16), channel_id=1, source_target_pairs={{0,1},{1,0},{2,3},{3,2},{4,5},{5,4},{6,7},{7,6},{8,9},{9,8},{10,11... | collective-permute-start | bytes 786440 | tf_op jit(solution)/shard_map/ppermute | solution.py:1106
  4.1 7.8 %copy-start = (bf16[1,8,2,128,128]{4,3,2,1,0:T(8,128)(2,1)S(1)}, bf16[1,8,2,128,128]{4,3,2,1,0:T(8,128)(2,1)}, u32[]{:S(2)}) copy-start(bf16[1,8,2,128,128]{4,3,2,1,0:T(8,128)(2,1)} %param.5) | copy-start | bytes 1572868
  4.1 7.8 %copy-start.1 = (f32[1,8,128,128]{3,2,1,0:T(8,128)S(1)}, f32[1,8,128,128]{3,2,1,0:T(8,128)}, u32[]{:S(2)}) copy-start(f32[1,8,128,128]{3,2,1,0:T(8,128)} %param.7) | copy-start | bytes 1572868
  4.1 7.8 %copy-start.2 = (bf16[1,8,128,128]{3,2,1,0:T(8,128)(2,1)S(1)}, bf16[1,8,128,128]{3,2,1,0:T(8,128)(2,1)}, u32[]{:S(2)}) copy-start(bf16[1,8,128,128]{3,2,1,0:T(8,128)(2,1)} %param.8) | copy-start | bytes 786436
  4.2 0.9 %copy-start.4 = (f32[128,128]{1,0:T(8,128)S(1)}, f32[128,128]{1,0:T(8,128)}, u32[]{:S(2)}) copy-start(f32[128,128]{1,0:T(8,128)} %shard_map.68.refs_0_) | copy-start | bytes 196612
  5.6 9.3 %copy-start.5 = (s32[4,8]{1,0:T(4,128)S(1)}, s32[4,8]{1,0:T(4,128)}, u32[]{:S(2)}) copy-start(s32[4,8]{1,0:T(4,128)} %refs_0_.7) | copy-start | bytes 388
  5.6 6.3 %collective-permute-start.3 = (f32[128,128]{1,0:T(8,128)S(1)}, f32[128,128]{1,0:T(8,128)S(1)}, u32[]{:S(2)}, u32[]{:S(2)}) collective-permute-start(f32[128,128]{1,0:T(8,128)S(1)} %shard_map.69), channel_id=1, source_target_pairs={{0,5},{2,7},{4,9},{5,0},{6,11},{7,2},{8,13},{9,4},{10,15},{11,6},{... | collective-permute-start | bytes 196616 | tf_op jit(solution)/shard_map/ppermute | solution.py:1106
  12.6 6.2 %collective-permute-start.5 = (bf16[816,128]{1,0:T(8,128)(2,1)S(1)}, bf16[816,128]{1,0:T(8,128)(2,1)S(1)}, u32[]{:S(2)}, u32[]{:S(2)}) collective-permute-start(bf16[816,128]{1,0:T(8,128)(2,1)S(1)} %shard_map.70.refs_8_), channel_id=1, source_target_pairs={{0,2},{1,3},{4,6},{5,7},{8,10},{9,11},{12,14},{13,15},{16,18},{17,... | collective-permute-start | bytes 626696 | tf_op jit(solution)/shard_map/ppermute | solution.py:1106
  17.2 7.5 %collective-permute-start.4 = (f32[272,128]{1,0:T(8,128)S(1)}, f32[272,128]{1,0:T(8,128)S(1)}, u32[]{:S(2)}, u32[]{:S(2)}) collective-permute-start(f32[272,128]{1,0:T(8,128)S(1)} %get-tuple-element.35.refs_1_), channel_id=1, source_target_pairs={{2,0},{3,1},{6,4},{7,5},{10,8},{11,9},{14,12},{15,13},{18,16},{19,... | collective-permute-start | bytes 417800 | tf_op jit(solution)/shard_map/ppermute | solution.py:1106
  24.7 5.0 %copy-start.3 = (bf16[1,8,2,128,128]{4,3,2,1,0:T(8,128)(2,1)S(1)}, bf16[1,8,2,128,128]{4,3,2,1,0:T(8,128)(2,1)}, u32[]{:S(2)}) copy-start(bf16[1,8,2,128,128]{4,3,2,1,0:T(8,128)(2,1)} %param.6) | copy-start | bytes 1572868
  26.8 3.0 %collective-permute-start.6 = (f32[4,2,128,128]{3,2,1,0:T(8,128)S(1)}, f32[4,2,128,128]{3,2,1,0:T(8,128)S(1)}, u32[]{:S(2)}, u32[]{:S(2)}) collective-permute-start(f32[4,2,128,128]{3,2,1,0:T(8,128)S(1)} %get-tuple-element.53), channel_id=1, source_target_pairs={{0,1},{1,0},{2,3},{3,2},{4,5},{5,4},{6,7},{7,6},{8,9},{9,8},{10,11... | collective-permute-start | bytes 1572872 | tf_op jit(solution)/shard_map/ppermute | solution.py:1106

commit v12 on v11

--- a/solution.py
+++ b/solution.py
@@ -538,7 +538,7 @@
 
 def lent_size(g):
     rows, less = lent_rows(g)
-    return 4 * rows + 2 * 16 * len(lent_forcing(g)) + 2 * less + 16
+    return 4 * rows + 2 * 16 * len(lent_forcing(g)) + less + 16
 
 
 def pair_of(visc):
@@ -608,7 +608,6 @@
 
     high, rest = pair_of(coarse_rows(3, 0, less))
     target.put(side_by_side(g, coarse_rows(2, 0, less), high))
-    target.put(rest)
     target.put(
         side_by_side(g, coarse_rows(0, g.half_side, 16), coarse_rows(1, g.half_side, 16))
     )
@@ -646,7 +645,7 @@
         return total
 
     fine_part = margins(1, rows)
-    target.put(fine_part[:less] + margins(0, less))
+    target.put(side_by_side(g, rest, fine_part[:less] + margins(0, less)))
     target.put(fine_part[less:])
 
 
@@ -680,8 +679,10 @@
         for first in lent_forcing(g):
             value = masked(source.take(16), covered[0] - first, False)
             fine.right[comp, 0, pl.ds(first, 16), :] = value
-    first, rest, window = source.take(less), source.take(less), source.take(16)
-    packed = source.take(rows)
+    first, window, rest = source.take(less), source.take(16), source.take(less)
+    packed = jnp.concatenate(
+        [pltpu.roll(rest, g.half_side, 1), source.take(rows - less)], axis=0
+    )
 
     def margins(level, q, size):
         moves = [margin_moves(g, level, index) for index in ((q,) if q < 3 else (3, 4))]
@@ -846,8 +847,22 @@
     corrected_step(g, 1, fine, start, stop, store_fine)
 
 
+def weigh_kernel(g, rows_ref, filled, weights):
+    level_here = lax.axis_index("level")
+    patch = lax.axis_index("patch")
+    odd = level_here % 2 == 1
+
+    @pl.when(level_here < g.levels - 2)
+    def _():
+        first = g.rows(2) // 2
+        for level, start in ((1, first), (0, first // 2)):
+            d = Level(filled[level].visc, weights[level], fric=filled[level].fric)
+            limits = lane_limits(g, level, near_counts(g, rows_ref, level, patch, odd), g.side)
+            smooth_weights(g, level, d, limits, start, g.rows(level), False)
+
+
 def up_kernel(
-    g, rows_ref, sums, lent, filled, kept, mine, theirs, own_rows, coarse_rows, edges, scratch, low, low_fine,
+    g, rows_ref, sums, lent, filled, kept, rest_weights, mine, theirs, own_rows, coarse_rows, edges, scratch, low, low_fine,
     low_coarse, finer, coarser,
 ):
     level_here = lax.axis_index("level")
@@ -922,9 +937,8 @@
     def _():
         rows = g.rows(1)
         first = g.rows(2) // 2
-        fine, coarse = levels[1], levels[0]._replace(cells=coarse_rows)
-        smooth_weights(g, 1, fine, limits_of(1), first, rows, False)
-        smooth_weights(g, 0, coarse, limits_of(0), first // 2, g.rows(0), False)
+        fine = levels[1]._replace(weight=rest_weights[1])
+        coarse = levels[0]._replace(weight=rest_weights[0], cells=coarse_rows)
 
         def store_fine(comp, k, row, chunk, value):
             if k == 0:
@@ -1192,13 +1206,20 @@
     filled = [*lower, *upper]
     sums_there = moved(sums, g, lambda p, l: (p, l - 2))
 
+    (rest_weights,) = run_kernel(
+        lambda *refs: weigh_kernel(g, *refs),
+        [(patch_rows, SM), (lower, VM)],
+        [([array(level, g.rows(level), make, True, False) for level in (0, 1)], VM)],
+        [],
+    )
+
     def up_scratch(level):
         both = array(level, g.rows(level), vmem, True, False)
         if level == 0:
-            return Level(None, both)
+            return Level(None, None)
         steps = step_arrays(g, level, g.rows(level))
         if level == 1:
-            return Level(None, both, held=both, left=both, **steps)
+            return Level(None, None, held=both, left=both, **steps)
         return Level(None, None, **steps)
 
     low_both = array(1, rows, vmem, True, False)
@@ -1211,6 +1232,7 @@
             (lent, VM),
             (filled, VM),
             (kept, VM),
+            (rest_weights, VM),
         ],
         [
             (half, VM),

time: 31.2 us -> 31.6 us (1.013); the launches traced: 31 us -> 31 us
  Pallas kernels: 14.7 us -> 15.4 us
  waiting for transfers between devices: 6.11 us -> 5.73 us
    pallas_call x8 -> x9, Pallas kernels: 14.7 us -> 15.4 us  [run_kernel(): pl.pallas_call(kernel, out_shape=[leaf for leaves, _ in out_trees for lea...]
    ppermute x7, waiting for transfers between devices: 6.11 us -> 5.73 us  [moved(): return lax.ppermute(value, ('patch', 'level'), pairs)]
  transfers between devices with their start and end apart: 7 -> 7, of which waited for: 4 -> 3; matrix products, arithmetic and copies ran while one was open for 0% -> 0% of each run, Pallas kernels for 33% -> 35%
where the time goes in v12:
time: 31.6 us; the launch traced here: 31 us
  Pallas kernels  15.4 us (49%)
  starting transfers between devices  8.11 us (26%)
  waiting for transfers between devices  5.73 us (18%)
  local copies, waits for them, and re-layouts  0.95 us (3%)
  between operations  0.78 us (2%)
    pallas_call x9, Pallas kernels, run_kernel(): pl.pallas_call(kernel, out_shape=[leaf for leaves, _ in out_trees for lea...  15.4 us
    ppermute x7, starting transfers between devices, moved(): return lax.ppermute(value, ('patch', 'level'), pairs)  8.11 us
    ppermute x7, waiting for transfers between devices, moved(): return lax.ppermute(value, ('patch', 'level'), pairs)  5.73 us
    unnamed x12, local copies, waits for them, and re-layouts  0.95 us
  transfers between devices with their start and end apart: 7, of which 3 were waited for; matrix products, arithmetic and copies ran while one was open for 0% of the time, Pallas kernels for 35%

profile of v12, /device:TPU:21, one launch (start us, length us, event | category | flops | bytes accessed | tf_op | source)
XLA Modules:
  0.0 31.0 jit_solution(9524030926738855039)
XLA Ops:
  0.6 0.7 %collective-permute-start = (bf16[8,2,128,128]{3,2,1,0:T(8,128)(2,1)}, bf16[8,2,128,128]{3,2,1,0:T(8,128)(2,1)S(1)}, u32[]{:S(2)}, u32[]{:S(2)}) collective-permute-start(bf16[8,2,128,128]{3,2,1,0:T(8,128)(2,1)} %bitcast.6), channel_id=1, source_target_pairs={{0,1},{1,0},{2,3},{3,2},{4,5},{5,4},{6,7},{7,6},{8,9},{9,8},{10,11... | collective-permute-start | bytes 1572872 | tf_op jit(solution)/shard_map/ppermute | solution.py:1120
  1.4 0.1 collective-permute-start.1
  1.5 0.4 %collective-permute-start.2 = (bf16[8,128,128]{2,1,0:T(8,128)(2,1)}, bf16[8,128,128]{2,1,0:T(8,128)(2,1)S(1)}, u32[]{:S(2)}, u32[]{:S(2)}) collective-permute-start(bf16[8,128,128]{2,1,0:T(8,128)(2,1)} %bitcast.16), channel_id=1, source_target_pairs={{0,1},{1,0},{2,3},{3,2},{4,5},{5,4},{6,7},{7,6},{8,9},{9,8},{10,11... | collective-permute-start | bytes 786440 | tf_op jit(solution)/shard_map/ppermute | solution.py:1120
  1.9 2.2 %shard_map.68.refs_0_ = f32[128,128]{1,0:T(8,128)} custom-call(bf16[8,2,128,128]{3,2,1,0:T(8,128)(2,1)} %bitcast.7, f32[8,128,128]{2,1,0:T(8,128)} %bitcast.12, bf16[8,128,128]{2,1,0:T(8,128)(2,1)} %bitcast.17), custom_call_target="tpu_custom_call" | custom-call | tf_op jit(solution)/shard_map/pallas_call | solution.py:1097
  4.1 0.0 copy-start
  4.1 0.0 copy-start.1
  4.1 0.0 copy-start.2
  4.1 0.1 collective-permute-done.2.refs_3_.refs_5_.refs_6_
  4.2 0.0 collective-permute-done.refs_1_.refs_3_.refs_4_
  4.2 0.0 collective-permute-done.1.refs_2_.refs_4_.refs_5_
  4.2 0.0 copy-start.4
  4.3 0.9 %copy-done.4 = f32[128,128]{1,0:T(8,128)S(1)} copy-done((f32[128,128]{1,0:T(8,128)S(1)}, f32[128,128]{1,0:T(8,128)}, u32[]{:S(2)}) %copy-start.4) | copy-done | bytes 65560
  5.2 0.4 %shard_map.69 = f32[128,128]{1,0:T(8,128)S(1)} custom-call(f32[128,128]{1,0:T(8,128)S(1)} %copy-done.4, bf16[8,2,128,128]{3,2,1,0:T(8,128)(2,1)S(1)} %collective-permute-done.refs_1_.refs_3_.refs_4_, f32[8,128,128]{2,1,0:T(8,128)S(1)} %collective-permute-done.1.refs_2_.refs_4_.refs_5_, bf16[8,128,128]{2,1,0:T(8,128)(2,1)S(1)} %collective-permute-done.2.refs_3_.refs_5_.refs_6_), custom_call_target="tpu_custom_call" | custom-call | tf_op jit(solution)/shard_map/pallas_call | solution.py:1097
  5.6 0.0 copy-start.5
  5.6 2.2 %collective-permute-start.3 = (f32[128,128]{1,0:T(8,128)S(1)}, f32[128,128]{1,0:T(8,128)S(1)}, u32[]{:S(2)}, u32[]{:S(2)}) collective-permute-start(f32[128,128]{1,0:T(8,128)S(1)} %shard_map.69), channel_id=1, source_target_pairs={{0,5},{2,7},{4,9},{5,0},{6,11},{7,2},{8,13},{9,4},{10,15},{11,6},{... | collective-permute-start | bytes 196616 | tf_op jit(solution)/shard_map/ppermute | solution.py:1120
  7.8 4.1 %collective-permute-done.3.refs_6_.refs_7_ = f32[128,128]{1,0:T(8,128)S(1)} collective-permute-done((f32[128,128]{1,0:T(8,128)S(1)}, f32[128,128]{1,0:T(8,128)S(1)}, u32[]{:S(2)}, u32[]{:S(2)}) %collective-permute-start.3) | collective-permute-done | bytes 65568 | tf_op jit(solution)/shard_map/ppermute | solution.py:1120
  11.9 0.0 copy-done
  11.9 0.0 copy-done.1
  11.9 0.0 copy-done.2
  11.9 0.8 %shard_map.70.refs_8_ = bf16[736,128]{1,0:T(8,128)(2,1)S(1)} custom-call(bf16[8,2,128,128]{3,2,1,0:T(8,128)(2,1)S(1)} %bitcast.8, f32[8,128,128]{2,1,0:T(8,128)S(1)} %bitcast.13, bf16[8,128,128]{2,1,0:T(8,128)(2,1)S(1)} %bitcast.18, bf16[8,2,128,128]{3,2,1,0:T(8,128)(2,1)S(1)} %collective-permute-done.refs_1_.refs_3_.refs_4_, ...), custom_call_target="tpu_custom_call" | custom-call | tf_op jit(solution)/shard_map/pallas_call | solution.py:1097
  12.7 2.2 %collective-permute-start.5 = (bf16[736,128]{1,0:T(8,128)(2,1)S(1)}, bf16[736,128]{1,0:T(8,128)(2,1)S(1)}, u32[]{:S(2)}, u32[]{:S(2)}) collective-permute-start(bf16[736,128]{1,0:T(8,128)(2,1)S(1)} %shard_map.70.refs_8_), channel_id=1, source_target_pairs={{0,2},{1,3},{4,6},{5,7},{8,10},{9,11},{12,14},{13,15},{16,18},{17,... | collective-permute-start | bytes 565256 | tf_op jit(solution)/shard_map/ppermute | solution.py:1120
  14.9 0.0 copy-done.5
  14.9 0.6 %shard_map.71 = (f32[3,272,128]{2,1,0:T(8,128)S(1)}, f32[2,3,256,128]{3,2,1,0:T(8,128)S(1)}, f32[3,256,128]{2,1,0:T(8,128)S(1)}, f32[5,144,128]{2,1,0:T(8,128)S(...) custom-call(s32[4,8]{1,0:T(4,128)S(1)} %copy-done.5, bf16[8,2,128,128]{3,2,1,0:T(8,128)(2,1)S(1)} %bitcast.9, ...), custom_call_target="tpu_custom_call" | custom-call | tf_op jit(solution)/shard_map/pallas_call | solution.py:1097
  15.5 1.7 %shard_map.72 = (f32[272,128]{1,0:T(8,128)S(1)}, f32[2,3,256,128]{3,2,1,0:T(8,128)S(1)}, f32[2,3,256,128]{3,2,1,0:T(8,128)S(1)}, f32[2,5,128,128]{3,2,1,0:T(8,12...) custom-call(s32[4,8]{1,0:T(4,128)S(1)} %copy-done.5, ...), custom_call_target="tpu_custom_call" | custom-call | tf_op jit(solution)/shard_map/pallas_call | solution.py:1097
  17.2 1.3 %collective-permute-start.4 = (f32[272,128]{1,0:T(8,128)S(1)}, f32[272,128]{1,0:T(8,128)S(1)}, u32[]{:S(2)}, u32[]{:S(2)}) collective-permute-start(f32[272,128]{1,0:T(8,128)S(1)} %get-tuple-element.37.refs_1_), channel_id=1, source_target_pairs={{2,0},{3,1},{6,4},{7,5},{10,8},{11,9},{14,12},{15,13},{18,16},{19,... | collective-permute-start | bytes 417800 | tf_op jit(solution)/shard_map/ppermute | solution.py:1120
  18.5 1.7 %shard_map.73 = (f32[2,1,1024,128]{3,2,1,0:T(8,128)S(1)}, f32[2,2,512,128]{3,2,1,0:T(8,128)S(1)}) custom-call(s32[4,8]{1,0:T(4,128)S(1)} %copy-done.5, f32[1,1040,128]{2,1,0:T(8,128)S(1)} %get-tuple-element.38.refs_1_.refs_3_.refs_2_, f32[2,1,1024,128]{3,2,1,0:T(8,128)S(1)} %get-tuple-element.39.refs_2_.refs_4_.refs_3_, ...), custom_call_target="tpu_custom_call" | custom-call | tf_op jit(solution)/shard_map/pallas_call | solution.py:1097
  20.2 0.0 collective-permute-done.5.refs_2_
  20.2 4.8 %shard_map.74 = (f32[4,2,128,128]{3,2,1,0:T(8,128)S(1)}, f32[4,2,128,128]{3,2,1,0:T(8,128)S(1)}, f32[2,512,128]{2,1,0:T(8,128)S(1)}, f32[2,1,1024,128]{3,2,1,0:T(8,128)S(1)}) custom-call(s32[4,8]{1,0:T(4,128)S(1)} %copy-done.5, f32[272,128]{1,0:T(8,128)S(1)} %get-tuple-element.37.refs_1_, bf16[736,128]{1,0:T(8,128)(2,1)S(1)} %collective-permute-done.5.refs_2_, ...), custom_call_target="tpu_custom_call" | custom-call | tf_op jit(solution)/shard_map/pallas_call | solution.py:1097
  25.0 0.0 collective-permute-done.4.refs_1_
  25.0 0.0 copy-start.3
  25.0 2.0 %shard_map.75 = (f32[4,2,128,128]{3,2,1,0:T(8,128)S(1)}, f32[4,2,128,128]{3,2,1,0:T(8,128)S(1)}) custom-call(s32[4,8]{1,0:T(4,128)S(1)} %copy-done.5, f32[272,128]{1,0:T(8,128)S(1)} %collective-permute-done.4.refs_1_, f32[1,1040,128]{2,1,0:T(8,128)S(1)} %get-tuple-element.38.refs_1_.refs_3_.refs_2_, ...), custom_call_target="tpu_custom_call" | custom-call | tf_op jit(solution)/shard_map/pallas_call | solution.py:1097
  27.0 1.2 %collective-permute-start.6 = (f32[4,2,128,128]{3,2,1,0:T(8,128)S(1)}, f32[4,2,128,128]{3,2,1,0:T(8,128)S(1)}, u32[]{:S(2)}, u32[]{:S(2)}) collective-permute-start(f32[4,2,128,128]{3,2,1,0:T(8,128)S(1)} %get-tuple-element.57), channel_id=1, source_target_pairs={{0,1},{1,0},{2,3},{3,2},{4,5},{5,4},{6,7},{7,6},{8,9},{9,8},{10,11... | collective-permute-start | bytes 1572872 | tf_op jit(solution)/shard_map/ppermute | solution.py:1120
  28.2 1.5 %collective-permute-done.6.refs_1_ = f32[4,2,128,128]{3,2,1,0:T(8,128)S(1)} collective-permute-done((f32[4,2,128,128]{3,2,1,0:T(8,128)S(1)}, f32[4,2,128,128]{3,2,1,0:T(8,128)S(1)}, u32[]{:S(2)}, u32[]{:S(2)}) %collective-permute-start.6) | collective-permute-done | bytes 524320 | tf_op jit(solution)/shard_map/ppermute | solution.py:1120
  29.7 0.0 copy-done.3
  29.7 1.2 %shard_map.76 = (f32[8,2,128,128]{3,2,1,0:T(8,128)}, bf16[8,128,128]{2,1,0:T(8,128)(2,1)}) custom-call(f32[4,2,128,128]{3,2,1,0:T(8,128)S(1)} %get-tuple-element.56.refs_0_, f32[4,2,128,128]{3,2,1,0:T(8,128)S(1)} %collective-permute-done.6.refs_1_, bf16[8,2,128,128]{3,2,1,0:T(8,128)(2,1)S(1)} %bitcast.22, bf16[8,128,128]{2,1,0:T(8,128)(2,1)S(1)} %bitcast.21), custom_call_target="tpu_custom_call" | custom-call | tf_op jit(solution)/shard_map/pallas_call | solution.py:1097
Async XLA Ops:
  0.6 3.6 %collective-permute-start = (bf16[8,2,128,128]{3,2,1,0:T(8,128)(2,1)}, bf16[8,2,128,128]{3,2,1,0:T(8,128)(2,1)S(1)}, u32[]{:S(2)}, u32[]{:S(2)}) collective-permute-start(bf16[8,2,128,128]{3,2,1,0:T(8,128)(2,1)} %bitcast.6), channel_id=1, source_target_pairs={{0,1},{1,0},{2,3},{3,2},{4,5},{5,4},{6,7},{7,6},{8,9},{9,8},{10,11... | collective-permute-start | bytes 1572872 | tf_op jit(solution)/shard_map/ppermute | solution.py:1120
  1.4 2.9 %collective-permute-start.1 = (f32[8,128,128]{2,1,0:T(8,128)}, f32[8,128,128]{2,1,0:T(8,128)S(1)}, u32[]{:S(2)}, u32[]{:S(2)}) collective-permute-start(f32[8,128,128]{2,1,0:T(8,128)} %bitcast.11), channel_id=1, source_target_pairs={{0,1},{1,0},{2,3},{3,2},{4,5},{5,4},{6,7},{7,6},{8,9},{9,8},{10,11... | collective-permute-start | bytes 1572872 | tf_op jit(solution)/shard_map/ppermute | solution.py:1120
  1.5 2.8 %collective-permute-start.2 = (bf16[8,128,128]{2,1,0:T(8,128)(2,1)}, bf16[8,128,128]{2,1,0:T(8,128)(2,1)S(1)}, u32[]{:S(2)}, u32[]{:S(2)}) collective-permute-start(bf16[8,128,128]{2,1,0:T(8,128)(2,1)} %bitcast.16), channel_id=1, source_target_pairs={{0,1},{1,0},{2,3},{3,2},{4,5},{5,4},{6,7},{7,6},{8,9},{9,8},{10,11... | collective-permute-start | bytes 786440 | tf_op jit(solution)/shard_map/ppermute | solution.py:1120
  4.1 7.8 %copy-start = (bf16[1,8,2,128,128]{4,3,2,1,0:T(8,128)(2,1)S(1)}, bf16[1,8,2,128,128]{4,3,2,1,0:T(8,128)(2,1)}, u32[]{:S(2)}) copy-start(bf16[1,8,2,128,128]{4,3,2,1,0:T(8,128)(2,1)} %param.5) | copy-start | bytes 1572868
  4.1 7.8 %copy-start.1 = (f32[1,8,128,128]{3,2,1,0:T(8,128)S(1)}, f32[1,8,128,128]{3,2,1,0:T(8,128)}, u32[]{:S(2)}) copy-start(f32[1,8,128,128]{3,2,1,0:T(8,128)} %param.7) | copy-start | bytes 1572868
  4.1 7.8 %copy-start.2 = (bf16[1,8,128,128]{3,2,1,0:T(8,128)(2,1)S(1)}, bf16[1,8,128,128]{3,2,1,0:T(8,128)(2,1)}, u32[]{:S(2)}) copy-start(bf16[1,8,128,128]{3,2,1,0:T(8,128)(2,1)} %param.8) | copy-start | bytes 786436
  4.2 0.9 %copy-start.4 = (f32[128,128]{1,0:T(8,128)S(1)}, f32[128,128]{1,0:T(8,128)}, u32[]{:S(2)}) copy-start(f32[128,128]{1,0:T(8,128)} %shard_map.68.refs_0_) | copy-start | bytes 196612
  5.6 9.3 %copy-start.5 = (s32[4,8]{1,0:T(4,128)S(1)}, s32[4,8]{1,0:T(4,128)}, u32[]{:S(2)}) copy-start(s32[4,8]{1,0:T(4,128)} %refs_0_.9) | copy-start | bytes 388
  5.6 6.3 %collective-permute-start.3 = (f32[128,128]{1,0:T(8,128)S(1)}, f32[128,128]{1,0:T(8,128)S(1)}, u32[]{:S(2)}, u32[]{:S(2)}) collective-permute-start(f32[128,128]{1,0:T(8,128)S(1)} %shard_map.69), channel_id=1, source_target_pairs={{0,5},{2,7},{4,9},{5,0},{6,11},{7,2},{8,13},{9,4},{10,15},{11,6},{... | collective-permute-start | bytes 196616 | tf_op jit(solution)/shard_map/ppermute | solution.py:1120
  12.7 7.5 %collective-permute-start.5 = (bf16[736,128]{1,0:T(8,128)(2,1)S(1)}, bf16[736,128]{1,0:T(8,128)(2,1)S(1)}, u32[]{:S(2)}, u32[]{:S(2)}) collective-permute-start(bf16[736,128]{1,0:T(8,128)(2,1)S(1)} %shard_map.70.refs_8_), channel_id=1, source_target_pairs={{0,2},{1,3},{4,6},{5,7},{8,10},{9,11},{12,14},{13,15},{16,18},{17,... | collective-permute-start | bytes 565256 | tf_op jit(solution)/shard_map/ppermute | solution.py:1120
  17.2 7.8 %collective-permute-start.4 = (f32[272,128]{1,0:T(8,128)S(1)}, f32[272,128]{1,0:T(8,128)S(1)}, u32[]{:S(2)}, u32[]{:S(2)}) collective-permute-start(f32[272,128]{1,0:T(8,128)S(1)} %get-tuple-element.37.refs_1_), channel_id=1, source_target_pairs={{2,0},{3,1},{6,4},{7,5},{10,8},{11,9},{14,12},{15,13},{18,16},{19,... | collective-permute-start | bytes 417800 | tf_op jit(solution)/shard_map/ppermute | solution.py:1120
  25.0 4.8 %copy-start.3 = (bf16[1,8,2,128,128]{4,3,2,1,0:T(8,128)(2,1)S(1)}, bf16[1,8,2,128,128]{4,3,2,1,0:T(8,128)(2,1)}, u32[]{:S(2)}) copy-start(bf16[1,8,2,128,128]{4,3,2,1,0:T(8,128)(2,1)} %param.6) | copy-start | bytes 1572868
  27.0 2.7 %collective-permute-start.6 = (f32[4,2,128,128]{3,2,1,0:T(8,128)S(1)}, f32[4,2,128,128]{3,2,1,0:T(8,128)S(1)}, u32[]{:S(2)}, u32[]{:S(2)}) collective-permute-start(f32[4,2,128,128]{3,2,1,0:T(8,128)S(1)} %get-tuple-element.57), channel_id=1, source_target_pairs={{0,1},{1,0},{2,3},{3,2},{4,5},{5,4},{6,7},{7,6},{8,9},{9,8},{10,11... | collective-permute-start | bytes 1572872 | tf_op jit(solution)/shard_map/ppermute | solution.py:1120
